TPU v7x, 32 devices: a whole 2x2x4 slice. The times are simulated.
32 devices in a mesh: groups: 2 (over y), expert: 4 (over x, core), inner: 4 (over z).
Axes of the slice: x: 2, y: 2, z: 4, core: 2. Of those that a mesh axis runs over, the one named last changes fastest.
Arguments:
- queries: bfloat16 [256, 8192], P(('groups', 'expert', 'inner')), parts along dimension 0, may hold values from -6 to 6
- new_key_value: bfloat16 [256, 1024], P(('groups', 'expert', 'inner')), parts along dimension 0, may hold values from -6 to 6
- cached_key_value: bfloat16 [32, 8, 192, 1024], P(('groups', 'expert', 'inner')), parts along dimension 0, may hold values from -6 to 6
- parents: int32 [32, 8], P(('groups', 'expert', 'inner')), parts along dimension 0, may hold values from 0 to 7
- hidden: bfloat16 [256, 4096], P(('groups', 'expert', 'inner')), parts along dimension 0, may hold values from -6 to 6
- routes: int32 [256, 2], P(('groups', 'expert', 'inner')), parts along dimension 0, may hold values from 0 to 7, all different within a row; in each aligned block of 8 rows (0 to 7, 8 to 15, ...) at most 3 rows name the same one
- gate_values: bfloat16 [256, 2], P(('groups', 'expert', 'inner')), parts along dimension 0, may hold values from 0.19921875 to 1
- gate_up_weight: bfloat16 [8, 2, 4096, 1536], P('expert', None, 'inner'), may hold values from -0.09375 to 0.09375
- down_weight: bfloat16 [8, 1536, 4096], P('expert', None, 'inner'), may hold values from -0.15625 to 0.15625
Outputs:
- attended: bfloat16 [256, 8192], P(('groups', 'expert', 'inner')), parts along dimension 0
- expert_out: bfloat16 [256, 4096], P(('groups', 'expert', 'inner')), parts along dimension 0
There are 2 independent parts, one for each index of `groups`. A program takes and returns all parts, laid end to end along the dimension named above; an argument that names none is the same for every part. Nothing has to cross between parts.
Inputs may be any that keep to these rules, and one draw needn't show every extreme that they name: `routes`: each row names 2 different experts; within the 8 rows of one device no expert is named by more than 3 rows, and in every draw some expert is named by exactly 3 rows of some device.
All inputs are finite; a program needn't handle non-finite values.
Results may differ from a plain program's by a relative error of at most 0.005.
Values may be sent and summed in bfloat16 or wider, within the bound.
No kernel may reach another device: no remote copies, remote signals or barrier semaphores. Data moves between devices by JAX's collectives and lax.ppermute only.
A program may use at most 128 MiB of HBM per device.

v0:
```python
import math

import jax
import jax.numpy as jnp
from jax import lax
from jax.sharding import PartitionSpec as P

QUERY_HEADS = 64
KEY_HEADS = 4
HEAD_SIZE = 128
CAP = 3
CACHED_LENGTH = 192


def attend_local(queries, new_key_value, cached_key_value, parents):
    query_group = QUERY_HEADS // KEY_HEADS
    score_scale = 1.0 / math.sqrt(HEAD_SIZE)
    flip_count = queries.shape[0]
    selected_parent = jax.vmap(lambda block, picks: jnp.take(block, picks, axis=0))(
        cached_key_value, parents
    )
    selected_parent = selected_parent.reshape(flip_count, CACHED_LENGTH, 2, KEY_HEADS, HEAD_SIZE)
    keys = selected_parent[:, :, 0]
    value_rows = selected_parent[:, :, 1]
    new_token_pairs_all = new_key_value.reshape(flip_count, 2, KEY_HEADS, HEAD_SIZE)
    query_vector = queries.reshape(flip_count, KEY_HEADS, query_group, HEAD_SIZE)
    scores = (
        jnp.einsum("bkgd,blkd->bkgl", query_vector, keys, preferred_element_type=jnp.float32)
        * score_scale
    )
    beam_private = (
        jnp.einsum(
            "wpaf,wpf->wpa",
            query_vector,
            new_token_pairs_all[:, 0],
            preferred_element_type=jnp.float32,
        )
        * score_scale
    )
    upper = jnp.maximum(jnp.max(scores, axis=-1), beam_private)
    expo = jnp.exp(scores - upper[..., None])
    own_expo = jnp.exp(beam_private - upper)
    total = jnp.sum(expo, axis=-1) + own_expo
    probs = (expo / total[..., None]).astype(jnp.bfloat16)
    own_prob = (own_expo / total).astype(jnp.bfloat16)
    result = jnp.einsum("bkgl,blkd->bkgd", probs, value_rows, preferred_element_type=jnp.float32)
    result = (
        result
        + own_prob.astype(jnp.float32)[..., None]
        * new_token_pairs_all[:, 1].astype(jnp.float32)[:, :, None, :]
    )
    return result.reshape(flip_count, QUERY_HEADS * HEAD_SIZE).astype(jnp.bfloat16)


def place_slots(member):
    ranks = jnp.cumsum(member, axis=1) - 1.0
    slot_ids = jnp.arange(CAP, dtype=jnp.float32)
    hits = (ranks[:, None, :, :] == slot_ids[None, :, None, None]).astype(jnp.float32) * member[
        :, None, :, :
    ]
    return jnp.swapaxes(hits, 2, 3)


def expert_block(slots, gate_up, down):
    summed = lax.psum_scatter(
        jnp.einsum("sxd,xkdf->sxkf", slots, gate_up, preferred_element_type=jnp.float32),
        "inner",
        scatter_dimension=0,
        tiled=True,
    )
    active = (jax.nn.silu(summed[:, :, 0]) * summed[:, :, 1]).astype(jnp.bfloat16)
    return jnp.einsum(
        "sxf,xfd->sxd",
        lax.all_gather(active, "inner", axis=0, tiled=True),
        down,
        preferred_element_type=jnp.float32,
    )


def body(
    queries,
    new_key_value,
    cached_key_value,
    parents,
    hidden,
    routes,
    gate_values,
    gate_up_weight,
    down_weight,
):
    attended = attend_local(queries, new_key_value, cached_key_value, parents)
    owners = lax.axis_size("expert")
    local_experts = gate_up_weight.shape[0]
    all_experts = owners * local_experts
    local_rows = hidden.shape[0]
    slice_width = gate_up_weight.shape[2]
    labels = jnp.arange(all_experts, dtype=jnp.int32)
    matches = routes[:, :, None] == labels[None, None, :]
    gate_float = gate_values.astype(jnp.float32)[:, :, None]
    shares = jnp.sum(jnp.where(matches, gate_float, jnp.zeros_like(gate_float)), axis=1)
    all_rows, all_shares = (
        lax.all_gather(hidden, ("expert", "inner"), axis=0, tiled=True),
        lax.all_gather(shares.astype(jnp.bfloat16), ("expert", "inner"), axis=0, tiled=True),
    )
    sources = all_rows.shape[0] // local_rows
    mine = lax.dynamic_slice_in_dim(
        all_shares, lax.axis_index("expert") * local_experts, local_experts, 1
    ).astype(jnp.float32)
    mine = mine.reshape(sources, local_rows, local_experts)
    placing = place_slots(jnp.where(mine > 0.0, 1.0, 0.0))
    row_slices = lax.dynamic_slice_in_dim(
        all_rows, lax.axis_index("inner") * slice_width, slice_width, 1
    )
    row_slices = row_slices.reshape(sources, local_rows, slice_width)
    slots = jnp.einsum(
        "icxj,ijd->icxd",
        placing.astype(jnp.bfloat16),
        row_slices,
        preferred_element_type=jnp.float32,
    ).astype(jnp.bfloat16)
    outputs = expert_block(
        slots.reshape(-1, local_experts, slice_width), gate_up_weight, down_weight
    )
    outputs = outputs.reshape(sources, CAP, local_experts, slice_width)
    weighting = placing * jnp.swapaxes(mine, 1, 2)[:, None, :, :]
    term = jnp.einsum("icxj,icxd->ijd", weighting, outputs, precision=lax.Precision.HIGHEST)
    term = term.reshape(sources * local_rows, slice_width)
    partial_rows = lax.psum_scatter(term, "expert", scatter_dimension=0, tiled=True)
    combined = lax.all_to_all(
        partial_rows.astype(jnp.bfloat16), "inner", split_axis=0, concat_axis=1, tiled=True
    ).astype(partial_rows.dtype)
    return (attended, combined.astype(jnp.bfloat16))


def solution(mesh):
    return jax.shard_map(
        body,
        mesh=mesh,
        in_specs=(
            P(("groups", "expert", "inner"), None),
            P(("groups", "expert", "inner"), None),
            P(("groups", "expert", "inner"), None, None, None),
            P(("groups", "expert", "inner"), None),
            P(("groups", "expert", "inner"), None),
            P(("groups", "expert", "inner"), None),
            P(("groups", "expert", "inner"), None),
            P("expert", None, "inner", None),
            P("expert", None, "inner"),
        ),
        out_specs=(P(("groups", "expert", "inner"), None), P(("groups", "expert", "inner"), None)),
        check_vma=False,
    )
```

profile of v0, /device:TPU:0, one launch (start us, length us, event | category | flops | bytes accessed | tf_op | source)
XLA Modules:
  0.0 178.2 jit_solution(17609418759745534086)
XLA Ops:
  7.2 0.0 copy-start
  7.2 0.0 all-gather.2.cloned.1.call-start
  7.2 0.7 all-gather.2.cloned.1.call-update
  7.9 0.0 all-reduce.3.cloned.1.call-start
  8.0 0.8 convert_element_type.54
  8.8 0.8 select_reduce_fusion
  9.5 34.2 %all_gather.9 = bf16[128,8]{1,0:T(8,128)(2,1)S(1)} all-gather(bf16[8,8]{1,0:T(8,128)(2,1)S(1)} %select_reduce_fusion), channel_id=1, replica_groups=mesh['groups'=2,'expert'=4,'inner'=4] {'expert','inner'}, dimensions={0}, use_global_device_ids=true | all-gather | bytes 2176 | tf_op jit(solution)/shard_map/all_gather | solution.py:103
  43.7 0.1 fusion.38
  43.8 0.2 copy.112
  44.0 0.3 reduce_window_sum.11
  44.4 0.7 fusion.33
  45.1 5.9 %all-gather.2.cloned.1.call-done = bf16[128,4096]{1,0:T(8,128)(2,1)} async-done(((bf16[8,4096]{1,0:T(8,128)(2,1)}), bf16[128,4096]{1,0:T(8,128)(2,1)}) %all-gather.2.cloned.1.call-update) | async-done | bytes 1048592 | tf_op jit(solution)/shard_map/all_gather | solution.py:102
  51.0 1.2 convolution_convert_fusion
  52.1 0.2 copy.67
  52.3 6.8 %convolution_bitcast_fusion = f32[48,2,2,1536]{3,0,2,1:T(8,128)S(1)} fusion(bf16[2,2,1024,1536]{3,2,1,0:T(8,128)(2,1)} %param.16, bf16[48,2,1024,1]{2,1,0,3:T(2,128)(2,1)S(1)} %bitcast.93), kind=kOutput, calls=%fused_computation.2 | convolution fusion | flops 603979776 | bytes 13959168 | tf_op jit(solution)/shard_map/sxd,xkdf->sxkf/dot_general | solution.py:66
  59.1 2.0 %copy.69 = f32[48,2,2,1536]{3,2,1,0:T(2,128)} copy(f32[48,2,2,1536]{3,0,2,1:T(8,128)S(1)} %convolution_bitcast_fusion) | data formatting | bytes 2359296 | tf_op jit(solution)/shard_map/sxd,xkdf->sxkf/transpose | solution.py:66
  61.1 0.0 all-reduce.3.cloned.1.call-update
  61.1 0.0 reduce-scatter.2.cloned.1.call-start
  61.2 0.0 copy-done
  61.2 2.4 %gather_fusion = bf16[8,192,1024]{2,1,0:T(8,128)(2,1)} fusion(bf16[1,8,192,1024]{3,2,1,0:T(8,128)(2,1)S(1)} %copy-done, s32[8]{0:T(128)S(1)} %or_bitcast_fusion), kind=kCustom, calls=%fused_computation | custom fusion | bytes 6291520 | tf_op jit(solution)/shard_map/vmap(jit(_take))/gather | solution.py:19
  63.6 6.1 %gather.7 = bf16[8,192,2,4,128]{4,3,2,1,0:T(4,128)(2,1)} reshape(bf16[8,192,1024]{2,1,0:T(8,128)(2,1)} %gather_fusion) | data formatting | bytes 6291456 | tf_op jit(solution)/shard_map/vmap(jit(_take))/gather | solution.py:19
  69.7 0.1 fusion.37
  69.8 0.2 copy.66
  70.0 0.0 copy-done.5
  70.0 0.6 dynamic-slice
  71.2 0.0 copy-done.4
  71.2 0.0 copy-start.3
  71.2 2.4 %copy_select_fusion = bf16[8,192,2,4,128]{4,1,3,0,2:T(8,128)(2,1)S(1)} fusion(bf16[8,192,2,4,128]{4,3,2,1,0:T(4,128)(2,1)} %gather.7, pred[8]{0:T(512)(128)(4,1)S(1)} %and_bitcast_fusion), kind=kLoop, calls=%fused_computation.1 | loop fusion | flops 1572864 | bytes 6291464 | tf_op jit(solution)/shard_map/vmap(jit(_take))/select_n | solution.py:19
  73.6 1.6 copy-done.1
  75.3 1.7 fusion.36
  77.0 39.1 %all-reduce.3.cloned.1.call-done = f32[48,2,2,1536]{3,2,1,0:T(2,128)} async-done(((f32[48,2,2,1536]{3,2,1,0:T(2,128)}), f32[48,2,2,1536]{3,2,1,0:T(2,128)}) %all-reduce.3.cloned.1.call-update) | async-done | bytes 1179664
  116.1 1.3 constant_dynamic-slice_fusion
  117.4 0.2 fusion.15
  117.6 13.9 %all_gather.11 = bf16[48,2,1536]{2,1,0:T(2,128)(2,1)S(1)} all-gather(bf16[12,2,1536]{2,1,0:T(2,128)(2,1)S(1)} %fusion.15), channel_id=1, replica_groups=mesh['groups'=2,'expert'=4,'inner'=4] {'inner'}, dimensions={0}, use_global_device_ids=true | all-gather | bytes 368640 | tf_op jit(solution)/shard_map/all_gather | solution.py:74
  131.6 4.0 %convolution_bitcast_fusion.2 = f32[48,2,1024]{2,0,1:T(8,128)S(1)} fusion(bf16[2,1536,1024]{2,1,0:T(8,128)(2,1)} %param.17, bf16[48,2,1536]{2,1,0:T(2,128)(2,1)S(1)} %all_gather.11), kind=kOutput, calls=%fused_computation.10 | convolution fusion | flops 301989888 | bytes 6979584 | tf_op jit(solution)/shard_map/sxf,xfd->sxd/dot_general | solution.py:72
  135.6 0.3 copy.72
  135.9 1.8 %convolution_bitcast_fusion.1 = f32[128,1024]{1,0:T(8,128)} fusion(f32[16,3,2,1024]{3,2,1,0:T(2,128)S(1)} %bitcast.92, f32[16,2,8]{2,1,0:T(2,128)S(1)} %copy.66, f32[16,2,8]{2,1,0:T(2,128)S(1)} %copy.65, f32[16,2,8]{2,1,0:T(2,128)S(1)} %copy.64), kind=kOutput, calls=%fused_computation.9 | convolution fusion | flops 9439488 | bytes 920576 | tf_op jit(solution)/shard_map/icxj,icxd->ijd/dot_general | solution.py:126
  137.7 0.0 reduce-scatter.2.cloned.1.call-update
  137.7 0.0 copy-done.2
  137.7 0.2 fusion.16
  137.9 1.3 fusion.7
  139.3 19.9 %reduce-scatter.2.cloned.1.call-done = f32[32,1024]{1,0:T(8,128)} async-done(((f32[128,1024]{1,0:T(8,128)}), f32[32,1024]{1,0:T(8,128)}) %reduce-scatter.2.cloned.1.call-update) | async-done | bytes 131088 | tf_op jit(solution)/shard_map/reduce_scatter | solution.py:128
  159.2 1.5 convert_bitcast_fusion
  160.7 4.6 %all-to-all-start = ((bf16[4,8,1024]{2,1,0:T(8,128)(2,1)}), bf16[4,8,1024]{2,1,0:T(8,128)(2,1)S(1)}, u32[]{:S(2)}, u32[]{:S(2)}) async-start(bf16[4,8,1024]{2,1,0:T(8,128)(2,1)} %convert_bitcast_fusion), calls=%async_computation.1 | async-start | bytes 131072 | tf_op jit(solution)/shard_map/all_to_all | solution.py:129
  165.3 2.2 %fusion.5 = bf16[8,4,16,128]{3,2,1,0:T(8,128)(2,1)S(1)} fusion(bf16[8,192,2,4,128]{4,1,3,0,2:T(8,128)(2,1)} %copy-done.1, f32[8,4,16,192]{3,2,1,0:T(8,128)} %get-tuple-element.11, f32[8,4,16]{2,1,0:T(4,128)S(1)} %get-tuple-element.5, f32[8,4,16]{2,1,0:T(4,128)S(1)} %multiply_maximum_fusion, f32[8,4,128]{2,1,0:T(4,128)S(1)} %fusion.27, ...), kind=kOutput, calls=%fused_computation.13 | convolution fusion | flops 25657344 | bytes 2250752 | tf_op jit(solution)/shard_map/bkgl,blkd->bkgd/dot_general | solution.py:46
  167.5 0.8 copy.116
  168.2 2.8 %all-to-all-done = bf16[4,8,1024]{2,1,0:T(8,128)(2,1)S(1)} async-done(((bf16[4,8,1024]{2,1,0:T(8,128)(2,1)}), bf16[4,8,1024]{2,1,0:T(8,128)(2,1)S(1)}, u32[]{:S(2)}, u32[]{:S(2)}) %all-to-all-start) | async-done | bytes 65568 | tf_op jit(solution)/shard_map/all_to_all | solution.py:129
  171.0 0.6 copy.119
  (16 shorter events, 0.1 us)
Async XLA Ops:
  7.2 54.0 %copy-start = (bf16[1,8,192,1024]{3,2,1,0:T(8,128)(2,1)S(1)}, bf16[1,8,192,1024]{3,2,1,0:T(8,128)(2,1)}, u32[]{:S(2)}) copy-start(bf16[1,8,192,1024]{3,2,1,0:T(8,128)(2,1)} %param.11) | copy-start | bytes 9437188
  7.2 43.8 %all-gather.2.cloned.1.call-start = ((), (), s32[]{:S(2)}) async-start(), calls=%async_computation.2 | async-start | bytes 1114112 | tf_op jit(solution)/shard_map/all_gather | solution.py:102
  7.9 108.2 %all-reduce.3.cloned.1.call-start = ((), (), s32[]{:S(2)}) async-start(), calls=%async_computation.4 | async-start | bytes 2359296
  61.1 98.0 %reduce-scatter.2.cloned.1.call-start = ((), (), s32[]{:S(2)}) async-start(), calls=%async_computation.3 | async-start | bytes 655360 | tf_op jit(solution)/shard_map/reduce_scatter | solution.py:128
  63.6 6.3 %copy-start.5 = (u32[32]{0:T(128)S(1)}, u32[32]{0:T(128)}, u32[]{:S(2)}) copy-start(u32[32]{0:T(128)} %constant.76) | copy-start | bytes 388
  63.6 7.6 %copy-start.4 = (s32[1,8]{1,0:T(1,128)S(1)}, s32[1,8]{1,0:T(1,128)}, u32[]{:S(2)}) copy-start(s32[1,8]{1,0:T(1,128)} %param.12) | copy-start | bytes 100
  71.2 4.0 %copy-start.3 = (bf16[8,8192]{1,0:T(8,128)(2,1)S(1)}, bf16[8,8192]{1,0:T(8,128)(2,1)}, u32[]{:S(2)}) copy-start(bf16[8,8192]{1,0:T(8,128)(2,1)} %param.9) | copy-start | bytes 393220
  73.6 1.6 copy-start.1
  131.6 6.1 %copy-start.2 = (bf16[8,1024]{1,0:T(8,128)(2,1)S(1)}, bf16[8,1024]{1,0:T(8,128)(2,1)}, u32[]{:S(2)}) copy-start(bf16[8,1024]{1,0:T(8,128)(2,1)} %param.10) | copy-start | bytes 49156
  160.7 10.3 %all-to-all-start = ((bf16[4,8,1024]{2,1,0:T(8,128)(2,1)}), bf16[4,8,1024]{2,1,0:T(8,128)(2,1)S(1)}, u32[]{:S(2)}, u32[]{:S(2)}) async-start(bf16[4,8,1024]{2,1,0:T(8,128)(2,1)} %convert_bitcast_fusion), calls=%async_computation.1 | async-start | bytes 131072 | tf_op jit(solution)/shard_map/all_to_all | solution.py:129
Sparse Core Ops, SparseCore 0:
  10.2 40.6 all-gather.1
  61.3 54.8 all-reduce.2
  137.8 21.3 reduce-scatter.1
where the time goes:
time: 179 us; the launch traced here: 178 us
  waiting for transfers between devices  68.5 us (38%)
  blocking collectives  48.2 us (27%)
  matrix products  17.8 us (10%)
  local copies, waits for them, and re-layouts  16.3 us (9%)
  between operations  14.6 us (8%)
  other arithmetic  8.19 us (5%)
  starting transfers between devices  4.7 us (3%)
    unnamed x4, waiting for transfers between devices  39.9 us
    all_gather x1, blocking collectives, body(): lax.all_gather(shares.astype(jnp.bfloat16), ('expert', 'inner'), axis=0,...  34.2 us
    reduce_scatter x1, waiting for transfers between devices, body(): lax.psum_scatter(term, 'expert', scatter_dimension=0, tiled=True)  19.9 us
    all_gather x1, blocking collectives, expert_block(): lax.all_gather(active, 'inner', axis=0, tiled=True)  13.9 us
    gather x3, local copies, waits for them, and re-layouts, attend_local(): jnp.take(block, picks, axis=0)  8.5 us
    dot_general x1, matrix products, expert_block(): jnp.einsum('sxd,xkdf->sxkf', slots, gate_up, preferred_element_type=jnp.f...  6.81 us
    all_gather x1, waiting for transfers between devices, body(): lax.all_gather(hidden, ('expert', 'inner'), axis=0, tiled=True)  5.9 us
    all_to_all x1, starting transfers between devices, body(): lax.all_to_all(partial_rows.astype(jnp.bfloat16), 'inner', split_axis=0,...  4.58 us
  transfers between devices with their start and end apart: 4, of which 4 were waited for; matrix products, arithmetic and copies ran while one was open for 12% of the time, Pallas kernels for 0%

commit v1 on v0

v1 whole, which is shorter than its diff:
```python
import functools
import math

import jax
import jax.numpy as jnp
from jax import lax
from jax.experimental import pallas as pl
from jax.experimental.pallas import tpu as pltpu
from jax.sharding import PartitionSpec as P

QUERY_HEADS = 64
KEY_HEADS = 4
HEAD_SIZE = 128
CAP = 3
CAP_PAD = 4


def params(limit, *semantics):
    return pltpu.CompilerParams(
        dimension_semantics=semantics or None, vmem_limit_bytes=limit * 1024 * 1024
    )


def attend_kernel(parents, q_ref, new_ref, cache_ref, out_ref):
    del parents
    group = QUERY_HEADS // KEY_HEADS
    scale = 1.0 / math.sqrt(HEAD_SIZE)
    width = KEY_HEADS * HEAD_SIZE
    q = q_ref[0]
    fresh = new_ref[0].astype(jnp.float32)
    scores, own = [], []
    for k in range(KEY_HEADS):
        qk = q[k * group:(k + 1) * group]
        keys = cache_ref[0, 0, :, k * HEAD_SIZE:(k + 1) * HEAD_SIZE]
        scores.append(
            lax.dot_general(qk, keys, (((1,), (1,)), ((), ())), preferred_element_type=jnp.float32)
        )
        own.append(
            jnp.sum(qk.astype(jnp.float32) * fresh[k:k + 1], axis=-1, keepdims=True)
        )
    scores = jnp.concatenate(scores, axis=0) * scale
    own = jnp.concatenate(own, axis=0) * scale
    upper = jnp.maximum(jnp.max(scores, axis=-1, keepdims=True), own)
    expo = jnp.exp(scores - upper)
    own_expo = jnp.exp(own - upper)
    total = jnp.sum(expo, axis=-1, keepdims=True) + own_expo
    probs = (expo / total).astype(jnp.bfloat16)
    own_prob = (own_expo / total).astype(jnp.bfloat16).astype(jnp.float32)
    for k in range(KEY_HEADS):
        rows = slice(k * group, (k + 1) * group)
        values = cache_ref[0, 0, :, width + k * HEAD_SIZE:width + (k + 1) * HEAD_SIZE]
        result = jnp.dot(probs[rows], values, preferred_element_type=jnp.float32)
        result = result + own_prob[rows] * fresh[KEY_HEADS + k:KEY_HEADS + k + 1]
        out_ref[0, rows] = result.astype(out_ref.dtype)


def attend(queries, new_key_value, cached_key_value, parents):
    rows = queries.shape[0]
    _, beams, length, width = cached_key_value.shape
    out = pl.pallas_call(
        attend_kernel,
        grid_spec=pltpu.PrefetchScalarGridSpec(
            num_scalar_prefetch=1,
            grid=(rows,),
            in_specs=[
                pl.BlockSpec((1, QUERY_HEADS, HEAD_SIZE), lambda r, p: (r, 0, 0)),
                pl.BlockSpec((1, 2 * KEY_HEADS, HEAD_SIZE), lambda r, p: (r, 0, 0)),
                pl.BlockSpec((1, 1, length, width), lambda r, p: (r // beams, p[r], 0, 0)),
            ],
            out_specs=pl.BlockSpec((1, QUERY_HEADS, HEAD_SIZE), lambda r, p: (r, 0, 0)),
        ),
        out_shape=jax.ShapeDtypeStruct((rows, QUERY_HEADS, HEAD_SIZE), jnp.bfloat16),
        compiler_params=params(8),
        cost_estimate=pl.CostEstimate(
            flops=4 * rows * QUERY_HEADS * HEAD_SIZE * length,
            bytes_accessed=2 * rows * length * width,
            transcendentals=rows * QUERY_HEADS * length,
        ),
        name="attend",
    )(
        parents.reshape(rows),
        queries.reshape(rows, QUERY_HEADS, HEAD_SIZE),
        new_key_value.reshape(rows, 2 * KEY_HEADS, HEAD_SIZE),
        cached_key_value,
    )
    return out.reshape(rows, QUERY_HEADS * HEAD_SIZE)


def placing(turned_routes, slots):
    top, rows = turned_routes.shape
    slot = lax.broadcasted_iota(jnp.int32, (slots, rows), 0)
    expert, rank = slot // CAP_PAD, slot % CAP_PAD
    member = jnp.zeros((slots, rows), jnp.float32)
    for t in range(top):
        member = jnp.where(turned_routes[t:t + 1] == expert, 1.0, member)
    before = (
        lax.broadcasted_iota(jnp.int32, (rows, rows), 0)
        < lax.broadcasted_iota(jnp.int32, (rows, rows), 1)
    ).astype(jnp.float32)
    ranks = jnp.dot(member, before, preferred_element_type=jnp.float32)
    return jnp.where(ranks == rank.astype(jnp.float32), member, 0.0)


def dispatch_kernel(routes_ref, hidden_ref, out_ref):
    owners, inner, block, width = out_ref.shape
    place = placing(routes_ref[...], owners * block).astype(jnp.bfloat16)
    for i in range(inner):
        moved = jnp.dot(
            place, hidden_ref[:, i * width:(i + 1) * width], preferred_element_type=jnp.float32
        ).astype(jnp.bfloat16)
        for e in range(owners):
            out_ref[e, i] = moved[e * block:(e + 1) * block]


def combine_kernel(routes_ref, gates_ref, back_ref, out_ref):
    owners, inner, block, width = back_ref.shape
    slots = owners * block
    routes, gates = routes_ref[...], gates_ref[...].astype(jnp.float32)
    place = placing(routes, slots)
    expert = lax.broadcasted_iota(jnp.int32, place.shape, 0) // CAP_PAD
    weight = jnp.zeros_like(place)
    for t in range(routes.shape[0]):
        weight = weight + jnp.where(routes[t:t + 1] == expert, gates[t:t + 1], 0.0)
    weight = (weight * place).astype(jnp.bfloat16)
    for i in range(inner):
        rows = jnp.concatenate([back_ref[e, i] for e in range(owners)], axis=0)
        out_ref[:, i * width:(i + 1) * width] = lax.dot_general(
            weight, rows, (((0,), (0,)), ((), ())), preferred_element_type=jnp.float32
        ).astype(out_ref.dtype)


def picks(sources, block, expert):
    shape = (sources * CAP, sources * block)
    row = lax.broadcasted_iota(jnp.int32, shape, 0)
    slot = lax.broadcasted_iota(jnp.int32, shape, 1)
    wanted = (row % sources) * block + expert * CAP_PAD + row // sources
    return (slot == wanted).astype(jnp.bfloat16)


def select_kernel(slots_ref, out_ref):
    sources, block, width = slots_ref.shape
    slots = slots_ref[...].reshape(sources * block, width)
    for x in range(out_ref.shape[0]):
        out_ref[x] = jnp.dot(
            picks(sources, block, x), slots, preferred_element_type=jnp.float32
        ).astype(out_ref.dtype)


def gate_up_kernel(chunk, rows_ref, weight_ref, out_ref):
    del chunk
    ff = weight_ref.shape[3]
    rows = rows_ref[0]
    for k in range(2):
        out_ref[0, :, k * ff:(k + 1) * ff] = jnp.dot(
            rows, weight_ref[0, k], preferred_element_type=jnp.float32
        ).astype(out_ref.dtype)


def gate_up(chunk, chunks, rows, weight, dtype):
    experts, count, depth = rows.shape
    ff = weight.shape[3] // chunks
    return pl.pallas_call(
        gate_up_kernel,
        grid_spec=pltpu.PrefetchScalarGridSpec(
            num_scalar_prefetch=1,
            grid=(experts,),
            in_specs=[
                pl.BlockSpec((1, count, depth), lambda x, c: (x, 0, 0)),
                pl.BlockSpec((1, 2, depth, ff), lambda x, c: (x, 0, 0, c[0])),
            ],
            out_specs=pl.BlockSpec((1, count, 2 * ff), lambda x, c: (x, 0, 0)),
        ),
        out_shape=jax.ShapeDtypeStruct((experts, count, 2 * ff), dtype),
        compiler_params=params(16),
        cost_estimate=pl.CostEstimate(
            flops=4 * experts * count * depth * ff,
            bytes_accessed=4 * experts * depth * ff,
            transcendentals=0,
        ),
        name="gate_up",
    )(chunk, rows, weight)


def activate_kernel(*refs):
    own_ref, other_refs, out_ref = refs[0], refs[1:-1], refs[-1]
    ff = out_ref.shape[2]
    for x in range(out_ref.shape[0]):
        total = own_ref[x]
        for ref in other_refs:
            total = total + ref[x].astype(jnp.float32)
        gate, up = total[:, :ff], total[:, ff:]
        out_ref[x] = (gate / (1.0 + jnp.exp(-gate)) * up).astype(out_ref.dtype)


def down_kernel(inner, *refs):
    del inner
    weight_ref, out_ref, sum_ref = refs[-3], refs[-2], refs[-1]
    chunks = len(refs) - 3
    step, x = pl.program_id(0), pl.program_id(1)
    experts, count, _ = sum_ref.shape
    for s in range(chunks):
        @pl.when(step == s)
        def _():
            product = jnp.dot(refs[s][x], weight_ref[0], preferred_element_type=jnp.float32)
            sum_ref[x] = product if s == 0 else sum_ref[x] + product

    @pl.when((step == chunks - 1) & (x == experts - 1))
    def _():
        sources, block, width = out_ref.shape
        back = jnp.zeros((sources * block, width), jnp.float32)
        for y in range(experts):
            back = back + lax.dot_general(
                picks(sources, block, y),
                sum_ref[y].astype(jnp.bfloat16),
                (((0,), (0,)), ((), ())),
                preferred_element_type=jnp.float32,
            )
        out_ref[...] = back.astype(out_ref.dtype).reshape(sources, block, width)


def down(inner, parts, weight, sources, block):
    chunks = len(parts)
    experts, count, ff = parts[0].shape
    width = weight.shape[2]
    return pl.pallas_call(
        down_kernel,
        grid_spec=pltpu.PrefetchScalarGridSpec(
            num_scalar_prefetch=1,
            grid=(chunks, experts),
            in_specs=[pl.BlockSpec((experts, count, ff), lambda s, x, i: (0, 0, 0))] * chunks
            + [
                pl.BlockSpec(
                    (1, ff, width), lambda s, x, i: (x, lax.rem(i[0] + chunks - s, chunks), 0)
                )
            ],
            out_specs=pl.BlockSpec((sources, block, width), lambda s, x, i: (0, 0, 0)),
            scratch_shapes=[pltpu.VMEM((experts, count, width), jnp.float32)],
        ),
        out_shape=jax.ShapeDtypeStruct((sources, block, width), jnp.bfloat16),
        compiler_params=params(24),
        cost_estimate=pl.CostEstimate(
            flops=2 * experts * count * chunks * ff * width,
            bytes_accessed=2 * experts * chunks * ff * width,
            transcendentals=0,
        ),
        name="down",
    )(inner, *parts, weight)


def shifted(value, steps):
    size = lax.axis_size("inner")
    return lax.ppermute(value, "inner", [(i, (i + steps) % size) for i in range(size)])


def experts_by_columns(held, gate_up_weight, down_weight, sources, block):
    inner = lax.axis_size("inner")
    experts, count, _ = held.shape
    ff = gate_up_weight.shape[3]
    me = lax.axis_index("inner").astype(jnp.int32)
    order = [s for s in range(1, inner)]
    order.sort(key=lambda s: -min(s, inner - s))
    others = []
    for s in order:
        part = gate_up(((me + s) % inner).reshape(1), inner, held, gate_up_weight, jnp.bfloat16)
        others.append(shifted(part, s))
    own = gate_up(me.reshape(1), inner, held, gate_up_weight, jnp.float32)
    active = pl.pallas_call(
        activate_kernel,
        out_shape=jax.ShapeDtypeStruct((experts, count, ff // inner), jnp.bfloat16),
        compiler_params=params(32),
        name="activate",
    )(own, *others)
    parts = [active] + [shifted(active, s) for s in range(1, inner)]
    return down(me.reshape(1), parts, down_weight, sources, block)


def experts_by_rows(held, gate_up_weight, down_weight, sources, block):
    experts, count, _ = held.shape
    partial = jnp.einsum("xsd,xkdf->sxkf", held, gate_up_weight, preferred_element_type=jnp.float32)
    summed = lax.psum_scatter(partial, "inner", scatter_dimension=0, tiled=True)
    active = (jax.nn.silu(summed[:, :, 0]) * summed[:, :, 1]).astype(jnp.bfloat16)
    active = lax.all_gather(active, "inner", axis=0, tiled=True)
    outputs = jnp.einsum("sxf,xfd->xsd", active, down_weight, preferred_element_type=jnp.float32)
    outputs = outputs.astype(jnp.bfloat16).reshape(experts, CAP, sources, -1)
    outputs = jnp.pad(outputs, ((0, 0), (0, CAP_PAD - CAP), (0, 0), (0, 0)))
    return jnp.transpose(outputs, (2, 0, 1, 3)).reshape(sources, block, -1)


def body(
    queries,
    new_key_value,
    cached_key_value,
    parents,
    hidden,
    routes,
    gate_values,
    gate_up_weight,
    down_weight,
):
    owners, inner = lax.axis_size("expert"), lax.axis_size("inner")
    sources = owners * inner
    experts, _, depth, ff = gate_up_weight.shape
    rows, model = hidden.shape
    width = down_weight.shape[2]
    block = experts * CAP_PAD
    turned_routes, turned_gates = routes.T, gate_values.T
    both = ("expert", "inner")

    sent = pl.pallas_call(
        dispatch_kernel,
        out_shape=jax.ShapeDtypeStruct((owners, inner, block, depth), jnp.bfloat16),
        compiler_params=params(16),
        name="dispatch",
    )(turned_routes, hidden)
    slots = lax.all_to_all(
        sent.reshape(sources, block, depth), both, split_axis=0, concat_axis=0, tiled=True
    )
    attended = attend(queries, new_key_value, cached_key_value, parents)

    held = pl.pallas_call(
        select_kernel,
        out_shape=jax.ShapeDtypeStruct((experts, sources * CAP, depth), jnp.bfloat16),
        compiler_params=params(24),
        name="select",
    )(slots)
    even = ff % (inner * 128) == 0
    back = (experts_by_columns if even else experts_by_rows)(
        held, gate_up_weight, down_weight, sources, block
    )
    returned = lax.all_to_all(back, both, split_axis=0, concat_axis=0, tiled=True)
    expert_out = pl.pallas_call(
        combine_kernel,
        out_shape=jax.ShapeDtypeStruct((rows, model), jnp.bfloat16),
        compiler_params=params(16),
        name="combine",
    )(turned_routes, turned_gates, returned.reshape(owners, inner, block, width))
    return attended, expert_out


def solution(mesh):
    rows = ("groups", "expert", "inner")
    return jax.shard_map(
        body,
        mesh=mesh,
        in_specs=(
            P(rows, None),
            P(rows, None),
            P(rows, None, None, None),
            P(rows, None),
            P(rows, None),
            P(rows, None),
            P(rows, None),
            P("expert", None, "inner", None),
            P("expert", None, "inner"),
        ),
        out_specs=(P(rows, None), P(rows, None)),
        check_vma=False,
    )
```

time: 179 us -> 69.8 us (0.39)
  blocking collectives: 48.2 us -> 0 us
  waiting for transfers between devices: 68.5 us -> 24.5 us
  matrix products: 17.8 us -> 0 us
  starting transfers between devices: 4.7 us -> 20.7 us
  Pallas kernels: 0 us -> 15.7 us
  between operations: 14.6 us -> 0.83 us
  local copies, waits for them, and re-layouts: 16.3 us -> 7.63 us
  other arithmetic: 8.19 us -> 0.01 us
    all_gather x2 -> x0, blocking collectives: 48.2 us -> none  [the longest x1 34.2 us: body(): lax.all_gather(shares.astype(jnp.bfloat16), ('expert', 'inner'), axis=0,...]
    unnamed x4 -> x0, waiting for transfers between devices: 39.9 us -> none
    reduce_scatter x1 -> x0, waiting for transfers between devices: 19.9 us -> none  [body(): lax.psum_scatter(term, 'expert', scatter_dimension=0, tiled=True)]
    dot_general x7 -> x0, matrix products: 17.8 us -> none  [the longest x1 6.81 us: expert_block(): jnp.einsum('sxd,xkdf->sxkf', slots, gate_up, preferred_element_type=jnp.f...]
    pallas_call x0 -> x10, Pallas kernels: none -> 15.7 us  [the longest x1 5.85 us: attend(): pl.pallas_call(attend_kernel, grid_spec=pltpu.PrefetchScalarGridSpec(num_...]
    ppermute x0 -> x6, waiting for transfers between devices: none -> 11.8 us  [shifted(): lax.ppermute(value, 'inner', [(i, (i + steps) % size) for i in range(size)])]
    all_to_all x1 -> x2, waiting for transfers between devices: 2.84 us -> 12.7 us  [the longest x1 10 us: body(): lax.all_to_all(sent.reshape(sources, block, depth), both, split_axis=0, c...]
    ppermute x0 -> x6, starting transfers between devices: none -> 8.71 us  [shifted(): lax.ppermute(value, 'inner', [(i, (i + steps) % size) for i in range(size)])]
  transfers between devices with their start and end apart: 4 -> 8, of which waited for: 4 -> 6; matrix products, arithmetic and copies ran while one was open for 12% -> 2% of each run, Pallas kernels for 0% -> 13%
where the time goes in v1:
time: 69.8 us; the launch traced here: 69.3 us
  waiting for transfers between devices  24.5 us (35%)
  starting transfers between devices  20.7 us (30%)
  Pallas kernels  15.7 us (22%)
  local copies, waits for them, and re-layouts  7.63 us (11%)
  between operations  0.83 us (1%)
    ppermute x6, waiting for transfers between devices, shifted(): lax.ppermute(value, 'inner', [(i, (i + steps) % size) for i in range(size)])  11.8 us
    all_to_all x1, waiting for transfers between devices, body(): lax.all_to_all(sent.reshape(sources, block, depth), both, split_axis=0, c...  10 us
    ppermute x6, starting transfers between devices, shifted(): lax.ppermute(value, 'inner', [(i, (i + steps) % size) for i in range(size)])  8.71 us
    unnamed x29, local copies, waits for them, and re-layouts  7.63 us
    all_to_all x1, starting transfers between devices, body(): lax.all_to_all(sent.reshape(sources, block, depth), both, split_axis=0, c...  7.36 us
    pallas_call x1, Pallas kernels, attend(): pl.pallas_call(attend_kernel, grid_spec=pltpu.PrefetchScalarGridSpec(num_...  5.85 us
    all_to_all x1, starting transfers between devices, body(): lax.all_to_all(back, both, split_axis=0, concat_axis=0, tiled=True)  4.6 us
    pallas_call x4, Pallas kernels, gate_up(): pl.pallas_call(gate_up_kernel, grid_spec=pltpu.PrefetchScalarGridSpec(num...  4.27 us
  transfers between devices with their start and end apart: 8, of which 6 were waited for; matrix products, arithmetic and copies ran while one was open for 2% of the time, Pallas kernels for 13%

profile of v1, /device:TPU:0, one launch (start us, length us, event | category | flops | bytes accessed | tf_op | source)
XLA Modules:
  0.0 69.3 jit_solution(8281395609159888942)
XLA Ops:
  0.6 0.0 copy-start.2
  0.6 0.8 %copy-done.2 = bf16[8,4096]{1,0:T(8,128)(2,1)S(1)} copy-done((bf16[8,4096]{1,0:T(8,128)(2,1)S(1)}, bf16[8,4096]{1,0:T(8,128)(2,1)}, u32[]{:S(2)}) %copy-start.2) | copy-done | bytes 65560
  1.5 0.7 copy-done.3
  2.1 1.0 %dispatch.1 = bf16[4,4,8,1024]{3,2,1,0:T(8,128)(2,1)} custom-call(s32[2,8]{1,0:T(2,128)S(1)} %bitcast.29, bf16[8,4096]{1,0:T(8,128)(2,1)S(1)} %copy-done.2), custom_call_target="tpu_custom_call" | custom-call | tf_op jit(solution)/shard_map/dispatch/pallas_call | solution.py:309
  3.2 7.4 %all-to-all-start = ((bf16[16,8,1024]{2,1,0:T(8,128)(2,1)}), bf16[16,8,1024]{2,1,0:T(8,128)(2,1)S(1)}, u32[]{:S(2)}, u32[]{:S(2)}) async-start(bf16[16,8,1024]{2,1,0:T(8,128)(2,1)} %bitcast.4), calls=%async_computation | async-start | bytes 524288 | tf_op jit(solution)/shard_map/all_to_all | solution.py:315
  10.6 10.0 %all-to-all-done.slots_ref = bf16[16,8,1024]{2,1,0:T(8,128)(2,1)S(1)} async-done(((bf16[16,8,1024]{2,1,0:T(8,128)(2,1)}), bf16[16,8,1024]{2,1,0:T(8,128)(2,1)S(1)}, u32[]{:S(2)}, u32[]{:S(2)}) %all-to-all-start) | async-done | bytes 262176 | tf_op jit(solution)/shard_map/all_to_all | solution.py:315
  20.6 0.2 select.7.rows_ref
  20.8 0.0 copy-start
  20.8 4.6 %copy-done = bf16[2,2,1024,1536]{3,2,1,0:T(8,128)(2,1)S(1)} copy-done((bf16[2,2,1024,1536]{3,2,1,0:T(8,128)(2,1)S(1)}, bf16[2,2,1024,1536]{3,2,1,0:T(8,128)(2,1)}, u32[]{:S(2)}) %copy-start) | copy-done | bytes 12582936
  25.4 1.1 %gate_up.5 = bf16[2,48,768]{2,1,0:T(8,128)(2,1)S(1)} custom-call(s32[1]{0:T(128)} %bitcast.5.chunk, bf16[2,48,1024]{2,1,0:T(8,128)(2,1)S(1)} %select.7.rows_ref, bf16[2,2,1024,1536]{3,2,1,0:T(8,128)(2,1)S(1)} %copy-done), custom_call_target="tpu_custom_call" | custom-call | flops 150994944 | bytes 3145728 | tf_op jit(solution)/shard_map/gate_up/pallas_call | solution.py:162
  26.5 0.5 collective-permute-start
  27.0 1.1 %gate_up.6 = bf16[2,48,768]{2,1,0:T(8,128)(2,1)S(1)} custom-call(s32[1]{0:T(128)} %bitcast.6.chunk, bf16[2,48,1024]{2,1,0:T(8,128)(2,1)S(1)} %select.7.rows_ref, bf16[2,2,1024,1536]{3,2,1,0:T(8,128)(2,1)S(1)} %copy-done), custom_call_target="tpu_custom_call" | custom-call | flops 150994944 | bytes 3145728 | tf_op jit(solution)/shard_map/gate_up/pallas_call | solution.py:162
  28.0 1.1 %collective-permute-start.1 = (bf16[2,48,768]{2,1,0:T(8,128)(2,1)S(1)}, bf16[2,48,768]{2,1,0:T(8,128)(2,1)S(1)}, u32[]{:S(2)}, u32[]{:S(2)}) collective-permute-start(bf16[2,48,768]{2,1,0:T(8,128)(2,1)S(1)} %gate_up.6), channel_id=1, source_target_pairs={{0,1},{1,2},{2,3},{3,0},{4,5},{5,6},{6,7},{7,4},{8,9},{9,10},{10,1... | collective-permute-start | bytes 442376 | tf_op jit(solution)/shard_map/ppermute | solution.py:252
  29.1 1.1 %gate_up.7 = bf16[2,48,768]{2,1,0:T(8,128)(2,1)S(1)} custom-call(s32[1]{0:T(128)} %bitcast.7.chunk, bf16[2,48,1024]{2,1,0:T(8,128)(2,1)S(1)} %select.7.rows_ref, bf16[2,2,1024,1536]{3,2,1,0:T(8,128)(2,1)S(1)} %copy-done), custom_call_target="tpu_custom_call" | custom-call | flops 150994944 | bytes 3145728 | tf_op jit(solution)/shard_map/gate_up/pallas_call | solution.py:162
  30.2 2.9 %collective-permute-start.2 = (bf16[2,48,768]{2,1,0:T(8,128)(2,1)S(1)}, bf16[2,48,768]{2,1,0:T(8,128)(2,1)S(1)}, u32[]{:S(2)}, u32[]{:S(2)}) collective-permute-start(bf16[2,48,768]{2,1,0:T(8,128)(2,1)S(1)} %gate_up.7), channel_id=1, source_target_pairs={{0,3},{1,0},{2,1},{3,2},{4,7},{5,4},{6,5},{7,6},{8,11},{9,8},{10,9... | collective-permute-start | bytes 442376 | tf_op jit(solution)/shard_map/ppermute | solution.py:252
  33.0 0.0 slice-done
  33.0 0.0 slice-done.1
  33.0 0.0 slice-done.2
  33.1 0.0 slice-start.4
  33.1 1.1 %gate_up.4.refs_0_ = f32[2,48,768]{2,1,0:T(8,128)S(1)} custom-call(s32[1]{0:T(128)} %bitcast.3.chunk.inner, bf16[2,48,1024]{2,1,0:T(8,128)(2,1)S(1)} %select.7.rows_ref, bf16[2,2,1024,1536]{3,2,1,0:T(8,128)(2,1)S(1)} %bitcast.22), custom_call_target="tpu_custom_call" | custom-call | flops 150994944 | bytes 3145728 | tf_op jit(solution)/shard_map/gate_up/pallas_call | solution.py:162
  34.2 0.0 copy-start.7
  34.2 0.0 copy-start.1
  34.2 0.0 copy-start.5
  34.2 0.0 copy-start.4
  34.2 0.0 copy-start.6
  34.2 5.4 %collective-permute-done.refs_1_ = bf16[2,48,768]{2,1,0:T(8,128)(2,1)S(1)} collective-permute-done((bf16[2,48,768]{2,1,0:T(8,128)(2,1)S(1)}, bf16[2,48,768]{2,1,0:T(8,128)(2,1)S(1)}, u32[]{:S(2)}, u32[]{:S(2)}) %collective-permute-start) | collective-permute-done | bytes 147488 | tf_op jit(solution)/shard_map/ppermute | solution.py:252
  39.6 0.0 collective-permute-done.1.refs_2_
  39.6 1.8 %collective-permute-done.2.refs_3_ = bf16[2,48,768]{2,1,0:T(8,128)(2,1)S(1)} collective-permute-done((bf16[2,48,768]{2,1,0:T(8,128)(2,1)S(1)}, bf16[2,48,768]{2,1,0:T(8,128)(2,1)S(1)}, u32[]{:S(2)}, u32[]{:S(2)}) %collective-permute-start.2) | collective-permute-done | bytes 147488 | tf_op jit(solution)/shard_map/ppermute | solution.py:252
  41.4 0.1 activate.1.refs_0_
  41.6 1.6 %collective-permute-start.3 = (bf16[2,48,384]{2,1,0:T(8,128)(2,1)S(1)}, bf16[2,48,384]{2,1,0:T(8,128)(2,1)S(1)}, u32[]{:S(2)}, u32[]{:S(2)}) collective-permute-start(bf16[2,48,384]{2,1,0:T(8,128)(2,1)S(1)} %activate.1.refs_0_), channel_id=1, source_target_pairs={{0,1},{1,2},{2,3},{3,0},{4,5},{5,6},{6,7},{7,4},{8,9},{9,10},{10,1... | collective-permute-start | bytes 221192 | tf_op jit(solution)/shard_map/ppermute | solution.py:252
  43.1 0.0 collective-permute-start.4
  43.1 2.7 %collective-permute-start.5 = (bf16[2,48,384]{2,1,0:T(8,128)(2,1)S(1)}, bf16[2,48,384]{2,1,0:T(8,128)(2,1)S(1)}, u32[]{:S(2)}, u32[]{:S(2)}) collective-permute-start(bf16[2,48,384]{2,1,0:T(8,128)(2,1)S(1)} %activate.1.refs_0_), channel_id=1, source_target_pairs={{0,3},{1,0},{2,1},{3,2},{4,7},{5,4},{6,5},{7,6},{8,11},{9,8},{10,9... | collective-permute-start | bytes 221192 | tf_op jit(solution)/shard_map/ppermute | solution.py:252
  45.9 2.5 %collective-permute-done.3.refs_1_ = bf16[2,48,384]{2,1,0:T(8,128)(2,1)S(1)} collective-permute-done((bf16[2,48,384]{2,1,0:T(8,128)(2,1)S(1)}, bf16[2,48,384]{2,1,0:T(8,128)(2,1)S(1)}, u32[]{:S(2)}, u32[]{:S(2)}) %collective-permute-start.3) | collective-permute-done | bytes 73760 | tf_op jit(solution)/shard_map/ppermute | solution.py:252
  48.3 2.0 %collective-permute-done.4.refs_2_ = bf16[2,48,384]{2,1,0:T(8,128)(2,1)S(1)} collective-permute-done((bf16[2,48,384]{2,1,0:T(8,128)(2,1)S(1)}, bf16[2,48,384]{2,1,0:T(8,128)(2,1)S(1)}, u32[]{:S(2)}, u32[]{:S(2)}) %collective-permute-start.4) | collective-permute-done | bytes 73760 | tf_op jit(solution)/shard_map/ppermute | solution.py:252
  50.4 0.0 collective-permute-done.5.refs_3_
  50.4 0.0 slice-done.3
  50.4 0.0 slice-done.4
  50.4 3.3 %down.1 = bf16[16,8,1024]{2,1,0:T(8,128)(2,1)} custom-call(s32[1]{0:T(128)} %bitcast.3.chunk.inner, bf16[2,48,384]{2,1,0:T(8,128)(2,1)S(1)} %activate.1.refs_0_, bf16[2,48,384]{2,1,0:T(8,128)(2,1)S(1)} %collective-permute-done.3.refs_1_, bf16[2,48,384]{2,1,0:T(8,128)(2,1)S(1)} %collective-permute-done.4.refs_2_, ...), custom_call_target="tpu_custom_call" | custom-call | flops 301989888 | bytes 6291456 | tf_op jit(solution)/shard_map/down/pallas_call | solution.py:225
  53.7 4.6 %all-to-all-start.1 = ((bf16[16,8,1024]{2,1,0:T(8,128)(2,1)}), bf16[16,8,1024]{2,1,0:T(8,128)(2,1)S(1)}, u32[]{:S(2)}, u32[]{:S(2)}) async-start(bf16[16,8,1024]{2,1,0:T(8,128)(2,1)} %down.1), calls=%async_computation.1 | async-start | bytes 524288 | tf_op jit(solution)/shard_map/all_to_all | solution.py:330
  58.3 0.0 copy-done.7
  58.3 0.7 %copy.19 = bf16[1,8,8,128]{3,2,1,0:T(8,128)(2,1)S(1)} copy(bf16[1,8,8,128]{3,1,2,0:T(8,128)(2,1)} %bitcast.35) | data formatting | bytes 32768
  59.1 0.0 copy-done.1
  59.1 0.0 copy-done.5
  59.1 5.9 %attend.1 = bf16[8,64,128]{2,1,0:T(8,128)(2,1)S(1)} custom-call(s32[8]{0:T(128)S(1)} %bitcast.31, bf16[8,64,128]{2,1,0:T(8,128)(2,1)S(1)} %bitcast.27, bf16[8,8,128]{2,1,0:T(8,128)(2,1)S(1)} %bitcast.28, bf16[1,8,192,1024]{3,2,1,0:T(8,128)(2,1)S(1)} %copy-done.1), custom_call_target="tpu_custom_call" | custom-call | flops 50331648 | bytes 3145728 | tf_op jit(solution)/shard_map/attend/pallas_call | solution.py:60
  64.9 0.8 %copy.17 = bf16[1,8,64,128]{3,1,2,0:T(8,128)(2,1)} copy(bf16[1,8,64,128]{3,2,1,0:T(8,128)(2,1)S(1)} %bitcast.26) | data formatting | bytes 262144
  65.7 2.7 %all-to-all-done.1 = bf16[16,8,1024]{2,1,0:T(8,128)(2,1)S(1)} async-done(((bf16[16,8,1024]{2,1,0:T(8,128)(2,1)}), bf16[16,8,1024]{2,1,0:T(8,128)(2,1)S(1)}, u32[]{:S(2)}, u32[]{:S(2)}) %all-to-all-start.1) | async-done | bytes 262176 | tf_op jit(solution)/shard_map/all_to_all | solution.py:330
  68.4 0.0 copy-done.6
  68.4 1.0 %combine.1 = bf16[8,4096]{1,0:T(8,128)(2,1)} custom-call(s32[2,8]{1,0:T(2,128)S(1)} %bitcast.30, bf16[2,8]{1,0:T(2,128)(2,1)S(1)} %bitcast.32, bf16[4,4,8,1024]{3,2,1,0:T(8,128)(2,1)S(1)} %bitcast.25), custom_call_target="tpu_custom_call" | custom-call | tf_op jit(solution)/shard_map/combine/pallas_call | solution.py:331
  (9 shorter events, 0.0 us)
Async XLA Ops:
  0.6 0.8 %copy-start.2 = (bf16[8,4096]{1,0:T(8,128)(2,1)S(1)}, bf16[8,4096]{1,0:T(8,128)(2,1)}, u32[]{:S(2)}) copy-start(bf16[8,4096]{1,0:T(8,128)(2,1)} %hidden_ref.1) | copy-start | bytes 196612
  1.5 0.7 copy-start.3
  3.2 17.4 %all-to-all-start = ((bf16[16,8,1024]{2,1,0:T(8,128)(2,1)}), bf16[16,8,1024]{2,1,0:T(8,128)(2,1)S(1)}, u32[]{:S(2)}, u32[]{:S(2)}) async-start(bf16[16,8,1024]{2,1,0:T(8,128)(2,1)} %bitcast.4), calls=%async_computation | async-start | bytes 524288 | tf_op jit(solution)/shard_map/all_to_all | solution.py:315
  20.8 4.6 %copy-start = (bf16[2,2,1024,1536]{3,2,1,0:T(8,128)(2,1)S(1)}, bf16[2,2,1024,1536]{3,2,1,0:T(8,128)(2,1)}, u32[]{:S(2)}) copy-start(bf16[2,2,1024,1536]{3,2,1,0:T(8,128)(2,1)} %weight_ref.7) | copy-start | bytes 37748740
  26.5 13.2 %collective-permute-start = (bf16[2,48,768]{2,1,0:T(8,128)(2,1)S(1)}, bf16[2,48,768]{2,1,0:T(8,128)(2,1)S(1)}, u32[]{:S(2)}, u32[]{:S(2)}) collective-permute-start(bf16[2,48,768]{2,1,0:T(8,128)(2,1)S(1)} %gate_up.5), channel_id=1, source_target_pairs={{0,2},{1,3},{2,0},{3,1},{4,6},{5,7},{6,4},{7,5},{8,10},{9,11},{10,... | collective-permute-start | bytes 442376 | tf_op jit(solution)/shard_map/ppermute | solution.py:252
  27.0 6.1 %slice-start = ((s8[12582912]{0:T(1024)(128)(4,1)}), s8[4194304]{0:T(1024)(128)(4,1)S(1)}, s32[]{:S(2)}) async-start(s8[12582912]{0:T(1024)(128)(4,1)} %bitcast.21), calls=%async_computation.2 | async-start | bytes 8388608
  27.0 6.1 %slice-start.1 = ((s8[12582912]{0:T(1024)(128)(4,1)}), s8[4194304]{0:T(1024)(128)(4,1)S(1)}, s32[]{:S(2)}) async-start(s8[12582912]{0:T(1024)(128)(4,1)} %bitcast.21), calls=%async_computation.3 | async-start | bytes 8388608
  28.0 11.6 %collective-permute-start.1 = (bf16[2,48,768]{2,1,0:T(8,128)(2,1)S(1)}, bf16[2,48,768]{2,1,0:T(8,128)(2,1)S(1)}, u32[]{:S(2)}, u32[]{:S(2)}) collective-permute-start(bf16[2,48,768]{2,1,0:T(8,128)(2,1)S(1)} %gate_up.6), channel_id=1, source_target_pairs={{0,1},{1,2},{2,3},{3,0},{4,5},{5,6},{6,7},{7,4},{8,9},{9,10},{10,1... | collective-permute-start | bytes 442376 | tf_op jit(solution)/shard_map/ppermute | solution.py:252
  29.1 4.0 %slice-start.2 = ((s8[12582912]{0:T(1024)(128)(4,1)}), s8[4194304]{0:T(1024)(128)(4,1)S(1)}, s32[]{:S(2)}) async-start(s8[12582912]{0:T(1024)(128)(4,1)} %bitcast.21), calls=%async_computation.4 | async-start | bytes 8388608
  29.1 21.3 %slice-start.3 = ((s8[6291456]{0:T(1024)(128)(4,1)}), s8[4194304]{0:T(1024)(128)(4,1)S(1)}, s32[]{:S(2)}) async-start(s8[6291456]{0:T(1024)(128)(4,1)} %bitcast.23), calls=%async_computation.5 | async-start | bytes 8388608
  30.2 11.3 %collective-permute-start.2 = (bf16[2,48,768]{2,1,0:T(8,128)(2,1)S(1)}, bf16[2,48,768]{2,1,0:T(8,128)(2,1)S(1)}, u32[]{:S(2)}, u32[]{:S(2)}) collective-permute-start(bf16[2,48,768]{2,1,0:T(8,128)(2,1)S(1)} %gate_up.7), channel_id=1, source_target_pairs={{0,3},{1,0},{2,1},{3,2},{4,7},{5,4},{6,5},{7,6},{8,11},{9,8},{10,9... | collective-permute-start | bytes 442376 | tf_op jit(solution)/shard_map/ppermute | solution.py:252
  33.1 17.3 %slice-start.4 = ((s8[6291456]{0:T(1024)(128)(4,1)}), s8[2097152]{0:T(1024)(128)(4,1)S(1)}, s32[]{:S(2)}) async-start(s8[6291456]{0:T(1024)(128)(4,1)} %bitcast.23), calls=%async_computation.6 | async-start | bytes 4194304
  34.2 24.1 %copy-start.7 = (bf16[8,8192]{1,0:T(8,128)(2,1)S(1)}, bf16[8,8192]{1,0:T(8,128)(2,1)}, u32[]{:S(2)}) copy-start(bf16[8,8192]{1,0:T(8,128)(2,1)} %param.9) | copy-start | bytes 393220
  34.2 24.9 %copy-start.1 = (bf16[1,8,192,1024]{3,2,1,0:T(8,128)(2,1)S(1)}, bf16[1,8,192,1024]{3,2,1,0:T(8,128)(2,1)}, u32[]{:S(2)}) copy-start(bf16[1,8,192,1024]{3,2,1,0:T(8,128)(2,1)} %cache_ref.1) | copy-start | bytes 9437188
  34.2 24.9 %copy-start.5 = (s32[1,8]{1,0:T(1,128)S(1)}, s32[1,8]{1,0:T(1,128)}, u32[]{:S(2)}) copy-start(s32[1,8]{1,0:T(1,128)} %param.12) | copy-start | bytes 100
  34.2 34.2 %copy-start.4 = (s32[8,2]{0,1:T(2,128)S(1)}, s32[8,2]{0,1:T(2,128)}, u32[]{:S(2)}) copy-start(s32[8,2]{0,1:T(2,128)} %param.14) | copy-start | bytes 196
  34.2 34.2 %copy-start.6 = (bf16[8,2]{0,1:T(2,128)(2,1)S(1)}, bf16[8,2]{0,1:T(2,128)(2,1)}, u32[]{:S(2)}) copy-start(bf16[8,2]{0,1:T(2,128)(2,1)} %param.15) | copy-start | bytes 100
  41.6 6.8 %collective-permute-start.3 = (bf16[2,48,384]{2,1,0:T(8,128)(2,1)S(1)}, bf16[2,48,384]{2,1,0:T(8,128)(2,1)S(1)}, u32[]{:S(2)}, u32[]{:S(2)}) collective-permute-start(bf16[2,48,384]{2,1,0:T(8,128)(2,1)S(1)} %activate.1.refs_0_), channel_id=1, source_target_pairs={{0,1},{1,2},{2,3},{3,0},{4,5},{5,6},{6,7},{7,4},{8,9},{9,10},{10,1... | collective-permute-start | bytes 221192 | tf_op jit(solution)/shard_map/ppermute | solution.py:252
  43.1 7.2 %collective-permute-start.4 = (bf16[2,48,384]{2,1,0:T(8,128)(2,1)S(1)}, bf16[2,48,384]{2,1,0:T(8,128)(2,1)S(1)}, u32[]{:S(2)}, u32[]{:S(2)}) collective-permute-start(bf16[2,48,384]{2,1,0:T(8,128)(2,1)S(1)} %activate.1.refs_0_), channel_id=1, source_target_pairs={{0,2},{1,3},{2,0},{3,1},{4,6},{5,7},{6,4},{7,5},{8,10},{9,11},{10,... | collective-permute-start | bytes 221192 | tf_op jit(solution)/shard_map/ppermute | solution.py:252
  43.1 7.2 %collective-permute-start.5 = (bf16[2,48,384]{2,1,0:T(8,128)(2,1)S(1)}, bf16[2,48,384]{2,1,0:T(8,128)(2,1)S(1)}, u32[]{:S(2)}, u32[]{:S(2)}) collective-permute-start(bf16[2,48,384]{2,1,0:T(8,128)(2,1)S(1)} %activate.1.refs_0_), channel_id=1, source_target_pairs={{0,3},{1,0},{2,1},{3,2},{4,7},{5,4},{6,5},{7,6},{8,11},{9,8},{10,9... | collective-permute-start | bytes 221192 | tf_op jit(solution)/shard_map/ppermute | solution.py:252
  53.7 14.7 %all-to-all-start.1 = ((bf16[16,8,1024]{2,1,0:T(8,128)(2,1)}), bf16[16,8,1024]{2,1,0:T(8,128)(2,1)S(1)}, u32[]{:S(2)}, u32[]{:S(2)}) async-start(bf16[16,8,1024]{2,1,0:T(8,128)(2,1)} %down.1), calls=%async_computation.1 | async-start | bytes 524288 | tf_op jit(solution)/shard_map/all_to_all | solution.py:330

commit v2 on v1

v2 whole, which is shorter than its diff:
```python
import functools
import math

import jax
import jax.numpy as jnp
from jax import lax
from jax.experimental import pallas as pl
from jax.experimental.pallas import tpu as pltpu
from jax.sharding import PartitionSpec as P

QUERY_HEADS = 64
KEY_HEADS = 4
HEAD_SIZE = 128
CAP = 3
LANES = 128


def params(limit, *semantics):
    return pltpu.CompilerParams(
        dimension_semantics=semantics or None, vmem_limit_bytes=limit * 1024 * 1024
    )


def attend_kernel(parents, q_ref, new_ref, cache_ref, after_ref, out_ref):
    del parents, after_ref
    group = QUERY_HEADS // KEY_HEADS
    scale = 1.0 / math.sqrt(HEAD_SIZE)
    width = KEY_HEADS * HEAD_SIZE
    q = q_ref[0]
    fresh = new_ref[0].astype(jnp.float32)
    scores, own = [], []
    for k in range(KEY_HEADS):
        qk = q[k * group:(k + 1) * group]
        keys = cache_ref[0, 0, :, k * HEAD_SIZE:(k + 1) * HEAD_SIZE]
        scores.append(
            lax.dot_general(qk, keys, (((1,), (1,)), ((), ())), preferred_element_type=jnp.float32)
        )
        own.append(
            jnp.sum(qk.astype(jnp.float32) * fresh[k:k + 1], axis=-1, keepdims=True)
        )
    scores = jnp.concatenate(scores, axis=0) * scale
    own = jnp.concatenate(own, axis=0) * scale
    upper = jnp.maximum(jnp.max(scores, axis=-1, keepdims=True), own)
    expo = jnp.exp(scores - upper)
    own_expo = jnp.exp(own - upper)
    total = jnp.sum(expo, axis=-1, keepdims=True) + own_expo
    probs = (expo / total).astype(jnp.bfloat16)
    own_prob = (own_expo / total).astype(jnp.bfloat16).astype(jnp.float32)
    for k in range(KEY_HEADS):
        rows = slice(k * group, (k + 1) * group)
        values = cache_ref[0, 0, :, width + k * HEAD_SIZE:width + (k + 1) * HEAD_SIZE]
        result = jnp.dot(probs[rows], values, preferred_element_type=jnp.float32)
        result = result + own_prob[rows] * fresh[KEY_HEADS + k:KEY_HEADS + k + 1]
        out_ref[0, rows] = result.astype(out_ref.dtype)


def attend(queries, new_key_value, cached_key_value, parents, after):
    rows = queries.shape[0]
    _, beams, length, width = cached_key_value.shape
    out = pl.pallas_call(
        attend_kernel,
        grid_spec=pltpu.PrefetchScalarGridSpec(
            num_scalar_prefetch=1,
            grid=(rows,),
            in_specs=[
                pl.BlockSpec((1, QUERY_HEADS, HEAD_SIZE), lambda r, p: (r, 0, 0)),
                pl.BlockSpec((1, 2 * KEY_HEADS, HEAD_SIZE), lambda r, p: (r, 0, 0)),
                pl.BlockSpec((1, 1, length, width), lambda r, p: (r // beams, p[r], 0, 0)),
                pl.BlockSpec(memory_space=pl.ANY),
            ],
            out_specs=pl.BlockSpec((1, QUERY_HEADS, HEAD_SIZE), lambda r, p: (r, 0, 0)),
        ),
        out_shape=jax.ShapeDtypeStruct((rows, QUERY_HEADS, HEAD_SIZE), jnp.bfloat16),
        compiler_params=params(50),
        cost_estimate=pl.CostEstimate(
            flops=4 * rows * QUERY_HEADS * HEAD_SIZE * length,
            bytes_accessed=2 * rows * length * width,
            transcendentals=rows * QUERY_HEADS * length,
        ),
        name="attend",
    )(
        parents.reshape(rows),
        queries.reshape(rows, QUERY_HEADS, HEAD_SIZE),
        new_key_value.reshape(rows, 2 * KEY_HEADS, HEAD_SIZE),
        cached_key_value,
        after,
    )
    return out.reshape(rows, QUERY_HEADS * HEAD_SIZE)


def spread(values, lanes, first):
    top = values.shape[0]
    shape = (top, lanes)
    chosen = (
        lax.broadcasted_iota(jnp.int32, shape, 1)
        == lax.broadcasted_iota(jnp.int32, shape, 0) + first
    ).astype(jnp.float32)
    return lax.dot_general(
        values.astype(jnp.float32), chosen, (((0,), (0,)), ((), ())), preferred_element_type=jnp.float32
    )


def prepare_kernel(me, routes_ref, gates_ref, hidden_ref, *out_refs):
    chunks = len(out_refs)
    width = hidden_ref.shape[1] // chunks
    top = routes_ref.shape[0]
    notes = spread(routes_ref[...], LANES, 0) + spread(gates_ref[...], LANES, top)
    notes = notes.astype(jnp.bfloat16)
    for s in range(chunks):
        start = pl.multiple_of(lax.rem(me[0] + s, chunks) * width, width)
        out_refs[s][:, :width] = hidden_ref[:, pl.ds(start, width)]
        out_refs[s][:, width:] = notes


def turned_notes(notes, top):
    shape = (max(8, 2 * top), LANES)
    chosen = (
        lax.broadcasted_iota(jnp.int32, shape, 0) == lax.broadcasted_iota(jnp.int32, shape, 1)
    ).astype(jnp.bfloat16)
    turned = lax.dot_general(
        chosen, notes, (((1,), (1,)), ((), ())), preferred_element_type=jnp.float32
    )
    return turned[:top], turned[top:2 * top]


def placing(routes, owner, level, experts, sources):
    top, rows = routes.shape
    count = CAP * sources
    shape = (experts * count, rows)
    slot = lax.broadcasted_iota(jnp.int32, shape, 0)
    row = lax.broadcasted_iota(jnp.int32, shape, 1)
    each = rows // sources
    local = jnp.zeros(shape, jnp.int32)
    for x in range(1, experts):
        local = local + (slot >= x * count).astype(jnp.int32)
    within = slot - local * count
    rank, source = within // sources, within % sources
    expert = (owner * experts + local).astype(jnp.float32)
    member = jnp.zeros(shape, jnp.float32)
    for t in range(top):
        member = jnp.where(routes[t:t + 1] == expert, 1.0, member)
    origin = level - row // each
    origin = jnp.where(origin < 0, origin + sources, origin)
    member = jnp.where(origin == source, member, 0.0)
    one = lax.broadcasted_iota(jnp.int32, (rows, rows), 0)
    other = lax.broadcasted_iota(jnp.int32, (rows, rows), 1)
    before = (one < other).astype(jnp.float32)
    ranks = jnp.dot(member, before, preferred_element_type=jnp.float32)
    return jnp.where(ranks == rank.astype(jnp.float32), member, 0.0), expert


def pack_kernel(top, experts, sources, column, level, *refs):
    owners = len(refs) - sources
    held, out_refs = refs[:sources], refs[sources:]
    width = out_refs[0].shape[1]
    rows = jnp.concatenate([ref[:, :width] for ref in held], axis=0)
    notes = jnp.concatenate([ref[:, width:] for ref in held], axis=0)
    routes, _ = turned_notes(notes, top)
    for t in range(owners):
        place, _ = placing(routes, lax.rem(column[0] + t, owners), level[0], experts, sources)
        out_refs[t][...] = jnp.dot(
            place.astype(jnp.bfloat16), rows, preferred_element_type=jnp.float32
        ).astype(out_refs[t].dtype)


def combine_kernel(top, experts, sources, column, level, *refs):
    owners = len(refs) - 2 * sources
    held, back, out_refs = refs[:sources], refs[sources:sources + owners], refs[sources + owners:]
    each, width = out_refs[0].shape
    notes = jnp.concatenate([ref[:, width:] for ref in held], axis=0)
    routes, gates = turned_notes(notes, top)
    total = jnp.zeros((sources * each, width), jnp.float32)
    for t in range(owners):
        place, expert = placing(routes, lax.rem(column[0] + t, owners), level[0], experts, sources)
        weight = jnp.zeros_like(place)
        for k in range(top):
            weight = weight + jnp.where(routes[k:k + 1] == expert, gates[k:k + 1], 0.0)
        total = total + lax.dot_general(
            (weight * place).astype(jnp.bfloat16),
            back[t][...],
            (((0,), (0,)), ((), ())),
            preferred_element_type=jnp.float32,
        )
    for s in range(sources):
        out_refs[s][...] = total[s * each:(s + 1) * each].astype(out_refs[s].dtype)


def assemble_kernel(me, *refs):
    chunks = len(refs) - 1
    out_ref = refs[-1]
    width = refs[0].shape[1]
    for s in range(chunks):
        start = pl.multiple_of(lax.rem(me[0] + s, chunks) * width, width)
        out_ref[:, pl.ds(start, width)] = refs[s][...]


def regroup(experts, owners, count):
    shape = (experts * owners * count, owners * experts * count)
    row = lax.broadcasted_iota(jnp.int32, shape, 0)
    other = lax.broadcasted_iota(jnp.int32, shape, 1)
    wanted = jnp.zeros(shape, jnp.int32) + row
    for x in range(experts):
        for t in range(owners):
            first = (x * owners + t) * count
            inside = (row >= first) & (row < first + count)
            wanted = jnp.where(inside, row - first + (t * experts + x) * count, wanted)
    return (other == wanted).astype(jnp.bfloat16)


def select_kernel(*refs):
    packs, out_ref = refs[:-1], refs[-1]
    experts, count, _ = out_ref.shape
    rows = jnp.concatenate([ref[...].astype(jnp.float32) for ref in packs], axis=0)
    moved = jnp.dot(
        regroup(experts, len(packs), count // len(packs)),
        rows.astype(jnp.bfloat16),
        preferred_element_type=jnp.float32,
    ).astype(out_ref.dtype)
    for x in range(experts):
        out_ref[x] = moved[x * count:(x + 1) * count]


def gate_up_kernel(chunk, rows_ref, weight_ref, out_ref, done_ref=None):
    del chunk
    if done_ref is not None:
        done_ref[...] = jnp.zeros_like(done_ref)
    ff = weight_ref.shape[3]
    rows = rows_ref[0]
    for k in range(2):
        out_ref[0, :, k * ff:(k + 1) * ff] = jnp.dot(
            rows, weight_ref[0, k], preferred_element_type=jnp.float32
        ).astype(out_ref.dtype)


def gate_up(chunk, chunks, rows, weight, dtype, done=False):
    experts, count, depth = rows.shape
    ff = weight.shape[3] // chunks
    return pl.pallas_call(
        gate_up_kernel,
        grid_spec=pltpu.PrefetchScalarGridSpec(
            num_scalar_prefetch=1,
            grid=(experts,),
            in_specs=[
                pl.BlockSpec((1, count, depth), lambda x, c: (x, 0, 0)),
                pl.BlockSpec((1, 2, depth, ff), lambda x, c: (x, 0, 0, c[0])),
            ],
            out_specs=[pl.BlockSpec((1, count, 2 * ff), lambda x, c: (x, 0, 0))]
            + [pl.BlockSpec((8, LANES), lambda x, c: (0, 0))] * done,
        ),
        out_shape=[jax.ShapeDtypeStruct((experts, count, 2 * ff), dtype)]
        + [jax.ShapeDtypeStruct((8, LANES), jnp.float32)] * done,
        compiler_params=params(52),
        cost_estimate=pl.CostEstimate(
            flops=4 * experts * count * depth * ff,
            bytes_accessed=4 * experts * depth * ff,
            transcendentals=0,
        ),
        name="gate_up",
    )(chunk, rows, weight)


def activate_kernel(own_ref, *refs):
    other_refs, out_ref = refs[:-2], refs[-1]
    ff = out_ref.shape[2]
    for x in range(out_ref.shape[0]):
        total = own_ref[x]
        for ref in other_refs:
            total = total + ref[x].astype(jnp.float32)
        gate, up = total[:, :ff], total[:, ff:]
        out_ref[x] = (gate / (1.0 + jnp.exp(-gate)) * up).astype(out_ref.dtype)


def down_own_kernel(me, part_ref, weight_ref, sum_ref):
    ff = part_ref.shape[2]
    chunk = pl.ds(pl.multiple_of(me[0] * ff, ff), ff)
    for x in range(part_ref.shape[0]):
        sum_ref[x] = jnp.dot(part_ref[x], weight_ref[x, chunk], preferred_element_type=jnp.float32)


def down_rest_kernel(chunks, me, sum_ref, *refs):
    parts, weight_ref, out_refs = refs[:chunks - 1], refs[chunks - 1], refs[chunks:]
    experts, count, width = sum_ref.shape
    ff = parts[0].shape[2]
    sums = []
    for x in range(experts):
        total = sum_ref[x]
        for s in range(1, chunks):
            chunk = lax.rem(me[0] + chunks - s, chunks)
            chunk = pl.ds(pl.multiple_of(chunk * ff, ff), ff)
            total = total + jnp.dot(
                parts[s - 1][x], weight_ref[x, chunk], preferred_element_type=jnp.float32
            )
        sums.append(total.astype(jnp.bfloat16))
    owners = len(out_refs)
    rows = experts * count // owners
    moved = lax.dot_general(
        regroup(experts, owners, count // owners),
        jnp.concatenate(sums, axis=0),
        (((0,), (0,)), ((), ())),
        preferred_element_type=jnp.float32,
    )
    for t in range(owners):
        out_refs[t][...] = moved[t * rows:(t + 1) * rows].astype(out_refs[t].dtype)


def shifted(value, axis, steps):
    size = lax.axis_size(axis)
    return lax.ppermute(value, axis, [(i, (i + steps) % size) for i in range(size)])


def farthest_first(size):
    return sorted(range(1, size), key=lambda s: -min(s, size - s))


def exchange(values, axis, back=False):
    out = [values[0]] + [None] * (len(values) - 1)
    for s in farthest_first(len(values)):
        out[s] = shifted(values[s], axis, -s if back else s)
    return out


def call(kernel, index, inputs, outputs, name, limit=16, after=()):
    single = not isinstance(outputs, list)
    return pl.pallas_call(
        kernel,
        in_specs=[pl.BlockSpec(memory_space=pltpu.SMEM)] * len(index)
        + [pl.BlockSpec(memory_space=pltpu.VMEM)] * len(inputs)
        + [pl.BlockSpec(memory_space=pl.ANY)] * len(after),
        out_specs=pl.BlockSpec(memory_space=pltpu.VMEM)
        if single
        else [pl.BlockSpec(memory_space=pltpu.VMEM)] * len(outputs),
        out_shape=outputs,
        compiler_params=params(limit),
        name=name,
    )(*index, *inputs, *after)


def experts_by_columns(held, gate_up_weight, down_weight, owners, attention):
    inner = lax.axis_size("inner")
    experts, count, _ = held.shape
    ff, width = down_weight.shape[1:]
    me = lax.axis_index("inner").astype(jnp.int32)
    level = me.reshape(1)
    others = []
    for s in farthest_first(inner):
        (part,) = gate_up(((me + s) % inner).reshape(1), inner, held, gate_up_weight, jnp.bfloat16)
        others.append(shifted(part, "inner", s))
    own, done = gate_up(level, inner, held, gate_up_weight, jnp.float32, True)
    attended = attention(done)
    active = call(
        activate_kernel,
        [],
        [own, *others],
        jax.ShapeDtypeStruct((experts, count, ff // inner), jnp.bfloat16),
        "activate",
        after=[attended],
    )
    parts = exchange([active] * inner, "inner")
    sums = call(
        down_own_kernel,
        [level],
        [parts[0], down_weight],
        jax.ShapeDtypeStruct((experts, count, width), jnp.float32),
        "down_own",
        24,
    )
    back = call(
        functools.partial(down_rest_kernel, inner),
        [level],
        [sums, *parts[1:], down_weight],
        [jax.ShapeDtypeStruct((experts * count // owners, width), jnp.bfloat16)] * owners,
        "down_rest",
        24,
    )
    return back, attended


def experts_by_rows(held, gate_up_weight, down_weight, owners, attention):
    experts, count, _ = held.shape
    partial = jnp.einsum("xsd,xkdf->sxkf", held, gate_up_weight, preferred_element_type=jnp.float32)
    summed = lax.psum_scatter(partial, "inner", scatter_dimension=0, tiled=True)
    active = (jax.nn.silu(summed[:, :, 0]) * summed[:, :, 1]).astype(jnp.bfloat16)
    active = lax.all_gather(active, "inner", axis=0, tiled=True)
    outputs = jnp.einsum("sxf,xfd->xsd", active, down_weight, preferred_element_type=jnp.float32)
    outputs = outputs.astype(jnp.bfloat16).reshape(experts, owners, count // owners, -1)
    back = [outputs[:, t].reshape(experts * count // owners, -1) for t in range(owners)]
    return back, attention(held)


def body(
    queries,
    new_key_value,
    cached_key_value,
    parents,
    hidden,
    routes,
    gate_values,
    gate_up_weight,
    down_weight,
):
    owners, inner = lax.axis_size("expert"), lax.axis_size("inner")
    experts, _, depth, ff = gate_up_weight.shape
    rows, model = hidden.shape
    width = down_weight.shape[2]
    top = routes.shape[1]
    column = lax.axis_index("expert").astype(jnp.int32).reshape(1)
    level = lax.axis_index("inner").astype(jnp.int32).reshape(1)
    slots = experts * CAP * inner

    attention = functools.partial(attend, queries, new_key_value, cached_key_value, parents)

    slices = call(
        prepare_kernel,
        [level],
        [routes.T, gate_values.T, hidden],
        [jax.ShapeDtypeStruct((rows, depth + LANES), jnp.bfloat16)] * inner,
        "prepare",
    )
    slices = exchange(slices, "inner")
    packs = call(
        functools.partial(pack_kernel, top, experts, inner),
        [column, level],
        slices,
        [jax.ShapeDtypeStruct((slots, depth), jnp.bfloat16)] * owners,
        "pack",
    )
    packs = exchange(packs, "expert")
    held = call(
        select_kernel,
        [],
        packs,
        jax.ShapeDtypeStruct((experts, owners * CAP * inner, depth), jnp.bfloat16),
        "select",
        24,
    )
    even = ff % (inner * LANES) == 0
    back, attended = (experts_by_columns if even else experts_by_rows)(
        held, gate_up_weight, down_weight, owners, attention
    )
    back = exchange(back, "expert", back=True)
    pieces = call(
        functools.partial(combine_kernel, top, experts, inner),
        [column, level],
        [*slices, *back],
        [jax.ShapeDtypeStruct((rows, width), jnp.bfloat16)] * inner,
        "combine",
    )
    pieces = exchange(pieces, "inner", back=True)
    expert_out = call(
        assemble_kernel,
        [level],
        pieces,
        jax.ShapeDtypeStruct((rows, model), jnp.bfloat16),
        "assemble",
    )
    return attended, expert_out


def solution(mesh):
    rows = ("groups", "expert", "inner")
    return jax.shard_map(
        body,
        mesh=mesh,
        in_specs=(
            P(rows, None),
            P(rows, None),
            P(rows, None, None, None),
            P(rows, None),
            P(rows, None),
            P(rows, None),
            P(rows, None),
            P("expert", None, "inner", None),
            P("expert", None, "inner"),
        ),
        out_specs=(P(rows, None), P(rows, None)),
        check_vma=False,
    )
```

time: 69.8 us -> 65.6 us (0.940)
  waiting for transfers between devices: 24.5 us -> 18.1 us
  local copies, waits for them, and re-layouts: 7.63 us -> 2.87 us
  Pallas kernels: 15.7 us -> 19.4 us
  starting transfers between devices: 20.7 us -> 24.2 us
    ppermute x6 -> x18, starting transfers between devices: 8.71 us -> 24.2 us  [shifted(): lax.ppermute(value, axis, [(i, (i + steps) % size) for i in range(size)])]
    all_to_all x2 -> x0, waiting for transfers between devices: 12.7 us -> none  [the longest x1 10 us: body(): lax.all_to_all(sent.reshape(sources, block, depth), both, split_axis=0, c...]
    all_to_all x2 -> x0, starting transfers between devices: 12 us -> none  [the longest x1 7.36 us: body(): lax.all_to_all(sent.reshape(sources, block, depth), both, split_axis=0, c...]
    ppermute x6 -> x18, waiting for transfers between devices: 11.8 us -> 18.1 us  [shifted(): lax.ppermute(value, axis, [(i, (i + steps) % size) for i in range(size)])]
    pallas_call x4, Pallas kernels: 4.27 us -> 9.29 us  [gate_up(): pl.pallas_call(gate_up_kernel, grid_spec=pltpu.PrefetchScalarGridSpec(num...]
    unnamed x29 -> x23, local copies, waits for them, and re-layouts: 7.63 us -> 2.87 us
    pallas_call x5 -> x8, Pallas kernels: 5.59 us -> 4.25 us  [call(): pl.pallas_call(kernel, in_specs=[pl.BlockSpec(memory_space=pltpu.SMEM)] *...]
  transfers between devices with their start and end apart: 8 -> 18, of which waited for: 6 -> 13; matrix products, arithmetic and copies ran while one was open for 2% -> 0% of each run, Pallas kernels for 13% -> 20%
where the time goes in v2:
time: 65.6 us; the launch traced here: 65.4 us
  starting transfers between devices  24.2 us (37%)
  Pallas kernels  19.4 us (30%)
  waiting for transfers between devices  18.1 us (28%)
  local copies, waits for them, and re-layouts  2.87 us (4%)
  between operations  0.84 us (1%)
    ppermute x18, starting transfers between devices, shifted(): lax.ppermute(value, axis, [(i, (i + steps) % size) for i in range(size)])  24.2 us
    ppermute x18, waiting for transfers between devices, shifted(): lax.ppermute(value, axis, [(i, (i + steps) % size) for i in range(size)])  18.1 us
    pallas_call x4, Pallas kernels, gate_up(): pl.pallas_call(gate_up_kernel, grid_spec=pltpu.PrefetchScalarGridSpec(num...  9.29 us
    pallas_call x1, Pallas kernels, attend(): pl.pallas_call(attend_kernel, grid_spec=pltpu.PrefetchScalarGridSpec(num_...  5.85 us
    pallas_call x8, Pallas kernels, call(): pl.pallas_call(kernel, in_specs=[pl.BlockSpec(memory_space=pltpu.SMEM)] *...  4.25 us
    unnamed x23, local copies, waits for them, and re-layouts  2.87 us
  transfers between devices with their start and end apart: 18, of which 13 were waited for; matrix products, arithmetic and copies ran while one was open for 0% of the time, Pallas kernels for 20%

profile of v2, /device:TPU:0, one launch (start us, length us, event | category | flops | bytes accessed | tf_op | source)
XLA Modules:
  0.0 65.4 jit_solution(5276590937454240751)
XLA Ops:
  0.6 0.8 %copy-done.2 = bf16[8,4096]{1,0:T(8,128)(2,1)S(1)} copy-done((bf16[8,4096]{1,0:T(8,128)(2,1)S(1)}, bf16[8,4096]{1,0:T(8,128)(2,1)}, u32[]{:S(2)}) %copy-start.2) | copy-done | bytes 65560
  1.5 0.7 %copy-done.3 = s32[8,2]{0,1:T(2,128)S(1)} copy-done((s32[8,2]{0,1:T(2,128)S(1)}, s32[8,2]{0,1:T(2,128)}, u32[]{:S(2)}) %copy-start.3) | copy-done | bytes 88
  2.2 0.7 copy-done.4
  2.8 0.2 prepare.1
  3.0 3.0 %collective-permute-start = (bf16[8,1152]{1,0:T(8,128)(2,1)S(1)}, bf16[8,1152]{1,0:T(8,128)(2,1)S(1)}, u32[]{:S(2)}, u32[]{:S(2)}) collective-permute-start(bf16[8,1152]{1,0:T(8,128)(2,1)S(1)} %get-tuple-element.21), channel_id=1, source_target_pairs={{0,1},{1,2},{2,3},{3,0},{4,5},{5,6},{6,7},{7,4},{8,9},{9,10},{10,1... | collective-permute-start | bytes 55304 | tf_op jit(solution)/shard_map/ppermute | solution.py:308
  6.0 2.6 %collective-permute-start.1 = (bf16[8,1152]{1,0:T(8,128)(2,1)S(1)}, bf16[8,1152]{1,0:T(8,128)(2,1)S(1)}, u32[]{:S(2)}, u32[]{:S(2)}) collective-permute-start(bf16[8,1152]{1,0:T(8,128)(2,1)S(1)} %get-tuple-element.22), channel_id=1, source_target_pairs={{0,2},{1,3},{2,0},{3,1},{4,6},{5,7},{6,4},{7,5},{8,10},{9,11},{10,... | collective-permute-start | bytes 55304 | tf_op jit(solution)/shard_map/ppermute | solution.py:308
  8.6 1.3 %collective-permute-start.2 = (bf16[8,1152]{1,0:T(8,128)(2,1)S(1)}, bf16[8,1152]{1,0:T(8,128)(2,1)S(1)}, u32[]{:S(2)}, u32[]{:S(2)}) collective-permute-start(bf16[8,1152]{1,0:T(8,128)(2,1)S(1)} %get-tuple-element.23), channel_id=1, source_target_pairs={{0,3},{1,0},{2,1},{3,2},{4,7},{5,4},{6,5},{7,6},{8,11},{9,8},{10,9... | collective-permute-start | bytes 55304 | tf_op jit(solution)/shard_map/ppermute | solution.py:308
  10.0 0.8 %collective-permute-done.1.refs_2_ = bf16[8,1152]{1,0:T(8,128)(2,1)S(1)} collective-permute-done((bf16[8,1152]{1,0:T(8,128)(2,1)S(1)}, bf16[8,1152]{1,0:T(8,128)(2,1)S(1)}, u32[]{:S(2)}, u32[]{:S(2)}) %collective-permute-start.1) | collective-permute-done | bytes 18464 | tf_op jit(solution)/shard_map/ppermute | solution.py:308
  10.8 1.6 %collective-permute-done.2.refs_3_ = bf16[8,1152]{1,0:T(8,128)(2,1)S(1)} collective-permute-done((bf16[8,1152]{1,0:T(8,128)(2,1)S(1)}, bf16[8,1152]{1,0:T(8,128)(2,1)S(1)}, u32[]{:S(2)}, u32[]{:S(2)}) %collective-permute-start.2) | collective-permute-done | bytes 18464 | tf_op jit(solution)/shard_map/ppermute | solution.py:308
  12.4 0.8 %pack.1 = (bf16[24,1024]{1,0:T(8,128)(2,1)S(1)}, bf16[24,1024]{1,0:T(8,128)(2,1)S(1)}, bf16[24,1024]{1,0:T(8,128)(2,1)S(1)}, bf16[24,1024]{1,0:T(8,128)(2,1)S(1)}) custom-call(s32[1]{0:T(128)} %bitcast.2.column, s32[1]{0:T(128)} %bitcast.1.me.level.chunk, bf16[8,1152]{1,0:T(8,128)(2,1)S(1)} %get-tuple-element.20.refs_0_, ...), custom_call_target="tpu_custom_call" | custom-call | tf_op jit(solution)/shard_map/pack/pallas_call | solution.py:324
  13.2 0.1 collective-permute-start.3
  13.2 1.6 %collective-permute-start.4 = (bf16[24,1024]{1,0:T(8,128)(2,1)S(1)}, bf16[24,1024]{1,0:T(8,128)(2,1)S(1)}, u32[]{:S(2)}, u32[]{:S(2)}) collective-permute-start(bf16[24,1024]{1,0:T(8,128)(2,1)S(1)} %get-tuple-element.26), channel_id=1, source_target_pairs={{0,8},{4,12},{8,0},{12,4},{1,9},{5,13},{9,1},{13,5},{2,10},{6,14},... | collective-permute-start | bytes 147464 | tf_op jit(solution)/shard_map/ppermute | solution.py:308
  14.8 1.4 %collective-permute-start.5 = (bf16[24,1024]{1,0:T(8,128)(2,1)S(1)}, bf16[24,1024]{1,0:T(8,128)(2,1)S(1)}, u32[]{:S(2)}, u32[]{:S(2)}) collective-permute-start(bf16[24,1024]{1,0:T(8,128)(2,1)S(1)} %get-tuple-element.27), channel_id=1, source_target_pairs={{0,12},{4,0},{8,4},{12,8},{1,13},{5,1},{9,5},{13,9},{2,14},{6,2},{... | collective-permute-start | bytes 147464 | tf_op jit(solution)/shard_map/ppermute | solution.py:308
  16.2 0.6 collective-permute-done.3.refs_1_
  16.7 0.7 collective-permute-done.4.refs_2_
  17.4 0.5 collective-permute-done.5.refs_3_
  17.9 0.2 select.7.rows_ref
  18.1 2.3 %gate_up.5 = bf16[2,48,768]{2,1,0:T(8,128)(2,1)S(1)} custom-call(s32[1]{0:T(128)} %bitcast.5.chunk, bf16[2,48,1024]{2,1,0:T(8,128)(2,1)S(1)} %select.7.rows_ref, bf16[2,2,1024,1536]{3,2,1,0:T(8,128)(2,1)} %weight_ref.8), custom_call_target="tpu_custom_call" | custom-call | flops 150994944 | bytes 3145728 | tf_op jit(solution)/shard_map/gate_up/pallas_call | solution.py:238
  20.4 1.0 %collective-permute-start.6 = (bf16[2,48,768]{2,1,0:T(8,128)(2,1)S(1)}, bf16[2,48,768]{2,1,0:T(8,128)(2,1)S(1)}, u32[]{:S(2)}, u32[]{:S(2)}) collective-permute-start(bf16[2,48,768]{2,1,0:T(8,128)(2,1)S(1)} %gate_up.5), channel_id=1, source_target_pairs={{0,2},{1,3},{2,0},{3,1},{4,6},{5,7},{6,4},{7,5},{8,10},{9,11},{10,... | collective-permute-start | bytes 442376 | tf_op jit(solution)/shard_map/ppermute | solution.py:308
  21.4 2.3 %gate_up.6 = bf16[2,48,768]{2,1,0:T(8,128)(2,1)S(1)} custom-call(s32[1]{0:T(128)} %bitcast.6.chunk, bf16[2,48,1024]{2,1,0:T(8,128)(2,1)S(1)} %select.7.rows_ref, bf16[2,2,1024,1536]{3,2,1,0:T(8,128)(2,1)} %weight_ref.8), custom_call_target="tpu_custom_call" | custom-call | flops 150994944 | bytes 3145728 | tf_op jit(solution)/shard_map/gate_up/pallas_call | solution.py:238
  23.7 2.9 %collective-permute-start.7 = (bf16[2,48,768]{2,1,0:T(8,128)(2,1)S(1)}, bf16[2,48,768]{2,1,0:T(8,128)(2,1)S(1)}, u32[]{:S(2)}, u32[]{:S(2)}) collective-permute-start(bf16[2,48,768]{2,1,0:T(8,128)(2,1)S(1)} %gate_up.6), channel_id=1, source_target_pairs={{0,1},{1,2},{2,3},{3,0},{4,5},{5,6},{6,7},{7,4},{8,9},{9,10},{10,1... | collective-permute-start | bytes 442376 | tf_op jit(solution)/shard_map/ppermute | solution.py:308
  26.6 2.3 %gate_up.7 = bf16[2,48,768]{2,1,0:T(8,128)(2,1)S(1)} custom-call(s32[1]{0:T(128)} %bitcast.7.chunk, bf16[2,48,1024]{2,1,0:T(8,128)(2,1)S(1)} %select.7.rows_ref, bf16[2,2,1024,1536]{3,2,1,0:T(8,128)(2,1)} %weight_ref.8), custom_call_target="tpu_custom_call" | custom-call | flops 150994944 | bytes 3145728 | tf_op jit(solution)/shard_map/gate_up/pallas_call | solution.py:238
  28.9 1.1 %collective-permute-start.8 = (bf16[2,48,768]{2,1,0:T(8,128)(2,1)S(1)}, bf16[2,48,768]{2,1,0:T(8,128)(2,1)S(1)}, u32[]{:S(2)}, u32[]{:S(2)}) collective-permute-start(bf16[2,48,768]{2,1,0:T(8,128)(2,1)S(1)} %gate_up.7), channel_id=1, source_target_pairs={{0,3},{1,0},{2,1},{3,2},{4,7},{5,4},{6,5},{7,6},{8,11},{9,8},{10,9... | collective-permute-start | bytes 442376 | tf_op jit(solution)/shard_map/ppermute | solution.py:308
  30.1 2.4 %gate_up.4 = (f32[2,48,768]{2,1,0:T(8,128)S(1)}, f32[8,128]{1,0:T(8,128)S(1)}) custom-call(s32[1]{0:T(128)} %bitcast.1.me.level.chunk, bf16[2,48,1024]{2,1,0:T(8,128)(2,1)S(1)} %select.7.rows_ref, bf16[2,2,1024,1536]{3,2,1,0:T(8,128)(2,1)} %weight_ref.8), custom_call_target="tpu_custom_call" | custom-call | flops 150994944 | bytes 3145728 | tf_op jit(solution)/shard_map/gate_up/pallas_call | solution.py:238
  32.5 0.5 copy-done
  33.0 5.8 %attend.1 = bf16[8,64,128]{2,1,0:T(8,128)(2,1)S(1)} custom-call(s32[8]{0:T(128)S(1)} %bitcast.29, bf16[8,64,128]{2,1,0:T(8,128)(2,1)S(1)} %bitcast.24, bf16[8,8,128]{2,1,0:T(8,128)(2,1)S(1)} %bitcast.26, bf16[1,8,192,1024]{3,2,1,0:T(8,128)(2,1)S(1)} %copy-done, f32[8,128]{1,0:T(8,128)S(1)} %get-tuple-element.28.after_ref), custom_call_target="tpu_custom_call" | custom-call | flops 50331648 | bytes 3145728 | tf_op jit(solution)/shard_map/attend/pallas_call | solution.py:60
  38.9 0.1 copy.17
  39.0 0.1 activate.1.part_ref
  39.1 1.1 %collective-permute-start.9 = (bf16[2,48,384]{2,1,0:T(8,128)(2,1)S(1)}, bf16[2,48,384]{2,1,0:T(8,128)(2,1)S(1)}, u32[]{:S(2)}, u32[]{:S(2)}) collective-permute-start(bf16[2,48,384]{2,1,0:T(8,128)(2,1)S(1)} %activate.1.part_ref), channel_id=1, source_target_pairs={{0,1},{1,2},{2,3},{3,0},{4,5},{5,6},{6,7},{7,4},{8,9},{9,10},{10,1... | collective-permute-start | bytes 221192 | tf_op jit(solution)/shard_map/ppermute | solution.py:308
  40.2 0.0 collective-permute-start.10
  40.2 2.8 %collective-permute-start.11 = (bf16[2,48,384]{2,1,0:T(8,128)(2,1)S(1)}, bf16[2,48,384]{2,1,0:T(8,128)(2,1)S(1)}, u32[]{:S(2)}, u32[]{:S(2)}) collective-permute-start(bf16[2,48,384]{2,1,0:T(8,128)(2,1)S(1)} %activate.1.part_ref), channel_id=1, source_target_pairs={{0,3},{1,0},{2,1},{3,2},{4,7},{5,4},{6,5},{7,6},{8,11},{9,8},{10,9... | collective-permute-start | bytes 221192 | tf_op jit(solution)/shard_map/ppermute | solution.py:308
  43.0 0.4 down_own.1.sum_ref
  43.4 2.8 %collective-permute-done.9.refs_0_ = bf16[2,48,384]{2,1,0:T(8,128)(2,1)S(1)} collective-permute-done((bf16[2,48,384]{2,1,0:T(8,128)(2,1)S(1)}, bf16[2,48,384]{2,1,0:T(8,128)(2,1)S(1)}, u32[]{:S(2)}, u32[]{:S(2)}) %collective-permute-start.9) | collective-permute-done | bytes 73760 | tf_op jit(solution)/shard_map/ppermute | solution.py:308
  46.2 2.0 %collective-permute-done.10.refs_1_ = bf16[2,48,384]{2,1,0:T(8,128)(2,1)S(1)} collective-permute-done((bf16[2,48,384]{2,1,0:T(8,128)(2,1)S(1)}, bf16[2,48,384]{2,1,0:T(8,128)(2,1)S(1)}, u32[]{:S(2)}, u32[]{:S(2)}) %collective-permute-start.10) | collective-permute-done | bytes 73760 | tf_op jit(solution)/shard_map/ppermute | solution.py:308
  48.2 1.1 %down_rest.1 = (bf16[24,1024]{1,0:T(8,128)(2,1)S(1)}, bf16[24,1024]{1,0:T(8,128)(2,1)S(1)}, bf16[24,1024]{1,0:T(8,128)(2,1)S(1)}, bf16[24,1024]{1,0:T(8,128)(2,1)S(1)}) custom-call(s32[1]{0:T(128)} %bitcast.1.me.level.chunk, f32[2,48,1024]{2,1,0:T(8,128)S(1)} %down_own.1.sum_ref, bf16[2,48,384]{2,1,0:T(8,128)(2,1)S(1)} %collective-permute-done.9.refs_0_, ...), custom_call_target="tpu_custom_call" | custom-call | tf_op jit(solution)/shard_map/down_rest/pallas_call | solution.py:324
  49.3 0.7 %collective-permute-start.12 = (bf16[24,1024]{1,0:T(8,128)(2,1)S(1)}, bf16[24,1024]{1,0:T(8,128)(2,1)S(1)}, u32[]{:S(2)}, u32[]{:S(2)}) collective-permute-start(bf16[24,1024]{1,0:T(8,128)(2,1)S(1)} %get-tuple-element.31), channel_id=1, source_target_pairs={{0,12},{4,0},{8,4},{12,8},{1,13},{5,1},{9,5},{13,9},{2,14},{6,2},{... | collective-permute-start | bytes 147464 | tf_op jit(solution)/shard_map/ppermute | solution.py:308
  50.1 0.9 %collective-permute-start.13 = (bf16[24,1024]{1,0:T(8,128)(2,1)S(1)}, bf16[24,1024]{1,0:T(8,128)(2,1)S(1)}, u32[]{:S(2)}, u32[]{:S(2)}) collective-permute-start(bf16[24,1024]{1,0:T(8,128)(2,1)S(1)} %get-tuple-element.32), channel_id=1, source_target_pairs={{0,8},{4,12},{8,0},{12,4},{1,9},{5,13},{9,1},{13,5},{2,10},{6,14},... | collective-permute-start | bytes 147464 | tf_op jit(solution)/shard_map/ppermute | solution.py:308
  51.0 0.2 collective-permute-start.14
  51.1 0.8 %collective-permute-done.12.refs_5_ = bf16[24,1024]{1,0:T(8,128)(2,1)S(1)} collective-permute-done((bf16[24,1024]{1,0:T(8,128)(2,1)S(1)}, bf16[24,1024]{1,0:T(8,128)(2,1)S(1)}, u32[]{:S(2)}, u32[]{:S(2)}) %collective-permute-start.12) | collective-permute-done | bytes 49184 | tf_op jit(solution)/shard_map/ppermute | solution.py:308
  51.9 2.4 %collective-permute-done.13.refs_6_ = bf16[24,1024]{1,0:T(8,128)(2,1)S(1)} collective-permute-done((bf16[24,1024]{1,0:T(8,128)(2,1)S(1)}, bf16[24,1024]{1,0:T(8,128)(2,1)S(1)}, u32[]{:S(2)}, u32[]{:S(2)}) %collective-permute-start.13) | collective-permute-done | bytes 49184 | tf_op jit(solution)/shard_map/ppermute | solution.py:308
  54.4 0.3 collective-permute-done.14.refs_7_
  54.7 0.8 %combine.1 = (bf16[8,1024]{1,0:T(8,128)(2,1)S(1)}, bf16[8,1024]{1,0:T(8,128)(2,1)S(1)}, bf16[8,1024]{1,0:T(8,128)(2,1)S(1)}, bf16[8,1024]{1,0:T(8,128)(2,1)S(1)}) custom-call(s32[1]{0:T(128)} %bitcast.2.column, s32[1]{0:T(128)} %bitcast.1.me.level.chunk, bf16[8,1152]{1,0:T(8,128)(2,1)S(1)} %get-tuple-element.20.refs_0_, ...), custom_call_target="tpu_custom_call" | custom-call | tf_op jit(solution)/shard_map/combine/pallas_call | solution.py:324
  55.5 2.0 %collective-permute-start.15 = (bf16[8,1024]{1,0:T(8,128)(2,1)S(1)}, bf16[8,1024]{1,0:T(8,128)(2,1)S(1)}, u32[]{:S(2)}, u32[]{:S(2)}) collective-permute-start(bf16[8,1024]{1,0:T(8,128)(2,1)S(1)} %get-tuple-element.35), channel_id=1, source_target_pairs={{0,3},{1,0},{2,1},{3,2},{4,7},{5,4},{6,5},{7,6},{8,11},{9,8},{10,9... | collective-permute-start | bytes 49160 | tf_op jit(solution)/shard_map/ppermute | solution.py:308
  57.6 1.6 %collective-permute-start.16 = (bf16[8,1024]{1,0:T(8,128)(2,1)S(1)}, bf16[8,1024]{1,0:T(8,128)(2,1)S(1)}, u32[]{:S(2)}, u32[]{:S(2)}) collective-permute-start(bf16[8,1024]{1,0:T(8,128)(2,1)S(1)} %get-tuple-element.36), channel_id=1, source_target_pairs={{0,2},{1,3},{2,0},{3,1},{4,6},{5,7},{6,4},{7,5},{8,10},{9,11},{10,... | collective-permute-start | bytes 49160 | tf_op jit(solution)/shard_map/ppermute | solution.py:308
  59.2 0.3 collective-permute-done.15.refs_1_
  59.5 2.8 %collective-permute-done.16.refs_2_ = bf16[8,1024]{1,0:T(8,128)(2,1)S(1)} collective-permute-done((bf16[8,1024]{1,0:T(8,128)(2,1)S(1)}, bf16[8,1024]{1,0:T(8,128)(2,1)S(1)}, u32[]{:S(2)}, u32[]{:S(2)}) %collective-permute-start.16) | collective-permute-done | bytes 16416 | tf_op jit(solution)/shard_map/ppermute | solution.py:308
  62.2 2.5 %collective-permute-done.17.refs_3_ = bf16[8,1024]{1,0:T(8,128)(2,1)S(1)} collective-permute-done((bf16[8,1024]{1,0:T(8,128)(2,1)S(1)}, bf16[8,1024]{1,0:T(8,128)(2,1)S(1)}, u32[]{:S(2)}, u32[]{:S(2)}) %collective-permute-start.17) | collective-permute-done | bytes 16416 | tf_op jit(solution)/shard_map/ppermute | solution.py:308
  64.7 0.6 assemble.1
  (25 shorter events, 0.1 us)
Async XLA Ops:
  0.6 0.8 %copy-start.2 = (bf16[8,4096]{1,0:T(8,128)(2,1)S(1)}, bf16[8,4096]{1,0:T(8,128)(2,1)}, u32[]{:S(2)}) copy-start(bf16[8,4096]{1,0:T(8,128)(2,1)} %hidden_ref.1) | copy-start | bytes 196612
  1.5 0.7 %copy-start.3 = (s32[8,2]{0,1:T(2,128)S(1)}, s32[8,2]{0,1:T(2,128)}, u32[]{:S(2)}) copy-start(s32[8,2]{0,1:T(2,128)} %param.14) | copy-start | bytes 196
  2.2 0.7 %copy-start.4 = (bf16[8,2]{0,1:T(2,128)(2,1)S(1)}, bf16[8,2]{0,1:T(2,128)(2,1)}, u32[]{:S(2)}) copy-start(bf16[8,2]{0,1:T(2,128)(2,1)} %param.15) | copy-start | bytes 100
  3.0 7.0 %collective-permute-start = (bf16[8,1152]{1,0:T(8,128)(2,1)S(1)}, bf16[8,1152]{1,0:T(8,128)(2,1)S(1)}, u32[]{:S(2)}, u32[]{:S(2)}) collective-permute-start(bf16[8,1152]{1,0:T(8,128)(2,1)S(1)} %get-tuple-element.21), channel_id=1, source_target_pairs={{0,1},{1,2},{2,3},{3,0},{4,5},{5,6},{6,7},{7,4},{8,9},{9,10},{10,1... | collective-permute-start | bytes 55304 | tf_op jit(solution)/shard_map/ppermute | solution.py:308
  6.0 4.8 %collective-permute-start.1 = (bf16[8,1152]{1,0:T(8,128)(2,1)S(1)}, bf16[8,1152]{1,0:T(8,128)(2,1)S(1)}, u32[]{:S(2)}, u32[]{:S(2)}) collective-permute-start(bf16[8,1152]{1,0:T(8,128)(2,1)S(1)} %get-tuple-element.22), channel_id=1, source_target_pairs={{0,2},{1,3},{2,0},{3,1},{4,6},{5,7},{6,4},{7,5},{8,10},{9,11},{10,... | collective-permute-start | bytes 55304 | tf_op jit(solution)/shard_map/ppermute | solution.py:308
  8.6 3.8 %collective-permute-start.2 = (bf16[8,1152]{1,0:T(8,128)(2,1)S(1)}, bf16[8,1152]{1,0:T(8,128)(2,1)S(1)}, u32[]{:S(2)}, u32[]{:S(2)}) collective-permute-start(bf16[8,1152]{1,0:T(8,128)(2,1)S(1)} %get-tuple-element.23), channel_id=1, source_target_pairs={{0,3},{1,0},{2,1},{3,2},{4,7},{5,4},{6,5},{7,6},{8,11},{9,8},{10,9... | collective-permute-start | bytes 55304 | tf_op jit(solution)/shard_map/ppermute | solution.py:308
  13.2 3.6 %collective-permute-start.3 = (bf16[24,1024]{1,0:T(8,128)(2,1)S(1)}, bf16[24,1024]{1,0:T(8,128)(2,1)S(1)}, u32[]{:S(2)}, u32[]{:S(2)}) collective-permute-start(bf16[24,1024]{1,0:T(8,128)(2,1)S(1)} %get-tuple-element.25), channel_id=1, source_target_pairs={{0,4},{4,8},{8,12},{12,0},{1,5},{5,9},{9,13},{13,1},{2,6},{6,10},{... | collective-permute-start | bytes 147464 | tf_op jit(solution)/shard_map/ppermute | solution.py:308
  13.2 4.2 %collective-permute-start.4 = (bf16[24,1024]{1,0:T(8,128)(2,1)S(1)}, bf16[24,1024]{1,0:T(8,128)(2,1)S(1)}, u32[]{:S(2)}, u32[]{:S(2)}) collective-permute-start(bf16[24,1024]{1,0:T(8,128)(2,1)S(1)} %get-tuple-element.26), channel_id=1, source_target_pairs={{0,8},{4,12},{8,0},{12,4},{1,9},{5,13},{9,1},{13,5},{2,10},{6,14},... | collective-permute-start | bytes 147464 | tf_op jit(solution)/shard_map/ppermute | solution.py:308
  14.8 3.1 %collective-permute-start.5 = (bf16[24,1024]{1,0:T(8,128)(2,1)S(1)}, bf16[24,1024]{1,0:T(8,128)(2,1)S(1)}, u32[]{:S(2)}, u32[]{:S(2)}) collective-permute-start(bf16[24,1024]{1,0:T(8,128)(2,1)S(1)} %get-tuple-element.27), channel_id=1, source_target_pairs={{0,12},{4,0},{8,4},{12,8},{1,13},{5,1},{9,5},{13,9},{2,14},{6,2},{... | collective-permute-start | bytes 147464 | tf_op jit(solution)/shard_map/ppermute | solution.py:308
  20.4 18.6 %collective-permute-start.6 = (bf16[2,48,768]{2,1,0:T(8,128)(2,1)S(1)}, bf16[2,48,768]{2,1,0:T(8,128)(2,1)S(1)}, u32[]{:S(2)}, u32[]{:S(2)}) collective-permute-start(bf16[2,48,768]{2,1,0:T(8,128)(2,1)S(1)} %gate_up.5), channel_id=1, source_target_pairs={{0,2},{1,3},{2,0},{3,1},{4,6},{5,7},{6,4},{7,5},{8,10},{9,11},{10,... | collective-permute-start | bytes 442376 | tf_op jit(solution)/shard_map/ppermute | solution.py:308
  23.7 15.3 %collective-permute-start.7 = (bf16[2,48,768]{2,1,0:T(8,128)(2,1)S(1)}, bf16[2,48,768]{2,1,0:T(8,128)(2,1)S(1)}, u32[]{:S(2)}, u32[]{:S(2)}) collective-permute-start(bf16[2,48,768]{2,1,0:T(8,128)(2,1)S(1)} %gate_up.6), channel_id=1, source_target_pairs={{0,1},{1,2},{2,3},{3,0},{4,5},{5,6},{6,7},{7,4},{8,9},{9,10},{10,1... | collective-permute-start | bytes 442376 | tf_op jit(solution)/shard_map/ppermute | solution.py:308
  26.6 3.4 %copy-start.6 = (bf16[8,8192]{1,0:T(8,128)(2,1)S(1)}, bf16[8,8192]{1,0:T(8,128)(2,1)}, u32[]{:S(2)}) copy-start(bf16[8,8192]{1,0:T(8,128)(2,1)} %param.9) | copy-start | bytes 393220
  26.6 3.4 %copy-start.7 = (bf16[8,1024]{1,0:T(8,128)(2,1)S(1)}, bf16[8,1024]{1,0:T(8,128)(2,1)}, u32[]{:S(2)}) copy-start(bf16[8,1024]{1,0:T(8,128)(2,1)} %param.10) | copy-start | bytes 49156
  28.9 10.1 %collective-permute-start.8 = (bf16[2,48,768]{2,1,0:T(8,128)(2,1)S(1)}, bf16[2,48,768]{2,1,0:T(8,128)(2,1)S(1)}, u32[]{:S(2)}, u32[]{:S(2)}) collective-permute-start(bf16[2,48,768]{2,1,0:T(8,128)(2,1)S(1)} %gate_up.7), channel_id=1, source_target_pairs={{0,3},{1,0},{2,1},{3,2},{4,7},{5,4},{6,5},{7,6},{8,11},{9,8},{10,9... | collective-permute-start | bytes 442376 | tf_op jit(solution)/shard_map/ppermute | solution.py:308
  30.0 13.0 %slice-start = ((s8[6291456]{0:T(1024)(128)(4,1)}), s8[4194304]{0:T(1024)(128)(4,1)S(1)}, s32[]{:S(2)}) async-start(s8[6291456]{0:T(1024)(128)(4,1)} %bitcast.20), calls=%async_computation | async-start | bytes 8388608
  30.0 3.0 %copy-start = (bf16[1,8,192,1024]{3,2,1,0:T(8,128)(2,1)S(1)}, bf16[1,8,192,1024]{3,2,1,0:T(8,128)(2,1)}, u32[]{:S(2)}) copy-start(bf16[1,8,192,1024]{3,2,1,0:T(8,128)(2,1)} %cache_ref.1) | copy-start | bytes 9437188
  30.0 3.0 %copy-start.5 = (s32[1,8]{1,0:T(1,128)S(1)}, s32[1,8]{1,0:T(1,128)}, u32[]{:S(2)}) copy-start(s32[1,8]{1,0:T(1,128)} %param.12) | copy-start | bytes 100
  30.0 13.0 %slice-start.1 = ((s8[6291456]{0:T(1024)(128)(4,1)}), s8[2097152]{0:T(1024)(128)(4,1)S(1)}, s32[]{:S(2)}) async-start(s8[6291456]{0:T(1024)(128)(4,1)} %bitcast.20), calls=%async_computation.1 | async-start | bytes 4194304
  39.0 10.4 %copy-start.1 = (bf16[1,8,64,128]{3,1,2,0:T(8,128)(2,1)}, bf16[1,8,64,128]{3,1,2,0:T(8,128)(2,1)S(1)}, u32[]{:S(2)}) copy-start(bf16[1,8,64,128]{3,1,2,0:T(8,128)(2,1)S(1)} %copy.17) | copy-start | bytes 393220
  39.1 7.1 %collective-permute-start.9 = (bf16[2,48,384]{2,1,0:T(8,128)(2,1)S(1)}, bf16[2,48,384]{2,1,0:T(8,128)(2,1)S(1)}, u32[]{:S(2)}, u32[]{:S(2)}) collective-permute-start(bf16[2,48,384]{2,1,0:T(8,128)(2,1)S(1)} %activate.1.part_ref), channel_id=1, source_target_pairs={{0,1},{1,2},{2,3},{3,0},{4,5},{5,6},{6,7},{7,4},{8,9},{9,10},{10,1... | collective-permute-start | bytes 221192 | tf_op jit(solution)/shard_map/ppermute | solution.py:308
  40.2 8.0 %collective-permute-start.10 = (bf16[2,48,384]{2,1,0:T(8,128)(2,1)S(1)}, bf16[2,48,384]{2,1,0:T(8,128)(2,1)S(1)}, u32[]{:S(2)}, u32[]{:S(2)}) collective-permute-start(bf16[2,48,384]{2,1,0:T(8,128)(2,1)S(1)} %activate.1.part_ref), channel_id=1, source_target_pairs={{0,2},{1,3},{2,0},{3,1},{4,6},{5,7},{6,4},{7,5},{8,10},{9,11},{10,... | collective-permute-start | bytes 221192 | tf_op jit(solution)/shard_map/ppermute | solution.py:308
  40.2 8.0 %collective-permute-start.11 = (bf16[2,48,384]{2,1,0:T(8,128)(2,1)S(1)}, bf16[2,48,384]{2,1,0:T(8,128)(2,1)S(1)}, u32[]{:S(2)}, u32[]{:S(2)}) collective-permute-start(bf16[2,48,384]{2,1,0:T(8,128)(2,1)S(1)} %activate.1.part_ref), channel_id=1, source_target_pairs={{0,3},{1,0},{2,1},{3,2},{4,7},{5,4},{6,5},{7,6},{8,11},{9,8},{10,9... | collective-permute-start | bytes 221192 | tf_op jit(solution)/shard_map/ppermute | solution.py:308
  49.3 2.6 %collective-permute-start.12 = (bf16[24,1024]{1,0:T(8,128)(2,1)S(1)}, bf16[24,1024]{1,0:T(8,128)(2,1)S(1)}, u32[]{:S(2)}, u32[]{:S(2)}) collective-permute-start(bf16[24,1024]{1,0:T(8,128)(2,1)S(1)} %get-tuple-element.31), channel_id=1, source_target_pairs={{0,12},{4,0},{8,4},{12,8},{1,13},{5,1},{9,5},{13,9},{2,14},{6,2},{... | collective-permute-start | bytes 147464 | tf_op jit(solution)/shard_map/ppermute | solution.py:308
  50.1 4.3 %collective-permute-start.13 = (bf16[24,1024]{1,0:T(8,128)(2,1)S(1)}, bf16[24,1024]{1,0:T(8,128)(2,1)S(1)}, u32[]{:S(2)}, u32[]{:S(2)}) collective-permute-start(bf16[24,1024]{1,0:T(8,128)(2,1)S(1)} %get-tuple-element.32), channel_id=1, source_target_pairs={{0,8},{4,12},{8,0},{12,4},{1,9},{5,13},{9,1},{13,5},{2,10},{6,14},... | collective-permute-start | bytes 147464 | tf_op jit(solution)/shard_map/ppermute | solution.py:308
  51.0 3.7 %collective-permute-start.14 = (bf16[24,1024]{1,0:T(8,128)(2,1)S(1)}, bf16[24,1024]{1,0:T(8,128)(2,1)S(1)}, u32[]{:S(2)}, u32[]{:S(2)}) collective-permute-start(bf16[24,1024]{1,0:T(8,128)(2,1)S(1)} %get-tuple-element.33), channel_id=1, source_target_pairs={{0,4},{4,8},{8,12},{12,0},{1,5},{5,9},{9,13},{13,1},{2,6},{6,10},{... | collective-permute-start | bytes 147464 | tf_op jit(solution)/shard_map/ppermute | solution.py:308
  55.5 3.9 %collective-permute-start.15 = (bf16[8,1024]{1,0:T(8,128)(2,1)S(1)}, bf16[8,1024]{1,0:T(8,128)(2,1)S(1)}, u32[]{:S(2)}, u32[]{:S(2)}) collective-permute-start(bf16[8,1024]{1,0:T(8,128)(2,1)S(1)} %get-tuple-element.35), channel_id=1, source_target_pairs={{0,3},{1,0},{2,1},{3,2},{4,7},{5,4},{6,5},{7,6},{8,11},{9,8},{10,9... | collective-permute-start | bytes 49160 | tf_op jit(solution)/shard_map/ppermute | solution.py:308
  57.6 4.7 %collective-permute-start.16 = (bf16[8,1024]{1,0:T(8,128)(2,1)S(1)}, bf16[8,1024]{1,0:T(8,128)(2,1)S(1)}, u32[]{:S(2)}, u32[]{:S(2)}) collective-permute-start(bf16[8,1024]{1,0:T(8,128)(2,1)S(1)} %get-tuple-element.36), channel_id=1, source_target_pairs={{0,2},{1,3},{2,0},{3,1},{4,6},{5,7},{6,4},{7,5},{8,10},{9,11},{10,... | collective-permute-start | bytes 49160 | tf_op jit(solution)/shard_map/ppermute | solution.py:308
  59.2 5.5 %collective-permute-start.17 = (bf16[8,1024]{1,0:T(8,128)(2,1)S(1)}, bf16[8,1024]{1,0:T(8,128)(2,1)S(1)}, u32[]{:S(2)}, u32[]{:S(2)}) collective-permute-start(bf16[8,1024]{1,0:T(8,128)(2,1)S(1)} %get-tuple-element.37), channel_id=1, source_target_pairs={{0,1},{1,2},{2,3},{3,0},{4,5},{5,6},{6,7},{7,4},{8,9},{9,10},{10,1... | collective-permute-start | bytes 49160 | tf_op jit(solution)/shard_map/ppermute | solution.py:308

commit v3 on v2

--- a/solution.py
+++ b/solution.py
@@ -21,57 +21,65 @@
     )
 
 
-def attend_kernel(parents, q_ref, new_ref, cache_ref, after_ref, out_ref):
-    del parents, after_ref
+def attend_kernel(beams, parents, q_ref, new_ref, *refs):
+    cache_refs, out_ref = refs[:beams], refs[-1]
     group = QUERY_HEADS // KEY_HEADS
     scale = 1.0 / math.sqrt(HEAD_SIZE)
     width = KEY_HEADS * HEAD_SIZE
-    q = q_ref[0]
-    fresh = new_ref[0].astype(jnp.float32)
-    scores, own = [], []
-    for k in range(KEY_HEADS):
-        qk = q[k * group:(k + 1) * group]
-        keys = cache_ref[0, 0, :, k * HEAD_SIZE:(k + 1) * HEAD_SIZE]
-        scores.append(
-            lax.dot_general(qk, keys, (((1,), (1,)), ((), ())), preferred_element_type=jnp.float32)
-        )
-        own.append(
-            jnp.sum(qk.astype(jnp.float32) * fresh[k:k + 1], axis=-1, keepdims=True)
-        )
-    scores = jnp.concatenate(scores, axis=0) * scale
-    own = jnp.concatenate(own, axis=0) * scale
-    upper = jnp.maximum(jnp.max(scores, axis=-1, keepdims=True), own)
-    expo = jnp.exp(scores - upper)
-    own_expo = jnp.exp(own - upper)
-    total = jnp.sum(expo, axis=-1, keepdims=True) + own_expo
-    probs = (expo / total).astype(jnp.bfloat16)
-    own_prob = (own_expo / total).astype(jnp.bfloat16).astype(jnp.float32)
-    for k in range(KEY_HEADS):
-        rows = slice(k * group, (k + 1) * group)
-        values = cache_ref[0, 0, :, width + k * HEAD_SIZE:width + (k + 1) * HEAD_SIZE]
-        result = jnp.dot(probs[rows], values, preferred_element_type=jnp.float32)
-        result = result + own_prob[rows] * fresh[KEY_HEADS + k:KEY_HEADS + k + 1]
-        out_ref[0, rows] = result.astype(out_ref.dtype)
+    for b in range(beams):
+        q, cache_ref = q_ref[b], cache_refs[b]
+        fresh = new_ref[b].astype(jnp.float32)
+        scores, own = [], []
+        for k in range(KEY_HEADS):
+            qk = q[k * group:(k + 1) * group]
+            keys = cache_ref[0, 0, :, k * HEAD_SIZE:(k + 1) * HEAD_SIZE]
+            scores.append(
+                lax.dot_general(
+                    qk, keys, (((1,), (1,)), ((), ())), preferred_element_type=jnp.float32
+                )
+            )
+            own.append(
+                jnp.sum(qk.astype(jnp.float32) * fresh[k:k + 1], axis=-1, keepdims=True)
+            )
+        scores = jnp.concatenate(scores, axis=0) * scale
+        own = jnp.concatenate(own, axis=0) * scale
+        upper = jnp.maximum(jnp.max(scores, axis=-1, keepdims=True), own)
+        expo = jnp.exp(scores - upper)
+        own_expo = jnp.exp(own - upper)
+        total = jnp.sum(expo, axis=-1, keepdims=True) + own_expo
+        probs = (expo / total).astype(jnp.bfloat16)
+        own_prob = (own_expo / total).astype(jnp.bfloat16).astype(jnp.float32)
+        for k in range(KEY_HEADS):
+            rows = slice(k * group, (k + 1) * group)
+            values = cache_ref[0, 0, :, width + k * HEAD_SIZE:width + (k + 1) * HEAD_SIZE]
+            result = jnp.dot(probs[rows], values, preferred_element_type=jnp.float32)
+            result = result + own_prob[rows] * fresh[KEY_HEADS + k:KEY_HEADS + k + 1]
+            out_ref[b, rows] = result.astype(out_ref.dtype)
 
 
 def attend(queries, new_key_value, cached_key_value, parents, after):
     rows = queries.shape[0]
     _, beams, length, width = cached_key_value.shape
+    step = 4
+
+    def parent_of(b):
+        return lambda r, p: ((r * step + b) // beams, p[r * step + b], 0, 0)
+
     out = pl.pallas_call(
-        attend_kernel,
+        functools.partial(attend_kernel, step),
         grid_spec=pltpu.PrefetchScalarGridSpec(
             num_scalar_prefetch=1,
-            grid=(rows,),
+            grid=(rows // step,),
             in_specs=[
-                pl.BlockSpec((1, QUERY_HEADS, HEAD_SIZE), lambda r, p: (r, 0, 0)),
-                pl.BlockSpec((1, 2 * KEY_HEADS, HEAD_SIZE), lambda r, p: (r, 0, 0)),
-                pl.BlockSpec((1, 1, length, width), lambda r, p: (r // beams, p[r], 0, 0)),
-                pl.BlockSpec(memory_space=pl.ANY),
-            ],
-            out_specs=pl.BlockSpec((1, QUERY_HEADS, HEAD_SIZE), lambda r, p: (r, 0, 0)),
+                pl.BlockSpec((step, QUERY_HEADS, HEAD_SIZE), lambda r, p: (r, 0, 0)),
+                pl.BlockSpec((step, 2 * KEY_HEADS, HEAD_SIZE), lambda r, p: (r, 0, 0)),
+            ]
+            + [pl.BlockSpec((1, 1, length, width), parent_of(b)) for b in range(step)]
+            + [pl.BlockSpec(memory_space=pl.ANY)],
+            out_specs=pl.BlockSpec((step, QUERY_HEADS, HEAD_SIZE), lambda r, p: (r, 0, 0)),
         ),
         out_shape=jax.ShapeDtypeStruct((rows, QUERY_HEADS, HEAD_SIZE), jnp.bfloat16),
-        compiler_params=params(50),
+        compiler_params=params(40),
         cost_estimate=pl.CostEstimate(
             flops=4 * rows * QUERY_HEADS * HEAD_SIZE * length,
             bytes_accessed=2 * rows * length * width,
@@ -82,7 +90,7 @@
         parents.reshape(rows),
         queries.reshape(rows, QUERY_HEADS, HEAD_SIZE),
         new_key_value.reshape(rows, 2 * KEY_HEADS, HEAD_SIZE),
-        cached_key_value,
+        *[cached_key_value] * step,
         after,
     )
     return out.reshape(rows, QUERY_HEADS * HEAD_SIZE)
@@ -164,34 +172,33 @@
 
 
 def combine_kernel(top, experts, sources, column, level, *refs):
-    owners = len(refs) - 2 * sources
-    held, back, out_refs = refs[:sources], refs[sources:sources + owners], refs[sources + owners:]
-    each, width = out_refs[0].shape
+    held, back_ref, out_ref = refs[:sources], refs[sources], refs[sources + 1]
+    owners = back_ref.shape[0]
+    _, each, width = out_ref.shape
     notes = jnp.concatenate([ref[:, width:] for ref in held], axis=0)
     routes, gates = turned_notes(notes, top)
     total = jnp.zeros((sources * each, width), jnp.float32)
     for t in range(owners):
-        place, expert = placing(routes, lax.rem(column[0] + t, owners), level[0], experts, sources)
+        place, expert = placing(routes, t, level[0], experts, sources)
         weight = jnp.zeros_like(place)
         for k in range(top):
             weight = weight + jnp.where(routes[k:k + 1] == expert, gates[k:k + 1], 0.0)
         total = total + lax.dot_general(
             (weight * place).astype(jnp.bfloat16),
-            back[t][...],
+            back_ref[t],
             (((0,), (0,)), ((), ())),
             preferred_element_type=jnp.float32,
         )
     for s in range(sources):
-        out_refs[s][...] = total[s * each:(s + 1) * each].astype(out_refs[s].dtype)
-
-
-def assemble_kernel(me, *refs):
-    chunks = len(refs) - 1
-    out_ref = refs[-1]
-    width = refs[0].shape[1]
-    for s in range(chunks):
-        start = pl.multiple_of(lax.rem(me[0] + s, chunks) * width, width)
-        out_ref[:, pl.ds(start, width)] = refs[s][...]
+        out_ref[lax.rem(level[0] + sources - s, sources)] = total[
+            s * each:(s + 1) * each
+        ].astype(out_ref.dtype)
+
+
+def assemble_kernel(pieces_ref, out_ref):
+    chunks, _, width = pieces_ref.shape
+    for k in range(chunks):
+        out_ref[:, k * width:(k + 1) * width] = pieces_ref[k]
 
 
 def regroup(experts, owners, count):
@@ -221,42 +228,30 @@
 
 
 def gate_up_kernel(chunk, rows_ref, weight_ref, out_ref, done_ref=None):
-    del chunk
     if done_ref is not None:
         done_ref[...] = jnp.zeros_like(done_ref)
-    ff = weight_ref.shape[3]
-    rows = rows_ref[0]
-    for k in range(2):
-        out_ref[0, :, k * ff:(k + 1) * ff] = jnp.dot(
-            rows, weight_ref[0, k], preferred_element_type=jnp.float32
-        ).astype(out_ref.dtype)
+    ff = out_ref.shape[2] // 2
+    columns = pl.ds(pl.multiple_of(chunk[0] * ff, ff), ff)
+    for x in range(out_ref.shape[0]):
+        for k in range(2):
+            out_ref[x, :, k * ff:(k + 1) * ff] = jnp.dot(
+                rows_ref[x], weight_ref[x, k, :, columns], preferred_element_type=jnp.float32
+            ).astype(out_ref.dtype)
 
 
 def gate_up(chunk, chunks, rows, weight, dtype, done=False):
     experts, count, depth = rows.shape
     ff = weight.shape[3] // chunks
-    return pl.pallas_call(
+    return call(
         gate_up_kernel,
-        grid_spec=pltpu.PrefetchScalarGridSpec(
-            num_scalar_prefetch=1,
-            grid=(experts,),
-            in_specs=[
-                pl.BlockSpec((1, count, depth), lambda x, c: (x, 0, 0)),
-                pl.BlockSpec((1, 2, depth, ff), lambda x, c: (x, 0, 0, c[0])),
-            ],
-            out_specs=[pl.BlockSpec((1, count, 2 * ff), lambda x, c: (x, 0, 0))]
-            + [pl.BlockSpec((8, LANES), lambda x, c: (0, 0))] * done,
-        ),
-        out_shape=[jax.ShapeDtypeStruct((experts, count, 2 * ff), dtype)]
+        [chunk],
+        [rows, weight],
+        [jax.ShapeDtypeStruct((experts, count, 2 * ff), dtype)]
         + [jax.ShapeDtypeStruct((8, LANES), jnp.float32)] * done,
-        compiler_params=params(52),
-        cost_estimate=pl.CostEstimate(
-            flops=4 * experts * count * depth * ff,
-            bytes_accessed=4 * experts * depth * ff,
-            transcendentals=0,
-        ),
-        name="gate_up",
-    )(chunk, rows, weight)
+        "gate_up",
+        24,
+        cost=1,
+    )
 
 
 def activate_kernel(own_ref, *refs):
@@ -277,8 +272,8 @@
         sum_ref[x] = jnp.dot(part_ref[x], weight_ref[x, chunk], preferred_element_type=jnp.float32)
 
 
-def down_rest_kernel(chunks, me, sum_ref, *refs):
-    parts, weight_ref, out_refs = refs[:chunks - 1], refs[chunks - 1], refs[chunks:]
+def down_rest_kernel(chunks, me, column, sum_ref, *refs):
+    parts, weight_ref, out_ref = refs[:chunks - 1], refs[chunks - 1], refs[chunks]
     experts, count, width = sum_ref.shape
     ff = parts[0].shape[2]
     sums = []
@@ -291,8 +286,7 @@
                 parts[s - 1][x], weight_ref[x, chunk], preferred_element_type=jnp.float32
             )
         sums.append(total.astype(jnp.bfloat16))
-    owners = len(out_refs)
-    rows = experts * count // owners
+    owners, rows, _ = out_ref.shape
     moved = lax.dot_general(
         regroup(experts, owners, count // owners),
         jnp.concatenate(sums, axis=0),
@@ -300,7 +294,9 @@
         preferred_element_type=jnp.float32,
     )
     for t in range(owners):
-        out_refs[t][...] = moved[t * rows:(t + 1) * rows].astype(out_refs[t].dtype)
+        out_ref[lax.rem(column[0] + owners - t, owners)] = moved[
+            t * rows:(t + 1) * rows
+        ].astype(out_ref.dtype)
 
 
 def shifted(value, axis, steps):
@@ -312,14 +308,14 @@
     return sorted(range(1, size), key=lambda s: -min(s, size - s))
 
 
-def exchange(values, axis, back=False):
+def exchange(values, axis):
     out = [values[0]] + [None] * (len(values) - 1)
     for s in farthest_first(len(values)):
-        out[s] = shifted(values[s], axis, -s if back else s)
+        out[s] = shifted(values[s], axis, s)
     return out
 
 
-def call(kernel, index, inputs, outputs, name, limit=16, after=()):
+def call(kernel, index, inputs, outputs, name, limit=16, after=(), cost=0):
     single = not isinstance(outputs, list)
     return pl.pallas_call(
         kernel,
@@ -331,6 +327,9 @@
         else [pl.BlockSpec(memory_space=pltpu.VMEM)] * len(outputs),
         out_shape=outputs,
         compiler_params=params(limit),
+        cost_estimate=pl.CostEstimate(
+            flops=cost * 10**9, bytes_accessed=cost * 3 * 10**6, transcendentals=0
+        ),
         name=name,
     )(*index, *inputs, *after)
 
@@ -366,9 +365,9 @@
     )
     back = call(
         functools.partial(down_rest_kernel, inner),
-        [level],
+        [level, lax.axis_index("expert").astype(jnp.int32).reshape(1)],
         [sums, *parts[1:], down_weight],
-        [jax.ShapeDtypeStruct((experts * count // owners, width), jnp.bfloat16)] * owners,
+        jax.ShapeDtypeStruct((owners, experts * count // owners, width), jnp.bfloat16),
         "down_rest",
         24,
     )
@@ -383,8 +382,9 @@
     active = lax.all_gather(active, "inner", axis=0, tiled=True)
     outputs = jnp.einsum("sxf,xfd->xsd", active, down_weight, preferred_element_type=jnp.float32)
     outputs = outputs.astype(jnp.bfloat16).reshape(experts, owners, count // owners, -1)
-    back = [outputs[:, t].reshape(experts * count // owners, -1) for t in range(owners)]
-    return back, attention(held)
+    back = jnp.transpose(outputs, (1, 0, 2, 3)).reshape(owners, experts * count // owners, -1)
+    origin = (lax.axis_index("expert") - jnp.arange(owners)) % owners
+    return back[origin], attention(held)
 
 
 def body(
@@ -415,6 +415,7 @@
         [routes.T, gate_values.T, hidden],
         [jax.ShapeDtypeStruct((rows, depth + LANES), jnp.bfloat16)] * inner,
         "prepare",
+        cost=2,
     )
     slices = exchange(slices, "inner")
     packs = call(
@@ -423,6 +424,7 @@
         slices,
         [jax.ShapeDtypeStruct((slots, depth), jnp.bfloat16)] * owners,
         "pack",
+        cost=3,
     )
     packs = exchange(packs, "expert")
     held = call(
@@ -432,24 +434,25 @@
         jax.ShapeDtypeStruct((experts, owners * CAP * inner, depth), jnp.bfloat16),
         "select",
         24,
+        cost=1,
     )
     even = ff % (inner * LANES) == 0
     back, attended = (experts_by_columns if even else experts_by_rows)(
         held, gate_up_weight, down_weight, owners, attention
     )
-    back = exchange(back, "expert", back=True)
+    back = lax.all_to_all(back, "expert", split_axis=0, concat_axis=0, tiled=True)
     pieces = call(
         functools.partial(combine_kernel, top, experts, inner),
         [column, level],
-        [*slices, *back],
-        [jax.ShapeDtypeStruct((rows, width), jnp.bfloat16)] * inner,
+        [*slices, back],
+        jax.ShapeDtypeStruct((inner, rows, width), jnp.bfloat16),
         "combine",
     )
-    pieces = exchange(pieces, "inner", back=True)
+    pieces = lax.all_to_all(pieces, "inner", split_axis=0, concat_axis=0, tiled=True)
     expert_out = call(
         assemble_kernel,
-        [level],
-        pieces,
+        [],
+        [pieces],
         jax.ShapeDtypeStruct((rows, model), jnp.bfloat16),
         "assemble",
     )

time: 65.6 us -> 68.9 us (1.050)
  blocking collectives: 0 us -> 16.7 us
  Pallas kernels: 19.4 us -> 11.6 us
  waiting for transfers between devices: 18.1 us -> 11.7 us
  local copies, waits for them, and re-layouts: 2.87 us -> 8.74 us
  starting transfers between devices: 24.2 us -> 19 us
    all_to_all x0 -> x2, blocking collectives: none -> 16.7 us  [the longest x1 8.65 us: body(): lax.all_to_all(pieces, 'inner', split_axis=0, concat_axis=0, tiled=True)]
    pallas_call x5 -> x1, Pallas kernels: 15.1 us -> 5.02 us  [attend(): pl.pallas_call(functools.partial(attend_kernel, step), grid_spec=pltpu.Pr...]
    ppermute x18 -> x12, waiting for transfers between devices: 18.1 us -> 11.7 us  [shifted(): lax.ppermute(value, axis, [(i, (i + steps) % size) for i in range(size)])]
    unnamed x23 -> x31, local copies, waits for them, and re-layouts: 2.87 us -> 8.74 us
    ppermute x18 -> x12, starting transfers between devices: 24.2 us -> 19 us  [shifted(): lax.ppermute(value, axis, [(i, (i + steps) % size) for i in range(size)])]
    pallas_call x8 -> x12, Pallas kernels: 4.25 us -> 6.58 us  [call(): pl.pallas_call(kernel, in_specs=[pl.BlockSpec(memory_space=pltpu.SMEM)] *...]
  transfers between devices with their start and end apart: 18 -> 12, of which waited for: 13 -> 9; matrix products, arithmetic and copies ran while one was open for 0% -> 0% of each run, Pallas kernels for 20% -> 10%
where the time goes in v3:
time: 68.9 us; the launch traced here: 68.6 us
  starting transfers between devices  19 us (28%)
  blocking collectives  16.7 us (24%)
  waiting for transfers between devices  11.7 us (17%)
  Pallas kernels  11.6 us (17%)
  local copies, waits for them, and re-layouts  8.74 us (13%)
  between operations  0.81 us (1%)
    ppermute x12, starting transfers between devices, shifted(): lax.ppermute(value, axis, [(i, (i + steps) % size) for i in range(size)])  19 us
    ppermute x12, waiting for transfers between devices, shifted(): lax.ppermute(value, axis, [(i, (i + steps) % size) for i in range(size)])  11.7 us
    unnamed x31, local copies, waits for them, and re-layouts  8.74 us
    all_to_all x1, blocking collectives, body(): lax.all_to_all(pieces, 'inner', split_axis=0, concat_axis=0, tiled=True)  8.65 us
    all_to_all x1, blocking collectives, body(): lax.all_to_all(back, 'expert', split_axis=0, concat_axis=0, tiled=True)  8.08 us
    pallas_call x12, Pallas kernels, call(): pl.pallas_call(kernel, in_specs=[pl.BlockSpec(memory_space=pltpu.SMEM)] *...  6.58 us
    pallas_call x1, Pallas kernels, attend(): pl.pallas_call(functools.partial(attend_kernel, step), grid_spec=pltpu.Pr...  5.02 us
  transfers between devices with their start and end apart: 12, of which 9 were waited for; matrix products, arithmetic and copies ran while one was open for 0% of the time, Pallas kernels for 10%

profile of v3, /device:TPU:0, one launch (start us, length us, event | category | flops | bytes accessed | tf_op | source)
XLA Modules:
  0.0 68.6 jit_solution(406742220207379917)
XLA Ops:
  0.6 0.8 %copy-done.4 = bf16[8,4096]{1,0:T(8,128)(2,1)S(1)} copy-done((bf16[8,4096]{1,0:T(8,128)(2,1)S(1)}, bf16[8,4096]{1,0:T(8,128)(2,1)}, u32[]{:S(2)}) %copy-start.4) | copy-done | bytes 65560
  1.5 0.7 copy-done.5
  2.2 0.7 copy-done.6
  2.8 0.2 prepare.1
  3.0 3.0 %collective-permute-start = (bf16[8,1152]{1,0:T(8,128)(2,1)S(1)}, bf16[8,1152]{1,0:T(8,128)(2,1)S(1)}, u32[]{:S(2)}, u32[]{:S(2)}) collective-permute-start(bf16[8,1152]{1,0:T(8,128)(2,1)S(1)} %get-tuple-element.13), channel_id=1, source_target_pairs={{0,1},{1,2},{2,3},{3,0},{4,5},{5,6},{6,7},{7,4},{8,9},{9,10},{10,1... | collective-permute-start | bytes 55304 | tf_op jit(solution)/shard_map/ppermute | solution.py:304
  6.0 2.6 %collective-permute-start.1 = (bf16[8,1152]{1,0:T(8,128)(2,1)S(1)}, bf16[8,1152]{1,0:T(8,128)(2,1)S(1)}, u32[]{:S(2)}, u32[]{:S(2)}) collective-permute-start(bf16[8,1152]{1,0:T(8,128)(2,1)S(1)} %get-tuple-element.14), channel_id=1, source_target_pairs={{0,2},{1,3},{2,0},{3,1},{4,6},{5,7},{6,4},{7,5},{8,10},{9,11},{10,... | collective-permute-start | bytes 55304 | tf_op jit(solution)/shard_map/ppermute | solution.py:304
  8.6 1.3 %collective-permute-start.2 = (bf16[8,1152]{1,0:T(8,128)(2,1)S(1)}, bf16[8,1152]{1,0:T(8,128)(2,1)S(1)}, u32[]{:S(2)}, u32[]{:S(2)}) collective-permute-start(bf16[8,1152]{1,0:T(8,128)(2,1)S(1)} %get-tuple-element.15), channel_id=1, source_target_pairs={{0,3},{1,0},{2,1},{3,2},{4,7},{5,4},{6,5},{7,6},{8,11},{9,8},{10,9... | collective-permute-start | bytes 55304 | tf_op jit(solution)/shard_map/ppermute | solution.py:304
  10.0 0.0 collective-permute-done.refs_1_
  10.0 0.8 %collective-permute-done.1.refs_2_ = bf16[8,1152]{1,0:T(8,128)(2,1)S(1)} collective-permute-done((bf16[8,1152]{1,0:T(8,128)(2,1)S(1)}, bf16[8,1152]{1,0:T(8,128)(2,1)S(1)}, u32[]{:S(2)}, u32[]{:S(2)}) %collective-permute-start.1) | collective-permute-done | bytes 18464 | tf_op jit(solution)/shard_map/ppermute | solution.py:304
  10.8 1.6 %collective-permute-done.2.refs_3_ = bf16[8,1152]{1,0:T(8,128)(2,1)S(1)} collective-permute-done((bf16[8,1152]{1,0:T(8,128)(2,1)S(1)}, bf16[8,1152]{1,0:T(8,128)(2,1)S(1)}, u32[]{:S(2)}, u32[]{:S(2)}) %collective-permute-start.2) | collective-permute-done | bytes 18464 | tf_op jit(solution)/shard_map/ppermute | solution.py:304
  12.4 0.8 %pack.1 = (bf16[24,1024]{1,0:T(8,128)(2,1)S(1)}, bf16[24,1024]{1,0:T(8,128)(2,1)S(1)}, bf16[24,1024]{1,0:T(8,128)(2,1)S(1)}, bf16[24,1024]{1,0:T(8,128)(2,1)S(1)}) custom-call(s32[1]{0:T(128)} %bitcast.2.column, s32[1]{0:T(128)} %bitcast.1.me.level.chunk, bf16[8,1152]{1,0:T(8,128)(2,1)S(1)} %get-tuple-element.12.refs_0_, ...), custom_call_target="tpu_custom_call" | custom-call | flops 3000000000 | bytes 9000000 | tf_op jit(solution)/shard_map/pack/pallas_call | solution.py:320
  13.2 0.1 collective-permute-start.3
  13.2 1.6 %collective-permute-start.4 = (bf16[24,1024]{1,0:T(8,128)(2,1)S(1)}, bf16[24,1024]{1,0:T(8,128)(2,1)S(1)}, u32[]{:S(2)}, u32[]{:S(2)}) collective-permute-start(bf16[24,1024]{1,0:T(8,128)(2,1)S(1)} %get-tuple-element.18), channel_id=1, source_target_pairs={{0,8},{4,12},{8,0},{12,4},{1,9},{5,13},{9,1},{13,5},{2,10},{6,14},... | collective-permute-start | bytes 147464 | tf_op jit(solution)/shard_map/ppermute | solution.py:304
  14.8 1.4 %collective-permute-start.5 = (bf16[24,1024]{1,0:T(8,128)(2,1)S(1)}, bf16[24,1024]{1,0:T(8,128)(2,1)S(1)}, u32[]{:S(2)}, u32[]{:S(2)}) collective-permute-start(bf16[24,1024]{1,0:T(8,128)(2,1)S(1)} %get-tuple-element.19), channel_id=1, source_target_pairs={{0,12},{4,0},{8,4},{12,8},{1,13},{5,1},{9,5},{13,9},{2,14},{6,2},{... | collective-permute-start | bytes 147464 | tf_op jit(solution)/shard_map/ppermute | solution.py:304
  16.2 0.6 collective-permute-done.3.refs_1_
  16.7 0.7 collective-permute-done.4.refs_2_
  17.4 0.5 collective-permute-done.5.refs_3_
  17.9 0.2 select.7.rows_ref
  18.1 0.0 copy-start
  18.1 4.6 %copy-done = bf16[2,2,1024,1536]{3,2,1,0:T(8,128)(2,1)S(1)} copy-done((bf16[2,2,1024,1536]{3,2,1,0:T(8,128)(2,1)S(1)}, bf16[2,2,1024,1536]{3,2,1,0:T(8,128)(2,1)}, u32[]{:S(2)}) %copy-start) | copy-done | bytes 12582936
  22.7 0.6 gate_up.5
  23.3 0.9 %collective-permute-start.6 = (bf16[2,48,768]{2,1,0:T(8,128)(2,1)S(1)}, bf16[2,48,768]{2,1,0:T(8,128)(2,1)S(1)}, u32[]{:S(2)}, u32[]{:S(2)}) collective-permute-start(bf16[2,48,768]{2,1,0:T(8,128)(2,1)S(1)} %gate_up.5), channel_id=1, source_target_pairs={{0,2},{1,3},{2,0},{3,1},{4,6},{5,7},{6,4},{7,5},{8,10},{9,11},{10,... | collective-permute-start | bytes 442376 | tf_op jit(solution)/shard_map/ppermute | solution.py:304
  24.3 0.6 gate_up.6
  24.9 2.9 %collective-permute-start.7 = (bf16[2,48,768]{2,1,0:T(8,128)(2,1)S(1)}, bf16[2,48,768]{2,1,0:T(8,128)(2,1)S(1)}, u32[]{:S(2)}, u32[]{:S(2)}) collective-permute-start(bf16[2,48,768]{2,1,0:T(8,128)(2,1)S(1)} %gate_up.6), channel_id=1, source_target_pairs={{0,1},{1,2},{2,3},{3,0},{4,5},{5,6},{6,7},{7,4},{8,9},{9,10},{10,1... | collective-permute-start | bytes 442376 | tf_op jit(solution)/shard_map/ppermute | solution.py:304
  27.8 0.6 gate_up.7
  28.4 1.1 %collective-permute-start.8 = (bf16[2,48,768]{2,1,0:T(8,128)(2,1)S(1)}, bf16[2,48,768]{2,1,0:T(8,128)(2,1)S(1)}, u32[]{:S(2)}, u32[]{:S(2)}) collective-permute-start(bf16[2,48,768]{2,1,0:T(8,128)(2,1)S(1)} %gate_up.7), channel_id=1, source_target_pairs={{0,3},{1,0},{2,1},{3,2},{4,7},{5,4},{6,5},{7,6},{8,11},{9,8},{10,9... | collective-permute-start | bytes 442376 | tf_op jit(solution)/shard_map/ppermute | solution.py:304
  29.5 0.5 slice-done.2
  30.1 0.6 gate_up.4
  30.7 1.3 %copy-done.1 = bf16[1,8,192,1024]{3,2,1,0:T(8,128)(2,1)S(1)} copy-done((bf16[1,8,192,1024]{3,2,1,0:T(8,128)(2,1)S(1)}, bf16[1,8,192,1024]{3,2,1,0:T(8,128)(2,1)}, u32[]{:S(2)}) %copy-start.1) | copy-done | bytes 3145752
  32.0 5.0 %attend.1 = bf16[8,64,128]{2,1,0:T(8,128)(2,1)S(1)} custom-call(s32[8]{0:T(128)S(1)} %bitcast.29, bf16[8,64,128]{2,1,0:T(8,128)(2,1)S(1)} %bitcast.24, bf16[8,8,128]{2,1,0:T(8,128)(2,1)S(1)} %bitcast.28, bf16[1,8,192,1024]{3,2,1,0:T(8,128)(2,1)S(1)} %copy-done.1, bf16[1,8,192,1024]{3,2,1,0:T(8,128)(2,1)S(1)} %copy-done.1, ...), custom_call_target="tpu_custom_call" | custom-call | flops 50331648 | bytes 3145728 | tf_op jit(solution)/shard_map/attend/pallas_call | solution.py:68
  37.0 0.1 copy.17
  37.1 0.0 copy-start.2
  37.1 0.3 collective-permute-done.6.refs_0_
  37.4 0.0 collective-permute-done.7.refs_1_
  37.4 2.6 %collective-permute-done.8.refs_2_ = bf16[2,48,768]{2,1,0:T(8,128)(2,1)S(1)} collective-permute-done((bf16[2,48,768]{2,1,0:T(8,128)(2,1)S(1)}, bf16[2,48,768]{2,1,0:T(8,128)(2,1)S(1)}, u32[]{:S(2)}, u32[]{:S(2)}) %collective-permute-start.8) | collective-permute-done | bytes 147488 | tf_op jit(solution)/shard_map/ppermute | solution.py:304
  40.0 0.1 activate.1.part_ref
  40.1 0.9 %collective-permute-start.9 = (bf16[2,48,384]{2,1,0:T(8,128)(2,1)S(1)}, bf16[2,48,384]{2,1,0:T(8,128)(2,1)S(1)}, u32[]{:S(2)}, u32[]{:S(2)}) collective-permute-start(bf16[2,48,384]{2,1,0:T(8,128)(2,1)S(1)} %activate.1.part_ref), channel_id=1, source_target_pairs={{0,1},{1,2},{2,3},{3,0},{4,5},{5,6},{6,7},{7,4},{8,9},{9,10},{10,1... | collective-permute-start | bytes 221192 | tf_op jit(solution)/shard_map/ppermute | solution.py:304
  41.0 0.4 collective-permute-start.10
  41.4 2.8 %collective-permute-start.11 = (bf16[2,48,384]{2,1,0:T(8,128)(2,1)S(1)}, bf16[2,48,384]{2,1,0:T(8,128)(2,1)S(1)}, u32[]{:S(2)}, u32[]{:S(2)}) collective-permute-start(bf16[2,48,384]{2,1,0:T(8,128)(2,1)S(1)} %activate.1.part_ref), channel_id=1, source_target_pairs={{0,3},{1,0},{2,1},{3,2},{4,7},{5,4},{6,5},{7,6},{8,11},{9,8},{10,9... | collective-permute-start | bytes 221192 | tf_op jit(solution)/shard_map/ppermute | solution.py:304
  44.2 0.4 down_own.1.sum_ref
  44.6 2.6 %collective-permute-done.9.refs_0_ = bf16[2,48,384]{2,1,0:T(8,128)(2,1)S(1)} collective-permute-done((bf16[2,48,384]{2,1,0:T(8,128)(2,1)S(1)}, bf16[2,48,384]{2,1,0:T(8,128)(2,1)S(1)}, u32[]{:S(2)}, u32[]{:S(2)}) %collective-permute-start.9) | collective-permute-done | bytes 73760 | tf_op jit(solution)/shard_map/ppermute | solution.py:304
  47.2 2.1 %collective-permute-done.10.refs_1_ = bf16[2,48,384]{2,1,0:T(8,128)(2,1)S(1)} collective-permute-done((bf16[2,48,384]{2,1,0:T(8,128)(2,1)S(1)}, bf16[2,48,384]{2,1,0:T(8,128)(2,1)S(1)}, u32[]{:S(2)}, u32[]{:S(2)}) %collective-permute-start.10) | collective-permute-done | bytes 73760 | tf_op jit(solution)/shard_map/ppermute | solution.py:304
  49.3 0.0 collective-permute-done.11.refs_2_
  49.3 1.1 %down_rest.1 = bf16[4,24,1024]{2,1,0:T(8,128)(2,1)S(1)} custom-call(s32[1]{0:T(128)} %bitcast.1.me.level.chunk, s32[1]{0:T(128)} %bitcast.2.column, f32[2,48,1024]{2,1,0:T(8,128)S(1)} %down_own.1.sum_ref, bf16[2,48,384]{2,1,0:T(8,128)(2,1)S(1)} %collective-permute-done.9.refs_0_, bf16[2,48,384]{2,1,0:T(8,128)(2,1)S(1)} %collective-permute-done.10.refs_1_, ...), custom_call_target="tpu_custom_call" | custom-call | tf_op jit(solution)/shard_map/down_rest/pallas_call | solution.py:320
  50.4 8.1 %all_to_all.10.refs_4_ = bf16[4,24,1024]{2,1,0:T(8,128)(2,1)S(1)} all-to-all(bf16[4,24,1024]{2,1,0:T(8,128)(2,1)S(1)} %down_rest.1), channel_id=1, replica_groups=mesh['groups'=2,'expert'=4,'inner'=4] {'expert'}, dimensions={0} | all-to-all | bytes 393216 | tf_op jit(solution)/shard_map/all_to_all | solution.py:443
  58.4 0.8 %combine.1 = bf16[4,8,1024]{2,1,0:T(8,128)(2,1)S(1)} custom-call(s32[1]{0:T(128)} %bitcast.2.column, s32[1]{0:T(128)} %bitcast.1.me.level.chunk, bf16[8,1152]{1,0:T(8,128)(2,1)S(1)} %get-tuple-element.12.refs_0_, bf16[8,1152]{1,0:T(8,128)(2,1)S(1)} %collective-permute-done.refs_1_, bf16[8,1152]{1,0:T(8,128)(2,1)S(1)} %collective-permute-done.1.refs_2_, ...), custom_call_target="tpu_custom_call" | custom-call | tf_op jit(solution)/shard_map/combine/pallas_call | solution.py:320
  59.3 8.7 %all_to_all.11.pieces_ref = bf16[4,8,1024]{2,1,0:T(8,128)(2,1)S(1)} all-to-all(bf16[4,8,1024]{2,1,0:T(8,128)(2,1)S(1)} %combine.1), channel_id=1, replica_groups=mesh['groups'=2,'expert'=4,'inner'=4] {'inner'}, dimensions={0} | all-to-all | bytes 131072 | tf_op jit(solution)/shard_map/all_to_all | solution.py:451
  68.0 0.6 assemble.1
  (24 shorter events, 0.1 us)
Async XLA Ops:
  0.6 0.8 %copy-start.4 = (bf16[8,4096]{1,0:T(8,128)(2,1)S(1)}, bf16[8,4096]{1,0:T(8,128)(2,1)}, u32[]{:S(2)}) copy-start(bf16[8,4096]{1,0:T(8,128)(2,1)} %hidden_ref.1) | copy-start | bytes 196612
  1.5 0.7 copy-start.5
  2.2 0.7 copy-start.6
  3.0 7.0 %collective-permute-start = (bf16[8,1152]{1,0:T(8,128)(2,1)S(1)}, bf16[8,1152]{1,0:T(8,128)(2,1)S(1)}, u32[]{:S(2)}, u32[]{:S(2)}) collective-permute-start(bf16[8,1152]{1,0:T(8,128)(2,1)S(1)} %get-tuple-element.13), channel_id=1, source_target_pairs={{0,1},{1,2},{2,3},{3,0},{4,5},{5,6},{6,7},{7,4},{8,9},{9,10},{10,1... | collective-permute-start | bytes 55304 | tf_op jit(solution)/shard_map/ppermute | solution.py:304
  6.0 4.8 %collective-permute-start.1 = (bf16[8,1152]{1,0:T(8,128)(2,1)S(1)}, bf16[8,1152]{1,0:T(8,128)(2,1)S(1)}, u32[]{:S(2)}, u32[]{:S(2)}) collective-permute-start(bf16[8,1152]{1,0:T(8,128)(2,1)S(1)} %get-tuple-element.14), channel_id=1, source_target_pairs={{0,2},{1,3},{2,0},{3,1},{4,6},{5,7},{6,4},{7,5},{8,10},{9,11},{10,... | collective-permute-start | bytes 55304 | tf_op jit(solution)/shard_map/ppermute | solution.py:304
  8.6 3.8 %collective-permute-start.2 = (bf16[8,1152]{1,0:T(8,128)(2,1)S(1)}, bf16[8,1152]{1,0:T(8,128)(2,1)S(1)}, u32[]{:S(2)}, u32[]{:S(2)}) collective-permute-start(bf16[8,1152]{1,0:T(8,128)(2,1)S(1)} %get-tuple-element.15), channel_id=1, source_target_pairs={{0,3},{1,0},{2,1},{3,2},{4,7},{5,4},{6,5},{7,6},{8,11},{9,8},{10,9... | collective-permute-start | bytes 55304 | tf_op jit(solution)/shard_map/ppermute | solution.py:304
  13.2 3.6 %collective-permute-start.3 = (bf16[24,1024]{1,0:T(8,128)(2,1)S(1)}, bf16[24,1024]{1,0:T(8,128)(2,1)S(1)}, u32[]{:S(2)}, u32[]{:S(2)}) collective-permute-start(bf16[24,1024]{1,0:T(8,128)(2,1)S(1)} %get-tuple-element.17), channel_id=1, source_target_pairs={{0,4},{4,8},{8,12},{12,0},{1,5},{5,9},{9,13},{13,1},{2,6},{6,10},{... | collective-permute-start | bytes 147464 | tf_op jit(solution)/shard_map/ppermute | solution.py:304
  13.2 4.2 %collective-permute-start.4 = (bf16[24,1024]{1,0:T(8,128)(2,1)S(1)}, bf16[24,1024]{1,0:T(8,128)(2,1)S(1)}, u32[]{:S(2)}, u32[]{:S(2)}) collective-permute-start(bf16[24,1024]{1,0:T(8,128)(2,1)S(1)} %get-tuple-element.18), channel_id=1, source_target_pairs={{0,8},{4,12},{8,0},{12,4},{1,9},{5,13},{9,1},{13,5},{2,10},{6,14},... | collective-permute-start | bytes 147464 | tf_op jit(solution)/shard_map/ppermute | solution.py:304
  14.8 3.1 %collective-permute-start.5 = (bf16[24,1024]{1,0:T(8,128)(2,1)S(1)}, bf16[24,1024]{1,0:T(8,128)(2,1)S(1)}, u32[]{:S(2)}, u32[]{:S(2)}) collective-permute-start(bf16[24,1024]{1,0:T(8,128)(2,1)S(1)} %get-tuple-element.19), channel_id=1, source_target_pairs={{0,12},{4,0},{8,4},{12,8},{1,13},{5,1},{9,5},{13,9},{2,14},{6,2},{... | collective-permute-start | bytes 147464 | tf_op jit(solution)/shard_map/ppermute | solution.py:304
  18.1 4.6 %copy-start = (bf16[2,2,1024,1536]{3,2,1,0:T(8,128)(2,1)S(1)}, bf16[2,2,1024,1536]{3,2,1,0:T(8,128)(2,1)}, u32[]{:S(2)}) copy-start(bf16[2,2,1024,1536]{3,2,1,0:T(8,128)(2,1)} %weight_ref.8) | copy-start | bytes 37748740
  23.3 14.1 %collective-permute-start.6 = (bf16[2,48,768]{2,1,0:T(8,128)(2,1)S(1)}, bf16[2,48,768]{2,1,0:T(8,128)(2,1)S(1)}, u32[]{:S(2)}, u32[]{:S(2)}) collective-permute-start(bf16[2,48,768]{2,1,0:T(8,128)(2,1)S(1)} %gate_up.5), channel_id=1, source_target_pairs={{0,2},{1,3},{2,0},{3,1},{4,6},{5,7},{6,4},{7,5},{8,10},{9,11},{10,... | collective-permute-start | bytes 442376 | tf_op jit(solution)/shard_map/ppermute | solution.py:304
  24.3 5.2 %slice-start = ((s8[12582912]{0:T(1024)(128)(4,1)}), s8[4194304]{0:T(1024)(128)(4,1)S(1)}, s32[]{:S(2)}) async-start(s8[12582912]{0:T(1024)(128)(4,1)} %bitcast.20), calls=%async_computation.2 | async-start | bytes 8388608
  24.3 5.2 %slice-start.1 = ((s8[12582912]{0:T(1024)(128)(4,1)}), s8[4194304]{0:T(1024)(128)(4,1)S(1)}, s32[]{:S(2)}) async-start(s8[12582912]{0:T(1024)(128)(4,1)} %bitcast.20), calls=%async_computation.3 | async-start | bytes 8388608
  24.9 12.5 %collective-permute-start.7 = (bf16[2,48,768]{2,1,0:T(8,128)(2,1)S(1)}, bf16[2,48,768]{2,1,0:T(8,128)(2,1)S(1)}, u32[]{:S(2)}, u32[]{:S(2)}) collective-permute-start(bf16[2,48,768]{2,1,0:T(8,128)(2,1)S(1)} %gate_up.6), channel_id=1, source_target_pairs={{0,1},{1,2},{2,3},{3,0},{4,5},{5,6},{6,7},{7,4},{8,9},{9,10},{10,1... | collective-permute-start | bytes 442376 | tf_op jit(solution)/shard_map/ppermute | solution.py:304
  27.8 1.7 %copy-start.7 = (bf16[8,8192]{1,0:T(8,128)(2,1)S(1)}, bf16[8,8192]{1,0:T(8,128)(2,1)}, u32[]{:S(2)}) copy-start(bf16[8,8192]{1,0:T(8,128)(2,1)} %param.9) | copy-start | bytes 393220
  27.8 1.7 %copy-start.8 = (bf16[8,1024]{1,0:T(8,128)(2,1)S(1)}, bf16[8,1024]{1,0:T(8,128)(2,1)}, u32[]{:S(2)}) copy-start(bf16[8,1024]{1,0:T(8,128)(2,1)} %param.10) | copy-start | bytes 49156
  27.8 2.3 %slice-start.2 = ((s8[12582912]{0:T(1024)(128)(4,1)}), s8[4194304]{0:T(1024)(128)(4,1)S(1)}, s32[]{:S(2)}) async-start(s8[12582912]{0:T(1024)(128)(4,1)} %bitcast.20), calls=%async_computation.4 | async-start | bytes 8388608
  28.4 11.6 %collective-permute-start.8 = (bf16[2,48,768]{2,1,0:T(8,128)(2,1)S(1)}, bf16[2,48,768]{2,1,0:T(8,128)(2,1)S(1)}, u32[]{:S(2)}, u32[]{:S(2)}) collective-permute-start(bf16[2,48,768]{2,1,0:T(8,128)(2,1)S(1)} %gate_up.7), channel_id=1, source_target_pairs={{0,3},{1,0},{2,1},{3,2},{4,7},{5,4},{6,5},{7,6},{8,11},{9,8},{10,9... | collective-permute-start | bytes 442376 | tf_op jit(solution)/shard_map/ppermute | solution.py:304
  30.1 1.9 %copy-start.1 = (bf16[1,8,192,1024]{3,2,1,0:T(8,128)(2,1)S(1)}, bf16[1,8,192,1024]{3,2,1,0:T(8,128)(2,1)}, u32[]{:S(2)}) copy-start(bf16[1,8,192,1024]{3,2,1,0:T(8,128)(2,1)} %refs_3_.2) | copy-start | bytes 9437188
  30.1 1.9 %copy-start.3 = (s32[1,8]{1,0:T(1,128)S(1)}, s32[1,8]{1,0:T(1,128)}, u32[]{:S(2)}) copy-start(s32[1,8]{1,0:T(1,128)} %param.12) | copy-start | bytes 100
  30.1 14.1 %slice-start.3 = ((s8[6291456]{0:T(1024)(128)(4,1)}), s8[4194304]{0:T(1024)(128)(4,1)S(1)}, s32[]{:S(2)}) async-start(s8[6291456]{0:T(1024)(128)(4,1)} %bitcast.22), calls=%async_computation.5 | async-start | bytes 8388608
  32.0 12.2 %slice-start.4 = ((s8[6291456]{0:T(1024)(128)(4,1)}), s8[2097152]{0:T(1024)(128)(4,1)S(1)}, s32[]{:S(2)}) async-start(s8[6291456]{0:T(1024)(128)(4,1)} %bitcast.22), calls=%async_computation.6 | async-start | bytes 4194304
  37.1 13.3 %copy-start.2 = (bf16[1,8,64,128]{3,1,2,0:T(8,128)(2,1)}, bf16[1,8,64,128]{3,1,2,0:T(8,128)(2,1)S(1)}, u32[]{:S(2)}) copy-start(bf16[1,8,64,128]{3,1,2,0:T(8,128)(2,1)S(1)} %copy.17) | copy-start | bytes 393220
  40.1 7.1 %collective-permute-start.9 = (bf16[2,48,384]{2,1,0:T(8,128)(2,1)S(1)}, bf16[2,48,384]{2,1,0:T(8,128)(2,1)S(1)}, u32[]{:S(2)}, u32[]{:S(2)}) collective-permute-start(bf16[2,48,384]{2,1,0:T(8,128)(2,1)S(1)} %activate.1.part_ref), channel_id=1, source_target_pairs={{0,1},{1,2},{2,3},{3,0},{4,5},{5,6},{6,7},{7,4},{8,9},{9,10},{10,1... | collective-permute-start | bytes 221192 | tf_op jit(solution)/shard_map/ppermute | solution.py:304
  41.0 8.3 %collective-permute-start.10 = (bf16[2,48,384]{2,1,0:T(8,128)(2,1)S(1)}, bf16[2,48,384]{2,1,0:T(8,128)(2,1)S(1)}, u32[]{:S(2)}, u32[]{:S(2)}) collective-permute-start(bf16[2,48,384]{2,1,0:T(8,128)(2,1)S(1)} %activate.1.part_ref), channel_id=1, source_target_pairs={{0,2},{1,3},{2,0},{3,1},{4,6},{5,7},{6,4},{7,5},{8,10},{9,11},{10,... | collective-permute-start | bytes 221192 | tf_op jit(solution)/shard_map/ppermute | solution.py:304
  41.4 7.9 %collective-permute-start.11 = (bf16[2,48,384]{2,1,0:T(8,128)(2,1)S(1)}, bf16[2,48,384]{2,1,0:T(8,128)(2,1)S(1)}, u32[]{:S(2)}, u32[]{:S(2)}) collective-permute-start(bf16[2,48,384]{2,1,0:T(8,128)(2,1)S(1)} %activate.1.part_ref), channel_id=1, source_target_pairs={{0,3},{1,0},{2,1},{3,2},{4,7},{5,4},{6,5},{7,6},{8,11},{9,8},{10,9... | collective-permute-start | bytes 221192 | tf_op jit(solution)/shard_map/ppermute | solution.py:304

commit v4 on v3

--- a/solution.py
+++ b/solution.py
@@ -57,13 +57,14 @@
             out_ref[b, rows] = result.astype(out_ref.dtype)
 
 
-def attend(queries, new_key_value, cached_key_value, parents, after):
-    rows = queries.shape[0]
+def attend(queries, new_key_value, cached_key_value, parents, after, part, parts):
+    rows = queries.shape[0] // parts
+    first = part * rows
     _, beams, length, width = cached_key_value.shape
     step = 4
 
     def parent_of(b):
-        return lambda r, p: ((r * step + b) // beams, p[r * step + b], 0, 0)
+        return lambda r, p: ((first + r * step + b) // beams, p[first + r * step + b], 0, 0)
 
     out = pl.pallas_call(
         functools.partial(attend_kernel, step),
@@ -71,8 +72,12 @@
             num_scalar_prefetch=1,
             grid=(rows // step,),
             in_specs=[
-                pl.BlockSpec((step, QUERY_HEADS, HEAD_SIZE), lambda r, p: (r, 0, 0)),
-                pl.BlockSpec((step, 2 * KEY_HEADS, HEAD_SIZE), lambda r, p: (r, 0, 0)),
+                pl.BlockSpec(
+                    (step, QUERY_HEADS, HEAD_SIZE), lambda r, p: (first // step + r, 0, 0)
+                ),
+                pl.BlockSpec(
+                    (step, 2 * KEY_HEADS, HEAD_SIZE), lambda r, p: (first // step + r, 0, 0)
+                ),
             ]
             + [pl.BlockSpec((1, 1, length, width), parent_of(b)) for b in range(step)]
             + [pl.BlockSpec(memory_space=pl.ANY)],
@@ -87,13 +92,13 @@
         ),
         name="attend",
     )(
-        parents.reshape(rows),
-        queries.reshape(rows, QUERY_HEADS, HEAD_SIZE),
-        new_key_value.reshape(rows, 2 * KEY_HEADS, HEAD_SIZE),
+        parents.reshape(-1),
+        queries.reshape(-1, QUERY_HEADS, HEAD_SIZE),
+        new_key_value.reshape(-1, 2 * KEY_HEADS, HEAD_SIZE),
         *[cached_key_value] * step,
         after,
     )
-    return out.reshape(rows, QUERY_HEADS * HEAD_SIZE)
+    return out
 
 
 def spread(values, lanes, first):
@@ -109,15 +114,15 @@
 
 
 def prepare_kernel(me, routes_ref, gates_ref, hidden_ref, *out_refs):
-    chunks = len(out_refs)
-    width = hidden_ref.shape[1] // chunks
+    _, _, padded = out_refs[0].shape
+    width = padded - LANES
     top = routes_ref.shape[0]
     notes = spread(routes_ref[...], LANES, 0) + spread(gates_ref[...], LANES, top)
     notes = notes.astype(jnp.bfloat16)
-    for s in range(chunks):
-        start = pl.multiple_of(lax.rem(me[0] + s, chunks) * width, width)
-        out_refs[s][:, :width] = hidden_ref[:, pl.ds(start, width)]
-        out_refs[s][:, width:] = notes
+    for s in range(hidden_ref.shape[1] // width):
+        start = pl.multiple_of((me[0] ^ s) * width, width)
+        out_refs[s % 2][s // 2, :, :width] = hidden_ref[:, pl.ds(start, width)]
+        out_refs[s % 2][s // 2, :, width:] = notes
 
 
 def turned_notes(notes, top):
@@ -147,8 +152,7 @@
     member = jnp.zeros(shape, jnp.float32)
     for t in range(top):
         member = jnp.where(routes[t:t + 1] == expert, 1.0, member)
-    origin = level - row // each
-    origin = jnp.where(origin < 0, origin + sources, origin)
+    origin = level ^ (row // each)
     member = jnp.where(origin == source, member, 0.0)
     one = lax.broadcasted_iota(jnp.int32, (rows, rows), 0)
     other = lax.broadcasted_iota(jnp.int32, (rows, rows), 1)
@@ -157,48 +161,47 @@
     return jnp.where(ranks == rank.astype(jnp.float32), member, 0.0), expert
 
 
-def pack_kernel(top, experts, sources, column, level, *refs):
-    owners = len(refs) - sources
-    held, out_refs = refs[:sources], refs[sources:]
-    width = out_refs[0].shape[1]
-    rows = jnp.concatenate([ref[:, :width] for ref in held], axis=0)
-    notes = jnp.concatenate([ref[:, width:] for ref in held], axis=0)
+def pack_kernel(top, experts, places, column, level, *refs):
+    held, out_refs = refs[:-2], refs[-2:]
+    half, _, width = out_refs[0].shape
+    rows = jnp.concatenate([held[a][i, :, :width] for a, i in places], axis=0)
+    notes = jnp.concatenate([held[a][i, :, width:] for a, i in places], axis=0)
     routes, _ = turned_notes(notes, top)
-    for t in range(owners):
-        place, _ = placing(routes, lax.rem(column[0] + t, owners), level[0], experts, sources)
-        out_refs[t][...] = jnp.dot(
+    for t in range(2 * half):
+        place, _ = placing(routes, column[0] ^ t, level[0], experts, len(places))
+        out_refs[t % 2][t // 2] = jnp.dot(
             place.astype(jnp.bfloat16), rows, preferred_element_type=jnp.float32
-        ).astype(out_refs[t].dtype)
-
-
-def combine_kernel(top, experts, sources, column, level, *refs):
-    held, back_ref, out_ref = refs[:sources], refs[sources], refs[sources + 1]
-    owners = back_ref.shape[0]
-    _, each, width = out_ref.shape
-    notes = jnp.concatenate([ref[:, width:] for ref in held], axis=0)
+        ).astype(out_refs[t % 2].dtype)
+
+
+def combine_kernel(top, experts, places, back_places, column, level, *refs):
+    count = 1 + max(a for a, _ in places)
+    held, back, out_refs = refs[:count], refs[count:-2], refs[-2:]
+    _, each, width = out_refs[0].shape
+    notes = jnp.concatenate([held[a][i, :, width:] for a, i in places], axis=0)
     routes, gates = turned_notes(notes, top)
-    total = jnp.zeros((sources * each, width), jnp.float32)
-    for t in range(owners):
-        place, expert = placing(routes, t, level[0], experts, sources)
+    total = jnp.zeros((len(places) * each, width), jnp.float32)
+    for t, (a, i) in enumerate(back_places):
+        place, expert = placing(routes, column[0] ^ t, level[0], experts, len(places))
         weight = jnp.zeros_like(place)
         for k in range(top):
             weight = weight + jnp.where(routes[k:k + 1] == expert, gates[k:k + 1], 0.0)
         total = total + lax.dot_general(
             (weight * place).astype(jnp.bfloat16),
-            back_ref[t],
+            back[a][i],
             (((0,), (0,)), ((), ())),
             preferred_element_type=jnp.float32,
         )
-    for s in range(sources):
-        out_ref[lax.rem(level[0] + sources - s, sources)] = total[
-            s * each:(s + 1) * each
-        ].astype(out_ref.dtype)
-
-
-def assemble_kernel(pieces_ref, out_ref):
-    chunks, _, width = pieces_ref.shape
-    for k in range(chunks):
-        out_ref[:, k * width:(k + 1) * width] = pieces_ref[k]
+    for s in range(len(places)):
+        out_refs[s % 2][s // 2] = total[s * each:(s + 1) * each].astype(out_refs[s % 2].dtype)
+
+
+def assemble_kernel(places, me, *refs):
+    pieces, out_ref = refs[:-1], refs[-1]
+    width = pieces[0].shape[2]
+    for s, (a, i) in enumerate(places):
+        start = pl.multiple_of((me[0] ^ s) * width, width)
+        out_ref[:, pl.ds(start, width)] = pieces[a][i]
 
 
 def regroup(experts, owners, count):
@@ -214,12 +217,12 @@
     return (other == wanted).astype(jnp.bfloat16)
 
 
-def select_kernel(*refs):
+def select_kernel(places, *refs):
     packs, out_ref = refs[:-1], refs[-1]
     experts, count, _ = out_ref.shape
-    rows = jnp.concatenate([ref[...].astype(jnp.float32) for ref in packs], axis=0)
+    rows = jnp.concatenate([packs[a][i].astype(jnp.float32) for a, i in places], axis=0)
     moved = jnp.dot(
-        regroup(experts, len(packs), count // len(packs)),
+        regroup(experts, len(places), count // len(places)),
         rows.astype(jnp.bfloat16),
         preferred_element_type=jnp.float32,
     ).astype(out_ref.dtype)
@@ -272,8 +275,8 @@
         sum_ref[x] = jnp.dot(part_ref[x], weight_ref[x, chunk], preferred_element_type=jnp.float32)
 
 
-def down_rest_kernel(chunks, me, column, sum_ref, *refs):
-    parts, weight_ref, out_ref = refs[:chunks - 1], refs[chunks - 1], refs[chunks]
+def down_rest_kernel(chunks, me, sum_ref, *refs):
+    parts, weight_ref, out_refs = refs[:chunks - 1], refs[chunks - 1], refs[chunks + 1:]
     experts, count, width = sum_ref.shape
     ff = parts[0].shape[2]
     sums = []
@@ -286,7 +289,8 @@
                 parts[s - 1][x], weight_ref[x, chunk], preferred_element_type=jnp.float32
             )
         sums.append(total.astype(jnp.bfloat16))
-    owners, rows, _ = out_ref.shape
+    half, rows, _ = out_refs[0].shape
+    owners = 2 * half
     moved = lax.dot_general(
         regroup(experts, owners, count // owners),
         jnp.concatenate(sums, axis=0),
@@ -294,9 +298,7 @@
         preferred_element_type=jnp.float32,
     )
     for t in range(owners):
-        out_ref[lax.rem(column[0] + owners - t, owners)] = moved[
-            t * rows:(t + 1) * rows
-        ].astype(out_ref.dtype)
+        out_refs[t % 2][t // 2] = moved[t * rows:(t + 1) * rows].astype(out_refs[t % 2].dtype)
 
 
 def shifted(value, axis, steps):
@@ -313,6 +315,36 @@
     for s in farthest_first(len(values)):
         out[s] = shifted(values[s], axis, s)
     return out
+
+
+def take_kernel(places, *refs):
+    for n, (a, i) in enumerate(places):
+        refs[-1][n] = refs[a][i]
+
+
+def trade(kept, sent, axis):
+    size = lax.axis_size(axis)
+    arrays = [kept]
+    where = {(r, 0): (0, r // 2) for r in range(0, size, 2)}
+    bit = 1
+    while bit < size:
+        moving = sorted(key for key in where if key[0] & bit)
+        if bit > 1:
+            sent = call(
+                functools.partial(take_kernel, [where.pop(key) for key in moving]),
+                [],
+                arrays,
+                jax.ShapeDtypeStruct((len(moving),) + kept.shape[1:], kept.dtype),
+                "take",
+            )
+        else:
+            moving = [(r, 0) for r in range(1, size, 2)]
+        got = lax.ppermute(sent, axis, [(i, i ^ bit) for i in range(size)])
+        for n, (r, s) in enumerate(moving):
+            where[r ^ bit, s | bit] = (len(arrays), n)
+        arrays.append(got)
+        bit *= 2
+    return arrays, [where[0, s] for s in range(size)]
 
 
 def call(kernel, index, inputs, outputs, name, limit=16, after=(), cost=0):
@@ -345,14 +377,14 @@
         (part,) = gate_up(((me + s) % inner).reshape(1), inner, held, gate_up_weight, jnp.bfloat16)
         others.append(shifted(part, "inner", s))
     own, done = gate_up(level, inner, held, gate_up_weight, jnp.float32, True)
-    attended = attention(done)
+    first = attention(done, 0, 2)
     active = call(
         activate_kernel,
         [],
         [own, *others],
         jax.ShapeDtypeStruct((experts, count, ff // inner), jnp.bfloat16),
         "activate",
-        after=[attended],
+        after=[first],
     )
     parts = exchange([active] * inner, "inner")
     sums = call(
@@ -363,15 +395,17 @@
         "down_own",
         24,
     )
+    second = attention(sums, 1, 2)
     back = call(
         functools.partial(down_rest_kernel, inner),
-        [level, lax.axis_index("expert").astype(jnp.int32).reshape(1)],
+        [level],
         [sums, *parts[1:], down_weight],
-        jax.ShapeDtypeStruct((owners, experts * count // owners, width), jnp.bfloat16),
+        [jax.ShapeDtypeStruct((owners // 2, experts * count // owners, width), jnp.bfloat16)] * 2,
         "down_rest",
         24,
-    )
-    return back, attended
+        after=[second],
+    )
+    return back, jnp.concatenate([first, second], axis=0)
 
 
 def experts_by_rows(held, gate_up_weight, down_weight, owners, attention):
@@ -383,8 +417,7 @@
     outputs = jnp.einsum("sxf,xfd->xsd", active, down_weight, preferred_element_type=jnp.float32)
     outputs = outputs.astype(jnp.bfloat16).reshape(experts, owners, count // owners, -1)
     back = jnp.transpose(outputs, (1, 0, 2, 3)).reshape(owners, experts * count // owners, -1)
-    origin = (lax.axis_index("expert") - jnp.arange(owners)) % owners
-    return back[origin], attention(held)
+    return [back[0::2], back[1::2]], attention(held, 0, 1)
 
 
 def body(
@@ -407,56 +440,57 @@
     level = lax.axis_index("inner").astype(jnp.int32).reshape(1)
     slots = experts * CAP * inner
 
-    attention = functools.partial(attend, queries, new_key_value, cached_key_value, parents)
-
-    slices = call(
+    def attention(after, part, parts):
+        return attend(queries, new_key_value, cached_key_value, parents, after, part, parts)
+
+    kept, sent = call(
         prepare_kernel,
         [level],
         [routes.T, gate_values.T, hidden],
-        [jax.ShapeDtypeStruct((rows, depth + LANES), jnp.bfloat16)] * inner,
+        [jax.ShapeDtypeStruct((inner // 2, rows, depth + LANES), jnp.bfloat16)] * 2,
         "prepare",
-        cost=2,
-    )
-    slices = exchange(slices, "inner")
-    packs = call(
-        functools.partial(pack_kernel, top, experts, inner),
+        cost=10,
+    )
+    slices, places = trade(kept, sent, "inner")
+    kept, sent = call(
+        functools.partial(pack_kernel, top, experts, places),
         [column, level],
         slices,
-        [jax.ShapeDtypeStruct((slots, depth), jnp.bfloat16)] * owners,
+        [jax.ShapeDtypeStruct((owners // 2, slots, depth), jnp.bfloat16)] * 2,
         "pack",
-        cost=3,
-    )
-    packs = exchange(packs, "expert")
+        cost=20,
+    )
+    packs, pack_places = trade(kept, sent, "expert")
     held = call(
-        select_kernel,
+        functools.partial(select_kernel, pack_places),
         [],
         packs,
         jax.ShapeDtypeStruct((experts, owners * CAP * inner, depth), jnp.bfloat16),
         "select",
         24,
-        cost=1,
+        cost=10,
     )
     even = ff % (inner * LANES) == 0
-    back, attended = (experts_by_columns if even else experts_by_rows)(
+    (kept, sent), attended = (experts_by_columns if even else experts_by_rows)(
         held, gate_up_weight, down_weight, owners, attention
     )
-    back = lax.all_to_all(back, "expert", split_axis=0, concat_axis=0, tiled=True)
-    pieces = call(
-        functools.partial(combine_kernel, top, experts, inner),
+    back, back_places = trade(kept, sent, "expert")
+    kept, sent = call(
+        functools.partial(combine_kernel, top, experts, places, back_places),
         [column, level],
-        [*slices, back],
-        jax.ShapeDtypeStruct((inner, rows, width), jnp.bfloat16),
+        [*slices, *back],
+        [jax.ShapeDtypeStruct((inner // 2, rows, width), jnp.bfloat16)] * 2,
         "combine",
     )
-    pieces = lax.all_to_all(pieces, "inner", split_axis=0, concat_axis=0, tiled=True)
+    pieces, piece_places = trade(kept, sent, "inner")
     expert_out = call(
-        assemble_kernel,
-        [],
-        [pieces],
+        functools.partial(assemble_kernel, piece_places),
+        [level],
+        pieces,
         jax.ShapeDtypeStruct((rows, model), jnp.bfloat16),
         "assemble",
     )
-    return attended, expert_out
+    return attended.reshape(rows, QUERY_HEADS * HEAD_SIZE), expert_out
 
 
 def solution(mesh):

time: 68.9 us -> 68.2 us (0.990)
  blocking collectives: 16.7 us -> 0 us
  waiting for transfers between devices: 11.7 us -> 20.2 us
  starting transfers between devices: 19 us -> 26 us
    ppermute x0 -> x8, waiting for transfers between devices: none -> 17.4 us  [trade(): got = lax.ppermute(sent, axis, [(i, i ^ bit) for i in range(size)])]
    all_to_all x2 -> x0, blocking collectives: 16.7 us -> none  [the longest x1 8.65 us: body(): lax.all_to_all(pieces, 'inner', split_axis=0, concat_axis=0, tiled=True)]
    ppermute x0 -> x8, starting transfers between devices: none -> 13.1 us  [trade(): got = lax.ppermute(sent, axis, [(i, i ^ bit) for i in range(size)])]
    ppermute x12 -> x6, waiting for transfers between devices: 11.7 us -> 2.8 us  [shifted(): lax.ppermute(value, axis, [(i, (i + steps) % size) for i in range(size)])]
    ppermute x12 -> x6, starting transfers between devices: 19 us -> 12.8 us  [shifted(): lax.ppermute(value, axis, [(i, (i + steps) % size) for i in range(size)])]
    pallas_call x1 -> x2, Pallas kernels: 5.02 us -> 5.55 us  [attend(): pl.pallas_call(functools.partial(attend_kernel, step), grid_spec=pltpu.Pr...]
    unnamed x31 -> x29, local copies, waits for them, and re-layouts: 8.74 us -> 8.82 us
    pallas_call x12 -> x16, Pallas kernels: 6.58 us -> 6.61 us  [call(): pl.pallas_call(kernel, in_specs=[pl.BlockSpec(memory_space=pltpu.SMEM)] *...]
  transfers between devices with their start and end apart: 12 -> 14, of which waited for: 9 -> 11; matrix products, arithmetic and copies ran while one was open for 0% -> 1% of each run, Pallas kernels for 10% -> 11%
where the time goes in v4:
time: 68.2 us; the launch traced here: 68 us
  starting transfers between devices  26 us (38%)
  waiting for transfers between devices  20.2 us (30%)
  Pallas kernels  12.2 us (18%)
  local copies, waits for them, and re-layouts  8.82 us (13%)
  between operations  0.84 us (1%)
    ppermute x8, waiting for transfers between devices, trade(): got = lax.ppermute(sent, axis, [(i, i ^ bit) for i in range(size)])  17.4 us
    ppermute x8, starting transfers between devices, trade(): got = lax.ppermute(sent, axis, [(i, i ^ bit) for i in range(size)])  13.1 us
    ppermute x6, starting transfers between devices, shifted(): lax.ppermute(value, axis, [(i, (i + steps) % size) for i in range(size)])  12.8 us
    unnamed x29, local copies, waits for them, and re-layouts  8.82 us
    pallas_call x16, Pallas kernels, call(): pl.pallas_call(kernel, in_specs=[pl.BlockSpec(memory_space=pltpu.SMEM)] *...  6.61 us
    pallas_call x2, Pallas kernels, attend(): pl.pallas_call(functools.partial(attend_kernel, step), grid_spec=pltpu.Pr...  5.55 us
    ppermute x6, waiting for transfers between devices, shifted(): lax.ppermute(value, axis, [(i, (i + steps) % size) for i in range(size)])  2.8 us
  transfers between devices with their start and end apart: 14, of which 11 were waited for; matrix products, arithmetic and copies ran while one was open for 1% of the time, Pallas kernels for 11%

profile of v4, /device:TPU:0, one launch (start us, length us, event | category | flops | bytes accessed | tf_op | source)
XLA Modules:
  0.0 68.0 jit_solution(18313686247070616566)
XLA Ops:
  0.6 0.8 %copy-done.3 = bf16[8,4096]{1,0:T(8,128)(2,1)S(1)} copy-done((bf16[8,4096]{1,0:T(8,128)(2,1)S(1)}, bf16[8,4096]{1,0:T(8,128)(2,1)}, u32[]{:S(2)}) %copy-start.3) | copy-done | bytes 65560
  1.5 0.7 copy-done.4
  2.2 0.7 copy-done.5
  2.8 0.2 prepare.1
  3.0 3.0 %collective-permute-start = (bf16[2,8,1152]{2,1,0:T(8,128)(2,1)S(1)}, bf16[2,8,1152]{2,1,0:T(8,128)(2,1)S(1)}, u32[]{:S(2)}, u32[]{:S(2)}) collective-permute-start(bf16[2,8,1152]{2,1,0:T(8,128)(2,1)S(1)} %get-tuple-element.13), channel_id=1, source_target_pairs={{0,1},{1,0},{2,3},{3,2},{4,5},{5,4},{6,7},{7,6},{8,9},{9,8},{10,11... | collective-permute-start | bytes 110600 | tf_op jit(solution)/shard_map/ppermute | solution.py:342
  6.0 1.9 %collective-permute-done.refs_1_ = bf16[2,8,1152]{2,1,0:T(8,128)(2,1)S(1)} collective-permute-done((bf16[2,8,1152]{2,1,0:T(8,128)(2,1)S(1)}, bf16[2,8,1152]{2,1,0:T(8,128)(2,1)S(1)}, u32[]{:S(2)}, u32[]{:S(2)}) %collective-permute-start) | collective-permute-done | bytes 36896 | tf_op jit(solution)/shard_map/ppermute | solution.py:342
  8.0 3.0 %collective-permute-start.1 = (bf16[2,8,1152]{2,1,0:T(8,128)(2,1)S(1)}, bf16[2,8,1152]{2,1,0:T(8,128)(2,1)S(1)}, u32[]{:S(2)}, u32[]{:S(2)}) collective-permute-start(bf16[2,8,1152]{2,1,0:T(8,128)(2,1)S(1)} %take.4), channel_id=1, source_target_pairs={{0,2},{1,3},{2,0},{3,1},{4,6},{5,7},{6,4},{7,5},{8,10},{9,11},{10,... | collective-permute-start | bytes 110600 | tf_op jit(solution)/shard_map/ppermute | solution.py:342
  11.0 1.9 %collective-permute-done.1.refs_2_ = bf16[2,8,1152]{2,1,0:T(8,128)(2,1)S(1)} collective-permute-done((bf16[2,8,1152]{2,1,0:T(8,128)(2,1)S(1)}, bf16[2,8,1152]{2,1,0:T(8,128)(2,1)S(1)}, u32[]{:S(2)}, u32[]{:S(2)}) %collective-permute-start.1) | collective-permute-done | bytes 36896 | tf_op jit(solution)/shard_map/ppermute | solution.py:342
  12.9 0.8 %pack.1 = (bf16[2,24,1024]{2,1,0:T(8,128)(2,1)S(1)}, bf16[2,24,1024]{2,1,0:T(8,128)(2,1)S(1)}) custom-call(s32[1]{0:T(128)} %bitcast.2.column, s32[1]{0:T(128)} %bitcast.1.me.level.chunk, bf16[2,8,1152]{2,1,0:T(8,128)(2,1)S(1)} %get-tuple-element.12.refs_0_, bf16[2,8,1152]{2,1,0:T(8,128)(2,1)S(1)} %collective-permute-done.refs_1_, ...), custom_call_target="tpu_custom_call" | custom-call | flops 20000000000 | bytes 60000000 | tf_op jit(solution)/shard_map/pack/pallas_call | solution.py:352
  13.7 0.1 collective-permute-start.2
  13.8 1.3 %collective-permute-done.2.refs_1_ = bf16[2,24,1024]{2,1,0:T(8,128)(2,1)S(1)} collective-permute-done((bf16[2,24,1024]{2,1,0:T(8,128)(2,1)S(1)}, bf16[2,24,1024]{2,1,0:T(8,128)(2,1)S(1)}, u32[]{:S(2)}, u32[]{:S(2)}) %collective-permute-start.2) | collective-permute-done | bytes 98336 | tf_op jit(solution)/shard_map/ppermute | solution.py:342
  15.1 1.9 %collective-permute-start.3 = (bf16[2,24,1024]{2,1,0:T(8,128)(2,1)S(1)}, bf16[2,24,1024]{2,1,0:T(8,128)(2,1)S(1)}, u32[]{:S(2)}, u32[]{:S(2)}) collective-permute-start(bf16[2,24,1024]{2,1,0:T(8,128)(2,1)S(1)} %take.5), channel_id=1, source_target_pairs={{0,8},{4,12},{8,0},{12,4},{1,9},{5,13},{9,1},{13,5},{2,10},{6,14},... | collective-permute-start | bytes 294920 | tf_op jit(solution)/shard_map/ppermute | solution.py:342
  17.0 3.1 %collective-permute-done.3.refs_2_ = bf16[2,24,1024]{2,1,0:T(8,128)(2,1)S(1)} collective-permute-done((bf16[2,24,1024]{2,1,0:T(8,128)(2,1)S(1)}, bf16[2,24,1024]{2,1,0:T(8,128)(2,1)S(1)}, u32[]{:S(2)}, u32[]{:S(2)}) %collective-permute-start.3) | collective-permute-done | bytes 98336 | tf_op jit(solution)/shard_map/ppermute | solution.py:342
  20.1 0.2 select.7.rows_ref
  20.3 0.0 copy-start
  20.3 4.6 %copy-done = bf16[2,2,1024,1536]{3,2,1,0:T(8,128)(2,1)S(1)} copy-done((bf16[2,2,1024,1536]{3,2,1,0:T(8,128)(2,1)S(1)}, bf16[2,2,1024,1536]{3,2,1,0:T(8,128)(2,1)}, u32[]{:S(2)}) %copy-start) | copy-done | bytes 12582936
  24.9 0.6 gate_up.5
  25.5 2.9 %collective-permute-start.4 = (bf16[2,48,768]{2,1,0:T(8,128)(2,1)S(1)}, bf16[2,48,768]{2,1,0:T(8,128)(2,1)S(1)}, u32[]{:S(2)}, u32[]{:S(2)}) collective-permute-start(bf16[2,48,768]{2,1,0:T(8,128)(2,1)S(1)} %gate_up.5), channel_id=1, source_target_pairs={{0,2},{1,3},{2,0},{3,1},{4,6},{5,7},{6,4},{7,5},{8,10},{9,11},{10,... | collective-permute-start | bytes 442376 | tf_op jit(solution)/shard_map/ppermute | solution.py:306
  28.4 0.6 gate_up.6
  29.0 1.9 %collective-permute-start.5 = (bf16[2,48,768]{2,1,0:T(8,128)(2,1)S(1)}, bf16[2,48,768]{2,1,0:T(8,128)(2,1)S(1)}, u32[]{:S(2)}, u32[]{:S(2)}) collective-permute-start(bf16[2,48,768]{2,1,0:T(8,128)(2,1)S(1)} %gate_up.6), channel_id=1, source_target_pairs={{0,1},{1,2},{2,3},{3,0},{4,5},{5,6},{6,7},{7,4},{8,9},{9,10},{10,1... | collective-permute-start | bytes 442376 | tf_op jit(solution)/shard_map/ppermute | solution.py:306
  30.9 0.6 gate_up.7
  31.5 2.0 %collective-permute-start.6 = (bf16[2,48,768]{2,1,0:T(8,128)(2,1)S(1)}, bf16[2,48,768]{2,1,0:T(8,128)(2,1)S(1)}, u32[]{:S(2)}, u32[]{:S(2)}) collective-permute-start(bf16[2,48,768]{2,1,0:T(8,128)(2,1)S(1)} %gate_up.7), channel_id=1, source_target_pairs={{0,3},{1,0},{2,1},{3,2},{4,7},{5,4},{6,5},{7,6},{8,11},{9,8},{10,9... | collective-permute-start | bytes 442376 | tf_op jit(solution)/shard_map/ppermute | solution.py:306
  33.6 0.0 copy-start.1
  33.6 0.0 slice-start.3
  33.6 0.6 gate_up.4
  34.2 1.3 %copy-done.1 = bf16[1,8,192,1024]{3,2,1,0:T(8,128)(2,1)S(1)} copy-done((bf16[1,8,192,1024]{3,2,1,0:T(8,128)(2,1)S(1)}, bf16[1,8,192,1024]{3,2,1,0:T(8,128)(2,1)}, u32[]{:S(2)}) %copy-start.1) | copy-done | bytes 3145752
  35.5 2.8 %attend.2.refs_3_ = bf16[4,64,128]{2,1,0:T(8,128)(2,1)S(1)} custom-call(s32[8]{0:T(128)S(1)} %bitcast.29, bf16[8,64,128]{2,1,0:T(8,128)(2,1)S(1)} %bitcast.25, bf16[8,8,128]{2,1,0:T(8,128)(2,1)S(1)} %bitcast.27, bf16[1,8,192,1024]{3,2,1,0:T(8,128)(2,1)S(1)} %copy-done.1, bf16[1,8,192,1024]{3,2,1,0:T(8,128)(2,1)S(1)} %copy-done.1, ...), custom_call_target="tpu_custom_call" | custom-call | flops 25165824 | bytes 1572864 | tf_op jit(solution)/shard_map/attend/pallas_call | solution.py:69
  38.3 1.2 %collective-permute-done.4.refs_0_ = bf16[2,48,768]{2,1,0:T(8,128)(2,1)S(1)} collective-permute-done((bf16[2,48,768]{2,1,0:T(8,128)(2,1)S(1)}, bf16[2,48,768]{2,1,0:T(8,128)(2,1)S(1)}, u32[]{:S(2)}, u32[]{:S(2)}) %collective-permute-start.4) | collective-permute-done | bytes 147488 | tf_op jit(solution)/shard_map/ppermute | solution.py:306
  39.5 1.3 %collective-permute-done.6.refs_2_ = bf16[2,48,768]{2,1,0:T(8,128)(2,1)S(1)} collective-permute-done((bf16[2,48,768]{2,1,0:T(8,128)(2,1)S(1)}, bf16[2,48,768]{2,1,0:T(8,128)(2,1)S(1)}, u32[]{:S(2)}, u32[]{:S(2)}) %collective-permute-start.6) | collective-permute-done | bytes 147488 | tf_op jit(solution)/shard_map/ppermute | solution.py:306
  40.8 0.1 activate.1.part_ref
  40.9 1.2 %collective-permute-start.7 = (bf16[2,48,384]{2,1,0:T(8,128)(2,1)S(1)}, bf16[2,48,384]{2,1,0:T(8,128)(2,1)S(1)}, u32[]{:S(2)}, u32[]{:S(2)}) collective-permute-start(bf16[2,48,384]{2,1,0:T(8,128)(2,1)S(1)} %activate.1.part_ref), channel_id=1, source_target_pairs={{0,1},{1,2},{2,3},{3,0},{4,5},{5,6},{6,7},{7,4},{8,9},{9,10},{10,1... | collective-permute-start | bytes 221192 | tf_op jit(solution)/shard_map/ppermute | solution.py:306
  42.0 2.0 %collective-permute-start.8 = (bf16[2,48,384]{2,1,0:T(8,128)(2,1)S(1)}, bf16[2,48,384]{2,1,0:T(8,128)(2,1)S(1)}, u32[]{:S(2)}, u32[]{:S(2)}) collective-permute-start(bf16[2,48,384]{2,1,0:T(8,128)(2,1)S(1)} %activate.1.part_ref), channel_id=1, source_target_pairs={{0,2},{1,3},{2,0},{3,1},{4,6},{5,7},{6,4},{7,5},{8,10},{9,11},{10,... | collective-permute-start | bytes 221192 | tf_op jit(solution)/shard_map/ppermute | solution.py:306
  44.0 2.8 %collective-permute-start.9 = (bf16[2,48,384]{2,1,0:T(8,128)(2,1)S(1)}, bf16[2,48,384]{2,1,0:T(8,128)(2,1)S(1)}, u32[]{:S(2)}, u32[]{:S(2)}) collective-permute-start(bf16[2,48,384]{2,1,0:T(8,128)(2,1)S(1)} %activate.1.part_ref), channel_id=1, source_target_pairs={{0,3},{1,0},{2,1},{3,2},{4,7},{5,4},{6,5},{7,6},{8,11},{9,8},{10,9... | collective-permute-start | bytes 221192 | tf_op jit(solution)/shard_map/ppermute | solution.py:306
  46.9 0.4 down_own.1.refs_4_.sum_ref
  47.3 2.8 %attend.3.refs_4_ = bf16[4,64,128]{2,1,0:T(8,128)(2,1)S(1)} custom-call(s32[8]{0:T(128)S(1)} %bitcast.30, bf16[8,64,128]{2,1,0:T(8,128)(2,1)S(1)} %bitcast.26, bf16[8,8,128]{2,1,0:T(8,128)(2,1)S(1)} %bitcast.28, bf16[1,8,192,1024]{3,2,1,0:T(8,128)(2,1)S(1)} %copy-done.1, bf16[1,8,192,1024]{3,2,1,0:T(8,128)(2,1)S(1)} %copy-done.1, ...), custom_call_target="tpu_custom_call" | custom-call | flops 25165824 | bytes 1572864 | tf_op jit(solution)/shard_map/attend/pallas_call | solution.py:69
  50.0 0.3 collective-permute-done.8.refs_1_
  50.4 1.1 %down_rest.1 = (bf16[2,24,1024]{2,1,0:T(8,128)(2,1)S(1)}, bf16[2,24,1024]{2,1,0:T(8,128)(2,1)S(1)}) custom-call(s32[1]{0:T(128)} %bitcast.1.me.level.chunk, f32[2,48,1024]{2,1,0:T(8,128)S(1)} %down_own.1.refs_4_.sum_ref, bf16[2,48,384]{2,1,0:T(8,128)(2,1)S(1)} %collective-permute-done.7.refs_0_, bf16[2,48,384]{2,1,0:T(8,128)(2,1)S(1)} %collective-permute-done.8.refs_1_, ...), custom_call_target="tpu_custom_call" | custom-call | tf_op jit(solution)/shard_map/down_rest/pallas_call | solution.py:352
  51.5 0.1 collective-permute-start.10
  51.5 1.3 %collective-permute-done.10.refs_1_.refs_4_ = bf16[2,24,1024]{2,1,0:T(8,128)(2,1)S(1)} collective-permute-done((bf16[2,24,1024]{2,1,0:T(8,128)(2,1)S(1)}, bf16[2,24,1024]{2,1,0:T(8,128)(2,1)S(1)}, u32[]{:S(2)}, u32[]{:S(2)}) %collective-permute-start.10) | collective-permute-done | bytes 98336 | tf_op jit(solution)/shard_map/ppermute | solution.py:342
  52.8 1.6 %collective-permute-start.11 = (bf16[2,24,1024]{2,1,0:T(8,128)(2,1)S(1)}, bf16[2,24,1024]{2,1,0:T(8,128)(2,1)S(1)}, u32[]{:S(2)}, u32[]{:S(2)}) collective-permute-start(bf16[2,24,1024]{2,1,0:T(8,128)(2,1)S(1)} %take.6), channel_id=1, source_target_pairs={{0,8},{4,12},{8,0},{12,4},{1,9},{5,13},{9,1},{13,5},{2,10},{6,14},... | collective-permute-start | bytes 294920 | tf_op jit(solution)/shard_map/ppermute | solution.py:342
  54.4 3.3 %collective-permute-done.11.refs_5_ = bf16[2,24,1024]{2,1,0:T(8,128)(2,1)S(1)} collective-permute-done((bf16[2,24,1024]{2,1,0:T(8,128)(2,1)S(1)}, bf16[2,24,1024]{2,1,0:T(8,128)(2,1)S(1)}, u32[]{:S(2)}, u32[]{:S(2)}) %collective-permute-start.11) | collective-permute-done | bytes 98336 | tf_op jit(solution)/shard_map/ppermute | solution.py:342
  57.7 0.8 %combine.1 = (bf16[2,8,1024]{2,1,0:T(8,128)(2,1)S(1)}, bf16[2,8,1024]{2,1,0:T(8,128)(2,1)S(1)}) custom-call(s32[1]{0:T(128)} %bitcast.2.column, s32[1]{0:T(128)} %bitcast.1.me.level.chunk, bf16[2,8,1152]{2,1,0:T(8,128)(2,1)S(1)} %get-tuple-element.12.refs_0_, bf16[2,8,1152]{2,1,0:T(8,128)(2,1)S(1)} %collective-permute-done.refs_1_, ...), custom_call_target="tpu_custom_call" | custom-call | tf_op jit(solution)/shard_map/combine/pallas_call | solution.py:352
  58.6 1.5 %collective-permute-start.12 = (bf16[2,8,1024]{2,1,0:T(8,128)(2,1)S(1)}, bf16[2,8,1024]{2,1,0:T(8,128)(2,1)S(1)}, u32[]{:S(2)}, u32[]{:S(2)}) collective-permute-start(bf16[2,8,1024]{2,1,0:T(8,128)(2,1)S(1)} %get-tuple-element.21), channel_id=1, source_target_pairs={{0,1},{1,0},{2,3},{3,2},{4,5},{5,4},{6,7},{7,6},{8,9},{9,8},{10,11... | collective-permute-start | bytes 98312 | tf_op jit(solution)/shard_map/ppermute | solution.py:342
  60.0 2.5 %collective-permute-done.12.refs_1_ = bf16[2,8,1024]{2,1,0:T(8,128)(2,1)S(1)} collective-permute-done((bf16[2,8,1024]{2,1,0:T(8,128)(2,1)S(1)}, bf16[2,8,1024]{2,1,0:T(8,128)(2,1)S(1)}, u32[]{:S(2)}, u32[]{:S(2)}) %collective-permute-start.12) | collective-permute-done | bytes 32800 | tf_op jit(solution)/shard_map/ppermute | solution.py:342
  62.5 1.9 %collective-permute-start.13 = (bf16[2,8,1024]{2,1,0:T(8,128)(2,1)S(1)}, bf16[2,8,1024]{2,1,0:T(8,128)(2,1)S(1)}, u32[]{:S(2)}, u32[]{:S(2)}) collective-permute-start(bf16[2,8,1024]{2,1,0:T(8,128)(2,1)S(1)} %take.7), channel_id=1, source_target_pairs={{0,2},{1,3},{2,0},{3,1},{4,6},{5,7},{6,4},{7,5},{8,10},{9,11},{10,... | collective-permute-start | bytes 98312 | tf_op jit(solution)/shard_map/ppermute | solution.py:342
  64.5 0.7 %copy.17 = bf16[1,8,64,128]{3,1,2,0:T(8,128)(2,1)} copy(bf16[1,8,64,128]{3,2,1,0:T(8,128)(2,1)S(1)} %maximum_bitcast_fusion) | data formatting | bytes 262144
  65.3 2.1 %collective-permute-done.13.refs_2_ = bf16[2,8,1024]{2,1,0:T(8,128)(2,1)S(1)} collective-permute-done((bf16[2,8,1024]{2,1,0:T(8,128)(2,1)S(1)}, bf16[2,8,1024]{2,1,0:T(8,128)(2,1)S(1)}, u32[]{:S(2)}, u32[]{:S(2)}) %collective-permute-start.13) | collective-permute-done | bytes 32800 | tf_op jit(solution)/shard_map/ppermute | solution.py:342
  67.4 0.6 assemble.1
  (30 shorter events, 0.1 us)
Async XLA Ops:
  0.6 0.8 %copy-start.3 = (bf16[8,4096]{1,0:T(8,128)(2,1)S(1)}, bf16[8,4096]{1,0:T(8,128)(2,1)}, u32[]{:S(2)}) copy-start(bf16[8,4096]{1,0:T(8,128)(2,1)} %hidden_ref.1) | copy-start | bytes 196612
  1.5 0.7 copy-start.4
  2.2 0.7 copy-start.5
  3.0 5.0 %collective-permute-start = (bf16[2,8,1152]{2,1,0:T(8,128)(2,1)S(1)}, bf16[2,8,1152]{2,1,0:T(8,128)(2,1)S(1)}, u32[]{:S(2)}, u32[]{:S(2)}) collective-permute-start(bf16[2,8,1152]{2,1,0:T(8,128)(2,1)S(1)} %get-tuple-element.13), channel_id=1, source_target_pairs={{0,1},{1,0},{2,3},{3,2},{4,5},{5,4},{6,7},{7,6},{8,9},{9,8},{10,11... | collective-permute-start | bytes 110600 | tf_op jit(solution)/shard_map/ppermute | solution.py:342
  8.0 5.0 %collective-permute-start.1 = (bf16[2,8,1152]{2,1,0:T(8,128)(2,1)S(1)}, bf16[2,8,1152]{2,1,0:T(8,128)(2,1)S(1)}, u32[]{:S(2)}, u32[]{:S(2)}) collective-permute-start(bf16[2,8,1152]{2,1,0:T(8,128)(2,1)S(1)} %take.4), channel_id=1, source_target_pairs={{0,2},{1,3},{2,0},{3,1},{4,6},{5,7},{6,4},{7,5},{8,10},{9,11},{10,... | collective-permute-start | bytes 110600 | tf_op jit(solution)/shard_map/ppermute | solution.py:342
  13.7 1.4 %collective-permute-start.2 = (bf16[2,24,1024]{2,1,0:T(8,128)(2,1)S(1)}, bf16[2,24,1024]{2,1,0:T(8,128)(2,1)S(1)}, u32[]{:S(2)}, u32[]{:S(2)}) collective-permute-start(bf16[2,24,1024]{2,1,0:T(8,128)(2,1)S(1)} %get-tuple-element.15), channel_id=1, source_target_pairs={{0,4},{4,0},{8,12},{12,8},{1,5},{5,1},{9,13},{13,9},{2,6},{6,2},{1... | collective-permute-start | bytes 294920 | tf_op jit(solution)/shard_map/ppermute | solution.py:342
  15.1 5.0 %collective-permute-start.3 = (bf16[2,24,1024]{2,1,0:T(8,128)(2,1)S(1)}, bf16[2,24,1024]{2,1,0:T(8,128)(2,1)S(1)}, u32[]{:S(2)}, u32[]{:S(2)}) collective-permute-start(bf16[2,24,1024]{2,1,0:T(8,128)(2,1)S(1)} %take.5), channel_id=1, source_target_pairs={{0,8},{4,12},{8,0},{12,4},{1,9},{5,13},{9,1},{13,5},{2,10},{6,14},... | collective-permute-start | bytes 294920 | tf_op jit(solution)/shard_map/ppermute | solution.py:342
  20.3 4.6 %copy-start = (bf16[2,2,1024,1536]{3,2,1,0:T(8,128)(2,1)S(1)}, bf16[2,2,1024,1536]{3,2,1,0:T(8,128)(2,1)}, u32[]{:S(2)}) copy-start(bf16[2,2,1024,1536]{3,2,1,0:T(8,128)(2,1)} %weight_ref.8) | copy-start | bytes 37748740
  25.5 14.0 %collective-permute-start.4 = (bf16[2,48,768]{2,1,0:T(8,128)(2,1)S(1)}, bf16[2,48,768]{2,1,0:T(8,128)(2,1)S(1)}, u32[]{:S(2)}, u32[]{:S(2)}) collective-permute-start(bf16[2,48,768]{2,1,0:T(8,128)(2,1)S(1)} %gate_up.5), channel_id=1, source_target_pairs={{0,2},{1,3},{2,0},{3,1},{4,6},{5,7},{6,4},{7,5},{8,10},{9,11},{10,... | collective-permute-start | bytes 442376 | tf_op jit(solution)/shard_map/ppermute | solution.py:306
  28.4 5.2 %slice-start = ((s8[12582912]{0:T(1024)(128)(4,1)}), s8[4194304]{0:T(1024)(128)(4,1)S(1)}, s32[]{:S(2)}) async-start(s8[12582912]{0:T(1024)(128)(4,1)} %bitcast.21), calls=%async_computation | async-start | bytes 8388608
  28.4 5.2 %slice-start.1 = ((s8[12582912]{0:T(1024)(128)(4,1)}), s8[4194304]{0:T(1024)(128)(4,1)S(1)}, s32[]{:S(2)}) async-start(s8[12582912]{0:T(1024)(128)(4,1)} %bitcast.21), calls=%async_computation.1 | async-start | bytes 8388608
  29.0 10.5 %collective-permute-start.5 = (bf16[2,48,768]{2,1,0:T(8,128)(2,1)S(1)}, bf16[2,48,768]{2,1,0:T(8,128)(2,1)S(1)}, u32[]{:S(2)}, u32[]{:S(2)}) collective-permute-start(bf16[2,48,768]{2,1,0:T(8,128)(2,1)S(1)} %gate_up.6), channel_id=1, source_target_pairs={{0,1},{1,2},{2,3},{3,0},{4,5},{5,6},{6,7},{7,4},{8,9},{9,10},{10,1... | collective-permute-start | bytes 442376 | tf_op jit(solution)/shard_map/ppermute | solution.py:306
  30.9 2.6 %copy-start.6 = (bf16[8,8192]{1,0:T(8,128)(2,1)S(1)}, bf16[8,8192]{1,0:T(8,128)(2,1)}, u32[]{:S(2)}) copy-start(bf16[8,8192]{1,0:T(8,128)(2,1)} %param.9) | copy-start | bytes 393220
  30.9 2.7 %copy-start.7 = (bf16[8,1024]{1,0:T(8,128)(2,1)S(1)}, bf16[8,1024]{1,0:T(8,128)(2,1)}, u32[]{:S(2)}) copy-start(bf16[8,1024]{1,0:T(8,128)(2,1)} %param.10) | copy-start | bytes 49156
  30.9 2.7 %slice-start.2 = ((s8[12582912]{0:T(1024)(128)(4,1)}), s8[4194304]{0:T(1024)(128)(4,1)S(1)}, s32[]{:S(2)}) async-start(s8[12582912]{0:T(1024)(128)(4,1)} %bitcast.21), calls=%async_computation.2 | async-start | bytes 8388608
  31.5 9.3 %collective-permute-start.6 = (bf16[2,48,768]{2,1,0:T(8,128)(2,1)S(1)}, bf16[2,48,768]{2,1,0:T(8,128)(2,1)S(1)}, u32[]{:S(2)}, u32[]{:S(2)}) collective-permute-start(bf16[2,48,768]{2,1,0:T(8,128)(2,1)S(1)} %gate_up.7), channel_id=1, source_target_pairs={{0,3},{1,0},{2,1},{3,2},{4,7},{5,4},{6,5},{7,6},{8,11},{9,8},{10,9... | collective-permute-start | bytes 442376 | tf_op jit(solution)/shard_map/ppermute | solution.py:306
  33.6 1.9 %copy-start.1 = (bf16[1,8,192,1024]{3,2,1,0:T(8,128)(2,1)S(1)}, bf16[1,8,192,1024]{3,2,1,0:T(8,128)(2,1)}, u32[]{:S(2)}) copy-start(bf16[1,8,192,1024]{3,2,1,0:T(8,128)(2,1)} %refs_3_.4) | copy-start | bytes 9437188
  33.6 1.9 %copy-start.2 = (s32[1,8]{1,0:T(1,128)S(1)}, s32[1,8]{1,0:T(1,128)}, u32[]{:S(2)}) copy-start(s32[1,8]{1,0:T(1,128)} %param.12) | copy-start | bytes 100
  33.6 13.2 %slice-start.3 = ((s8[6291456]{0:T(1024)(128)(4,1)}), s8[4194304]{0:T(1024)(128)(4,1)S(1)}, s32[]{:S(2)}) async-start(s8[6291456]{0:T(1024)(128)(4,1)} %bitcast.23), calls=%async_computation.3 | async-start | bytes 8388608
  35.5 11.4 %slice-start.4 = ((s8[6291456]{0:T(1024)(128)(4,1)}), s8[2097152]{0:T(1024)(128)(4,1)S(1)}, s32[]{:S(2)}) async-start(s8[6291456]{0:T(1024)(128)(4,1)} %bitcast.23), calls=%async_computation.4 | async-start | bytes 4194304
  40.9 9.2 %collective-permute-start.7 = (bf16[2,48,384]{2,1,0:T(8,128)(2,1)S(1)}, bf16[2,48,384]{2,1,0:T(8,128)(2,1)S(1)}, u32[]{:S(2)}, u32[]{:S(2)}) collective-permute-start(bf16[2,48,384]{2,1,0:T(8,128)(2,1)S(1)} %activate.1.part_ref), channel_id=1, source_target_pairs={{0,1},{1,2},{2,3},{3,0},{4,5},{5,6},{6,7},{7,4},{8,9},{9,10},{10,1... | collective-permute-start | bytes 221192 | tf_op jit(solution)/shard_map/ppermute | solution.py:306
  42.0 8.3 %collective-permute-start.8 = (bf16[2,48,384]{2,1,0:T(8,128)(2,1)S(1)}, bf16[2,48,384]{2,1,0:T(8,128)(2,1)S(1)}, u32[]{:S(2)}, u32[]{:S(2)}) collective-permute-start(bf16[2,48,384]{2,1,0:T(8,128)(2,1)S(1)} %activate.1.part_ref), channel_id=1, source_target_pairs={{0,2},{1,3},{2,0},{3,1},{4,6},{5,7},{6,4},{7,5},{8,10},{9,11},{10,... | collective-permute-start | bytes 221192 | tf_op jit(solution)/shard_map/ppermute | solution.py:306
  44.0 6.3 %collective-permute-start.9 = (bf16[2,48,384]{2,1,0:T(8,128)(2,1)S(1)}, bf16[2,48,384]{2,1,0:T(8,128)(2,1)S(1)}, u32[]{:S(2)}, u32[]{:S(2)}) collective-permute-start(bf16[2,48,384]{2,1,0:T(8,128)(2,1)S(1)} %activate.1.part_ref), channel_id=1, source_target_pairs={{0,3},{1,0},{2,1},{3,2},{4,7},{5,4},{6,5},{7,6},{8,11},{9,8},{10,9... | collective-permute-start | bytes 221192 | tf_op jit(solution)/shard_map/ppermute | solution.py:306
  51.5 1.4 %collective-permute-start.10 = (bf16[2,24,1024]{2,1,0:T(8,128)(2,1)S(1)}, bf16[2,24,1024]{2,1,0:T(8,128)(2,1)S(1)}, u32[]{:S(2)}, u32[]{:S(2)}) collective-permute-start(bf16[2,24,1024]{2,1,0:T(8,128)(2,1)S(1)} %get-tuple-element.19), channel_id=1, source_target_pairs={{0,4},{4,0},{8,12},{12,8},{1,5},{5,1},{9,13},{13,9},{2,6},{6,2},{1... | collective-permute-start | bytes 294920 | tf_op jit(solution)/shard_map/ppermute | solution.py:342
  52.8 4.9 %collective-permute-start.11 = (bf16[2,24,1024]{2,1,0:T(8,128)(2,1)S(1)}, bf16[2,24,1024]{2,1,0:T(8,128)(2,1)S(1)}, u32[]{:S(2)}, u32[]{:S(2)}) collective-permute-start(bf16[2,24,1024]{2,1,0:T(8,128)(2,1)S(1)} %take.6), channel_id=1, source_target_pairs={{0,8},{4,12},{8,0},{12,4},{1,9},{5,13},{9,1},{13,5},{2,10},{6,14},... | collective-permute-start | bytes 294920 | tf_op jit(solution)/shard_map/ppermute | solution.py:342
  58.6 4.0 %collective-permute-start.12 = (bf16[2,8,1024]{2,1,0:T(8,128)(2,1)S(1)}, bf16[2,8,1024]{2,1,0:T(8,128)(2,1)S(1)}, u32[]{:S(2)}, u32[]{:S(2)}) collective-permute-start(bf16[2,8,1024]{2,1,0:T(8,128)(2,1)S(1)} %get-tuple-element.21), channel_id=1, source_target_pairs={{0,1},{1,0},{2,3},{3,2},{4,5},{5,4},{6,7},{7,6},{8,9},{9,8},{10,11... | collective-permute-start | bytes 98312 | tf_op jit(solution)/shard_map/ppermute | solution.py:342
  62.5 4.8 %collective-permute-start.13 = (bf16[2,8,1024]{2,1,0:T(8,128)(2,1)S(1)}, bf16[2,8,1024]{2,1,0:T(8,128)(2,1)S(1)}, u32[]{:S(2)}, u32[]{:S(2)}) collective-permute-start(bf16[2,8,1024]{2,1,0:T(8,128)(2,1)S(1)} %take.7), channel_id=1, source_target_pairs={{0,2},{1,3},{2,0},{3,1},{4,6},{5,7},{6,4},{7,5},{8,10},{9,11},{10,... | collective-permute-start | bytes 98312 | tf_op jit(solution)/shard_map/ppermute | solution.py:342

commit v5 on v3

--- a/solution.py
+++ b/solution.py
@@ -57,13 +57,14 @@
             out_ref[b, rows] = result.astype(out_ref.dtype)
 
 
-def attend(queries, new_key_value, cached_key_value, parents, after):
-    rows = queries.shape[0]
+def attend(queries, new_key_value, cached_key_value, parents, after, part, parts):
+    rows = queries.shape[0] // parts
+    first = part * rows
     _, beams, length, width = cached_key_value.shape
     step = 4
 
     def parent_of(b):
-        return lambda r, p: ((r * step + b) // beams, p[r * step + b], 0, 0)
+        return lambda r, p: ((first + r * step + b) // beams, p[first + r * step + b], 0, 0)
 
     out = pl.pallas_call(
         functools.partial(attend_kernel, step),
@@ -71,8 +72,12 @@
             num_scalar_prefetch=1,
             grid=(rows // step,),
             in_specs=[
-                pl.BlockSpec((step, QUERY_HEADS, HEAD_SIZE), lambda r, p: (r, 0, 0)),
-                pl.BlockSpec((step, 2 * KEY_HEADS, HEAD_SIZE), lambda r, p: (r, 0, 0)),
+                pl.BlockSpec(
+                    (step, QUERY_HEADS, HEAD_SIZE), lambda r, p: (first // step + r, 0, 0)
+                ),
+                pl.BlockSpec(
+                    (step, 2 * KEY_HEADS, HEAD_SIZE), lambda r, p: (first // step + r, 0, 0)
+                ),
             ]
             + [pl.BlockSpec((1, 1, length, width), parent_of(b)) for b in range(step)]
             + [pl.BlockSpec(memory_space=pl.ANY)],
@@ -87,13 +92,13 @@
         ),
         name="attend",
     )(
-        parents.reshape(rows),
-        queries.reshape(rows, QUERY_HEADS, HEAD_SIZE),
-        new_key_value.reshape(rows, 2 * KEY_HEADS, HEAD_SIZE),
+        parents.reshape(-1),
+        queries.reshape(-1, QUERY_HEADS, HEAD_SIZE),
+        new_key_value.reshape(-1, 2 * KEY_HEADS, HEAD_SIZE),
         *[cached_key_value] * step,
         after,
     )
-    return out.reshape(rows, QUERY_HEADS * HEAD_SIZE)
+    return out
 
 
 def spread(values, lanes, first):
@@ -109,15 +114,14 @@
 
 
 def prepare_kernel(me, routes_ref, gates_ref, hidden_ref, *out_refs):
-    chunks = len(out_refs)
-    width = hidden_ref.shape[1] // chunks
+    width = hidden_ref.shape[1] // len(out_refs)
     top = routes_ref.shape[0]
     notes = spread(routes_ref[...], LANES, 0) + spread(gates_ref[...], LANES, top)
     notes = notes.astype(jnp.bfloat16)
-    for s in range(chunks):
-        start = pl.multiple_of(lax.rem(me[0] + s, chunks) * width, width)
-        out_refs[s][:, :width] = hidden_ref[:, pl.ds(start, width)]
-        out_refs[s][:, width:] = notes
+    for s, out_ref in enumerate(out_refs):
+        start = pl.multiple_of((me[0] ^ s) * width, width)
+        out_ref[:, :width] = hidden_ref[:, pl.ds(start, width)]
+        out_ref[:, width:] = notes
 
 
 def turned_notes(notes, top):
@@ -147,8 +151,7 @@
     member = jnp.zeros(shape, jnp.float32)
     for t in range(top):
         member = jnp.where(routes[t:t + 1] == expert, 1.0, member)
-    origin = level - row // each
-    origin = jnp.where(origin < 0, origin + sources, origin)
+    origin = level ^ (row // each)
     member = jnp.where(origin == source, member, 0.0)
     one = lax.broadcasted_iota(jnp.int32, (rows, rows), 0)
     other = lax.broadcasted_iota(jnp.int32, (rows, rows), 1)
@@ -158,47 +161,52 @@
 
 
 def pack_kernel(top, experts, sources, column, level, *refs):
-    owners = len(refs) - sources
     held, out_refs = refs[:sources], refs[sources:]
     width = out_refs[0].shape[1]
     rows = jnp.concatenate([ref[:, :width] for ref in held], axis=0)
     notes = jnp.concatenate([ref[:, width:] for ref in held], axis=0)
     routes, _ = turned_notes(notes, top)
-    for t in range(owners):
-        place, _ = placing(routes, lax.rem(column[0] + t, owners), level[0], experts, sources)
-        out_refs[t][...] = jnp.dot(
+    for t, out_ref in enumerate(out_refs):
+        place, _ = placing(routes, column[0] ^ t, level[0], experts, sources)
+        out_ref[...] = jnp.dot(
             place.astype(jnp.bfloat16), rows, preferred_element_type=jnp.float32
-        ).astype(out_refs[t].dtype)
-
-
-def combine_kernel(top, experts, sources, column, level, *refs):
-    held, back_ref, out_ref = refs[:sources], refs[sources], refs[sources + 1]
-    owners = back_ref.shape[0]
-    _, each, width = out_ref.shape
-    notes = jnp.concatenate([ref[:, width:] for ref in held], axis=0)
+        ).astype(out_ref.dtype)
+
+
+def weigh_kernel(top, experts, column, level, *refs):
+    held, out_ref = refs[:-1], refs[-1]
+    notes = jnp.concatenate([ref[:, -LANES:] for ref in held], axis=0)
     routes, gates = turned_notes(notes, top)
-    total = jnp.zeros((sources * each, width), jnp.float32)
-    for t in range(owners):
-        place, expert = placing(routes, t, level[0], experts, sources)
+    for t in range(out_ref.shape[0]):
+        place, expert = placing(routes, column[0] ^ t, level[0], experts, len(held))
         weight = jnp.zeros_like(place)
         for k in range(top):
             weight = weight + jnp.where(routes[k:k + 1] == expert, gates[k:k + 1], 0.0)
+        out_ref[t] = (weight * place).astype(out_ref.dtype)
+
+
+def combine_kernel(weight_ref, *refs):
+    owners = weight_ref.shape[0]
+    back, out_refs = refs[:owners], refs[owners:]
+    each = out_refs[0].shape[0]
+    total = 0.0
+    for t in range(owners):
         total = total + lax.dot_general(
-            (weight * place).astype(jnp.bfloat16),
-            back_ref[t],
+            weight_ref[t],
+            back[t][...],
             (((0,), (0,)), ((), ())),
             preferred_element_type=jnp.float32,
         )
-    for s in range(sources):
-        out_ref[lax.rem(level[0] + sources - s, sources)] = total[
-            s * each:(s + 1) * each
-        ].astype(out_ref.dtype)
-
-
-def assemble_kernel(pieces_ref, out_ref):
-    chunks, _, width = pieces_ref.shape
-    for k in range(chunks):
-        out_ref[:, k * width:(k + 1) * width] = pieces_ref[k]
+    for s, out_ref in enumerate(out_refs):
+        out_ref[...] = total[s * each:(s + 1) * each].astype(out_ref.dtype)
+
+
+def assemble_kernel(me, *refs):
+    pieces, out_ref = refs[:-1], refs[-1]
+    width = pieces[0].shape[1]
+    for s, piece in enumerate(pieces):
+        start = pl.multiple_of((me[0] ^ s) * width, width)
+        out_ref[:, pl.ds(start, width)] = piece[...]
 
 
 def regroup(experts, owners, count):
@@ -227,31 +235,64 @@
         out_ref[x] = moved[x * count:(x + 1) * count]
 
 
-def gate_up_kernel(chunk, rows_ref, weight_ref, out_ref, done_ref=None):
-    if done_ref is not None:
-        done_ref[...] = jnp.zeros_like(done_ref)
-    ff = out_ref.shape[2] // 2
+def gate_up_kernel(pieces, afters, chunk, rows_ref, weight_hbm, *refs):
+    refs = refs[afters:]
+    out_ref, held, sems = refs[0], refs[-2], refs[-1]
+    experts, _, depth, ff = held.shape
     columns = pl.ds(pl.multiple_of(chunk[0] * ff, ff), ff)
-    for x in range(out_ref.shape[0]):
+    step = depth // pieces
+    copies = {}
+    for x in range(experts):
         for k in range(2):
-            out_ref[x, :, k * ff:(k + 1) * ff] = jnp.dot(
-                rows_ref[x], weight_ref[x, k, :, columns], preferred_element_type=jnp.float32
-            ).astype(out_ref.dtype)
-
-
-def gate_up(chunk, chunks, rows, weight, dtype, done=False):
+            for n in range(pieces):
+                part = pl.ds(n * step, step)
+                copies[x, k, n] = pltpu.make_async_copy(
+                    weight_hbm.at[x, k, part, columns],
+                    held.at[x, k, part],
+                    sems.at[(x * 2 + k) * pieces + n],
+                )
+                copies[x, k, n].start()
+    if len(refs) > 3:
+        refs[1][...] = jnp.zeros_like(refs[1])
+    for x in range(experts):
+        for k in range(2):
+            total = 0.0
+            for n in range(pieces):
+                part = slice(n * step, (n + 1) * step)
+                copies[x, k, n].wait()
+                total = total + jnp.dot(
+                    rows_ref[x, :, part], held[x, k, part], preferred_element_type=jnp.float32
+                )
+            out_ref[x, :, k * ff:(k + 1) * ff] = total.astype(out_ref.dtype)
+
+
+def gate_up(chunk, chunks, rows, weight, dtype, done=False, after=()):
     experts, count, depth = rows.shape
     ff = weight.shape[3] // chunks
-    return call(
-        gate_up_kernel,
-        [chunk],
-        [rows, weight],
-        [jax.ShapeDtypeStruct((experts, count, 2 * ff), dtype)]
+    pieces = 2
+    return pl.pallas_call(
+        functools.partial(gate_up_kernel, pieces, len(after)),
+        in_specs=[
+            pl.BlockSpec(memory_space=pltpu.SMEM),
+            pl.BlockSpec(memory_space=pltpu.VMEM),
+            pl.BlockSpec(memory_space=pl.ANY),
+        ]
+        + [pl.BlockSpec(memory_space=pl.ANY)] * len(after),
+        out_specs=[pl.BlockSpec(memory_space=pltpu.VMEM)] * (1 + done),
+        out_shape=[jax.ShapeDtypeStruct((experts, count, 2 * ff), dtype)]
         + [jax.ShapeDtypeStruct((8, LANES), jnp.float32)] * done,
-        "gate_up",
-        24,
-        cost=1,
-    )
+        scratch_shapes=[
+            pltpu.VMEM((experts, 2, depth, ff), weight.dtype),
+            pltpu.SemaphoreType.DMA((experts * 2 * pieces,)),
+        ],
+        compiler_params=params(52),
+        cost_estimate=pl.CostEstimate(
+            flops=4 * experts * count * depth * ff,
+            bytes_accessed=4 * experts * depth * ff,
+            transcendentals=0,
+        ),
+        name="gate_up",
+    )(chunk, rows, weight, *after)
 
 
 def activate_kernel(own_ref, *refs):
@@ -265,53 +306,52 @@
         out_ref[x] = (gate / (1.0 + jnp.exp(-gate)) * up).astype(out_ref.dtype)
 
 
-def down_own_kernel(me, part_ref, weight_ref, sum_ref):
+def down_product(part_ref, weight_ref, x, chunk):
     ff = part_ref.shape[2]
-    chunk = pl.ds(pl.multiple_of(me[0] * ff, ff), ff)
+    rows = pl.ds(pl.multiple_of(chunk * ff, ff), ff)
+    return jnp.dot(part_ref[x], weight_ref[x, rows], preferred_element_type=jnp.float32)
+
+
+def down_first_kernel(me, part_ref, weight_ref, sum_ref):
     for x in range(part_ref.shape[0]):
-        sum_ref[x] = jnp.dot(part_ref[x], weight_ref[x, chunk], preferred_element_type=jnp.float32)
-
-
-def down_rest_kernel(chunks, me, column, sum_ref, *refs):
-    parts, weight_ref, out_ref = refs[:chunks - 1], refs[chunks - 1], refs[chunks]
-    experts, count, width = sum_ref.shape
-    ff = parts[0].shape[2]
+        sum_ref[x] = down_product(part_ref, weight_ref, x, me[0])
+
+
+def down_more_kernel(index, me, before_ref, part_ref, weight_ref, sum_ref):
+    for x in range(part_ref.shape[0]):
+        sum_ref[x] = before_ref[x] + down_product(part_ref, weight_ref, x, me[0] ^ index)
+
+
+def down_rest_kernel(indices, me, sum_ref, *refs):
+    count = len(indices)
+    parts, weight_ref, out_refs = refs[:count], refs[count], refs[count + 2:]
+    experts, slots, _ = sum_ref.shape
     sums = []
     for x in range(experts):
         total = sum_ref[x]
-        for s in range(1, chunks):
-            chunk = lax.rem(me[0] + chunks - s, chunks)
-            chunk = pl.ds(pl.multiple_of(chunk * ff, ff), ff)
-            total = total + jnp.dot(
-                parts[s - 1][x], weight_ref[x, chunk], preferred_element_type=jnp.float32
-            )
+        for part_ref, index in zip(parts, indices):
+            total = total + down_product(part_ref, weight_ref, x, me[0] ^ index)
         sums.append(total.astype(jnp.bfloat16))
-    owners, rows, _ = out_ref.shape
+    owners = len(out_refs)
+    rows = experts * slots // owners
     moved = lax.dot_general(
-        regroup(experts, owners, count // owners),
+        regroup(experts, owners, slots // owners),
         jnp.concatenate(sums, axis=0),
         (((0,), (0,)), ((), ())),
         preferred_element_type=jnp.float32,
     )
-    for t in range(owners):
-        out_ref[lax.rem(column[0] + owners - t, owners)] = moved[
-            t * rows:(t + 1) * rows
-        ].astype(out_ref.dtype)
-
-
-def shifted(value, axis, steps):
-    size = lax.axis_size(axis)
-    return lax.ppermute(value, axis, [(i, (i + steps) % size) for i in range(size)])
-
-
-def farthest_first(size):
-    return sorted(range(1, size), key=lambda s: -min(s, size - s))
-
-
-def exchange(values, axis):
+    for t, out_ref in enumerate(out_refs):
+        out_ref[...] = moved[t * rows:(t + 1) * rows].astype(out_ref.dtype)
+
+
+def traded(value, axis, index):
+    return lax.ppermute(value, axis, [(i, i ^ index) for i in range(lax.axis_size(axis))])
+
+
+def trade(values, axis):
     out = [values[0]] + [None] * (len(values) - 1)
-    for s in farthest_first(len(values)):
-        out[s] = shifted(values[s], axis, s)
+    for s in reversed(range(1, len(values))):
+        out[s] = traded(values[s], axis, s)
     return out
 
 
@@ -340,38 +380,44 @@
     ff, width = down_weight.shape[1:]
     me = lax.axis_index("inner").astype(jnp.int32)
     level = me.reshape(1)
-    others = []
-    for s in farthest_first(inner):
-        (part,) = gate_up(((me + s) % inner).reshape(1), inner, held, gate_up_weight, jnp.bfloat16)
-        others.append(shifted(part, "inner", s))
-    own, done = gate_up(level, inner, held, gate_up_weight, jnp.float32, True)
-    attended = attention(done)
+    others, last = [], []
+    for s in reversed(range(1, inner)):
+        last = gate_up(
+            (me ^ s).reshape(1), inner, held, gate_up_weight, jnp.bfloat16, after=last
+        )
+        others.append(traded(last[0], "inner", s))
+    own, done = gate_up(level, inner, held, gate_up_weight, jnp.float32, True, last)
+    first = attention(done, 0, 2)
     active = call(
         activate_kernel,
         [],
         [own, *others],
         jax.ShapeDtypeStruct((experts, count, ff // inner), jnp.bfloat16),
         "activate",
-        after=[attended],
-    )
-    parts = exchange([active] * inner, "inner")
+        after=[first],
+    )
+    parts = trade([active] * inner, "inner")
+    sums_shape = jax.ShapeDtypeStruct((experts, count, width), jnp.float32)
+    sums = call(down_first_kernel, [level], [active, down_weight], sums_shape, "down_first", 24)
+    second = attention(sums, 1, 2)
     sums = call(
-        down_own_kernel,
+        functools.partial(down_more_kernel, 1),
         [level],
-        [parts[0], down_weight],
-        jax.ShapeDtypeStruct((experts, count, width), jnp.float32),
-        "down_own",
+        [sums, parts[1], down_weight],
+        sums_shape,
+        "down_more",
         24,
     )
     back = call(
-        functools.partial(down_rest_kernel, inner),
-        [level, lax.axis_index("expert").astype(jnp.int32).reshape(1)],
-        [sums, *parts[1:], down_weight],
-        jax.ShapeDtypeStruct((owners, experts * count // owners, width), jnp.bfloat16),
+        functools.partial(down_rest_kernel, list(range(2, inner))),
+        [level],
+        [sums, *parts[2:], down_weight],
+        [jax.ShapeDtypeStruct((experts * count // owners, width), jnp.bfloat16)] * owners,
         "down_rest",
         24,
-    )
-    return back, attended
+        after=[second],
+    )
+    return back, jnp.concatenate([first, second], axis=0)
 
 
 def experts_by_rows(held, gate_up_weight, down_weight, owners, attention):
@@ -382,9 +428,8 @@
     active = lax.all_gather(active, "inner", axis=0, tiled=True)
     outputs = jnp.einsum("sxf,xfd->xsd", active, down_weight, preferred_element_type=jnp.float32)
     outputs = outputs.astype(jnp.bfloat16).reshape(experts, owners, count // owners, -1)
-    back = jnp.transpose(outputs, (1, 0, 2, 3)).reshape(owners, experts * count // owners, -1)
-    origin = (lax.axis_index("expert") - jnp.arange(owners)) % owners
-    return back[origin], attention(held)
+    back = [outputs[:, t].reshape(experts * count // owners, -1) for t in range(owners)]
+    return back, attention(held, 0, 1)
 
 
 def body(
@@ -407,7 +452,8 @@
     level = lax.axis_index("inner").astype(jnp.int32).reshape(1)
     slots = experts * CAP * inner
 
-    attention = functools.partial(attend, queries, new_key_value, cached_key_value, parents)
+    def attention(after, part, parts):
+        return attend(queries, new_key_value, cached_key_value, parents, after, part, parts)
 
     slices = call(
         prepare_kernel,
@@ -415,18 +461,16 @@
         [routes.T, gate_values.T, hidden],
         [jax.ShapeDtypeStruct((rows, depth + LANES), jnp.bfloat16)] * inner,
         "prepare",
-        cost=2,
-    )
-    slices = exchange(slices, "inner")
+    )
+    slices = trade(slices, "inner")
     packs = call(
         functools.partial(pack_kernel, top, experts, inner),
         [column, level],
         slices,
         [jax.ShapeDtypeStruct((slots, depth), jnp.bfloat16)] * owners,
         "pack",
-        cost=3,
-    )
-    packs = exchange(packs, "expert")
+    )
+    packs = trade(packs, "expert")
     held = call(
         select_kernel,
         [],
@@ -434,29 +478,36 @@
         jax.ShapeDtypeStruct((experts, owners * CAP * inner, depth), jnp.bfloat16),
         "select",
         24,
-        cost=1,
     )
     even = ff % (inner * LANES) == 0
     back, attended = (experts_by_columns if even else experts_by_rows)(
         held, gate_up_weight, down_weight, owners, attention
     )
-    back = lax.all_to_all(back, "expert", split_axis=0, concat_axis=0, tiled=True)
+    back = trade(back, "expert")
+    weights = call(
+        functools.partial(weigh_kernel, top, experts),
+        [column, level],
+        slices,
+        jax.ShapeDtypeStruct((owners, slots, inner * rows), jnp.bfloat16),
+        "weigh",
+        cost=1,
+    )
     pieces = call(
-        functools.partial(combine_kernel, top, experts, inner),
-        [column, level],
-        [*slices, back],
-        jax.ShapeDtypeStruct((inner, rows, width), jnp.bfloat16),
+        combine_kernel,
+        [],
+        [weights, *back],
+        [jax.ShapeDtypeStruct((rows, width), jnp.bfloat16)] * inner,
         "combine",
     )
-    pieces = lax.all_to_all(pieces, "inner", split_axis=0, concat_axis=0, tiled=True)
+    pieces = trade(pieces, "inner")
     expert_out = call(
         assemble_kernel,
-        [],
-        [pieces],
+        [level],
+        pieces,
         jax.ShapeDtypeStruct((rows, model), jnp.bfloat16),
         "assemble",
     )
-    return attended, expert_out
+    return attended.reshape(rows, QUERY_HEADS * HEAD_SIZE), expert_out
 
 
 def solution(mesh):

time: 68.9 us -> 62.9 us (0.913)
  blocking collectives: 16.7 us -> 0 us
  Pallas kernels: 11.6 us -> 19.4 us
  local copies, waits for them, and re-layouts: 8.74 us -> 3.23 us
  waiting for transfers between devices: 11.7 us -> 16.3 us
  starting transfers between devices: 19 us -> 22.9 us
    all_to_all x2 -> x0, blocking collectives: 16.7 us -> none  [the longest x1 8.65 us: body(): lax.all_to_all(pieces, 'inner', split_axis=0, concat_axis=0, tiled=True)]
    pallas_call x0 -> x4, Pallas kernels: none -> 9.86 us  [gate_up(): pl.pallas_call(functools.partial(gate_up_kernel, pieces, len(after)), in_...]
    unnamed x31 -> x21, local copies, waits for them, and re-layouts: 8.74 us -> 3.23 us
    ppermute x12 -> x18, waiting for transfers between devices: 11.7 us -> 16.3 us  [traded(): lax.ppermute(value, axis, [(i, i ^ index) for i in range(lax.axis_size(ax...]
    ppermute x12 -> x18, starting transfers between devices: 19 us -> 22.9 us  [traded(): lax.ppermute(value, axis, [(i, i ^ index) for i in range(lax.axis_size(ax...]
    pallas_call x12 -> x10, Pallas kernels: 6.58 us -> 4.04 us  [call(): pl.pallas_call(kernel, in_specs=[pl.BlockSpec(memory_space=pltpu.SMEM)] *...]
    pallas_call x1 -> x2, Pallas kernels: 5.02 us -> 5.56 us  [attend(): pl.pallas_call(functools.partial(attend_kernel, step), grid_spec=pltpu.Pr...]
  transfers between devices with their start and end apart: 12 -> 18, of which waited for: 9 -> 10; matrix products, arithmetic and copies ran while one was open for 0% -> 1% of each run, Pallas kernels for 10% -> 22%
where the time goes in v5:
time: 62.9 us; the launch traced here: 62.7 us
  starting transfers between devices  22.9 us (36%)
  Pallas kernels  19.4 us (31%)
  waiting for transfers between devices  16.3 us (26%)
  local copies, waits for them, and re-layouts  3.23 us (5%)
  between operations  0.85 us (1%)
    ppermute x18, starting transfers between devices, traded(): lax.ppermute(value, axis, [(i, i ^ index) for i in range(lax.axis_size(ax...  22.9 us
    ppermute x18, waiting for transfers between devices, traded(): lax.ppermute(value, axis, [(i, i ^ index) for i in range(lax.axis_size(ax...  16.3 us
    pallas_call x4, Pallas kernels, gate_up(): pl.pallas_call(functools.partial(gate_up_kernel, pieces, len(after)), in_...  9.86 us
    pallas_call x2, Pallas kernels, attend(): pl.pallas_call(functools.partial(attend_kernel, step), grid_spec=pltpu.Pr...  5.56 us
    pallas_call x10, Pallas kernels, call(): pl.pallas_call(kernel, in_specs=[pl.BlockSpec(memory_space=pltpu.SMEM)] *...  4.04 us
    unnamed x21, local copies, waits for them, and re-layouts  3.23 us
  transfers between devices with their start and end apart: 18, of which 10 were waited for; matrix products, arithmetic and copies ran while one was open for 1% of the time, Pallas kernels for 22%

profile of v5, /device:TPU:0, one launch (start us, length us, event | category | flops | bytes accessed | tf_op | source)
XLA Modules:
  0.0 62.7 jit_solution(7036283285901345926)
XLA Ops:
  0.6 0.8 %copy-done.1 = bf16[8,4096]{1,0:T(8,128)(2,1)S(1)} copy-done((bf16[8,4096]{1,0:T(8,128)(2,1)S(1)}, bf16[8,4096]{1,0:T(8,128)(2,1)}, u32[]{:S(2)}) %copy-start.1) | copy-done | bytes 65560
  1.5 0.7 %copy-done.3 = s32[8,2]{0,1:T(2,128)S(1)} copy-done((s32[8,2]{0,1:T(2,128)S(1)}, s32[8,2]{0,1:T(2,128)}, u32[]{:S(2)}) %copy-start.3) | copy-done | bytes 88
  2.2 0.7 %copy-done.4 = bf16[8,2]{0,1:T(2,128)(2,1)S(1)} copy-done((bf16[8,2]{0,1:T(2,128)(2,1)S(1)}, bf16[8,2]{0,1:T(2,128)(2,1)}, u32[]{:S(2)}) %copy-start.4) | copy-done | bytes 56
  2.8 0.2 prepare.1
  3.0 3.0 %collective-permute-start = (bf16[8,1152]{1,0:T(8,128)(2,1)S(1)}, bf16[8,1152]{1,0:T(8,128)(2,1)S(1)}, u32[]{:S(2)}, u32[]{:S(2)}) collective-permute-start(bf16[8,1152]{1,0:T(8,128)(2,1)S(1)} %get-tuple-element.21), channel_id=1, source_target_pairs={{0,1},{1,0},{2,3},{3,2},{4,5},{5,4},{6,7},{7,6},{8,9},{9,8},{10,11... | collective-permute-start | bytes 55304 | tf_op jit(solution)/shard_map/ppermute | solution.py:348
  6.0 2.6 %collective-permute-start.1 = (bf16[8,1152]{1,0:T(8,128)(2,1)S(1)}, bf16[8,1152]{1,0:T(8,128)(2,1)S(1)}, u32[]{:S(2)}, u32[]{:S(2)}) collective-permute-start(bf16[8,1152]{1,0:T(8,128)(2,1)S(1)} %get-tuple-element.22), channel_id=1, source_target_pairs={{0,2},{1,3},{2,0},{3,1},{4,6},{5,7},{6,4},{7,5},{8,10},{9,11},{10,... | collective-permute-start | bytes 55304 | tf_op jit(solution)/shard_map/ppermute | solution.py:348
  8.6 2.2 %collective-permute-done.1.refs_2_ = bf16[8,1152]{1,0:T(8,128)(2,1)S(1)} collective-permute-done((bf16[8,1152]{1,0:T(8,128)(2,1)S(1)}, bf16[8,1152]{1,0:T(8,128)(2,1)S(1)}, u32[]{:S(2)}, u32[]{:S(2)}) %collective-permute-start.1) | collective-permute-done | bytes 18464 | tf_op jit(solution)/shard_map/ppermute | solution.py:348
  10.8 3.3 %collective-permute-done.2.refs_3_ = bf16[8,1152]{1,0:T(8,128)(2,1)S(1)} collective-permute-done((bf16[8,1152]{1,0:T(8,128)(2,1)S(1)}, bf16[8,1152]{1,0:T(8,128)(2,1)S(1)}, u32[]{:S(2)}, u32[]{:S(2)}) %collective-permute-start.2) | collective-permute-done | bytes 18464 | tf_op jit(solution)/shard_map/ppermute | solution.py:348
  14.2 0.8 %pack.1 = (bf16[24,1024]{1,0:T(8,128)(2,1)S(1)}, bf16[24,1024]{1,0:T(8,128)(2,1)S(1)}, bf16[24,1024]{1,0:T(8,128)(2,1)S(1)}, bf16[24,1024]{1,0:T(8,128)(2,1)S(1)}) custom-call(s32[1]{0:T(128)} %bitcast.2.column, s32[1]{0:T(128)} %bitcast.1.me.level.chunk, bf16[8,1152]{1,0:T(8,128)(2,1)S(1)} %get-tuple-element.20.refs_0_, ...), custom_call_target="tpu_custom_call" | custom-call | tf_op jit(solution)/shard_map/pack/pallas_call | solution.py:360
  15.0 0.1 collective-permute-start.3
  15.1 1.6 %collective-permute-start.4 = (bf16[24,1024]{1,0:T(8,128)(2,1)S(1)}, bf16[24,1024]{1,0:T(8,128)(2,1)S(1)}, u32[]{:S(2)}, u32[]{:S(2)}) collective-permute-start(bf16[24,1024]{1,0:T(8,128)(2,1)S(1)} %get-tuple-element.26), channel_id=1, source_target_pairs={{0,8},{4,12},{8,0},{12,4},{1,9},{5,13},{9,1},{13,5},{2,10},{6,14},... | collective-permute-start | bytes 147464 | tf_op jit(solution)/shard_map/ppermute | solution.py:348
  16.6 0.3 collective-permute-start.5
  16.9 2.3 %collective-permute-done.4.refs_2_ = bf16[24,1024]{1,0:T(8,128)(2,1)S(1)} collective-permute-done((bf16[24,1024]{1,0:T(8,128)(2,1)S(1)}, bf16[24,1024]{1,0:T(8,128)(2,1)S(1)}, u32[]{:S(2)}, u32[]{:S(2)}) %collective-permute-start.4) | collective-permute-done | bytes 49184 | tf_op jit(solution)/shard_map/ppermute | solution.py:348
  19.2 1.1 %collective-permute-done.5.refs_3_ = bf16[24,1024]{1,0:T(8,128)(2,1)S(1)} collective-permute-done((bf16[24,1024]{1,0:T(8,128)(2,1)S(1)}, bf16[24,1024]{1,0:T(8,128)(2,1)S(1)}, u32[]{:S(2)}, u32[]{:S(2)}) %collective-permute-start.5) | collective-permute-done | bytes 49184 | tf_op jit(solution)/shard_map/ppermute | solution.py:348
  20.3 0.2 select.1.rows_ref
  20.5 2.4 %gate_up.4.refs_0_ = bf16[2,48,768]{2,1,0:T(8,128)(2,1)S(1)} custom-call(s32[1]{0:T(128)} %bitcast.7.chunk, bf16[2,48,1024]{2,1,0:T(8,128)(2,1)S(1)} %select.1.rows_ref, bf16[2,2,1024,1536]{3,2,1,0:T(8,128)(2,1)} %weight_hbm.7), custom_call_target="tpu_custom_call" | custom-call | flops 150994944 | bytes 3145728 | tf_op jit(solution)/shard_map/gate_up/pallas_call | solution.py:273
  22.9 0.3 collective-permute-start.6
  23.2 2.4 %gate_up.5.refs_0_ = bf16[2,48,768]{2,1,0:T(8,128)(2,1)S(1)} custom-call(s32[1]{0:T(128)} %bitcast.6.chunk, bf16[2,48,1024]{2,1,0:T(8,128)(2,1)S(1)} %select.1.rows_ref, bf16[2,2,1024,1536]{3,2,1,0:T(8,128)(2,1)} %weight_hbm.7, bf16[2,48,768]{2,1,0:T(8,128)(2,1)S(1)} %gate_up.4.refs_0_), custom_call_target="tpu_custom_call" | custom-call | flops 150994944 | bytes 3145728 | tf_op jit(solution)/shard_map/gate_up/pallas_call | solution.py:273
  25.6 0.1 collective-permute-start.7
  25.7 2.5 %gate_up.6.refs_0_ = bf16[2,48,768]{2,1,0:T(8,128)(2,1)S(1)} custom-call(s32[1]{0:T(128)} %bitcast.5.chunk, bf16[2,48,1024]{2,1,0:T(8,128)(2,1)S(1)} %select.1.rows_ref, bf16[2,2,1024,1536]{3,2,1,0:T(8,128)(2,1)} %weight_hbm.7, bf16[2,48,768]{2,1,0:T(8,128)(2,1)S(1)} %gate_up.5.refs_0_), custom_call_target="tpu_custom_call" | custom-call | flops 150994944 | bytes 3145728 | tf_op jit(solution)/shard_map/gate_up/pallas_call | solution.py:273
  28.2 4.2 %collective-permute-start.8 = (bf16[2,48,768]{2,1,0:T(8,128)(2,1)S(1)}, bf16[2,48,768]{2,1,0:T(8,128)(2,1)S(1)}, u32[]{:S(2)}, u32[]{:S(2)}) collective-permute-start(bf16[2,48,768]{2,1,0:T(8,128)(2,1)S(1)} %gate_up.6.refs_0_), channel_id=1, source_target_pairs={{0,1},{1,0},{2,3},{3,2},{4,5},{5,4},{6,7},{7,6},{8,9},{9,8},{10,11... | collective-permute-start | bytes 442376 | tf_op jit(solution)/shard_map/ppermute | solution.py:348
  32.5 2.6 %gate_up.7 = (f32[2,48,768]{2,1,0:T(8,128)S(1)}, f32[8,128]{1,0:T(8,128)S(1)}) custom-call(s32[1]{0:T(128)} %bitcast.1.me.level.chunk, bf16[2,48,1024]{2,1,0:T(8,128)(2,1)S(1)} %select.1.rows_ref, bf16[2,2,1024,1536]{3,2,1,0:T(8,128)(2,1)} %weight_hbm.7, bf16[2,48,768]{2,1,0:T(8,128)(2,1)S(1)} %gate_up.6.refs_0_), custom_call_target="tpu_custom_call" | custom-call | flops 150994944 | bytes 3145728 | tf_op jit(solution)/shard_map/gate_up/pallas_call | solution.py:273
  35.0 0.3 copy-done
  35.3 2.8 %attend.2.refs_3_ = bf16[4,64,128]{2,1,0:T(8,128)(2,1)S(1)} custom-call(s32[8]{0:T(128)S(1)} %bitcast.27, bf16[8,64,128]{2,1,0:T(8,128)(2,1)S(1)} %bitcast.23, bf16[8,8,128]{2,1,0:T(8,128)(2,1)S(1)} %bitcast.25, bf16[1,8,192,1024]{3,2,1,0:T(8,128)(2,1)S(1)} %copy-done, bf16[1,8,192,1024]{3,2,1,0:T(8,128)(2,1)S(1)} %copy-done, ...), custom_call_target="tpu_custom_call" | custom-call | flops 25165824 | bytes 1572864 | tf_op jit(solution)/shard_map/attend/pallas_call | solution.py:69
  38.1 1.0 %collective-permute-done.8.refs_2_ = bf16[2,48,768]{2,1,0:T(8,128)(2,1)S(1)} collective-permute-done((bf16[2,48,768]{2,1,0:T(8,128)(2,1)S(1)}, bf16[2,48,768]{2,1,0:T(8,128)(2,1)S(1)}, u32[]{:S(2)}, u32[]{:S(2)}) %collective-permute-start.8) | collective-permute-done | bytes 147488 | tf_op jit(solution)/shard_map/ppermute | solution.py:348
  39.1 0.1 activate.1.part_ref
  39.2 0.1 collective-permute-start.9
  39.3 2.2 %collective-permute-start.10 = (bf16[2,48,384]{2,1,0:T(8,128)(2,1)S(1)}, bf16[2,48,384]{2,1,0:T(8,128)(2,1)S(1)}, u32[]{:S(2)}, u32[]{:S(2)}) collective-permute-start(bf16[2,48,384]{2,1,0:T(8,128)(2,1)S(1)} %activate.1.part_ref), channel_id=1, source_target_pairs={{0,2},{1,3},{2,0},{3,1},{4,6},{5,7},{6,4},{7,5},{8,10},{9,11},{10,... | collective-permute-start | bytes 221192 | tf_op jit(solution)/shard_map/ppermute | solution.py:348
  41.4 2.2 %collective-permute-start.11 = (bf16[2,48,384]{2,1,0:T(8,128)(2,1)S(1)}, bf16[2,48,384]{2,1,0:T(8,128)(2,1)S(1)}, u32[]{:S(2)}, u32[]{:S(2)}) collective-permute-start(bf16[2,48,384]{2,1,0:T(8,128)(2,1)S(1)} %activate.1.part_ref), channel_id=1, source_target_pairs={{0,3},{1,2},{2,1},{3,0},{4,7},{5,6},{6,5},{7,4},{8,11},{9,10},{10,... | collective-permute-start | bytes 221192 | tf_op jit(solution)/shard_map/ppermute | solution.py:348
  43.7 0.4 down_first.1.refs_4_.before_ref
  44.0 2.8 %attend.3.refs_3_ = bf16[4,64,128]{2,1,0:T(8,128)(2,1)S(1)} custom-call(s32[8]{0:T(128)S(1)} %bitcast.28, bf16[8,64,128]{2,1,0:T(8,128)(2,1)S(1)} %bitcast.24, bf16[8,8,128]{2,1,0:T(8,128)(2,1)S(1)} %bitcast.26, bf16[1,8,192,1024]{3,2,1,0:T(8,128)(2,1)S(1)} %copy-done, bf16[1,8,192,1024]{3,2,1,0:T(8,128)(2,1)S(1)} %copy-done, ...), custom_call_target="tpu_custom_call" | custom-call | flops 25165824 | bytes 1572864 | tf_op jit(solution)/shard_map/attend/pallas_call | solution.py:69
  46.8 0.4 down_more.1.sum_ref
  47.2 0.4 collective-permute-done.10.refs_0_
  47.6 0.8 %down_rest.1 = (bf16[24,1024]{1,0:T(8,128)(2,1)S(1)}, bf16[24,1024]{1,0:T(8,128)(2,1)S(1)}, bf16[24,1024]{1,0:T(8,128)(2,1)S(1)}, bf16[24,1024]{1,0:T(8,128)(2,1)S(1)}) custom-call(s32[1]{0:T(128)} %bitcast.1.me.level.chunk, f32[2,48,1024]{2,1,0:T(8,128)S(1)} %down_more.1.sum_ref, bf16[2,48,384]{2,1,0:T(8,128)(2,1)S(1)} %collective-permute-done.10.refs_0_, ...), custom_call_target="tpu_custom_call" | custom-call | tf_op jit(solution)/shard_map/down_rest/pallas_call | solution.py:360
  48.5 0.1 collective-permute-start.12
  48.6 1.3 %collective-permute-start.13 = (bf16[24,1024]{1,0:T(8,128)(2,1)S(1)}, bf16[24,1024]{1,0:T(8,128)(2,1)S(1)}, u32[]{:S(2)}, u32[]{:S(2)}) collective-permute-start(bf16[24,1024]{1,0:T(8,128)(2,1)S(1)} %get-tuple-element.32), channel_id=1, source_target_pairs={{0,8},{4,12},{8,0},{12,4},{1,9},{5,13},{9,1},{13,5},{2,10},{6,14},... | collective-permute-start | bytes 147464 | tf_op jit(solution)/shard_map/ppermute | solution.py:348
  49.8 0.6 collective-permute-start.14
  50.4 0.3 weigh.1.weight_ref
  50.7 2.0 %collective-permute-done.13.refs_2_ = bf16[24,1024]{1,0:T(8,128)(2,1)S(1)} collective-permute-done((bf16[24,1024]{1,0:T(8,128)(2,1)S(1)}, bf16[24,1024]{1,0:T(8,128)(2,1)S(1)}, u32[]{:S(2)}, u32[]{:S(2)}) %collective-permute-start.13) | collective-permute-done | bytes 49184 | tf_op jit(solution)/shard_map/ppermute | solution.py:348
  52.7 0.8 %collective-permute-done.14.refs_3_ = bf16[24,1024]{1,0:T(8,128)(2,1)S(1)} collective-permute-done((bf16[24,1024]{1,0:T(8,128)(2,1)S(1)}, bf16[24,1024]{1,0:T(8,128)(2,1)S(1)}, u32[]{:S(2)}, u32[]{:S(2)}) %collective-permute-start.14) | collective-permute-done | bytes 49184 | tf_op jit(solution)/shard_map/ppermute | solution.py:348
  53.5 0.2 combine.1
  53.8 1.4 %collective-permute-start.15 = (bf16[8,1024]{1,0:T(8,128)(2,1)S(1)}, bf16[8,1024]{1,0:T(8,128)(2,1)S(1)}, u32[]{:S(2)}, u32[]{:S(2)}) collective-permute-start(bf16[8,1024]{1,0:T(8,128)(2,1)S(1)} %get-tuple-element.35), channel_id=1, source_target_pairs={{0,1},{1,0},{2,3},{3,2},{4,5},{5,4},{6,7},{7,6},{8,9},{9,8},{10,11... | collective-permute-start | bytes 49160 | tf_op jit(solution)/shard_map/ppermute | solution.py:348
  55.2 1.4 %collective-permute-start.16 = (bf16[8,1024]{1,0:T(8,128)(2,1)S(1)}, bf16[8,1024]{1,0:T(8,128)(2,1)S(1)}, u32[]{:S(2)}, u32[]{:S(2)}) collective-permute-start(bf16[8,1024]{1,0:T(8,128)(2,1)S(1)} %get-tuple-element.36), channel_id=1, source_target_pairs={{0,2},{1,3},{2,0},{3,1},{4,6},{5,7},{6,4},{7,5},{8,10},{9,11},{10,... | collective-permute-start | bytes 49160 | tf_op jit(solution)/shard_map/ppermute | solution.py:348
  56.6 1.7 %collective-permute-start.17 = (bf16[8,1024]{1,0:T(8,128)(2,1)S(1)}, bf16[8,1024]{1,0:T(8,128)(2,1)S(1)}, u32[]{:S(2)}, u32[]{:S(2)}) collective-permute-start(bf16[8,1024]{1,0:T(8,128)(2,1)S(1)} %get-tuple-element.37), channel_id=1, source_target_pairs={{0,3},{1,2},{2,1},{3,0},{4,7},{5,6},{6,5},{7,4},{8,11},{9,10},{10,... | collective-permute-start | bytes 49160 | tf_op jit(solution)/shard_map/ppermute | solution.py:348
  58.2 0.7 %copy.17 = bf16[1,8,64,128]{3,1,2,0:T(8,128)(2,1)} copy(bf16[1,8,64,128]{3,2,1,0:T(8,128)(2,1)S(1)} %maximum_bitcast_fusion) | data formatting | bytes 262144
  59.0 0.8 %collective-permute-done.16.refs_2_ = bf16[8,1024]{1,0:T(8,128)(2,1)S(1)} collective-permute-done((bf16[8,1024]{1,0:T(8,128)(2,1)S(1)}, bf16[8,1024]{1,0:T(8,128)(2,1)S(1)}, u32[]{:S(2)}, u32[]{:S(2)}) %collective-permute-start.16) | collective-permute-done | bytes 16416 | tf_op jit(solution)/shard_map/ppermute | solution.py:348
  59.8 2.3 %collective-permute-done.17.refs_3_ = bf16[8,1024]{1,0:T(8,128)(2,1)S(1)} collective-permute-done((bf16[8,1024]{1,0:T(8,128)(2,1)S(1)}, bf16[8,1024]{1,0:T(8,128)(2,1)S(1)}, u32[]{:S(2)}, u32[]{:S(2)}) %collective-permute-start.17) | collective-permute-done | bytes 16416 | tf_op jit(solution)/shard_map/ppermute | solution.py:348
  62.1 0.6 %assemble.1 = bf16[8,4096]{1,0:T(8,128)(2,1)} custom-call(s32[1]{0:T(128)} %bitcast.1.me.level.chunk, bf16[8,1024]{1,0:T(8,128)(2,1)S(1)} %get-tuple-element.34.refs_0_, bf16[8,1024]{1,0:T(8,128)(2,1)S(1)} %collective-permute-done.15.refs_1_, bf16[8,1024]{1,0:T(8,128)(2,1)S(1)} %collective-permute-done.16.refs_2_, ...), custom_call_target="tpu_custom_call" | custom-call | tf_op jit(solution)/shard_map/assemble/pallas_call | solution.py:360
  (27 shorter events, 0.1 us)
Async XLA Ops:
  0.6 0.8 %copy-start.1 = (bf16[8,4096]{1,0:T(8,128)(2,1)S(1)}, bf16[8,4096]{1,0:T(8,128)(2,1)}, u32[]{:S(2)}) copy-start(bf16[8,4096]{1,0:T(8,128)(2,1)} %hidden_ref.1) | copy-start | bytes 196612
  1.5 0.7 %copy-start.3 = (s32[8,2]{0,1:T(2,128)S(1)}, s32[8,2]{0,1:T(2,128)}, u32[]{:S(2)}) copy-start(s32[8,2]{0,1:T(2,128)} %param.14) | copy-start | bytes 196
  2.2 0.7 %copy-start.4 = (bf16[8,2]{0,1:T(2,128)(2,1)S(1)}, bf16[8,2]{0,1:T(2,128)(2,1)}, u32[]{:S(2)}) copy-start(bf16[8,2]{0,1:T(2,128)(2,1)} %param.15) | copy-start | bytes 100
  3.0 5.6 %collective-permute-start = (bf16[8,1152]{1,0:T(8,128)(2,1)S(1)}, bf16[8,1152]{1,0:T(8,128)(2,1)S(1)}, u32[]{:S(2)}, u32[]{:S(2)}) collective-permute-start(bf16[8,1152]{1,0:T(8,128)(2,1)S(1)} %get-tuple-element.21), channel_id=1, source_target_pairs={{0,1},{1,0},{2,3},{3,2},{4,5},{5,4},{6,7},{7,6},{8,9},{9,8},{10,11... | collective-permute-start | bytes 55304 | tf_op jit(solution)/shard_map/ppermute | solution.py:348
  6.0 4.8 %collective-permute-start.1 = (bf16[8,1152]{1,0:T(8,128)(2,1)S(1)}, bf16[8,1152]{1,0:T(8,128)(2,1)S(1)}, u32[]{:S(2)}, u32[]{:S(2)}) collective-permute-start(bf16[8,1152]{1,0:T(8,128)(2,1)S(1)} %get-tuple-element.22), channel_id=1, source_target_pairs={{0,2},{1,3},{2,0},{3,1},{4,6},{5,7},{6,4},{7,5},{8,10},{9,11},{10,... | collective-permute-start | bytes 55304 | tf_op jit(solution)/shard_map/ppermute | solution.py:348
  8.6 5.6 %collective-permute-start.2 = (bf16[8,1152]{1,0:T(8,128)(2,1)S(1)}, bf16[8,1152]{1,0:T(8,128)(2,1)S(1)}, u32[]{:S(2)}, u32[]{:S(2)}) collective-permute-start(bf16[8,1152]{1,0:T(8,128)(2,1)S(1)} %get-tuple-element.23), channel_id=1, source_target_pairs={{0,3},{1,2},{2,1},{3,0},{4,7},{5,6},{6,5},{7,4},{8,11},{9,10},{10,... | collective-permute-start | bytes 55304 | tf_op jit(solution)/shard_map/ppermute | solution.py:348
  15.0 1.9 %collective-permute-start.3 = (bf16[24,1024]{1,0:T(8,128)(2,1)S(1)}, bf16[24,1024]{1,0:T(8,128)(2,1)S(1)}, u32[]{:S(2)}, u32[]{:S(2)}) collective-permute-start(bf16[24,1024]{1,0:T(8,128)(2,1)S(1)} %get-tuple-element.25), channel_id=1, source_target_pairs={{0,4},{4,0},{8,12},{12,8},{1,5},{5,1},{9,13},{13,9},{2,6},{6,2},{1... | collective-permute-start | bytes 147464 | tf_op jit(solution)/shard_map/ppermute | solution.py:348
  15.1 4.2 %collective-permute-start.4 = (bf16[24,1024]{1,0:T(8,128)(2,1)S(1)}, bf16[24,1024]{1,0:T(8,128)(2,1)S(1)}, u32[]{:S(2)}, u32[]{:S(2)}) collective-permute-start(bf16[24,1024]{1,0:T(8,128)(2,1)S(1)} %get-tuple-element.26), channel_id=1, source_target_pairs={{0,8},{4,12},{8,0},{12,4},{1,9},{5,13},{9,1},{13,5},{2,10},{6,14},... | collective-permute-start | bytes 147464 | tf_op jit(solution)/shard_map/ppermute | solution.py:348
  16.6 3.7 %collective-permute-start.5 = (bf16[24,1024]{1,0:T(8,128)(2,1)S(1)}, bf16[24,1024]{1,0:T(8,128)(2,1)S(1)}, u32[]{:S(2)}, u32[]{:S(2)}) collective-permute-start(bf16[24,1024]{1,0:T(8,128)(2,1)S(1)} %get-tuple-element.27), channel_id=1, source_target_pairs={{0,12},{4,8},{8,4},{12,0},{1,13},{5,9},{9,5},{13,1},{2,14},{6,10},... | collective-permute-start | bytes 147464 | tf_op jit(solution)/shard_map/ppermute | solution.py:348
  22.9 15.2 %collective-permute-start.6 = (bf16[2,48,768]{2,1,0:T(8,128)(2,1)S(1)}, bf16[2,48,768]{2,1,0:T(8,128)(2,1)S(1)}, u32[]{:S(2)}, u32[]{:S(2)}) collective-permute-start(bf16[2,48,768]{2,1,0:T(8,128)(2,1)S(1)} %gate_up.4.refs_0_), channel_id=1, source_target_pairs={{0,3},{1,2},{2,1},{3,0},{4,7},{5,6},{6,5},{7,4},{8,11},{9,10},{10,... | collective-permute-start | bytes 442376 | tf_op jit(solution)/shard_map/ppermute | solution.py:348
  25.6 12.5 %collective-permute-start.7 = (bf16[2,48,768]{2,1,0:T(8,128)(2,1)S(1)}, bf16[2,48,768]{2,1,0:T(8,128)(2,1)S(1)}, u32[]{:S(2)}, u32[]{:S(2)}) collective-permute-start(bf16[2,48,768]{2,1,0:T(8,128)(2,1)S(1)} %gate_up.5.refs_0_), channel_id=1, source_target_pairs={{0,2},{1,3},{2,0},{3,1},{4,6},{5,7},{6,4},{7,5},{8,10},{9,11},{10,... | collective-permute-start | bytes 442376 | tf_op jit(solution)/shard_map/ppermute | solution.py:348
  25.7 6.7 %copy-start.5 = (bf16[8,8192]{1,0:T(8,128)(2,1)S(1)}, bf16[8,8192]{1,0:T(8,128)(2,1)}, u32[]{:S(2)}) copy-start(bf16[8,8192]{1,0:T(8,128)(2,1)} %param.9) | copy-start | bytes 393220
  25.7 6.7 %copy-start.6 = (bf16[8,1024]{1,0:T(8,128)(2,1)S(1)}, bf16[8,1024]{1,0:T(8,128)(2,1)}, u32[]{:S(2)}) copy-start(bf16[8,1024]{1,0:T(8,128)(2,1)} %param.10) | copy-start | bytes 49156
  28.2 10.9 %collective-permute-start.8 = (bf16[2,48,768]{2,1,0:T(8,128)(2,1)S(1)}, bf16[2,48,768]{2,1,0:T(8,128)(2,1)S(1)}, u32[]{:S(2)}, u32[]{:S(2)}) collective-permute-start(bf16[2,48,768]{2,1,0:T(8,128)(2,1)S(1)} %gate_up.6.refs_0_), channel_id=1, source_target_pairs={{0,1},{1,0},{2,3},{3,2},{4,5},{5,4},{6,7},{7,6},{8,9},{9,8},{10,11... | collective-permute-start | bytes 442376 | tf_op jit(solution)/shard_map/ppermute | solution.py:348
  32.4 2.9 %copy-start = (bf16[1,8,192,1024]{3,2,1,0:T(8,128)(2,1)S(1)}, bf16[1,8,192,1024]{3,2,1,0:T(8,128)(2,1)}, u32[]{:S(2)}) copy-start(bf16[1,8,192,1024]{3,2,1,0:T(8,128)(2,1)} %refs_3_.3) | copy-start | bytes 9437188
  32.5 2.9 %copy-start.2 = (s32[1,8]{1,0:T(1,128)S(1)}, s32[1,8]{1,0:T(1,128)}, u32[]{:S(2)}) copy-start(s32[1,8]{1,0:T(1,128)} %param.12) | copy-start | bytes 100
  32.5 11.2 %slice-start = ((s8[6291456]{0:T(1024)(128)(4,1)}), s8[4194304]{0:T(1024)(128)(4,1)S(1)}, s32[]{:S(2)}) async-start(s8[6291456]{0:T(1024)(128)(4,1)} %bitcast.21), calls=%async_computation | async-start | bytes 8388608
  35.3 8.3 %slice-start.1 = ((s8[6291456]{0:T(1024)(128)(4,1)}), s8[2097152]{0:T(1024)(128)(4,1)S(1)}, s32[]{:S(2)}) async-start(s8[6291456]{0:T(1024)(128)(4,1)} %bitcast.21), calls=%async_computation.1 | async-start | bytes 4194304
  39.2 7.6 %collective-permute-start.9 = (bf16[2,48,384]{2,1,0:T(8,128)(2,1)S(1)}, bf16[2,48,384]{2,1,0:T(8,128)(2,1)S(1)}, u32[]{:S(2)}, u32[]{:S(2)}) collective-permute-start(bf16[2,48,384]{2,1,0:T(8,128)(2,1)S(1)} %activate.1.part_ref), channel_id=1, source_target_pairs={{0,1},{1,0},{2,3},{3,2},{4,5},{5,4},{6,7},{7,6},{8,9},{9,8},{10,11... | collective-permute-start | bytes 221192 | tf_op jit(solution)/shard_map/ppermute | solution.py:348
  39.3 8.4 %collective-permute-start.10 = (bf16[2,48,384]{2,1,0:T(8,128)(2,1)S(1)}, bf16[2,48,384]{2,1,0:T(8,128)(2,1)S(1)}, u32[]{:S(2)}, u32[]{:S(2)}) collective-permute-start(bf16[2,48,384]{2,1,0:T(8,128)(2,1)S(1)} %activate.1.part_ref), channel_id=1, source_target_pairs={{0,2},{1,3},{2,0},{3,1},{4,6},{5,7},{6,4},{7,5},{8,10},{9,11},{10,... | collective-permute-start | bytes 221192 | tf_op jit(solution)/shard_map/ppermute | solution.py:348
  41.4 6.2 %collective-permute-start.11 = (bf16[2,48,384]{2,1,0:T(8,128)(2,1)S(1)}, bf16[2,48,384]{2,1,0:T(8,128)(2,1)S(1)}, u32[]{:S(2)}, u32[]{:S(2)}) collective-permute-start(bf16[2,48,384]{2,1,0:T(8,128)(2,1)S(1)} %activate.1.part_ref), channel_id=1, source_target_pairs={{0,3},{1,2},{2,1},{3,0},{4,7},{5,6},{6,5},{7,4},{8,11},{9,10},{10,... | collective-permute-start | bytes 221192 | tf_op jit(solution)/shard_map/ppermute | solution.py:348
  48.5 2.2 %collective-permute-start.12 = (bf16[24,1024]{1,0:T(8,128)(2,1)S(1)}, bf16[24,1024]{1,0:T(8,128)(2,1)S(1)}, u32[]{:S(2)}, u32[]{:S(2)}) collective-permute-start(bf16[24,1024]{1,0:T(8,128)(2,1)S(1)} %get-tuple-element.31), channel_id=1, source_target_pairs={{0,4},{4,0},{8,12},{12,8},{1,5},{5,1},{9,13},{13,9},{2,6},{6,2},{1... | collective-permute-start | bytes 147464 | tf_op jit(solution)/shard_map/ppermute | solution.py:348
  48.6 4.2 %collective-permute-start.13 = (bf16[24,1024]{1,0:T(8,128)(2,1)S(1)}, bf16[24,1024]{1,0:T(8,128)(2,1)S(1)}, u32[]{:S(2)}, u32[]{:S(2)}) collective-permute-start(bf16[24,1024]{1,0:T(8,128)(2,1)S(1)} %get-tuple-element.32), channel_id=1, source_target_pairs={{0,8},{4,12},{8,0},{12,4},{1,9},{5,13},{9,1},{13,5},{2,10},{6,14},... | collective-permute-start | bytes 147464 | tf_op jit(solution)/shard_map/ppermute | solution.py:348
  49.8 3.7 %collective-permute-start.14 = (bf16[24,1024]{1,0:T(8,128)(2,1)S(1)}, bf16[24,1024]{1,0:T(8,128)(2,1)S(1)}, u32[]{:S(2)}, u32[]{:S(2)}) collective-permute-start(bf16[24,1024]{1,0:T(8,128)(2,1)S(1)} %get-tuple-element.33), channel_id=1, source_target_pairs={{0,12},{4,8},{8,4},{12,0},{1,13},{5,9},{9,5},{13,1},{2,14},{6,10},... | collective-permute-start | bytes 147464 | tf_op jit(solution)/shard_map/ppermute | solution.py:348
  53.8 5.2 %collective-permute-start.15 = (bf16[8,1024]{1,0:T(8,128)(2,1)S(1)}, bf16[8,1024]{1,0:T(8,128)(2,1)S(1)}, u32[]{:S(2)}, u32[]{:S(2)}) collective-permute-start(bf16[8,1024]{1,0:T(8,128)(2,1)S(1)} %get-tuple-element.35), channel_id=1, source_target_pairs={{0,1},{1,0},{2,3},{3,2},{4,5},{5,4},{6,7},{7,6},{8,9},{9,8},{10,11... | collective-permute-start | bytes 49160 | tf_op jit(solution)/shard_map/ppermute | solution.py:348
  55.2 4.6 %collective-permute-start.16 = (bf16[8,1024]{1,0:T(8,128)(2,1)S(1)}, bf16[8,1024]{1,0:T(8,128)(2,1)S(1)}, u32[]{:S(2)}, u32[]{:S(2)}) collective-permute-start(bf16[8,1024]{1,0:T(8,128)(2,1)S(1)} %get-tuple-element.36), channel_id=1, source_target_pairs={{0,2},{1,3},{2,0},{3,1},{4,6},{5,7},{6,4},{7,5},{8,10},{9,11},{10,... | collective-permute-start | bytes 49160 | tf_op jit(solution)/shard_map/ppermute | solution.py:348
  56.6 5.5 %collective-permute-start.17 = (bf16[8,1024]{1,0:T(8,128)(2,1)S(1)}, bf16[8,1024]{1,0:T(8,128)(2,1)S(1)}, u32[]{:S(2)}, u32[]{:S(2)}) collective-permute-start(bf16[8,1024]{1,0:T(8,128)(2,1)S(1)} %get-tuple-element.37), channel_id=1, source_target_pairs={{0,3},{1,2},{2,1},{3,0},{4,7},{5,6},{6,5},{7,4},{8,11},{9,10},{10,... | collective-permute-start | bytes 49160 | tf_op jit(solution)/shard_map/ppermute | solution.py:348

commit v6 on v5

--- a/solution.py
+++ b/solution.py
@@ -160,8 +160,8 @@
     return jnp.where(ranks == rank.astype(jnp.float32), member, 0.0), expert
 
 
-def pack_kernel(top, experts, sources, column, level, *refs):
-    held, out_refs = refs[:sources], refs[sources:]
+def pack_kernel(top, experts, sources, afters, column, level, *refs):
+    held, out_refs = refs[:sources], refs[sources + afters:]
     width = out_refs[0].shape[1]
     rows = jnp.concatenate([ref[:, :width] for ref in held], axis=0)
     notes = jnp.concatenate([ref[:, width:] for ref in held], axis=0)
@@ -222,8 +222,8 @@
     return (other == wanted).astype(jnp.bfloat16)
 
 
-def select_kernel(*refs):
-    packs, out_ref = refs[:-1], refs[-1]
+def select_kernel(owners, *refs):
+    packs, out_ref = refs[:owners], refs[-1]
     experts, count, _ = out_ref.shape
     rows = jnp.concatenate([ref[...].astype(jnp.float32) for ref in packs], axis=0)
     moved = jnp.dot(
@@ -235,64 +235,70 @@
         out_ref[x] = moved[x * count:(x + 1) * count]
 
 
-def gate_up_kernel(pieces, afters, chunk, rows_ref, weight_hbm, *refs):
-    refs = refs[afters:]
-    out_ref, held, sems = refs[0], refs[-2], refs[-1]
-    experts, _, depth, ff = held.shape
+def load_kernel(expert, pieces, weight_hbm, after_ref, out_ref, done_ref, sems):
+    del after_ref
+    step = out_ref.shape[1] // pieces
+    copies = [
+        pltpu.make_async_copy(
+            weight_hbm.at[expert, k, pl.ds(n * step, step)],
+            out_ref.at[k, pl.ds(n * step, step)],
+            sems.at[k * pieces + n],
+        )
+        for k in range(2)
+        for n in range(pieces)
+    ]
+    for copy in copies:
+        copy.start()
+    done_ref[...] = jnp.zeros_like(done_ref)
+    for copy in copies:
+        copy.wait()
+
+
+def load(weight, expert, after, limit):
+    pieces = 2
+    return pl.pallas_call(
+        functools.partial(load_kernel, expert, pieces),
+        in_specs=[pl.BlockSpec(memory_space=pl.ANY)] * 2,
+        out_specs=[pl.BlockSpec(memory_space=pltpu.VMEM)] * 2,
+        out_shape=[
+            jax.ShapeDtypeStruct(weight.shape[1:], weight.dtype),
+            jax.ShapeDtypeStruct((8, LANES), jnp.float32),
+        ],
+        scratch_shapes=[pltpu.SemaphoreType.DMA((2 * pieces,))],
+        compiler_params=params(limit),
+        cost_estimate=pl.CostEstimate(flops=2 * 10**9, bytes_accessed=0, transcendentals=0),
+        name="load",
+    )(weight, after)
+
+
+def gate_up_kernel(experts, afters, chunk, rows_ref, *refs):
+    weight_refs, out_refs = refs[:experts], refs[experts + afters:]
+    out_ref = out_refs[0]
+    if len(out_refs) > 1:
+        out_refs[1][...] = jnp.zeros_like(out_refs[1])
+    ff = out_ref.shape[2] // 2
     columns = pl.ds(pl.multiple_of(chunk[0] * ff, ff), ff)
-    step = depth // pieces
-    copies = {}
     for x in range(experts):
         for k in range(2):
-            for n in range(pieces):
-                part = pl.ds(n * step, step)
-                copies[x, k, n] = pltpu.make_async_copy(
-                    weight_hbm.at[x, k, part, columns],
-                    held.at[x, k, part],
-                    sems.at[(x * 2 + k) * pieces + n],
-                )
-                copies[x, k, n].start()
-    if len(refs) > 3:
-        refs[1][...] = jnp.zeros_like(refs[1])
-    for x in range(experts):
-        for k in range(2):
-            total = 0.0
-            for n in range(pieces):
-                part = slice(n * step, (n + 1) * step)
-                copies[x, k, n].wait()
-                total = total + jnp.dot(
-                    rows_ref[x, :, part], held[x, k, part], preferred_element_type=jnp.float32
-                )
-            out_ref[x, :, k * ff:(k + 1) * ff] = total.astype(out_ref.dtype)
-
-
-def gate_up(chunk, chunks, rows, weight, dtype, done=False, after=()):
-    experts, count, depth = rows.shape
-    ff = weight.shape[3] // chunks
-    pieces = 2
-    return pl.pallas_call(
-        functools.partial(gate_up_kernel, pieces, len(after)),
-        in_specs=[
-            pl.BlockSpec(memory_space=pltpu.SMEM),
-            pl.BlockSpec(memory_space=pltpu.VMEM),
-            pl.BlockSpec(memory_space=pl.ANY),
-        ]
-        + [pl.BlockSpec(memory_space=pl.ANY)] * len(after),
-        out_specs=[pl.BlockSpec(memory_space=pltpu.VMEM)] * (1 + done),
-        out_shape=[jax.ShapeDtypeStruct((experts, count, 2 * ff), dtype)]
+            out_ref[x, :, k * ff:(k + 1) * ff] = jnp.dot(
+                rows_ref[x], weight_refs[x][k, :, columns], preferred_element_type=jnp.float32
+            ).astype(out_ref.dtype)
+
+
+def gate_up(chunk, chunks, rows, weights, dtype, done=False, after=()):
+    experts, count, _ = rows.shape
+    ff = weights[0].shape[2] // chunks
+    return call(
+        functools.partial(gate_up_kernel, experts, len(after)),
+        [chunk],
+        [rows, *weights],
+        [jax.ShapeDtypeStruct((experts, count, 2 * ff), dtype)]
         + [jax.ShapeDtypeStruct((8, LANES), jnp.float32)] * done,
-        scratch_shapes=[
-            pltpu.VMEM((experts, 2, depth, ff), weight.dtype),
-            pltpu.SemaphoreType.DMA((experts * 2 * pieces,)),
-        ],
-        compiler_params=params(52),
-        cost_estimate=pl.CostEstimate(
-            flops=4 * experts * count * depth * ff,
-            bytes_accessed=4 * experts * depth * ff,
-            transcendentals=0,
-        ),
-        name="gate_up",
-    )(chunk, rows, weight, *after)
+        "gate_up",
+        24,
+        after=after,
+        cost=2,
+    )
 
 
 def activate_kernel(own_ref, *refs):
@@ -368,13 +374,13 @@
         out_shape=outputs,
         compiler_params=params(limit),
         cost_estimate=pl.CostEstimate(
-            flops=cost * 10**9, bytes_accessed=cost * 3 * 10**6, transcendentals=0
+            flops=cost * 10**9, bytes_accessed=0, transcendentals=0
         ),
         name=name,
     )(*index, *inputs, *after)
 
 
-def experts_by_columns(held, gate_up_weight, down_weight, owners, attention):
+def experts_by_columns(held, loaded, down_weight, owners, attention):
     inner = lax.axis_size("inner")
     experts, count, _ = held.shape
     ff, width = down_weight.shape[1:]
@@ -383,10 +389,10 @@
     others, last = [], []
     for s in reversed(range(1, inner)):
         last = gate_up(
-            (me ^ s).reshape(1), inner, held, gate_up_weight, jnp.bfloat16, after=last
+            (me ^ s).reshape(1), inner, held, loaded, jnp.bfloat16, after=last
         )
         others.append(traded(last[0], "inner", s))
-    own, done = gate_up(level, inner, held, gate_up_weight, jnp.float32, True, last)
+    own, done = gate_up(level, inner, held, loaded, jnp.float32, True, last)
     first = attention(done, 0, 2)
     active = call(
         activate_kernel,
@@ -462,26 +468,31 @@
         [jax.ShapeDtypeStruct((rows, depth + LANES), jnp.bfloat16)] * inner,
         "prepare",
     )
+    even = ff % (inner * LANES) == 0
+    loaded = [load(gate_up_weight, 0, slices[0], 45)] if even else []
     slices = trade(slices, "inner")
     packs = call(
-        functools.partial(pack_kernel, top, experts, inner),
+        functools.partial(pack_kernel, top, experts, inner, len(loaded)),
         [column, level],
         slices,
         [jax.ShapeDtypeStruct((slots, depth), jnp.bfloat16)] * owners,
         "pack",
-    )
+        after=[done for _, done in loaded],
+    )
+    if even:
+        loaded += [load(gate_up_weight, x, packs[0], 40) for x in range(1, experts)]
     packs = trade(packs, "expert")
     held = call(
-        select_kernel,
+        functools.partial(select_kernel, owners),
         [],
         packs,
         jax.ShapeDtypeStruct((experts, owners * CAP * inner, depth), jnp.bfloat16),
         "select",
         24,
-    )
-    even = ff % (inner * LANES) == 0
+        after=[done for _, done in loaded[1:]],
+    )
     back, attended = (experts_by_columns if even else experts_by_rows)(
-        held, gate_up_weight, down_weight, owners, attention
+        held, [part for part, _ in loaded] or gate_up_weight, down_weight, owners, attention
     )
     back = trade(back, "expert")
     weights = call(

time: 62.9 us -> 61.8 us (0.983)
  local copies, waits for them, and re-layouts: 3.23 us -> 6 us
  waiting for transfers between devices: 16.3 us -> 13.9 us
  Pallas kernels: 19.4 us -> 17.8 us
    pallas_call x4 -> x2, Pallas kernels: 9.86 us -> 5.91 us  [load(): pl.pallas_call(functools.partial(load_kernel, expert, pieces), in_specs=[...]
    unnamed x21 -> x27, local copies, waits for them, and re-layouts: 3.23 us -> 6 us
    ppermute x18, waiting for transfers between devices: 16.3 us -> 13.9 us  [traded(): lax.ppermute(value, axis, [(i, i ^ index) for i in range(lax.axis_size(ax...]
    pallas_call x10 -> x14, Pallas kernels: 4.04 us -> 6.38 us  [call(): pl.pallas_call(kernel, in_specs=[pl.BlockSpec(memory_space=pltpu.SMEM)] *...]
  transfers between devices with their start and end apart: 18 -> 18, of which waited for: 10 -> 9; matrix products, arithmetic and copies ran while one was open for 1% -> 1% of each run, Pallas kernels for 22% -> 23%
where the time goes in v6:
time: 61.8 us; the launch traced here: 61.6 us
  starting transfers between devices  23 us (37%)
  Pallas kernels  17.8 us (29%)
  waiting for transfers between devices  13.9 us (22%)
  local copies, waits for them, and re-layouts  6 us (10%)
  between operations  0.9 us (1%)
    ppermute x18, starting transfers between devices, traded(): lax.ppermute(value, axis, [(i, i ^ index) for i in range(lax.axis_size(ax...  23 us
    ppermute x18, waiting for transfers between devices, traded(): lax.ppermute(value, axis, [(i, i ^ index) for i in range(lax.axis_size(ax...  13.9 us
    pallas_call x14, Pallas kernels, call(): pl.pallas_call(kernel, in_specs=[pl.BlockSpec(memory_space=pltpu.SMEM)] *...  6.38 us
    unnamed x27, local copies, waits for them, and re-layouts  6 us
    pallas_call x2, Pallas kernels, load(): pl.pallas_call(functools.partial(load_kernel, expert, pieces), in_specs=[...  5.91 us
    pallas_call x2, Pallas kernels, attend(): pl.pallas_call(functools.partial(attend_kernel, step), grid_spec=pltpu.Pr...  5.56 us
  transfers between devices with their start and end apart: 18, of which 9 were waited for; matrix products, arithmetic and copies ran while one was open for 1% of the time, Pallas kernels for 23%

profile of v6, /device:TPU:0, one launch (start us, length us, event | category | flops | bytes accessed | tf_op | source)
XLA Modules:
  0.0 61.6 jit_solution(8965380431185810399)
XLA Ops:
  0.6 0.8 %copy-done.2 = bf16[8,4096]{1,0:T(8,128)(2,1)S(1)} copy-done((bf16[8,4096]{1,0:T(8,128)(2,1)S(1)}, bf16[8,4096]{1,0:T(8,128)(2,1)}, u32[]{:S(2)}) %copy-start.2) | copy-done | bytes 65560
  1.5 0.7 %copy-done.4 = s32[8,2]{0,1:T(2,128)S(1)} copy-done((s32[8,2]{0,1:T(2,128)S(1)}, s32[8,2]{0,1:T(2,128)}, u32[]{:S(2)}) %copy-start.4) | copy-done | bytes 88
  2.2 0.7 %copy-done.5 = bf16[8,2]{0,1:T(2,128)(2,1)S(1)} copy-done((bf16[8,2]{0,1:T(2,128)(2,1)S(1)}, bf16[8,2]{0,1:T(2,128)(2,1)}, u32[]{:S(2)}) %copy-start.5) | copy-done | bytes 56
  2.8 0.2 prepare.1
  3.0 3.0 %collective-permute-start = (bf16[8,1152]{1,0:T(8,128)(2,1)S(1)}, bf16[8,1152]{1,0:T(8,128)(2,1)S(1)}, u32[]{:S(2)}, u32[]{:S(2)}) collective-permute-start(bf16[8,1152]{1,0:T(8,128)(2,1)S(1)} %get-tuple-element.25), channel_id=1, source_target_pairs={{0,1},{1,0},{2,3},{3,2},{4,5},{5,4},{6,7},{7,6},{8,9},{9,8},{10,11... | collective-permute-start | bytes 55304 | tf_op jit(solution)/shard_map/ppermute | solution.py:354
  6.0 2.6 %collective-permute-start.1 = (bf16[8,1152]{1,0:T(8,128)(2,1)S(1)}, bf16[8,1152]{1,0:T(8,128)(2,1)S(1)}, u32[]{:S(2)}, u32[]{:S(2)}) collective-permute-start(bf16[8,1152]{1,0:T(8,128)(2,1)S(1)} %get-tuple-element.26), channel_id=1, source_target_pairs={{0,2},{1,3},{2,0},{3,1},{4,6},{5,7},{6,4},{7,5},{8,10},{9,11},{10,... | collective-permute-start | bytes 55304 | tf_op jit(solution)/shard_map/ppermute | solution.py:354
  8.6 2.9 %load.2 = (bf16[2,1024,1536]{2,1,0:T(8,128)(2,1)S(1)}, f32[8,128]{1,0:T(8,128)S(1)}) custom-call(bf16[2,2,1024,1536]{3,2,1,0:T(8,128)(2,1)} %weight_hbm.3, bf16[8,1152]{1,0:T(8,128)(2,1)S(1)} %get-tuple-element.24.after_ref.refs_0_), custom_call_target="tpu_custom_call" | custom-call | flops 2000000000 | tf_op jit(solution)/shard_map/load/pallas_call | solution.py:259
  11.5 2.6 %copy-done.1 = bf16[2,1024,1536]{2,1,0:T(8,128)(2,1)} copy-done((bf16[2,1024,1536]{2,1,0:T(8,128)(2,1)}, bf16[2,1024,1536]{2,1,0:T(8,128)(2,1)S(1)}, u32[]{:S(2)}) %copy-start.1) | copy-done | bytes 6291480
  14.2 0.8 %pack.1 = (bf16[24,1024]{1,0:T(8,128)(2,1)S(1)}, bf16[24,1024]{1,0:T(8,128)(2,1)S(1)}, bf16[24,1024]{1,0:T(8,128)(2,1)S(1)}, bf16[24,1024]{1,0:T(8,128)(2,1)S(1)}) custom-call(s32[1]{0:T(128)} %bitcast.2.column, s32[1]{0:T(128)} %bitcast.1.me.level.chunk, bf16[8,1152]{1,0:T(8,128)(2,1)S(1)} %get-tuple-element.24.after_ref.refs_0_, ...), custom_call_target="tpu_custom_call" | custom-call | tf_op jit(solution)/shard_map/pack/pallas_call | solution.py:366
  15.1 0.1 collective-permute-start.3
  15.1 1.8 %collective-permute-start.4 = (bf16[24,1024]{1,0:T(8,128)(2,1)S(1)}, bf16[24,1024]{1,0:T(8,128)(2,1)S(1)}, u32[]{:S(2)}, u32[]{:S(2)}) collective-permute-start(bf16[24,1024]{1,0:T(8,128)(2,1)S(1)} %get-tuple-element.31), channel_id=1, source_target_pairs={{0,8},{4,12},{8,0},{12,4},{1,9},{5,13},{9,1},{13,5},{2,10},{6,14},... | collective-permute-start | bytes 147464 | tf_op jit(solution)/shard_map/ppermute | solution.py:354
  16.9 0.1 collective-permute-start.5
  17.0 3.0 %load.3 = (bf16[2,1024,1536]{2,1,0:T(8,128)(2,1)S(1)}, f32[8,128]{1,0:T(8,128)S(1)}) custom-call(bf16[2,2,1024,1536]{3,2,1,0:T(8,128)(2,1)} %weight_hbm.3, bf16[24,1024]{1,0:T(8,128)(2,1)S(1)} %get-tuple-element.29.after_ref.refs_0_), custom_call_target="tpu_custom_call" | custom-call | flops 2000000000 | tf_op jit(solution)/shard_map/load/pallas_call | solution.py:259
  20.0 0.6 collective-permute-done.5.refs_3_
  20.6 0.2 select.1.rows_ref
  20.8 0.6 gate_up.4.refs_2_
  21.4 3.7 %collective-permute-start.6 = (bf16[2,48,768]{2,1,0:T(8,128)(2,1)S(1)}, bf16[2,48,768]{2,1,0:T(8,128)(2,1)S(1)}, u32[]{:S(2)}, u32[]{:S(2)}) collective-permute-start(bf16[2,48,768]{2,1,0:T(8,128)(2,1)S(1)} %gate_up.4.refs_2_), channel_id=1, source_target_pairs={{0,3},{1,2},{2,1},{3,0},{4,7},{5,6},{6,5},{7,4},{8,11},{9,10},{10,... | collective-permute-start | bytes 442376 | tf_op jit(solution)/shard_map/ppermute | solution.py:354
  25.1 0.6 gate_up.5.refs_2_
  25.8 0.6 gate_up.6.refs_2_
  26.4 0.9 %collective-permute-start.8 = (bf16[2,48,768]{2,1,0:T(8,128)(2,1)S(1)}, bf16[2,48,768]{2,1,0:T(8,128)(2,1)S(1)}, u32[]{:S(2)}, u32[]{:S(2)}) collective-permute-start(bf16[2,48,768]{2,1,0:T(8,128)(2,1)S(1)} %gate_up.6.refs_2_), channel_id=1, source_target_pairs={{0,1},{1,0},{2,3},{3,2},{4,5},{5,4},{6,7},{7,6},{8,9},{9,8},{10,11... | collective-permute-start | bytes 442376 | tf_op jit(solution)/shard_map/ppermute | solution.py:354
  27.3 0.6 gate_up.7
  27.9 0.4 copy-done
  28.3 2.8 %attend.2.refs_3_ = bf16[4,64,128]{2,1,0:T(8,128)(2,1)S(1)} custom-call(s32[8]{0:T(128)S(1)} %bitcast.29, bf16[8,64,128]{2,1,0:T(8,128)(2,1)S(1)} %bitcast.25, bf16[8,8,128]{2,1,0:T(8,128)(2,1)S(1)} %bitcast.27, bf16[1,8,192,1024]{3,2,1,0:T(8,128)(2,1)S(1)} %copy-done, bf16[1,8,192,1024]{3,2,1,0:T(8,128)(2,1)S(1)} %copy-done, ...), custom_call_target="tpu_custom_call" | custom-call | flops 25165824 | bytes 1572864 | tf_op jit(solution)/shard_map/attend/pallas_call | solution.py:69
  31.0 3.9 %collective-permute-done.8.refs_2_ = bf16[2,48,768]{2,1,0:T(8,128)(2,1)S(1)} collective-permute-done((bf16[2,48,768]{2,1,0:T(8,128)(2,1)S(1)}, bf16[2,48,768]{2,1,0:T(8,128)(2,1)S(1)}, u32[]{:S(2)}, u32[]{:S(2)}) %collective-permute-start.8) | collective-permute-done | bytes 147488 | tf_op jit(solution)/shard_map/ppermute | solution.py:354
  34.9 2.1 %collective-permute-done.7.refs_1_ = bf16[2,48,768]{2,1,0:T(8,128)(2,1)S(1)} collective-permute-done((bf16[2,48,768]{2,1,0:T(8,128)(2,1)S(1)}, bf16[2,48,768]{2,1,0:T(8,128)(2,1)S(1)}, u32[]{:S(2)}, u32[]{:S(2)}) %collective-permute-start.7) | collective-permute-done | bytes 147488 | tf_op jit(solution)/shard_map/ppermute | solution.py:354
  37.0 0.1 activate.1.part_ref
  37.1 0.5 collective-permute-start.9
  37.6 2.6 %collective-permute-start.10 = (bf16[2,48,384]{2,1,0:T(8,128)(2,1)S(1)}, bf16[2,48,384]{2,1,0:T(8,128)(2,1)S(1)}, u32[]{:S(2)}, u32[]{:S(2)}) collective-permute-start(bf16[2,48,384]{2,1,0:T(8,128)(2,1)S(1)} %activate.1.part_ref), channel_id=1, source_target_pairs={{0,2},{1,3},{2,0},{3,1},{4,6},{5,7},{6,4},{7,5},{8,10},{9,11},{10,... | collective-permute-start | bytes 221192 | tf_op jit(solution)/shard_map/ppermute | solution.py:354
  40.2 1.3 %collective-permute-start.11 = (bf16[2,48,384]{2,1,0:T(8,128)(2,1)S(1)}, bf16[2,48,384]{2,1,0:T(8,128)(2,1)S(1)}, u32[]{:S(2)}, u32[]{:S(2)}) collective-permute-start(bf16[2,48,384]{2,1,0:T(8,128)(2,1)S(1)} %activate.1.part_ref), channel_id=1, source_target_pairs={{0,3},{1,2},{2,1},{3,0},{4,7},{5,6},{6,5},{7,4},{8,11},{9,10},{10,... | collective-permute-start | bytes 221192 | tf_op jit(solution)/shard_map/ppermute | solution.py:354
  41.6 0.4 down_first.1.refs_4_.before_ref
  42.0 2.8 %attend.3.refs_3_ = bf16[4,64,128]{2,1,0:T(8,128)(2,1)S(1)} custom-call(s32[8]{0:T(128)S(1)} %bitcast.30, bf16[8,64,128]{2,1,0:T(8,128)(2,1)S(1)} %bitcast.26, bf16[8,8,128]{2,1,0:T(8,128)(2,1)S(1)} %bitcast.28, bf16[1,8,192,1024]{3,2,1,0:T(8,128)(2,1)S(1)} %copy-done, bf16[1,8,192,1024]{3,2,1,0:T(8,128)(2,1)S(1)} %copy-done, ...), custom_call_target="tpu_custom_call" | custom-call | flops 25165824 | bytes 1572864 | tf_op jit(solution)/shard_map/attend/pallas_call | solution.py:69
  44.8 0.4 down_more.1.sum_ref
  45.2 0.3 collective-permute-done.10.refs_0_
  45.4 1.1 %collective-permute-done.11.refs_1_ = bf16[2,48,384]{2,1,0:T(8,128)(2,1)S(1)} collective-permute-done((bf16[2,48,384]{2,1,0:T(8,128)(2,1)S(1)}, bf16[2,48,384]{2,1,0:T(8,128)(2,1)S(1)}, u32[]{:S(2)}, u32[]{:S(2)}) %collective-permute-start.11) | collective-permute-done | bytes 73760 | tf_op jit(solution)/shard_map/ppermute | solution.py:354
  46.5 0.8 %down_rest.1 = (bf16[24,1024]{1,0:T(8,128)(2,1)S(1)}, bf16[24,1024]{1,0:T(8,128)(2,1)S(1)}, bf16[24,1024]{1,0:T(8,128)(2,1)S(1)}, bf16[24,1024]{1,0:T(8,128)(2,1)S(1)}) custom-call(s32[1]{0:T(128)} %bitcast.1.me.level.chunk, f32[2,48,1024]{2,1,0:T(8,128)S(1)} %down_more.1.sum_ref, bf16[2,48,384]{2,1,0:T(8,128)(2,1)S(1)} %collective-permute-done.10.refs_0_, ...), custom_call_target="tpu_custom_call" | custom-call | tf_op jit(solution)/shard_map/down_rest/pallas_call | solution.py:366
  47.4 1.6 %collective-permute-start.13 = (bf16[24,1024]{1,0:T(8,128)(2,1)S(1)}, bf16[24,1024]{1,0:T(8,128)(2,1)S(1)}, u32[]{:S(2)}, u32[]{:S(2)}) collective-permute-start(bf16[24,1024]{1,0:T(8,128)(2,1)S(1)} %get-tuple-element.40), channel_id=1, source_target_pairs={{0,8},{4,12},{8,0},{12,4},{1,9},{5,13},{9,1},{13,5},{2,10},{6,14},... | collective-permute-start | bytes 147464 | tf_op jit(solution)/shard_map/ppermute | solution.py:354
  49.0 0.3 collective-permute-start.14
  49.3 0.3 weigh.1.weight_ref
  49.5 2.0 %collective-permute-done.13.refs_2_ = bf16[24,1024]{1,0:T(8,128)(2,1)S(1)} collective-permute-done((bf16[24,1024]{1,0:T(8,128)(2,1)S(1)}, bf16[24,1024]{1,0:T(8,128)(2,1)S(1)}, u32[]{:S(2)}, u32[]{:S(2)}) %collective-permute-start.13) | collective-permute-done | bytes 49184 | tf_op jit(solution)/shard_map/ppermute | solution.py:354
  51.6 1.1 %collective-permute-done.14.refs_3_ = bf16[24,1024]{1,0:T(8,128)(2,1)S(1)} collective-permute-done((bf16[24,1024]{1,0:T(8,128)(2,1)S(1)}, bf16[24,1024]{1,0:T(8,128)(2,1)S(1)}, u32[]{:S(2)}, u32[]{:S(2)}) %collective-permute-start.14) | collective-permute-done | bytes 49184 | tf_op jit(solution)/shard_map/ppermute | solution.py:354
  52.7 0.2 combine.1
  52.9 1.2 %collective-permute-start.15 = (bf16[8,1024]{1,0:T(8,128)(2,1)S(1)}, bf16[8,1024]{1,0:T(8,128)(2,1)S(1)}, u32[]{:S(2)}, u32[]{:S(2)}) collective-permute-start(bf16[8,1024]{1,0:T(8,128)(2,1)S(1)} %get-tuple-element.43), channel_id=1, source_target_pairs={{0,1},{1,0},{2,3},{3,2},{4,5},{5,4},{6,7},{7,6},{8,9},{9,8},{10,11... | collective-permute-start | bytes 49160 | tf_op jit(solution)/shard_map/ppermute | solution.py:354
  54.1 1.3 %collective-permute-start.16 = (bf16[8,1024]{1,0:T(8,128)(2,1)S(1)}, bf16[8,1024]{1,0:T(8,128)(2,1)S(1)}, u32[]{:S(2)}, u32[]{:S(2)}) collective-permute-start(bf16[8,1024]{1,0:T(8,128)(2,1)S(1)} %get-tuple-element.44), channel_id=1, source_target_pairs={{0,2},{1,3},{2,0},{3,1},{4,6},{5,7},{6,4},{7,5},{8,10},{9,11},{10,... | collective-permute-start | bytes 49160 | tf_op jit(solution)/shard_map/ppermute | solution.py:354
  55.4 1.9 %collective-permute-start.17 = (bf16[8,1024]{1,0:T(8,128)(2,1)S(1)}, bf16[8,1024]{1,0:T(8,128)(2,1)S(1)}, u32[]{:S(2)}, u32[]{:S(2)}) collective-permute-start(bf16[8,1024]{1,0:T(8,128)(2,1)S(1)} %get-tuple-element.45), channel_id=1, source_target_pairs={{0,3},{1,2},{2,1},{3,0},{4,7},{5,6},{6,5},{7,4},{8,11},{9,10},{10,... | collective-permute-start | bytes 49160 | tf_op jit(solution)/shard_map/ppermute | solution.py:354
  57.4 0.7 %copy.17 = bf16[1,8,64,128]{3,1,2,0:T(8,128)(2,1)} copy(bf16[1,8,64,128]{3,2,1,0:T(8,128)(2,1)S(1)} %maximum_bitcast_fusion) | data formatting | bytes 262144
  58.1 0.7 %collective-permute-done.16.refs_2_ = bf16[8,1024]{1,0:T(8,128)(2,1)S(1)} collective-permute-done((bf16[8,1024]{1,0:T(8,128)(2,1)S(1)}, bf16[8,1024]{1,0:T(8,128)(2,1)S(1)}, u32[]{:S(2)}, u32[]{:S(2)}) %collective-permute-start.16) | collective-permute-done | bytes 16416 | tf_op jit(solution)/shard_map/ppermute | solution.py:354
  58.8 2.2 %collective-permute-done.17.refs_3_ = bf16[8,1024]{1,0:T(8,128)(2,1)S(1)} collective-permute-done((bf16[8,1024]{1,0:T(8,128)(2,1)S(1)}, bf16[8,1024]{1,0:T(8,128)(2,1)S(1)}, u32[]{:S(2)}, u32[]{:S(2)}) %collective-permute-start.17) | collective-permute-done | bytes 16416 | tf_op jit(solution)/shard_map/ppermute | solution.py:354
  61.0 0.6 %assemble.1 = bf16[8,4096]{1,0:T(8,128)(2,1)} custom-call(s32[1]{0:T(128)} %bitcast.1.me.level.chunk, bf16[8,1024]{1,0:T(8,128)(2,1)S(1)} %get-tuple-element.42.refs_0_, bf16[8,1024]{1,0:T(8,128)(2,1)S(1)} %collective-permute-done.15.refs_1_, bf16[8,1024]{1,0:T(8,128)(2,1)S(1)} %collective-permute-done.16.refs_2_, ...), custom_call_target="tpu_custom_call" | custom-call | tf_op jit(solution)/shard_map/assemble/pallas_call | solution.py:366
  (36 shorter events, 0.2 us)
Async XLA Ops:
  0.6 0.8 %copy-start.2 = (bf16[8,4096]{1,0:T(8,128)(2,1)S(1)}, bf16[8,4096]{1,0:T(8,128)(2,1)}, u32[]{:S(2)}) copy-start(bf16[8,4096]{1,0:T(8,128)(2,1)} %hidden_ref.1) | copy-start | bytes 196612
  1.5 0.7 %copy-start.4 = (s32[8,2]{0,1:T(2,128)S(1)}, s32[8,2]{0,1:T(2,128)}, u32[]{:S(2)}) copy-start(s32[8,2]{0,1:T(2,128)} %param.14) | copy-start | bytes 196
  2.2 0.7 %copy-start.5 = (bf16[8,2]{0,1:T(2,128)(2,1)S(1)}, bf16[8,2]{0,1:T(2,128)(2,1)}, u32[]{:S(2)}) copy-start(bf16[8,2]{0,1:T(2,128)(2,1)} %param.15) | copy-start | bytes 100
  3.0 11.2 %collective-permute-start = (bf16[8,1152]{1,0:T(8,128)(2,1)S(1)}, bf16[8,1152]{1,0:T(8,128)(2,1)S(1)}, u32[]{:S(2)}, u32[]{:S(2)}) collective-permute-start(bf16[8,1152]{1,0:T(8,128)(2,1)S(1)} %get-tuple-element.25), channel_id=1, source_target_pairs={{0,1},{1,0},{2,3},{3,2},{4,5},{5,4},{6,7},{7,6},{8,9},{9,8},{10,11... | collective-permute-start | bytes 55304 | tf_op jit(solution)/shard_map/ppermute | solution.py:354
  6.0 8.2 %collective-permute-start.1 = (bf16[8,1152]{1,0:T(8,128)(2,1)S(1)}, bf16[8,1152]{1,0:T(8,128)(2,1)S(1)}, u32[]{:S(2)}, u32[]{:S(2)}) collective-permute-start(bf16[8,1152]{1,0:T(8,128)(2,1)S(1)} %get-tuple-element.26), channel_id=1, source_target_pairs={{0,2},{1,3},{2,0},{3,1},{4,6},{5,7},{6,4},{7,5},{8,10},{9,11},{10,... | collective-permute-start | bytes 55304 | tf_op jit(solution)/shard_map/ppermute | solution.py:354
  8.6 5.6 %collective-permute-start.2 = (bf16[8,1152]{1,0:T(8,128)(2,1)S(1)}, bf16[8,1152]{1,0:T(8,128)(2,1)S(1)}, u32[]{:S(2)}, u32[]{:S(2)}) collective-permute-start(bf16[8,1152]{1,0:T(8,128)(2,1)S(1)} %get-tuple-element.27), channel_id=1, source_target_pairs={{0,3},{1,2},{2,1},{3,0},{4,7},{5,6},{6,5},{7,4},{8,11},{9,10},{10,... | collective-permute-start | bytes 55304 | tf_op jit(solution)/shard_map/ppermute | solution.py:354
  8.6 5.6 %copy-start.6 = (bf16[8,8192]{1,0:T(8,128)(2,1)S(1)}, bf16[8,8192]{1,0:T(8,128)(2,1)}, u32[]{:S(2)}) copy-start(bf16[8,8192]{1,0:T(8,128)(2,1)} %param.9) | copy-start | bytes 393220
  8.6 5.6 %copy-start.7 = (bf16[8,1024]{1,0:T(8,128)(2,1)S(1)}, bf16[8,1024]{1,0:T(8,128)(2,1)}, u32[]{:S(2)}) copy-start(bf16[8,1024]{1,0:T(8,128)(2,1)} %param.10) | copy-start | bytes 49156
  11.5 2.6 %copy-start.1 = (bf16[2,1024,1536]{2,1,0:T(8,128)(2,1)}, bf16[2,1024,1536]{2,1,0:T(8,128)(2,1)S(1)}, u32[]{:S(2)}) copy-start(bf16[2,1024,1536]{2,1,0:T(8,128)(2,1)S(1)} %get-tuple-element.34.refs_0_) | copy-start | bytes 18874372
  14.2 6.6 %slice-start = ((s8[6291456]{0:T(1024)(128)(4,1)}), s8[4194304]{0:T(1024)(128)(4,1)S(1)}, s32[]{:S(2)}) async-start(s8[6291456]{0:T(1024)(128)(4,1)} %bitcast.21), calls=%async_computation | async-start | bytes 8388608
  15.1 5.0 %collective-permute-start.3 = (bf16[24,1024]{1,0:T(8,128)(2,1)S(1)}, bf16[24,1024]{1,0:T(8,128)(2,1)S(1)}, u32[]{:S(2)}, u32[]{:S(2)}) collective-permute-start(bf16[24,1024]{1,0:T(8,128)(2,1)S(1)} %get-tuple-element.30), channel_id=1, source_target_pairs={{0,4},{4,0},{8,12},{12,8},{1,5},{5,1},{9,13},{13,9},{2,6},{6,2},{1... | collective-permute-start | bytes 147464 | tf_op jit(solution)/shard_map/ppermute | solution.py:354
  15.1 4.9 %collective-permute-start.4 = (bf16[24,1024]{1,0:T(8,128)(2,1)S(1)}, bf16[24,1024]{1,0:T(8,128)(2,1)S(1)}, u32[]{:S(2)}, u32[]{:S(2)}) collective-permute-start(bf16[24,1024]{1,0:T(8,128)(2,1)S(1)} %get-tuple-element.31), channel_id=1, source_target_pairs={{0,8},{4,12},{8,0},{12,4},{1,9},{5,13},{9,1},{13,5},{2,10},{6,14},... | collective-permute-start | bytes 147464 | tf_op jit(solution)/shard_map/ppermute | solution.py:354
  16.9 3.7 %collective-permute-start.5 = (bf16[24,1024]{1,0:T(8,128)(2,1)S(1)}, bf16[24,1024]{1,0:T(8,128)(2,1)S(1)}, u32[]{:S(2)}, u32[]{:S(2)}) collective-permute-start(bf16[24,1024]{1,0:T(8,128)(2,1)S(1)} %get-tuple-element.32), channel_id=1, source_target_pairs={{0,12},{4,8},{8,4},{12,0},{1,13},{5,9},{9,5},{13,1},{2,14},{6,10},... | collective-permute-start | bytes 147464 | tf_op jit(solution)/shard_map/ppermute | solution.py:354
  17.0 3.8 %slice-start.1 = ((s8[6291456]{0:T(1024)(128)(4,1)}), s8[2097152]{0:T(1024)(128)(4,1)S(1)}, s32[]{:S(2)}) async-start(s8[6291456]{0:T(1024)(128)(4,1)} %bitcast.21), calls=%async_computation.1 | async-start | bytes 4194304
  21.4 15.6 %collective-permute-start.6 = (bf16[2,48,768]{2,1,0:T(8,128)(2,1)S(1)}, bf16[2,48,768]{2,1,0:T(8,128)(2,1)S(1)}, u32[]{:S(2)}, u32[]{:S(2)}) collective-permute-start(bf16[2,48,768]{2,1,0:T(8,128)(2,1)S(1)} %gate_up.4.refs_2_), channel_id=1, source_target_pairs={{0,3},{1,2},{2,1},{3,0},{4,7},{5,6},{6,5},{7,4},{8,11},{9,10},{10,... | collective-permute-start | bytes 442376 | tf_op jit(solution)/shard_map/ppermute | solution.py:354
  25.7 11.3 %collective-permute-start.7 = (bf16[2,48,768]{2,1,0:T(8,128)(2,1)S(1)}, bf16[2,48,768]{2,1,0:T(8,128)(2,1)S(1)}, u32[]{:S(2)}, u32[]{:S(2)}) collective-permute-start(bf16[2,48,768]{2,1,0:T(8,128)(2,1)S(1)} %gate_up.5.refs_2_), channel_id=1, source_target_pairs={{0,2},{1,3},{2,0},{3,1},{4,6},{5,7},{6,4},{7,5},{8,10},{9,11},{10,... | collective-permute-start | bytes 442376 | tf_op jit(solution)/shard_map/ppermute | solution.py:354
  26.4 1.9 %copy-start = (bf16[1,8,192,1024]{3,2,1,0:T(8,128)(2,1)S(1)}, bf16[1,8,192,1024]{3,2,1,0:T(8,128)(2,1)}, u32[]{:S(2)}) copy-start(bf16[1,8,192,1024]{3,2,1,0:T(8,128)(2,1)} %refs_3_.3) | copy-start | bytes 9437188
  26.4 1.9 %copy-start.3 = (s32[1,8]{1,0:T(1,128)S(1)}, s32[1,8]{1,0:T(1,128)}, u32[]{:S(2)}) copy-start(s32[1,8]{1,0:T(1,128)} %param.12) | copy-start | bytes 100
  26.4 8.6 %collective-permute-start.8 = (bf16[2,48,768]{2,1,0:T(8,128)(2,1)S(1)}, bf16[2,48,768]{2,1,0:T(8,128)(2,1)S(1)}, u32[]{:S(2)}, u32[]{:S(2)}) collective-permute-start(bf16[2,48,768]{2,1,0:T(8,128)(2,1)S(1)} %gate_up.6.refs_2_), channel_id=1, source_target_pairs={{0,1},{1,0},{2,3},{3,2},{4,5},{5,4},{6,7},{7,6},{8,9},{9,8},{10,11... | collective-permute-start | bytes 442376 | tf_op jit(solution)/shard_map/ppermute | solution.py:354
  27.2 14.3 %slice-start.2 = ((s8[6291456]{0:T(1024)(128)(4,1)}), s8[2097152]{0:T(1024)(128)(4,1)S(1)}, s32[]{:S(2)}) async-start(s8[6291456]{0:T(1024)(128)(4,1)} %bitcast.23), calls=%async_computation.2 | async-start | bytes 4194304
  28.3 13.3 %slice-start.3 = ((s8[6291456]{0:T(1024)(128)(4,1)}), s8[4194304]{0:T(1024)(128)(4,1)S(1)}, s32[]{:S(2)}) async-start(s8[6291456]{0:T(1024)(128)(4,1)} %bitcast.23), calls=%async_computation.3 | async-start | bytes 8388608
  37.1 7.6 %collective-permute-start.9 = (bf16[2,48,384]{2,1,0:T(8,128)(2,1)S(1)}, bf16[2,48,384]{2,1,0:T(8,128)(2,1)S(1)}, u32[]{:S(2)}, u32[]{:S(2)}) collective-permute-start(bf16[2,48,384]{2,1,0:T(8,128)(2,1)S(1)} %activate.1.part_ref), channel_id=1, source_target_pairs={{0,1},{1,0},{2,3},{3,2},{4,5},{5,4},{6,7},{7,6},{8,9},{9,8},{10,11... | collective-permute-start | bytes 221192 | tf_op jit(solution)/shard_map/ppermute | solution.py:354
  37.6 7.8 %collective-permute-start.10 = (bf16[2,48,384]{2,1,0:T(8,128)(2,1)S(1)}, bf16[2,48,384]{2,1,0:T(8,128)(2,1)S(1)}, u32[]{:S(2)}, u32[]{:S(2)}) collective-permute-start(bf16[2,48,384]{2,1,0:T(8,128)(2,1)S(1)} %activate.1.part_ref), channel_id=1, source_target_pairs={{0,2},{1,3},{2,0},{3,1},{4,6},{5,7},{6,4},{7,5},{8,10},{9,11},{10,... | collective-permute-start | bytes 221192 | tf_op jit(solution)/shard_map/ppermute | solution.py:354
  40.2 6.3 %collective-permute-start.11 = (bf16[2,48,384]{2,1,0:T(8,128)(2,1)S(1)}, bf16[2,48,384]{2,1,0:T(8,128)(2,1)S(1)}, u32[]{:S(2)}, u32[]{:S(2)}) collective-permute-start(bf16[2,48,384]{2,1,0:T(8,128)(2,1)S(1)} %activate.1.part_ref), channel_id=1, source_target_pairs={{0,3},{1,2},{2,1},{3,0},{4,7},{5,6},{6,5},{7,4},{8,11},{9,10},{10,... | collective-permute-start | bytes 221192 | tf_op jit(solution)/shard_map/ppermute | solution.py:354
  47.3 2.2 %collective-permute-start.12 = (bf16[24,1024]{1,0:T(8,128)(2,1)S(1)}, bf16[24,1024]{1,0:T(8,128)(2,1)S(1)}, u32[]{:S(2)}, u32[]{:S(2)}) collective-permute-start(bf16[24,1024]{1,0:T(8,128)(2,1)S(1)} %get-tuple-element.39), channel_id=1, source_target_pairs={{0,4},{4,0},{8,12},{12,8},{1,5},{5,1},{9,13},{13,9},{2,6},{6,2},{1... | collective-permute-start | bytes 147464 | tf_op jit(solution)/shard_map/ppermute | solution.py:354
  47.4 4.2 %collective-permute-start.13 = (bf16[24,1024]{1,0:T(8,128)(2,1)S(1)}, bf16[24,1024]{1,0:T(8,128)(2,1)S(1)}, u32[]{:S(2)}, u32[]{:S(2)}) collective-permute-start(bf16[24,1024]{1,0:T(8,128)(2,1)S(1)} %get-tuple-element.40), channel_id=1, source_target_pairs={{0,8},{4,12},{8,0},{12,4},{1,9},{5,13},{9,1},{13,5},{2,10},{6,14},... | collective-permute-start | bytes 147464 | tf_op jit(solution)/shard_map/ppermute | solution.py:354
  49.0 3.7 %collective-permute-start.14 = (bf16[24,1024]{1,0:T(8,128)(2,1)S(1)}, bf16[24,1024]{1,0:T(8,128)(2,1)S(1)}, u32[]{:S(2)}, u32[]{:S(2)}) collective-permute-start(bf16[24,1024]{1,0:T(8,128)(2,1)S(1)} %get-tuple-element.41), channel_id=1, source_target_pairs={{0,12},{4,8},{8,4},{12,0},{1,13},{5,9},{9,5},{13,1},{2,14},{6,10},... | collective-permute-start | bytes 147464 | tf_op jit(solution)/shard_map/ppermute | solution.py:354
  52.9 5.2 %collective-permute-start.15 = (bf16[8,1024]{1,0:T(8,128)(2,1)S(1)}, bf16[8,1024]{1,0:T(8,128)(2,1)S(1)}, u32[]{:S(2)}, u32[]{:S(2)}) collective-permute-start(bf16[8,1024]{1,0:T(8,128)(2,1)S(1)} %get-tuple-element.43), channel_id=1, source_target_pairs={{0,1},{1,0},{2,3},{3,2},{4,5},{5,4},{6,7},{7,6},{8,9},{9,8},{10,11... | collective-permute-start | bytes 49160 | tf_op jit(solution)/shard_map/ppermute | solution.py:354
  54.1 4.7 %collective-permute-start.16 = (bf16[8,1024]{1,0:T(8,128)(2,1)S(1)}, bf16[8,1024]{1,0:T(8,128)(2,1)S(1)}, u32[]{:S(2)}, u32[]{:S(2)}) collective-permute-start(bf16[8,1024]{1,0:T(8,128)(2,1)S(1)} %get-tuple-element.44), channel_id=1, source_target_pairs={{0,2},{1,3},{2,0},{3,1},{4,6},{5,7},{6,4},{7,5},{8,10},{9,11},{10,... | collective-permute-start | bytes 49160 | tf_op jit(solution)/shard_map/ppermute | solution.py:354
  55.4 5.5 %collective-permute-start.17 = (bf16[8,1024]{1,0:T(8,128)(2,1)S(1)}, bf16[8,1024]{1,0:T(8,128)(2,1)S(1)}, u32[]{:S(2)}, u32[]{:S(2)}) collective-permute-start(bf16[8,1024]{1,0:T(8,128)(2,1)S(1)} %get-tuple-element.45), channel_id=1, source_target_pairs={{0,3},{1,2},{2,1},{3,0},{4,7},{5,6},{6,5},{7,4},{8,11},{9,10},{10,... | collective-permute-start | bytes 49160 | tf_op jit(solution)/shard_map/ppermute | solution.py:354

commit v7 on v6

--- a/solution.py
+++ b/solution.py
@@ -57,14 +57,13 @@
             out_ref[b, rows] = result.astype(out_ref.dtype)
 
 
-def attend(queries, new_key_value, cached_key_value, parents, after, part, parts):
-    rows = queries.shape[0] // parts
-    first = part * rows
+def attend(queries, new_key_value, cached_key_value, parents, after):
+    rows = queries.shape[0]
     _, beams, length, width = cached_key_value.shape
     step = 4
 
     def parent_of(b):
-        return lambda r, p: ((first + r * step + b) // beams, p[first + r * step + b], 0, 0)
+        return lambda r, p: ((r * step + b) // beams, p[r * step + b], 0, 0)
 
     out = pl.pallas_call(
         functools.partial(attend_kernel, step),
@@ -72,12 +71,8 @@
             num_scalar_prefetch=1,
             grid=(rows // step,),
             in_specs=[
-                pl.BlockSpec(
-                    (step, QUERY_HEADS, HEAD_SIZE), lambda r, p: (first // step + r, 0, 0)
-                ),
-                pl.BlockSpec(
-                    (step, 2 * KEY_HEADS, HEAD_SIZE), lambda r, p: (first // step + r, 0, 0)
-                ),
+                pl.BlockSpec((step, QUERY_HEADS, HEAD_SIZE), lambda r, p: (r, 0, 0)),
+                pl.BlockSpec((step, 2 * KEY_HEADS, HEAD_SIZE), lambda r, p: (r, 0, 0)),
             ]
             + [pl.BlockSpec((1, 1, length, width), parent_of(b)) for b in range(step)]
             + [pl.BlockSpec(memory_space=pl.ANY)],
@@ -135,19 +130,19 @@
     return turned[:top], turned[top:2 * top]
 
 
-def placing(routes, owner, level, experts, sources):
+def placing(routes, column, level, owners, experts, sources):
     top, rows = routes.shape
     count = CAP * sources
-    shape = (experts * count, rows)
+    shape = (owners * experts * count, rows)
     slot = lax.broadcasted_iota(jnp.int32, shape, 0)
     row = lax.broadcasted_iota(jnp.int32, shape, 1)
     each = rows // sources
-    local = jnp.zeros(shape, jnp.int32)
-    for x in range(1, experts):
-        local = local + (slot >= x * count).astype(jnp.int32)
-    within = slot - local * count
+    block = jnp.zeros(shape, jnp.int32)
+    for n in range(1, owners * experts):
+        block = block + (slot >= n * count).astype(jnp.int32)
+    within = slot - block * count
     rank, source = within // sources, within % sources
-    expert = (owner * experts + local).astype(jnp.float32)
+    expert = ((column ^ (block // experts)) * experts + block % experts).astype(jnp.float32)
     member = jnp.zeros(shape, jnp.float32)
     for t in range(top):
         member = jnp.where(routes[t:t + 1] == expert, 1.0, member)
@@ -162,27 +157,28 @@
 
 def pack_kernel(top, experts, sources, afters, column, level, *refs):
     held, out_refs = refs[:sources], refs[sources + afters:]
-    width = out_refs[0].shape[1]
+    slots, width = out_refs[0].shape
     rows = jnp.concatenate([ref[:, :width] for ref in held], axis=0)
     notes = jnp.concatenate([ref[:, width:] for ref in held], axis=0)
     routes, _ = turned_notes(notes, top)
+    place, _ = placing(routes, column[0], level[0], len(out_refs), experts, sources)
+    moved = jnp.dot(place.astype(jnp.bfloat16), rows, preferred_element_type=jnp.float32)
     for t, out_ref in enumerate(out_refs):
-        place, _ = placing(routes, column[0] ^ t, level[0], experts, sources)
-        out_ref[...] = jnp.dot(
-            place.astype(jnp.bfloat16), rows, preferred_element_type=jnp.float32
-        ).astype(out_ref.dtype)
+        out_ref[...] = moved[t * slots:(t + 1) * slots].astype(out_ref.dtype)
 
 
 def weigh_kernel(top, experts, column, level, *refs):
     held, out_ref = refs[:-1], refs[-1]
+    owners, slots, _ = out_ref.shape
     notes = jnp.concatenate([ref[:, -LANES:] for ref in held], axis=0)
     routes, gates = turned_notes(notes, top)
-    for t in range(out_ref.shape[0]):
-        place, expert = placing(routes, column[0] ^ t, level[0], experts, len(held))
-        weight = jnp.zeros_like(place)
-        for k in range(top):
-            weight = weight + jnp.where(routes[k:k + 1] == expert, gates[k:k + 1], 0.0)
-        out_ref[t] = (weight * place).astype(out_ref.dtype)
+    place, expert = placing(routes, column[0], level[0], owners, experts, len(held))
+    weight = jnp.zeros_like(place)
+    for k in range(top):
+        weight = weight + jnp.where(routes[k:k + 1] == expert, gates[k:k + 1], 0.0)
+    weight = weight * place
+    for t in range(owners):
+        out_ref[t] = weight[t * slots:(t + 1) * slots].astype(out_ref.dtype)
 
 
 def combine_kernel(weight_ref, *refs):
@@ -255,7 +251,7 @@
 
 
 def load(weight, expert, after, limit):
-    pieces = 2
+    pieces = 8
     return pl.pallas_call(
         functools.partial(load_kernel, expert, pieces),
         in_specs=[pl.BlockSpec(memory_space=pl.ANY)] * 2,
@@ -266,7 +262,7 @@
         ],
         scratch_shapes=[pltpu.SemaphoreType.DMA((2 * pieces,))],
         compiler_params=params(limit),
-        cost_estimate=pl.CostEstimate(flops=2 * 10**9, bytes_accessed=0, transcendentals=0),
+        cost_estimate=pl.CostEstimate(flops=10**8, bytes_accessed=0, transcendentals=0),
         name="load",
     )(weight, after)
 
@@ -330,7 +326,7 @@
 
 def down_rest_kernel(indices, me, sum_ref, *refs):
     count = len(indices)
-    parts, weight_ref, out_refs = refs[:count], refs[count], refs[count + 2:]
+    parts, weight_ref, out_refs = refs[:count], refs[count], refs[count + 1:]
     experts, slots, _ = sum_ref.shape
     sums = []
     for x in range(experts):
@@ -393,19 +389,18 @@
         )
         others.append(traded(last[0], "inner", s))
     own, done = gate_up(level, inner, held, loaded, jnp.float32, True, last)
-    first = attention(done, 0, 2)
+    attended = attention(done)
     active = call(
         activate_kernel,
         [],
         [own, *others],
         jax.ShapeDtypeStruct((experts, count, ff // inner), jnp.bfloat16),
         "activate",
-        after=[first],
+        after=[attended],
     )
     parts = trade([active] * inner, "inner")
     sums_shape = jax.ShapeDtypeStruct((experts, count, width), jnp.float32)
     sums = call(down_first_kernel, [level], [active, down_weight], sums_shape, "down_first", 24)
-    second = attention(sums, 1, 2)
     sums = call(
         functools.partial(down_more_kernel, 1),
         [level],
@@ -421,9 +416,8 @@
         [jax.ShapeDtypeStruct((experts * count // owners, width), jnp.bfloat16)] * owners,
         "down_rest",
         24,
-        after=[second],
-    )
-    return back, jnp.concatenate([first, second], axis=0)
+    )
+    return back, attended
 
 
 def experts_by_rows(held, gate_up_weight, down_weight, owners, attention):
@@ -435,7 +429,7 @@
     outputs = jnp.einsum("sxf,xfd->xsd", active, down_weight, preferred_element_type=jnp.float32)
     outputs = outputs.astype(jnp.bfloat16).reshape(experts, owners, count // owners, -1)
     back = [outputs[:, t].reshape(experts * count // owners, -1) for t in range(owners)]
-    return back, attention(held, 0, 1)
+    return back, attention(held)
 
 
 def body(
@@ -458,8 +452,7 @@
     level = lax.axis_index("inner").astype(jnp.int32).reshape(1)
     slots = experts * CAP * inner
 
-    def attention(after, part, parts):
-        return attend(queries, new_key_value, cached_key_value, parents, after, part, parts)
+    attention = functools.partial(attend, queries, new_key_value, cached_key_value, parents)
 
     slices = call(
         prepare_kernel,

time: 61.8 us -> 62.6 us (1.013)
  local copies, waits for them, and re-layouts: 6 us -> 7.21 us
  Pallas kernels: 17.8 us -> 17 us
    unnamed x27, local copies, waits for them, and re-layouts: 6 us -> 7.21 us
    pallas_call x2 -> x1, Pallas kernels: 5.56 us -> 5.02 us  [attend(): pl.pallas_call(functools.partial(attend_kernel, step), grid_spec=pltpu.Pr...]
  transfers between devices with their start and end apart: 18 -> 18, of which waited for: 9 -> 9; matrix products, arithmetic and copies ran while one was open for 1% -> 1% of each run, Pallas kernels for 23% -> 22%
where the time goes in v7:
time: 62.6 us; the launch traced here: 62.4 us
  starting transfers between devices  23 us (37%)
  Pallas kernels  17 us (27%)
  waiting for transfers between devices  14.4 us (23%)
  local copies, waits for them, and re-layouts  7.21 us (12%)
  between operations  0.87 us (1%)
    ppermute x18, starting transfers between devices, traded(): lax.ppermute(value, axis, [(i, i ^ index) for i in range(lax.axis_size(ax...  23 us
    ppermute x18, waiting for transfers between devices, traded(): lax.ppermute(value, axis, [(i, i ^ index) for i in range(lax.axis_size(ax...  14.4 us
    unnamed x27, local copies, waits for them, and re-layouts  7.21 us
    pallas_call x2, Pallas kernels, load(): pl.pallas_call(functools.partial(load_kernel, expert, pieces), in_specs=[...  5.99 us
    pallas_call x14, Pallas kernels, call(): pl.pallas_call(kernel, in_specs=[pl.BlockSpec(memory_space=pltpu.SMEM)] *...  5.98 us
    pallas_call x1, Pallas kernels, attend(): pl.pallas_call(functools.partial(attend_kernel, step), grid_spec=pltpu.Pr...  5.02 us
  transfers between devices with their start and end apart: 18, of which 9 were waited for; matrix products, arithmetic and copies ran while one was open for 1% of the time, Pallas kernels for 22%

profile of v7, /device:TPU:0, one launch (start us, length us, event | category | flops | bytes accessed | tf_op | source)
XLA Modules:
  0.0 62.4 jit_solution(10766364500922949608)
XLA Ops:
  0.6 0.8 %copy-done.2 = bf16[8,4096]{1,0:T(8,128)(2,1)S(1)} copy-done((bf16[8,4096]{1,0:T(8,128)(2,1)S(1)}, bf16[8,4096]{1,0:T(8,128)(2,1)}, u32[]{:S(2)}) %copy-start.2) | copy-done | bytes 65560
  1.5 0.7 %copy-done.3 = s32[8,2]{0,1:T(2,128)S(1)} copy-done((s32[8,2]{0,1:T(2,128)S(1)}, s32[8,2]{0,1:T(2,128)}, u32[]{:S(2)}) %copy-start.3) | copy-done | bytes 88
  2.2 0.7 %copy-done.4 = bf16[8,2]{0,1:T(2,128)(2,1)S(1)} copy-done((bf16[8,2]{0,1:T(2,128)(2,1)S(1)}, bf16[8,2]{0,1:T(2,128)(2,1)}, u32[]{:S(2)}) %copy-start.4) | copy-done | bytes 56
  2.8 0.2 prepare.1
  3.0 3.0 %collective-permute-start = (bf16[8,1152]{1,0:T(8,128)(2,1)S(1)}, bf16[8,1152]{1,0:T(8,128)(2,1)S(1)}, u32[]{:S(2)}, u32[]{:S(2)}) collective-permute-start(bf16[8,1152]{1,0:T(8,128)(2,1)S(1)} %get-tuple-element.25), channel_id=1, source_target_pairs={{0,1},{1,0},{2,3},{3,2},{4,5},{5,4},{6,7},{7,6},{8,9},{9,8},{10,11... | collective-permute-start | bytes 55304 | tf_op jit(solution)/shard_map/ppermute | solution.py:350
  6.0 2.6 %collective-permute-start.1 = (bf16[8,1152]{1,0:T(8,128)(2,1)S(1)}, bf16[8,1152]{1,0:T(8,128)(2,1)S(1)}, u32[]{:S(2)}, u32[]{:S(2)}) collective-permute-start(bf16[8,1152]{1,0:T(8,128)(2,1)S(1)} %get-tuple-element.26), channel_id=1, source_target_pairs={{0,2},{1,3},{2,0},{3,1},{4,6},{5,7},{6,4},{7,5},{8,10},{9,11},{10,... | collective-permute-start | bytes 55304 | tf_op jit(solution)/shard_map/ppermute | solution.py:350
  8.6 2.9 %load.2 = (bf16[2,1024,1536]{2,1,0:T(8,128)(2,1)S(1)}, f32[8,128]{1,0:T(8,128)S(1)}) custom-call(bf16[2,2,1024,1536]{3,2,1,0:T(8,128)(2,1)} %weight_hbm.3, bf16[8,1152]{1,0:T(8,128)(2,1)S(1)} %get-tuple-element.24.after_ref.refs_0_), custom_call_target="tpu_custom_call" | custom-call | flops 100000000 | tf_op jit(solution)/shard_map/load/pallas_call | solution.py:255
  11.6 2.6 %copy-done = bf16[2,1024,1536]{2,1,0:T(8,128)(2,1)} copy-done((bf16[2,1024,1536]{2,1,0:T(8,128)(2,1)}, bf16[2,1024,1536]{2,1,0:T(8,128)(2,1)S(1)}, u32[]{:S(2)}) %copy-start) | copy-done | bytes 6291480
  14.2 0.4 pack.1
  14.7 1.8 %collective-permute-start.4 = (bf16[24,1024]{1,0:T(8,128)(2,1)S(1)}, bf16[24,1024]{1,0:T(8,128)(2,1)S(1)}, u32[]{:S(2)}, u32[]{:S(2)}) collective-permute-start(bf16[24,1024]{1,0:T(8,128)(2,1)S(1)} %get-tuple-element.31), channel_id=1, source_target_pairs={{0,8},{4,12},{8,0},{12,4},{1,9},{5,13},{9,1},{13,5},{2,10},{6,14},... | collective-permute-start | bytes 147464 | tf_op jit(solution)/shard_map/ppermute | solution.py:350
  16.5 0.1 collective-permute-start.5
  16.6 3.1 %load.3 = (bf16[2,1024,1536]{2,1,0:T(8,128)(2,1)S(1)}, f32[8,128]{1,0:T(8,128)S(1)}) custom-call(bf16[2,2,1024,1536]{3,2,1,0:T(8,128)(2,1)} %weight_hbm.3, bf16[24,1024]{1,0:T(8,128)(2,1)S(1)} %get-tuple-element.29.after_ref.refs_0_), custom_call_target="tpu_custom_call" | custom-call | flops 100000000 | tf_op jit(solution)/shard_map/load/pallas_call | solution.py:255
  19.7 0.5 collective-permute-done.5.refs_3_
  20.2 0.2 select.1.rows_ref
  20.4 0.3 slice-done
  20.6 0.7 %slice-done.1 = s8[2097152]{0:T(1024)(128)(4,1)S(1)} async-done(((s8[6291456]{0:T(1024)(128)(4,1)}), s8[2097152]{0:T(1024)(128)(4,1)S(1)}, s32[]{:S(2)}) %slice-start.1) | async-done | bytes 2097176
  21.3 0.6 gate_up.4.refs_2_
  21.9 3.9 %collective-permute-start.6 = (bf16[2,48,768]{2,1,0:T(8,128)(2,1)S(1)}, bf16[2,48,768]{2,1,0:T(8,128)(2,1)S(1)}, u32[]{:S(2)}, u32[]{:S(2)}) collective-permute-start(bf16[2,48,768]{2,1,0:T(8,128)(2,1)S(1)} %gate_up.4.refs_2_), channel_id=1, source_target_pairs={{0,3},{1,2},{2,1},{3,0},{4,7},{5,6},{6,5},{7,4},{8,11},{9,10},{10,... | collective-permute-start | bytes 442376 | tf_op jit(solution)/shard_map/ppermute | solution.py:350
  25.8 0.6 gate_up.5.refs_2_
  26.5 0.6 gate_up.6.refs_2_
  27.1 0.6 collective-permute-start.8
  27.7 0.6 gate_up.7
  28.3 0.7 %copy-done.1 = bf16[1,8,192,1024]{3,2,1,0:T(8,128)(2,1)S(1)} copy-done((bf16[1,8,192,1024]{3,2,1,0:T(8,128)(2,1)S(1)}, bf16[1,8,192,1024]{3,2,1,0:T(8,128)(2,1)}, u32[]{:S(2)}) %copy-start.1) | copy-done | bytes 3145752
  29.0 5.0 %attend.1.refs_3_ = bf16[8,64,128]{2,1,0:T(8,128)(2,1)S(1)} custom-call(s32[8]{0:T(128)S(1)} %bitcast.29, bf16[8,64,128]{2,1,0:T(8,128)(2,1)S(1)} %bitcast.25, bf16[8,8,128]{2,1,0:T(8,128)(2,1)S(1)} %bitcast.26, bf16[1,8,192,1024]{3,2,1,0:T(8,128)(2,1)S(1)} %copy-done.1, bf16[1,8,192,1024]{3,2,1,0:T(8,128)(2,1)S(1)} %copy-done.1, ...), custom_call_target="tpu_custom_call" | custom-call | flops 50331648 | bytes 3145728 | tf_op jit(solution)/shard_map/attend/pallas_call | solution.py:68
  34.0 1.8 %collective-permute-done.8.refs_2_ = bf16[2,48,768]{2,1,0:T(8,128)(2,1)S(1)} collective-permute-done((bf16[2,48,768]{2,1,0:T(8,128)(2,1)S(1)}, bf16[2,48,768]{2,1,0:T(8,128)(2,1)S(1)}, u32[]{:S(2)}, u32[]{:S(2)}) %collective-permute-start.8) | collective-permute-done | bytes 147488 | tf_op jit(solution)/shard_map/ppermute | solution.py:350
  35.8 2.1 %collective-permute-done.7.refs_1_ = bf16[2,48,768]{2,1,0:T(8,128)(2,1)S(1)} collective-permute-done((bf16[2,48,768]{2,1,0:T(8,128)(2,1)S(1)}, bf16[2,48,768]{2,1,0:T(8,128)(2,1)S(1)}, u32[]{:S(2)}, u32[]{:S(2)}) %collective-permute-start.7) | collective-permute-done | bytes 147488 | tf_op jit(solution)/shard_map/ppermute | solution.py:350
  37.9 0.1 activate.1.part_ref
  38.0 0.4 collective-permute-start.9
  38.5 2.7 %collective-permute-start.10 = (bf16[2,48,384]{2,1,0:T(8,128)(2,1)S(1)}, bf16[2,48,384]{2,1,0:T(8,128)(2,1)S(1)}, u32[]{:S(2)}, u32[]{:S(2)}) collective-permute-start(bf16[2,48,384]{2,1,0:T(8,128)(2,1)S(1)} %activate.1.part_ref), channel_id=1, source_target_pairs={{0,2},{1,3},{2,0},{3,1},{4,6},{5,7},{6,4},{7,5},{8,10},{9,11},{10,... | collective-permute-start | bytes 221192 | tf_op jit(solution)/shard_map/ppermute | solution.py:350
  41.1 1.3 %collective-permute-start.11 = (bf16[2,48,384]{2,1,0:T(8,128)(2,1)S(1)}, bf16[2,48,384]{2,1,0:T(8,128)(2,1)S(1)}, u32[]{:S(2)}, u32[]{:S(2)}) collective-permute-start(bf16[2,48,384]{2,1,0:T(8,128)(2,1)S(1)} %activate.1.part_ref), channel_id=1, source_target_pairs={{0,3},{1,2},{2,1},{3,0},{4,7},{5,6},{6,5},{7,4},{8,11},{9,10},{10,... | collective-permute-start | bytes 221192 | tf_op jit(solution)/shard_map/ppermute | solution.py:350
  42.5 0.4 down_first.1.before_ref
  42.9 0.4 down_more.1.sum_ref
  43.3 3.1 %collective-permute-done.10.refs_0_ = bf16[2,48,384]{2,1,0:T(8,128)(2,1)S(1)} collective-permute-done((bf16[2,48,384]{2,1,0:T(8,128)(2,1)S(1)}, bf16[2,48,384]{2,1,0:T(8,128)(2,1)S(1)}, u32[]{:S(2)}, u32[]{:S(2)}) %collective-permute-start.10) | collective-permute-done | bytes 73760 | tf_op jit(solution)/shard_map/ppermute | solution.py:350
  46.4 1.0 %collective-permute-done.11.refs_1_ = bf16[2,48,384]{2,1,0:T(8,128)(2,1)S(1)} collective-permute-done((bf16[2,48,384]{2,1,0:T(8,128)(2,1)S(1)}, bf16[2,48,384]{2,1,0:T(8,128)(2,1)S(1)}, u32[]{:S(2)}, u32[]{:S(2)}) %collective-permute-start.11) | collective-permute-done | bytes 73760 | tf_op jit(solution)/shard_map/ppermute | solution.py:350
  47.4 0.8 %down_rest.1 = (bf16[24,1024]{1,0:T(8,128)(2,1)S(1)}, bf16[24,1024]{1,0:T(8,128)(2,1)S(1)}, bf16[24,1024]{1,0:T(8,128)(2,1)S(1)}, bf16[24,1024]{1,0:T(8,128)(2,1)S(1)}) custom-call(s32[1]{0:T(128)} %bitcast.1.me.level.chunk, f32[2,48,1024]{2,1,0:T(8,128)S(1)} %down_more.1.sum_ref, bf16[2,48,384]{2,1,0:T(8,128)(2,1)S(1)} %collective-permute-done.10.refs_0_, ...), custom_call_target="tpu_custom_call" | custom-call | tf_op jit(solution)/shard_map/down_rest/pallas_call | solution.py:362
  48.3 1.6 %collective-permute-start.13 = (bf16[24,1024]{1,0:T(8,128)(2,1)S(1)}, bf16[24,1024]{1,0:T(8,128)(2,1)S(1)}, u32[]{:S(2)}, u32[]{:S(2)}) collective-permute-start(bf16[24,1024]{1,0:T(8,128)(2,1)S(1)} %get-tuple-element.40), channel_id=1, source_target_pairs={{0,8},{4,12},{8,0},{12,4},{1,9},{5,13},{9,1},{13,5},{2,10},{6,14},... | collective-permute-start | bytes 147464 | tf_op jit(solution)/shard_map/ppermute | solution.py:350
  49.8 0.3 collective-permute-start.14
  50.2 0.3 weigh.1.weight_ref
  50.4 2.0 %collective-permute-done.13.refs_2_ = bf16[24,1024]{1,0:T(8,128)(2,1)S(1)} collective-permute-done((bf16[24,1024]{1,0:T(8,128)(2,1)S(1)}, bf16[24,1024]{1,0:T(8,128)(2,1)S(1)}, u32[]{:S(2)}, u32[]{:S(2)}) %collective-permute-start.13) | collective-permute-done | bytes 49184 | tf_op jit(solution)/shard_map/ppermute | solution.py:350
  52.5 1.1 %collective-permute-done.14.refs_3_ = bf16[24,1024]{1,0:T(8,128)(2,1)S(1)} collective-permute-done((bf16[24,1024]{1,0:T(8,128)(2,1)S(1)}, bf16[24,1024]{1,0:T(8,128)(2,1)S(1)}, u32[]{:S(2)}, u32[]{:S(2)}) %collective-permute-start.14) | collective-permute-done | bytes 49184 | tf_op jit(solution)/shard_map/ppermute | solution.py:350
  53.5 0.2 combine.1
  53.8 1.2 %collective-permute-start.15 = (bf16[8,1024]{1,0:T(8,128)(2,1)S(1)}, bf16[8,1024]{1,0:T(8,128)(2,1)S(1)}, u32[]{:S(2)}, u32[]{:S(2)}) collective-permute-start(bf16[8,1024]{1,0:T(8,128)(2,1)S(1)} %get-tuple-element.43), channel_id=1, source_target_pairs={{0,1},{1,0},{2,3},{3,2},{4,5},{5,4},{6,7},{7,6},{8,9},{9,8},{10,11... | collective-permute-start | bytes 49160 | tf_op jit(solution)/shard_map/ppermute | solution.py:350
  55.0 1.3 %collective-permute-start.16 = (bf16[8,1024]{1,0:T(8,128)(2,1)S(1)}, bf16[8,1024]{1,0:T(8,128)(2,1)S(1)}, u32[]{:S(2)}, u32[]{:S(2)}) collective-permute-start(bf16[8,1024]{1,0:T(8,128)(2,1)S(1)} %get-tuple-element.44), channel_id=1, source_target_pairs={{0,2},{1,3},{2,0},{3,1},{4,6},{5,7},{6,4},{7,5},{8,10},{9,11},{10,... | collective-permute-start | bytes 49160 | tf_op jit(solution)/shard_map/ppermute | solution.py:350
  56.3 2.0 %collective-permute-start.17 = (bf16[8,1024]{1,0:T(8,128)(2,1)S(1)}, bf16[8,1024]{1,0:T(8,128)(2,1)S(1)}, u32[]{:S(2)}, u32[]{:S(2)}) collective-permute-start(bf16[8,1024]{1,0:T(8,128)(2,1)S(1)} %get-tuple-element.45), channel_id=1, source_target_pairs={{0,3},{1,2},{2,1},{3,0},{4,7},{5,6},{6,5},{7,4},{8,11},{9,10},{10,... | collective-permute-start | bytes 49160 | tf_op jit(solution)/shard_map/ppermute | solution.py:350
  58.3 0.7 %copy.17 = bf16[1,8,64,128]{3,1,2,0:T(8,128)(2,1)} copy(bf16[1,8,64,128]{3,2,1,0:T(8,128)(2,1)S(1)} %bitcast.24) | data formatting | bytes 262144
  59.0 0.6 collective-permute-done.16.refs_2_
  59.6 2.2 %collective-permute-done.17.refs_3_ = bf16[8,1024]{1,0:T(8,128)(2,1)S(1)} collective-permute-done((bf16[8,1024]{1,0:T(8,128)(2,1)S(1)}, bf16[8,1024]{1,0:T(8,128)(2,1)S(1)}, u32[]{:S(2)}, u32[]{:S(2)}) %collective-permute-start.17) | collective-permute-done | bytes 16416 | tf_op jit(solution)/shard_map/ppermute | solution.py:350
  61.8 0.6 %assemble.1 = bf16[8,4096]{1,0:T(8,128)(2,1)} custom-call(s32[1]{0:T(128)} %bitcast.1.me.level.chunk, bf16[8,1024]{1,0:T(8,128)(2,1)S(1)} %get-tuple-element.42.refs_0_, bf16[8,1024]{1,0:T(8,128)(2,1)S(1)} %collective-permute-done.15.refs_1_, bf16[8,1024]{1,0:T(8,128)(2,1)S(1)} %collective-permute-done.16.refs_2_, ...), custom_call_target="tpu_custom_call" | custom-call | tf_op jit(solution)/shard_map/assemble/pallas_call | solution.py:362
  (34 shorter events, 0.3 us)
Async XLA Ops:
  0.6 0.8 %copy-start.2 = (bf16[8,4096]{1,0:T(8,128)(2,1)S(1)}, bf16[8,4096]{1,0:T(8,128)(2,1)}, u32[]{:S(2)}) copy-start(bf16[8,4096]{1,0:T(8,128)(2,1)} %hidden_ref.1) | copy-start | bytes 196612
  1.5 0.7 %copy-start.3 = (s32[8,2]{0,1:T(2,128)S(1)}, s32[8,2]{0,1:T(2,128)}, u32[]{:S(2)}) copy-start(s32[8,2]{0,1:T(2,128)} %param.14) | copy-start | bytes 196
  2.2 0.7 %copy-start.4 = (bf16[8,2]{0,1:T(2,128)(2,1)S(1)}, bf16[8,2]{0,1:T(2,128)(2,1)}, u32[]{:S(2)}) copy-start(bf16[8,2]{0,1:T(2,128)(2,1)} %param.15) | copy-start | bytes 100
  3.0 11.2 %collective-permute-start = (bf16[8,1152]{1,0:T(8,128)(2,1)S(1)}, bf16[8,1152]{1,0:T(8,128)(2,1)S(1)}, u32[]{:S(2)}, u32[]{:S(2)}) collective-permute-start(bf16[8,1152]{1,0:T(8,128)(2,1)S(1)} %get-tuple-element.25), channel_id=1, source_target_pairs={{0,1},{1,0},{2,3},{3,2},{4,5},{5,4},{6,7},{7,6},{8,9},{9,8},{10,11... | collective-permute-start | bytes 55304 | tf_op jit(solution)/shard_map/ppermute | solution.py:350
  6.0 8.2 %collective-permute-start.1 = (bf16[8,1152]{1,0:T(8,128)(2,1)S(1)}, bf16[8,1152]{1,0:T(8,128)(2,1)S(1)}, u32[]{:S(2)}, u32[]{:S(2)}) collective-permute-start(bf16[8,1152]{1,0:T(8,128)(2,1)S(1)} %get-tuple-element.26), channel_id=1, source_target_pairs={{0,2},{1,3},{2,0},{3,1},{4,6},{5,7},{6,4},{7,5},{8,10},{9,11},{10,... | collective-permute-start | bytes 55304 | tf_op jit(solution)/shard_map/ppermute | solution.py:350
  8.6 5.6 %collective-permute-start.2 = (bf16[8,1152]{1,0:T(8,128)(2,1)S(1)}, bf16[8,1152]{1,0:T(8,128)(2,1)S(1)}, u32[]{:S(2)}, u32[]{:S(2)}) collective-permute-start(bf16[8,1152]{1,0:T(8,128)(2,1)S(1)} %get-tuple-element.27), channel_id=1, source_target_pairs={{0,3},{1,2},{2,1},{3,0},{4,7},{5,6},{6,5},{7,4},{8,11},{9,10},{10,... | collective-permute-start | bytes 55304 | tf_op jit(solution)/shard_map/ppermute | solution.py:350
  8.6 8.0 %copy-start.6 = (bf16[8,8192]{1,0:T(8,128)(2,1)S(1)}, bf16[8,8192]{1,0:T(8,128)(2,1)}, u32[]{:S(2)}) copy-start(bf16[8,8192]{1,0:T(8,128)(2,1)} %param.9) | copy-start | bytes 393220
  8.6 8.0 %copy-start.7 = (bf16[8,1024]{1,0:T(8,128)(2,1)S(1)}, bf16[8,1024]{1,0:T(8,128)(2,1)}, u32[]{:S(2)}) copy-start(bf16[8,1024]{1,0:T(8,128)(2,1)} %param.10) | copy-start | bytes 49156
  11.6 2.6 %copy-start = (bf16[2,1024,1536]{2,1,0:T(8,128)(2,1)}, bf16[2,1024,1536]{2,1,0:T(8,128)(2,1)S(1)}, u32[]{:S(2)}) copy-start(bf16[2,1024,1536]{2,1,0:T(8,128)(2,1)S(1)} %get-tuple-element.34.refs_0_) | copy-start | bytes 18874372
  14.6 5.1 %collective-permute-start.3 = (bf16[24,1024]{1,0:T(8,128)(2,1)S(1)}, bf16[24,1024]{1,0:T(8,128)(2,1)S(1)}, u32[]{:S(2)}, u32[]{:S(2)}) collective-permute-start(bf16[24,1024]{1,0:T(8,128)(2,1)S(1)} %get-tuple-element.30), channel_id=1, source_target_pairs={{0,4},{4,0},{8,12},{12,8},{1,5},{5,1},{9,13},{13,9},{2,6},{6,2},{1... | collective-permute-start | bytes 147464 | tf_op jit(solution)/shard_map/ppermute | solution.py:350
  14.7 5.0 %collective-permute-start.4 = (bf16[24,1024]{1,0:T(8,128)(2,1)S(1)}, bf16[24,1024]{1,0:T(8,128)(2,1)S(1)}, u32[]{:S(2)}, u32[]{:S(2)}) collective-permute-start(bf16[24,1024]{1,0:T(8,128)(2,1)S(1)} %get-tuple-element.31), channel_id=1, source_target_pairs={{0,8},{4,12},{8,0},{12,4},{1,9},{5,13},{9,1},{13,5},{2,10},{6,14},... | collective-permute-start | bytes 147464 | tf_op jit(solution)/shard_map/ppermute | solution.py:350
  16.5 3.7 %collective-permute-start.5 = (bf16[24,1024]{1,0:T(8,128)(2,1)S(1)}, bf16[24,1024]{1,0:T(8,128)(2,1)S(1)}, u32[]{:S(2)}, u32[]{:S(2)}) collective-permute-start(bf16[24,1024]{1,0:T(8,128)(2,1)S(1)} %get-tuple-element.32), channel_id=1, source_target_pairs={{0,12},{4,8},{8,4},{12,0},{1,13},{5,9},{9,5},{13,1},{2,14},{6,10},... | collective-permute-start | bytes 147464 | tf_op jit(solution)/shard_map/ppermute | solution.py:350
  16.6 4.1 %slice-start = ((s8[6291456]{0:T(1024)(128)(4,1)}), s8[4194304]{0:T(1024)(128)(4,1)S(1)}, s32[]{:S(2)}) async-start(s8[6291456]{0:T(1024)(128)(4,1)} %bitcast.20), calls=%async_computation | async-start | bytes 8388608
  16.6 4.7 %slice-start.1 = ((s8[6291456]{0:T(1024)(128)(4,1)}), s8[2097152]{0:T(1024)(128)(4,1)S(1)}, s32[]{:S(2)}) async-start(s8[6291456]{0:T(1024)(128)(4,1)} %bitcast.20), calls=%async_computation.1 | async-start | bytes 4194304
  21.9 16.0 %collective-permute-start.6 = (bf16[2,48,768]{2,1,0:T(8,128)(2,1)S(1)}, bf16[2,48,768]{2,1,0:T(8,128)(2,1)S(1)}, u32[]{:S(2)}, u32[]{:S(2)}) collective-permute-start(bf16[2,48,768]{2,1,0:T(8,128)(2,1)S(1)} %gate_up.4.refs_2_), channel_id=1, source_target_pairs={{0,3},{1,2},{2,1},{3,0},{4,7},{5,6},{6,5},{7,4},{8,11},{9,10},{10,... | collective-permute-start | bytes 442376 | tf_op jit(solution)/shard_map/ppermute | solution.py:350
  26.4 11.5 %collective-permute-start.7 = (bf16[2,48,768]{2,1,0:T(8,128)(2,1)S(1)}, bf16[2,48,768]{2,1,0:T(8,128)(2,1)S(1)}, u32[]{:S(2)}, u32[]{:S(2)}) collective-permute-start(bf16[2,48,768]{2,1,0:T(8,128)(2,1)S(1)} %gate_up.5.refs_2_), channel_id=1, source_target_pairs={{0,2},{1,3},{2,0},{3,1},{4,6},{5,7},{6,4},{7,5},{8,10},{9,11},{10,... | collective-permute-start | bytes 442376 | tf_op jit(solution)/shard_map/ppermute | solution.py:350
  27.1 1.9 %copy-start.1 = (bf16[1,8,192,1024]{3,2,1,0:T(8,128)(2,1)S(1)}, bf16[1,8,192,1024]{3,2,1,0:T(8,128)(2,1)}, u32[]{:S(2)}) copy-start(bf16[1,8,192,1024]{3,2,1,0:T(8,128)(2,1)} %refs_3_.1) | copy-start | bytes 9437188
  27.1 1.9 %copy-start.5 = (s32[1,8]{1,0:T(1,128)S(1)}, s32[1,8]{1,0:T(1,128)}, u32[]{:S(2)}) copy-start(s32[1,8]{1,0:T(1,128)} %param.12) | copy-start | bytes 100
  27.1 8.7 %collective-permute-start.8 = (bf16[2,48,768]{2,1,0:T(8,128)(2,1)S(1)}, bf16[2,48,768]{2,1,0:T(8,128)(2,1)S(1)}, u32[]{:S(2)}, u32[]{:S(2)}) collective-permute-start(bf16[2,48,768]{2,1,0:T(8,128)(2,1)S(1)} %gate_up.6.refs_2_), channel_id=1, source_target_pairs={{0,1},{1,0},{2,3},{3,2},{4,5},{5,4},{6,7},{7,6},{8,9},{9,8},{10,11... | collective-permute-start | bytes 442376 | tf_op jit(solution)/shard_map/ppermute | solution.py:350
  27.7 14.7 %slice-start.2 = ((s8[6291456]{0:T(1024)(128)(4,1)}), s8[2097152]{0:T(1024)(128)(4,1)S(1)}, s32[]{:S(2)}) async-start(s8[6291456]{0:T(1024)(128)(4,1)} %bitcast.22), calls=%async_computation.2 | async-start | bytes 4194304
  29.0 13.5 %slice-start.3 = ((s8[6291456]{0:T(1024)(128)(4,1)}), s8[4194304]{0:T(1024)(128)(4,1)S(1)}, s32[]{:S(2)}) async-start(s8[6291456]{0:T(1024)(128)(4,1)} %bitcast.22), calls=%async_computation.3 | async-start | bytes 8388608
  38.0 4.8 %collective-permute-start.9 = (bf16[2,48,384]{2,1,0:T(8,128)(2,1)S(1)}, bf16[2,48,384]{2,1,0:T(8,128)(2,1)S(1)}, u32[]{:S(2)}, u32[]{:S(2)}) collective-permute-start(bf16[2,48,384]{2,1,0:T(8,128)(2,1)S(1)} %activate.1.part_ref), channel_id=1, source_target_pairs={{0,1},{1,0},{2,3},{3,2},{4,5},{5,4},{6,7},{7,6},{8,9},{9,8},{10,11... | collective-permute-start | bytes 221192 | tf_op jit(solution)/shard_map/ppermute | solution.py:350
  38.5 7.9 %collective-permute-start.10 = (bf16[2,48,384]{2,1,0:T(8,128)(2,1)S(1)}, bf16[2,48,384]{2,1,0:T(8,128)(2,1)S(1)}, u32[]{:S(2)}, u32[]{:S(2)}) collective-permute-start(bf16[2,48,384]{2,1,0:T(8,128)(2,1)S(1)} %activate.1.part_ref), channel_id=1, source_target_pairs={{0,2},{1,3},{2,0},{3,1},{4,6},{5,7},{6,4},{7,5},{8,10},{9,11},{10,... | collective-permute-start | bytes 221192 | tf_op jit(solution)/shard_map/ppermute | solution.py:350
  41.1 6.3 %collective-permute-start.11 = (bf16[2,48,384]{2,1,0:T(8,128)(2,1)S(1)}, bf16[2,48,384]{2,1,0:T(8,128)(2,1)S(1)}, u32[]{:S(2)}, u32[]{:S(2)}) collective-permute-start(bf16[2,48,384]{2,1,0:T(8,128)(2,1)S(1)} %activate.1.part_ref), channel_id=1, source_target_pairs={{0,3},{1,2},{2,1},{3,0},{4,7},{5,6},{6,5},{7,4},{8,11},{9,10},{10,... | collective-permute-start | bytes 221192 | tf_op jit(solution)/shard_map/ppermute | solution.py:350
  48.2 2.2 %collective-permute-start.12 = (bf16[24,1024]{1,0:T(8,128)(2,1)S(1)}, bf16[24,1024]{1,0:T(8,128)(2,1)S(1)}, u32[]{:S(2)}, u32[]{:S(2)}) collective-permute-start(bf16[24,1024]{1,0:T(8,128)(2,1)S(1)} %get-tuple-element.39), channel_id=1, source_target_pairs={{0,4},{4,0},{8,12},{12,8},{1,5},{5,1},{9,13},{13,9},{2,6},{6,2},{1... | collective-permute-start | bytes 147464 | tf_op jit(solution)/shard_map/ppermute | solution.py:350
  48.3 4.2 %collective-permute-start.13 = (bf16[24,1024]{1,0:T(8,128)(2,1)S(1)}, bf16[24,1024]{1,0:T(8,128)(2,1)S(1)}, u32[]{:S(2)}, u32[]{:S(2)}) collective-permute-start(bf16[24,1024]{1,0:T(8,128)(2,1)S(1)} %get-tuple-element.40), channel_id=1, source_target_pairs={{0,8},{4,12},{8,0},{12,4},{1,9},{5,13},{9,1},{13,5},{2,10},{6,14},... | collective-permute-start | bytes 147464 | tf_op jit(solution)/shard_map/ppermute | solution.py:350
  49.8 3.7 %collective-permute-start.14 = (bf16[24,1024]{1,0:T(8,128)(2,1)S(1)}, bf16[24,1024]{1,0:T(8,128)(2,1)S(1)}, u32[]{:S(2)}, u32[]{:S(2)}) collective-permute-start(bf16[24,1024]{1,0:T(8,128)(2,1)S(1)} %get-tuple-element.41), channel_id=1, source_target_pairs={{0,12},{4,8},{8,4},{12,0},{1,13},{5,9},{9,5},{13,1},{2,14},{6,10},... | collective-permute-start | bytes 147464 | tf_op jit(solution)/shard_map/ppermute | solution.py:350
  53.8 5.2 %collective-permute-start.15 = (bf16[8,1024]{1,0:T(8,128)(2,1)S(1)}, bf16[8,1024]{1,0:T(8,128)(2,1)S(1)}, u32[]{:S(2)}, u32[]{:S(2)}) collective-permute-start(bf16[8,1024]{1,0:T(8,128)(2,1)S(1)} %get-tuple-element.43), channel_id=1, source_target_pairs={{0,1},{1,0},{2,3},{3,2},{4,5},{5,4},{6,7},{7,6},{8,9},{9,8},{10,11... | collective-permute-start | bytes 49160 | tf_op jit(solution)/shard_map/ppermute | solution.py:350
  55.0 4.6 %collective-permute-start.16 = (bf16[8,1024]{1,0:T(8,128)(2,1)S(1)}, bf16[8,1024]{1,0:T(8,128)(2,1)S(1)}, u32[]{:S(2)}, u32[]{:S(2)}) collective-permute-start(bf16[8,1024]{1,0:T(8,128)(2,1)S(1)} %get-tuple-element.44), channel_id=1, source_target_pairs={{0,2},{1,3},{2,0},{3,1},{4,6},{5,7},{6,4},{7,5},{8,10},{9,11},{10,... | collective-permute-start | bytes 49160 | tf_op jit(solution)/shard_map/ppermute | solution.py:350
  56.3 5.5 %collective-permute-start.17 = (bf16[8,1024]{1,0:T(8,128)(2,1)S(1)}, bf16[8,1024]{1,0:T(8,128)(2,1)S(1)}, u32[]{:S(2)}, u32[]{:S(2)}) collective-permute-start(bf16[8,1024]{1,0:T(8,128)(2,1)S(1)} %get-tuple-element.45), channel_id=1, source_target_pairs={{0,3},{1,2},{2,1},{3,0},{4,7},{5,6},{6,5},{7,4},{8,11},{9,10},{10,... | collective-permute-start | bytes 49160 | tf_op jit(solution)/shard_map/ppermute | solution.py:350

commit v8 on v7

--- a/solution.py
+++ b/solution.py
@@ -231,8 +231,8 @@
         out_ref[x] = moved[x * count:(x + 1) * count]
 
 
-def load_kernel(expert, pieces, weight_hbm, after_ref, out_ref, done_ref, sems):
-    del after_ref
+def load_kernel(expert, pieces, weight_hbm, *refs):
+    out_ref, sems = refs[-2:]
     step = out_ref.shape[1] // pieces
     copies = [
         pltpu.make_async_copy(
@@ -245,7 +245,6 @@
     ]
     for copy in copies:
         copy.start()
-    done_ref[...] = jnp.zeros_like(done_ref)
     for copy in copies:
         copy.wait()
 
@@ -254,17 +253,14 @@
     pieces = 8
     return pl.pallas_call(
         functools.partial(load_kernel, expert, pieces),
-        in_specs=[pl.BlockSpec(memory_space=pl.ANY)] * 2,
-        out_specs=[pl.BlockSpec(memory_space=pltpu.VMEM)] * 2,
-        out_shape=[
-            jax.ShapeDtypeStruct(weight.shape[1:], weight.dtype),
-            jax.ShapeDtypeStruct((8, LANES), jnp.float32),
-        ],
+        in_specs=[pl.BlockSpec(memory_space=pl.ANY)] * (1 + len(after)),
+        out_specs=pl.BlockSpec(memory_space=pltpu.VMEM),
+        out_shape=jax.ShapeDtypeStruct(weight.shape[1:], weight.dtype),
         scratch_shapes=[pltpu.SemaphoreType.DMA((2 * pieces,))],
         compiler_params=params(limit),
         cost_estimate=pl.CostEstimate(flops=10**8, bytes_accessed=0, transcendentals=0),
         name="load",
-    )(weight, after)
+    )(weight, *after)
 
 
 def gate_up_kernel(experts, afters, chunk, rows_ref, *refs):
@@ -462,7 +458,7 @@
         "prepare",
     )
     even = ff % (inner * LANES) == 0
-    loaded = [load(gate_up_weight, 0, slices[0], 45)] if even else []
+    loaded = [load(gate_up_weight, 0, slices[:1], 45)] if even else []
     slices = trade(slices, "inner")
     packs = call(
         functools.partial(pack_kernel, top, experts, inner, len(loaded)),
@@ -470,10 +466,11 @@
         slices,
         [jax.ShapeDtypeStruct((slots, depth), jnp.bfloat16)] * owners,
         "pack",
-        after=[done for _, done in loaded],
+        after=loaded,
     )
     if even:
-        loaded += [load(gate_up_weight, x, packs[0], 40) for x in range(1, experts)]
+        for x in range(1, experts):
+            loaded = loaded + [load(gate_up_weight, x, [packs[0], *loaded], 40)]
     packs = trade(packs, "expert")
     held = call(
         functools.partial(select_kernel, owners),
@@ -482,10 +479,10 @@
         jax.ShapeDtypeStruct((experts, owners * CAP * inner, depth), jnp.bfloat16),
         "select",
         24,
-        after=[done for _, done in loaded[1:]],
+        after=loaded,
     )
     back, attended = (experts_by_columns if even else experts_by_rows)(
-        held, [part for part, _ in loaded] or gate_up_weight, down_weight, owners, attention
+        held, loaded or gate_up_weight, down_weight, owners, attention
     )
     back = trade(back, "expert")
     weights = call(

time: 62.6 us -> 64.4 us (1.029)
  local copies, waits for them, and re-layouts: 7.21 us -> 8.38 us
  waiting for transfers between devices: 14.4 us -> 15.3 us
    unnamed x27 -> x25, local copies, waits for them, and re-layouts: 7.21 us -> 8.38 us
    ppermute x18, waiting for transfers between devices: 14.4 us -> 15.3 us  [traded(): lax.ppermute(value, axis, [(i, i ^ index) for i in range(lax.axis_size(ax...]
  transfers between devices with their start and end apart: 18 -> 18, of which waited for: 9 -> 9; matrix products, arithmetic and copies ran while one was open for 1% -> 1% of each run, Pallas kernels for 22% -> 21%
where the time goes in v8:
time: 64.4 us; the launch traced here: 64.2 us
  starting transfers between devices  22.8 us (35%)
  Pallas kernels  16.8 us (26%)
  waiting for transfers between devices  15.3 us (24%)
  local copies, waits for them, and re-layouts  8.38 us (13%)
  between operations  0.92 us (1%)
    ppermute x18, starting transfers between devices, traded(): lax.ppermute(value, axis, [(i, i ^ index) for i in range(lax.axis_size(ax...  22.8 us
    ppermute x18, waiting for transfers between devices, traded(): lax.ppermute(value, axis, [(i, i ^ index) for i in range(lax.axis_size(ax...  15.3 us
    unnamed x25, local copies, waits for them, and re-layouts  8.38 us
    pallas_call x14, Pallas kernels, call(): pl.pallas_call(kernel, in_specs=[pl.BlockSpec(memory_space=pltpu.SMEM)] *...  5.98 us
    pallas_call x2, Pallas kernels, load(): pl.pallas_call(functools.partial(load_kernel, expert, pieces), in_specs=[...  5.8 us
    pallas_call x1, Pallas kernels, attend(): pl.pallas_call(functools.partial(attend_kernel, step), grid_spec=pltpu.Pr...  5.03 us
  transfers between devices with their start and end apart: 18, of which 9 were waited for; matrix products, arithmetic and copies ran while one was open for 1% of the time, Pallas kernels for 21%

profile of v8, /device:TPU:0, one launch (start us, length us, event | category | flops | bytes accessed | tf_op | source)
XLA Modules:
  0.0 64.2 jit_solution(12845104828325880062)
XLA Ops:
  0.6 0.8 %copy-done.3 = bf16[8,4096]{1,0:T(8,128)(2,1)S(1)} copy-done((bf16[8,4096]{1,0:T(8,128)(2,1)S(1)}, bf16[8,4096]{1,0:T(8,128)(2,1)}, u32[]{:S(2)}) %copy-start.3) | copy-done | bytes 65560
  1.5 0.7 %copy-done.4 = s32[8,2]{0,1:T(2,128)S(1)} copy-done((s32[8,2]{0,1:T(2,128)S(1)}, s32[8,2]{0,1:T(2,128)}, u32[]{:S(2)}) %copy-start.4) | copy-done | bytes 88
  2.2 0.7 %copy-done.5 = bf16[8,2]{0,1:T(2,128)(2,1)S(1)} copy-done((bf16[8,2]{0,1:T(2,128)(2,1)S(1)}, bf16[8,2]{0,1:T(2,128)(2,1)}, u32[]{:S(2)}) %copy-start.5) | copy-done | bytes 56
  2.8 0.2 prepare.1
  3.0 3.0 %collective-permute-start = (bf16[8,1152]{1,0:T(8,128)(2,1)S(1)}, bf16[8,1152]{1,0:T(8,128)(2,1)S(1)}, u32[]{:S(2)}, u32[]{:S(2)}) collective-permute-start(bf16[8,1152]{1,0:T(8,128)(2,1)S(1)} %get-tuple-element.21), channel_id=1, source_target_pairs={{0,1},{1,0},{2,3},{3,2},{4,5},{5,4},{6,7},{7,6},{8,9},{9,8},{10,11... | collective-permute-start | bytes 55304 | tf_op jit(solution)/shard_map/ppermute | solution.py:346
  6.0 2.6 %collective-permute-start.1 = (bf16[8,1152]{1,0:T(8,128)(2,1)S(1)}, bf16[8,1152]{1,0:T(8,128)(2,1)S(1)}, u32[]{:S(2)}, u32[]{:S(2)}) collective-permute-start(bf16[8,1152]{1,0:T(8,128)(2,1)S(1)} %get-tuple-element.22), channel_id=1, source_target_pairs={{0,2},{1,3},{2,0},{3,1},{4,6},{5,7},{6,4},{7,5},{8,10},{9,11},{10,... | collective-permute-start | bytes 55304 | tf_op jit(solution)/shard_map/ppermute | solution.py:346
  8.6 2.9 %load.2.refs_4_.refs_1_.refs_0_ = bf16[2,1024,1536]{2,1,0:T(8,128)(2,1)S(1)} custom-call(bf16[2,2,1024,1536]{3,2,1,0:T(8,128)(2,1)} %weight_hbm.3, bf16[8,1152]{1,0:T(8,128)(2,1)S(1)} %get-tuple-element.20.refs_0_), custom_call_target="tpu_custom_call" | custom-call | flops 100000000 | tf_op jit(solution)/shard_map/load/pallas_call | solution.py:254
  11.6 2.6 %collective-permute-done.2.refs_3_ = bf16[8,1152]{1,0:T(8,128)(2,1)S(1)} collective-permute-done((bf16[8,1152]{1,0:T(8,128)(2,1)S(1)}, bf16[8,1152]{1,0:T(8,128)(2,1)S(1)}, u32[]{:S(2)}, u32[]{:S(2)}) %collective-permute-start.2) | collective-permute-done | bytes 18464 | tf_op jit(solution)/shard_map/ppermute | solution.py:346
  14.2 0.4 pack.1
  14.6 2.6 %copy-done = bf16[2,1024,1536]{2,1,0:T(8,128)(2,1)} copy-done((bf16[2,1024,1536]{2,1,0:T(8,128)(2,1)}, bf16[2,1024,1536]{2,1,0:T(8,128)(2,1)S(1)}, u32[]{:S(2)}) %copy-start) | copy-done | bytes 6291480
  17.2 1.5 %collective-permute-start.4 = (bf16[24,1024]{1,0:T(8,128)(2,1)S(1)}, bf16[24,1024]{1,0:T(8,128)(2,1)S(1)}, u32[]{:S(2)}, u32[]{:S(2)}) collective-permute-start(bf16[24,1024]{1,0:T(8,128)(2,1)S(1)} %get-tuple-element.26), channel_id=1, source_target_pairs={{0,8},{4,12},{8,0},{12,4},{1,9},{5,13},{9,1},{13,5},{2,10},{6,14},... | collective-permute-start | bytes 147464 | tf_op jit(solution)/shard_map/ppermute | solution.py:346
  18.7 0.4 collective-permute-start.5
  19.1 2.8 %copy-done.1 = bf16[2,1024,1536]{2,1,0:T(8,128)(2,1)S(1)} copy-done((bf16[2,1024,1536]{2,1,0:T(8,128)(2,1)S(1)}, bf16[2,1024,1536]{2,1,0:T(8,128)(2,1)}, u32[]{:S(2)}) %copy-start.1) | copy-done | bytes 6291480
  21.9 2.9 %load.3.refs_5_.refs_1_ = bf16[2,1024,1536]{2,1,0:T(8,128)(2,1)S(1)} custom-call(bf16[2,2,1024,1536]{3,2,1,0:T(8,128)(2,1)} %weight_hbm.3, bf16[24,1024]{1,0:T(8,128)(2,1)S(1)} %get-tuple-element.24.refs_0_, bf16[2,1024,1536]{2,1,0:T(8,128)(2,1)S(1)} %copy-done.1), custom_call_target="tpu_custom_call" | custom-call | flops 100000000 | tf_op jit(solution)/shard_map/load/pallas_call | solution.py:254
  24.9 0.2 select.1.rows_ref
  25.1 0.6 gate_up.4.refs_2_
  25.6 1.3 %collective-permute-start.6 = (bf16[2,48,768]{2,1,0:T(8,128)(2,1)S(1)}, bf16[2,48,768]{2,1,0:T(8,128)(2,1)S(1)}, u32[]{:S(2)}, u32[]{:S(2)}) collective-permute-start(bf16[2,48,768]{2,1,0:T(8,128)(2,1)S(1)} %gate_up.4.refs_2_), channel_id=1, source_target_pairs={{0,3},{1,2},{2,1},{3,0},{4,7},{5,6},{6,5},{7,4},{8,11},{9,10},{10,... | collective-permute-start | bytes 442376 | tf_op jit(solution)/shard_map/ppermute | solution.py:346
  26.9 0.6 gate_up.5.refs_2_
  27.5 0.1 collective-permute-start.7
  27.6 0.6 gate_up.6.refs_2_
  28.3 3.2 %collective-permute-start.8 = (bf16[2,48,768]{2,1,0:T(8,128)(2,1)S(1)}, bf16[2,48,768]{2,1,0:T(8,128)(2,1)S(1)}, u32[]{:S(2)}, u32[]{:S(2)}) collective-permute-start(bf16[2,48,768]{2,1,0:T(8,128)(2,1)S(1)} %gate_up.6.refs_2_), channel_id=1, source_target_pairs={{0,1},{1,0},{2,3},{3,2},{4,5},{5,4},{6,7},{7,6},{8,9},{9,8},{10,11... | collective-permute-start | bytes 442376 | tf_op jit(solution)/shard_map/ppermute | solution.py:346
  31.4 0.6 gate_up.7
  32.0 5.0 %attend.1.refs_3_ = bf16[8,64,128]{2,1,0:T(8,128)(2,1)S(1)} custom-call(s32[8]{0:T(128)S(1)} %bitcast.27, bf16[8,64,128]{2,1,0:T(8,128)(2,1)S(1)} %bitcast.23, bf16[8,8,128]{2,1,0:T(8,128)(2,1)S(1)} %bitcast.24, bf16[1,8,192,1024]{3,2,1,0:T(8,128)(2,1)S(1)} %copy-done.2, bf16[1,8,192,1024]{3,2,1,0:T(8,128)(2,1)S(1)} %copy-done.2, ...), custom_call_target="tpu_custom_call" | custom-call | flops 50331648 | bytes 3145728 | tf_op jit(solution)/shard_map/attend/pallas_call | solution.py:68
  37.1 0.3 collective-permute-done.8.refs_2_
  37.4 2.5 %collective-permute-done.7.refs_1_ = bf16[2,48,768]{2,1,0:T(8,128)(2,1)S(1)} collective-permute-done((bf16[2,48,768]{2,1,0:T(8,128)(2,1)S(1)}, bf16[2,48,768]{2,1,0:T(8,128)(2,1)S(1)}, u32[]{:S(2)}, u32[]{:S(2)}) %collective-permute-start.7) | collective-permute-done | bytes 147488 | tf_op jit(solution)/shard_map/ppermute | solution.py:346
  39.9 0.1 activate.1.part_ref
  40.0 0.1 collective-permute-start.9
  40.1 2.2 %collective-permute-start.10 = (bf16[2,48,384]{2,1,0:T(8,128)(2,1)S(1)}, bf16[2,48,384]{2,1,0:T(8,128)(2,1)S(1)}, u32[]{:S(2)}, u32[]{:S(2)}) collective-permute-start(bf16[2,48,384]{2,1,0:T(8,128)(2,1)S(1)} %activate.1.part_ref), channel_id=1, source_target_pairs={{0,2},{1,3},{2,0},{3,1},{4,6},{5,7},{6,4},{7,5},{8,10},{9,11},{10,... | collective-permute-start | bytes 221192 | tf_op jit(solution)/shard_map/ppermute | solution.py:346
  42.2 2.2 %collective-permute-start.11 = (bf16[2,48,384]{2,1,0:T(8,128)(2,1)S(1)}, bf16[2,48,384]{2,1,0:T(8,128)(2,1)S(1)}, u32[]{:S(2)}, u32[]{:S(2)}) collective-permute-start(bf16[2,48,384]{2,1,0:T(8,128)(2,1)S(1)} %activate.1.part_ref), channel_id=1, source_target_pairs={{0,3},{1,2},{2,1},{3,0},{4,7},{5,6},{6,5},{7,4},{8,11},{9,10},{10,... | collective-permute-start | bytes 221192 | tf_op jit(solution)/shard_map/ppermute | solution.py:346
  44.4 0.4 down_first.1.before_ref
  44.8 0.5 collective-permute-done.9.part_ref
  45.3 0.4 down_more.1.sum_ref
  45.7 3.4 %collective-permute-done.10.refs_0_ = bf16[2,48,384]{2,1,0:T(8,128)(2,1)S(1)} collective-permute-done((bf16[2,48,384]{2,1,0:T(8,128)(2,1)S(1)}, bf16[2,48,384]{2,1,0:T(8,128)(2,1)S(1)}, u32[]{:S(2)}, u32[]{:S(2)}) %collective-permute-start.10) | collective-permute-done | bytes 73760 | tf_op jit(solution)/shard_map/ppermute | solution.py:346
  49.2 0.8 %down_rest.1 = (bf16[24,1024]{1,0:T(8,128)(2,1)S(1)}, bf16[24,1024]{1,0:T(8,128)(2,1)S(1)}, bf16[24,1024]{1,0:T(8,128)(2,1)S(1)}, bf16[24,1024]{1,0:T(8,128)(2,1)S(1)}) custom-call(s32[1]{0:T(128)} %bitcast.1.me.level.chunk, f32[2,48,1024]{2,1,0:T(8,128)S(1)} %down_more.1.sum_ref, bf16[2,48,384]{2,1,0:T(8,128)(2,1)S(1)} %collective-permute-done.10.refs_0_, ...), custom_call_target="tpu_custom_call" | custom-call | tf_op jit(solution)/shard_map/down_rest/pallas_call | solution.py:358
  50.0 0.1 collective-permute-start.12
  50.1 1.6 %collective-permute-start.13 = (bf16[24,1024]{1,0:T(8,128)(2,1)S(1)}, bf16[24,1024]{1,0:T(8,128)(2,1)S(1)}, u32[]{:S(2)}, u32[]{:S(2)}) collective-permute-start(bf16[24,1024]{1,0:T(8,128)(2,1)S(1)} %get-tuple-element.32), channel_id=1, source_target_pairs={{0,8},{4,12},{8,0},{12,4},{1,9},{5,13},{9,1},{13,5},{2,10},{6,14},... | collective-permute-start | bytes 147464 | tf_op jit(solution)/shard_map/ppermute | solution.py:346
  51.6 0.3 collective-permute-start.14
  51.9 0.3 weigh.1.weight_ref
  52.2 2.0 %collective-permute-done.13.refs_2_ = bf16[24,1024]{1,0:T(8,128)(2,1)S(1)} collective-permute-done((bf16[24,1024]{1,0:T(8,128)(2,1)S(1)}, bf16[24,1024]{1,0:T(8,128)(2,1)S(1)}, u32[]{:S(2)}, u32[]{:S(2)}) %collective-permute-start.13) | collective-permute-done | bytes 49184 | tf_op jit(solution)/shard_map/ppermute | solution.py:346
  54.2 1.1 %collective-permute-done.14.refs_3_ = bf16[24,1024]{1,0:T(8,128)(2,1)S(1)} collective-permute-done((bf16[24,1024]{1,0:T(8,128)(2,1)S(1)}, bf16[24,1024]{1,0:T(8,128)(2,1)S(1)}, u32[]{:S(2)}, u32[]{:S(2)}) %collective-permute-start.14) | collective-permute-done | bytes 49184 | tf_op jit(solution)/shard_map/ppermute | solution.py:346
  55.3 0.2 combine.1
  55.6 1.4 %collective-permute-start.15 = (bf16[8,1024]{1,0:T(8,128)(2,1)S(1)}, bf16[8,1024]{1,0:T(8,128)(2,1)S(1)}, u32[]{:S(2)}, u32[]{:S(2)}) collective-permute-start(bf16[8,1024]{1,0:T(8,128)(2,1)S(1)} %get-tuple-element.35), channel_id=1, source_target_pairs={{0,1},{1,0},{2,3},{3,2},{4,5},{5,4},{6,7},{7,6},{8,9},{9,8},{10,11... | collective-permute-start | bytes 49160 | tf_op jit(solution)/shard_map/ppermute | solution.py:346
  57.0 1.0 %collective-permute-start.16 = (bf16[8,1024]{1,0:T(8,128)(2,1)S(1)}, bf16[8,1024]{1,0:T(8,128)(2,1)S(1)}, u32[]{:S(2)}, u32[]{:S(2)}) collective-permute-start(bf16[8,1024]{1,0:T(8,128)(2,1)S(1)} %get-tuple-element.36), channel_id=1, source_target_pairs={{0,2},{1,3},{2,0},{3,1},{4,6},{5,7},{6,4},{7,5},{8,10},{9,11},{10,... | collective-permute-start | bytes 49160 | tf_op jit(solution)/shard_map/ppermute | solution.py:346
  58.0 2.0 %collective-permute-start.17 = (bf16[8,1024]{1,0:T(8,128)(2,1)S(1)}, bf16[8,1024]{1,0:T(8,128)(2,1)S(1)}, u32[]{:S(2)}, u32[]{:S(2)}) collective-permute-start(bf16[8,1024]{1,0:T(8,128)(2,1)S(1)} %get-tuple-element.37), channel_id=1, source_target_pairs={{0,3},{1,2},{2,1},{3,0},{4,7},{5,6},{6,5},{7,4},{8,11},{9,10},{10,... | collective-permute-start | bytes 49160 | tf_op jit(solution)/shard_map/ppermute | solution.py:346
  60.0 0.7 %copy.17 = bf16[1,8,64,128]{3,1,2,0:T(8,128)(2,1)} copy(bf16[1,8,64,128]{3,2,1,0:T(8,128)(2,1)S(1)} %bitcast.22) | data formatting | bytes 262144
  60.8 0.9 %collective-permute-done.16.refs_2_ = bf16[8,1024]{1,0:T(8,128)(2,1)S(1)} collective-permute-done((bf16[8,1024]{1,0:T(8,128)(2,1)S(1)}, bf16[8,1024]{1,0:T(8,128)(2,1)S(1)}, u32[]{:S(2)}, u32[]{:S(2)}) %collective-permute-start.16) | collective-permute-done | bytes 16416 | tf_op jit(solution)/shard_map/ppermute | solution.py:346
  61.6 1.9 %collective-permute-done.17.refs_3_ = bf16[8,1024]{1,0:T(8,128)(2,1)S(1)} collective-permute-done((bf16[8,1024]{1,0:T(8,128)(2,1)S(1)}, bf16[8,1024]{1,0:T(8,128)(2,1)S(1)}, u32[]{:S(2)}, u32[]{:S(2)}) %collective-permute-start.17) | collective-permute-done | bytes 16416 | tf_op jit(solution)/shard_map/ppermute | solution.py:346
  63.6 0.6 assemble.1
  (31 shorter events, 0.1 us)
Async XLA Ops:
  0.6 0.8 %copy-start.3 = (bf16[8,4096]{1,0:T(8,128)(2,1)S(1)}, bf16[8,4096]{1,0:T(8,128)(2,1)}, u32[]{:S(2)}) copy-start(bf16[8,4096]{1,0:T(8,128)(2,1)} %hidden_ref.1) | copy-start | bytes 196612
  1.5 0.7 %copy-start.4 = (s32[8,2]{0,1:T(2,128)S(1)}, s32[8,2]{0,1:T(2,128)}, u32[]{:S(2)}) copy-start(s32[8,2]{0,1:T(2,128)} %param.14) | copy-start | bytes 196
  2.2 0.7 %copy-start.5 = (bf16[8,2]{0,1:T(2,128)(2,1)S(1)}, bf16[8,2]{0,1:T(2,128)(2,1)}, u32[]{:S(2)}) copy-start(bf16[8,2]{0,1:T(2,128)(2,1)} %param.15) | copy-start | bytes 100
  3.0 8.6 %collective-permute-start = (bf16[8,1152]{1,0:T(8,128)(2,1)S(1)}, bf16[8,1152]{1,0:T(8,128)(2,1)S(1)}, u32[]{:S(2)}, u32[]{:S(2)}) collective-permute-start(bf16[8,1152]{1,0:T(8,128)(2,1)S(1)} %get-tuple-element.21), channel_id=1, source_target_pairs={{0,1},{1,0},{2,3},{3,2},{4,5},{5,4},{6,7},{7,6},{8,9},{9,8},{10,11... | collective-permute-start | bytes 55304 | tf_op jit(solution)/shard_map/ppermute | solution.py:346
  6.0 5.5 %collective-permute-start.1 = (bf16[8,1152]{1,0:T(8,128)(2,1)S(1)}, bf16[8,1152]{1,0:T(8,128)(2,1)S(1)}, u32[]{:S(2)}, u32[]{:S(2)}) collective-permute-start(bf16[8,1152]{1,0:T(8,128)(2,1)S(1)} %get-tuple-element.22), channel_id=1, source_target_pairs={{0,2},{1,3},{2,0},{3,1},{4,6},{5,7},{6,4},{7,5},{8,10},{9,11},{10,... | collective-permute-start | bytes 55304 | tf_op jit(solution)/shard_map/ppermute | solution.py:346
  8.6 5.6 %collective-permute-start.2 = (bf16[8,1152]{1,0:T(8,128)(2,1)S(1)}, bf16[8,1152]{1,0:T(8,128)(2,1)S(1)}, u32[]{:S(2)}, u32[]{:S(2)}) collective-permute-start(bf16[8,1152]{1,0:T(8,128)(2,1)S(1)} %get-tuple-element.23), channel_id=1, source_target_pairs={{0,3},{1,2},{2,1},{3,0},{4,7},{5,6},{6,5},{7,4},{8,11},{9,10},{10,... | collective-permute-start | bytes 55304 | tf_op jit(solution)/shard_map/ppermute | solution.py:346
  11.5 7.6 %copy-start.7 = (bf16[8,8192]{1,0:T(8,128)(2,1)S(1)}, bf16[8,8192]{1,0:T(8,128)(2,1)}, u32[]{:S(2)}) copy-start(bf16[8,8192]{1,0:T(8,128)(2,1)} %param.9) | copy-start | bytes 393220
  11.5 7.6 %copy-start.8 = (bf16[8,1024]{1,0:T(8,128)(2,1)S(1)}, bf16[8,1024]{1,0:T(8,128)(2,1)}, u32[]{:S(2)}) copy-start(bf16[8,1024]{1,0:T(8,128)(2,1)} %param.10) | copy-start | bytes 49156
  14.6 2.6 %copy-start = (bf16[2,1024,1536]{2,1,0:T(8,128)(2,1)}, bf16[2,1024,1536]{2,1,0:T(8,128)(2,1)S(1)}, u32[]{:S(2)}) copy-start(bf16[2,1024,1536]{2,1,0:T(8,128)(2,1)S(1)} %load.2.refs_4_.refs_1_.refs_0_) | copy-start | bytes 18874372
  17.2 7.6 %collective-permute-start.3 = (bf16[24,1024]{1,0:T(8,128)(2,1)S(1)}, bf16[24,1024]{1,0:T(8,128)(2,1)S(1)}, u32[]{:S(2)}, u32[]{:S(2)}) collective-permute-start(bf16[24,1024]{1,0:T(8,128)(2,1)S(1)} %get-tuple-element.25), channel_id=1, source_target_pairs={{0,4},{4,0},{8,12},{12,8},{1,5},{5,1},{9,13},{13,9},{2,6},{6,2},{1... | collective-permute-start | bytes 147464 | tf_op jit(solution)/shard_map/ppermute | solution.py:346
  17.2 7.6 %collective-permute-start.4 = (bf16[24,1024]{1,0:T(8,128)(2,1)S(1)}, bf16[24,1024]{1,0:T(8,128)(2,1)S(1)}, u32[]{:S(2)}, u32[]{:S(2)}) collective-permute-start(bf16[24,1024]{1,0:T(8,128)(2,1)S(1)} %get-tuple-element.26), channel_id=1, source_target_pairs={{0,8},{4,12},{8,0},{12,4},{1,9},{5,13},{9,1},{13,5},{2,10},{6,14},... | collective-permute-start | bytes 147464 | tf_op jit(solution)/shard_map/ppermute | solution.py:346
  18.7 6.1 %collective-permute-start.5 = (bf16[24,1024]{1,0:T(8,128)(2,1)S(1)}, bf16[24,1024]{1,0:T(8,128)(2,1)S(1)}, u32[]{:S(2)}, u32[]{:S(2)}) collective-permute-start(bf16[24,1024]{1,0:T(8,128)(2,1)S(1)} %get-tuple-element.27), channel_id=1, source_target_pairs={{0,12},{4,8},{8,4},{12,0},{1,13},{5,9},{9,5},{13,1},{2,14},{6,10},... | collective-permute-start | bytes 147464 | tf_op jit(solution)/shard_map/ppermute | solution.py:346
  19.1 2.8 %copy-start.1 = (bf16[2,1024,1536]{2,1,0:T(8,128)(2,1)S(1)}, bf16[2,1024,1536]{2,1,0:T(8,128)(2,1)}, u32[]{:S(2)}) copy-start(bf16[2,1024,1536]{2,1,0:T(8,128)(2,1)} %copy-done) | copy-start | bytes 18874372
  25.6 14.2 %collective-permute-start.6 = (bf16[2,48,768]{2,1,0:T(8,128)(2,1)S(1)}, bf16[2,48,768]{2,1,0:T(8,128)(2,1)S(1)}, u32[]{:S(2)}, u32[]{:S(2)}) collective-permute-start(bf16[2,48,768]{2,1,0:T(8,128)(2,1)S(1)} %gate_up.4.refs_2_), channel_id=1, source_target_pairs={{0,3},{1,2},{2,1},{3,0},{4,7},{5,6},{6,5},{7,4},{8,11},{9,10},{10,... | collective-permute-start | bytes 442376 | tf_op jit(solution)/shard_map/ppermute | solution.py:346
  27.5 12.3 %collective-permute-start.7 = (bf16[2,48,768]{2,1,0:T(8,128)(2,1)S(1)}, bf16[2,48,768]{2,1,0:T(8,128)(2,1)S(1)}, u32[]{:S(2)}, u32[]{:S(2)}) collective-permute-start(bf16[2,48,768]{2,1,0:T(8,128)(2,1)S(1)} %gate_up.5.refs_2_), channel_id=1, source_target_pairs={{0,2},{1,3},{2,0},{3,1},{4,6},{5,7},{6,4},{7,5},{8,10},{9,11},{10,... | collective-permute-start | bytes 442376 | tf_op jit(solution)/shard_map/ppermute | solution.py:346
  28.2 3.8 %copy-start.2 = (bf16[1,8,192,1024]{3,2,1,0:T(8,128)(2,1)S(1)}, bf16[1,8,192,1024]{3,2,1,0:T(8,128)(2,1)}, u32[]{:S(2)}) copy-start(bf16[1,8,192,1024]{3,2,1,0:T(8,128)(2,1)} %refs_3_.1) | copy-start | bytes 9437188
  28.2 3.8 %copy-start.6 = (s32[1,8]{1,0:T(1,128)S(1)}, s32[1,8]{1,0:T(1,128)}, u32[]{:S(2)}) copy-start(s32[1,8]{1,0:T(1,128)} %param.12) | copy-start | bytes 100
  28.3 9.1 %collective-permute-start.8 = (bf16[2,48,768]{2,1,0:T(8,128)(2,1)S(1)}, bf16[2,48,768]{2,1,0:T(8,128)(2,1)S(1)}, u32[]{:S(2)}, u32[]{:S(2)}) collective-permute-start(bf16[2,48,768]{2,1,0:T(8,128)(2,1)S(1)} %gate_up.6.refs_2_), channel_id=1, source_target_pairs={{0,1},{1,0},{2,3},{3,2},{4,5},{5,4},{6,7},{7,6},{8,9},{9,8},{10,11... | collective-permute-start | bytes 442376 | tf_op jit(solution)/shard_map/ppermute | solution.py:346
  31.4 13.0 %slice-start = ((s8[6291456]{0:T(1024)(128)(4,1)}), s8[2097152]{0:T(1024)(128)(4,1)S(1)}, s32[]{:S(2)}) async-start(s8[6291456]{0:T(1024)(128)(4,1)} %bitcast.20), calls=%async_computation | async-start | bytes 4194304
  32.0 12.4 %slice-start.1 = ((s8[6291456]{0:T(1024)(128)(4,1)}), s8[4194304]{0:T(1024)(128)(4,1)S(1)}, s32[]{:S(2)}) async-start(s8[6291456]{0:T(1024)(128)(4,1)} %bitcast.20), calls=%async_computation.1 | async-start | bytes 8388608
  40.0 5.3 %collective-permute-start.9 = (bf16[2,48,384]{2,1,0:T(8,128)(2,1)S(1)}, bf16[2,48,384]{2,1,0:T(8,128)(2,1)S(1)}, u32[]{:S(2)}, u32[]{:S(2)}) collective-permute-start(bf16[2,48,384]{2,1,0:T(8,128)(2,1)S(1)} %activate.1.part_ref), channel_id=1, source_target_pairs={{0,1},{1,0},{2,3},{3,2},{4,5},{5,4},{6,7},{7,6},{8,9},{9,8},{10,11... | collective-permute-start | bytes 221192 | tf_op jit(solution)/shard_map/ppermute | solution.py:346
  40.1 9.1 %collective-permute-start.10 = (bf16[2,48,384]{2,1,0:T(8,128)(2,1)S(1)}, bf16[2,48,384]{2,1,0:T(8,128)(2,1)S(1)}, u32[]{:S(2)}, u32[]{:S(2)}) collective-permute-start(bf16[2,48,384]{2,1,0:T(8,128)(2,1)S(1)} %activate.1.part_ref), channel_id=1, source_target_pairs={{0,2},{1,3},{2,0},{3,1},{4,6},{5,7},{6,4},{7,5},{8,10},{9,11},{10,... | collective-permute-start | bytes 221192 | tf_op jit(solution)/shard_map/ppermute | solution.py:346
  42.2 7.0 %collective-permute-start.11 = (bf16[2,48,384]{2,1,0:T(8,128)(2,1)S(1)}, bf16[2,48,384]{2,1,0:T(8,128)(2,1)S(1)}, u32[]{:S(2)}, u32[]{:S(2)}) collective-permute-start(bf16[2,48,384]{2,1,0:T(8,128)(2,1)S(1)} %activate.1.part_ref), channel_id=1, source_target_pairs={{0,3},{1,2},{2,1},{3,0},{4,7},{5,6},{6,5},{7,4},{8,11},{9,10},{10,... | collective-permute-start | bytes 221192 | tf_op jit(solution)/shard_map/ppermute | solution.py:346
  50.0 2.2 %collective-permute-start.12 = (bf16[24,1024]{1,0:T(8,128)(2,1)S(1)}, bf16[24,1024]{1,0:T(8,128)(2,1)S(1)}, u32[]{:S(2)}, u32[]{:S(2)}) collective-permute-start(bf16[24,1024]{1,0:T(8,128)(2,1)S(1)} %get-tuple-element.31), channel_id=1, source_target_pairs={{0,4},{4,0},{8,12},{12,8},{1,5},{5,1},{9,13},{13,9},{2,6},{6,2},{1... | collective-permute-start | bytes 147464 | tf_op jit(solution)/shard_map/ppermute | solution.py:346
  50.1 4.2 %collective-permute-start.13 = (bf16[24,1024]{1,0:T(8,128)(2,1)S(1)}, bf16[24,1024]{1,0:T(8,128)(2,1)S(1)}, u32[]{:S(2)}, u32[]{:S(2)}) collective-permute-start(bf16[24,1024]{1,0:T(8,128)(2,1)S(1)} %get-tuple-element.32), channel_id=1, source_target_pairs={{0,8},{4,12},{8,0},{12,4},{1,9},{5,13},{9,1},{13,5},{2,10},{6,14},... | collective-permute-start | bytes 147464 | tf_op jit(solution)/shard_map/ppermute | solution.py:346
  51.6 3.7 %collective-permute-start.14 = (bf16[24,1024]{1,0:T(8,128)(2,1)S(1)}, bf16[24,1024]{1,0:T(8,128)(2,1)S(1)}, u32[]{:S(2)}, u32[]{:S(2)}) collective-permute-start(bf16[24,1024]{1,0:T(8,128)(2,1)S(1)} %get-tuple-element.33), channel_id=1, source_target_pairs={{0,12},{4,8},{8,4},{12,0},{1,13},{5,9},{9,5},{13,1},{2,14},{6,10},... | collective-permute-start | bytes 147464 | tf_op jit(solution)/shard_map/ppermute | solution.py:346
  55.6 5.2 %collective-permute-start.15 = (bf16[8,1024]{1,0:T(8,128)(2,1)S(1)}, bf16[8,1024]{1,0:T(8,128)(2,1)S(1)}, u32[]{:S(2)}, u32[]{:S(2)}) collective-permute-start(bf16[8,1024]{1,0:T(8,128)(2,1)S(1)} %get-tuple-element.35), channel_id=1, source_target_pairs={{0,1},{1,0},{2,3},{3,2},{4,5},{5,4},{6,7},{7,6},{8,9},{9,8},{10,11... | collective-permute-start | bytes 49160 | tf_op jit(solution)/shard_map/ppermute | solution.py:346
  57.0 4.6 %collective-permute-start.16 = (bf16[8,1024]{1,0:T(8,128)(2,1)S(1)}, bf16[8,1024]{1,0:T(8,128)(2,1)S(1)}, u32[]{:S(2)}, u32[]{:S(2)}) collective-permute-start(bf16[8,1024]{1,0:T(8,128)(2,1)S(1)} %get-tuple-element.36), channel_id=1, source_target_pairs={{0,2},{1,3},{2,0},{3,1},{4,6},{5,7},{6,4},{7,5},{8,10},{9,11},{10,... | collective-permute-start | bytes 49160 | tf_op jit(solution)/shard_map/ppermute | solution.py:346
  58.0 5.5 %collective-permute-start.17 = (bf16[8,1024]{1,0:T(8,128)(2,1)S(1)}, bf16[8,1024]{1,0:T(8,128)(2,1)S(1)}, u32[]{:S(2)}, u32[]{:S(2)}) collective-permute-start(bf16[8,1024]{1,0:T(8,128)(2,1)S(1)} %get-tuple-element.37), channel_id=1, source_target_pairs={{0,3},{1,2},{2,1},{3,0},{4,7},{5,6},{6,5},{7,4},{8,11},{9,10},{10,... | collective-permute-start | bytes 49160 | tf_op jit(solution)/shard_map/ppermute | solution.py:346

commit v9 on v8

--- a/solution.py
+++ b/solution.py
@@ -21,26 +21,40 @@
     )
 
 
-def attend_kernel(beams, parents, q_ref, new_ref, *refs):
-    cache_refs, out_ref = refs[:beams], refs[-1]
+def attend_kernel(
+    parents, q_ref, new_ref, cache_ref, after_ref, out_ref, done_ref, q_rows, new_rows, out_rows
+):
+    del after_ref
+    done_ref[...] = jnp.zeros_like(done_ref)
     group = QUERY_HEADS // KEY_HEADS
     scale = 1.0 / math.sqrt(HEAD_SIZE)
     width = KEY_HEADS * HEAD_SIZE
-    for b in range(beams):
-        q, cache_ref = q_ref[b], cache_refs[b]
-        fresh = new_ref[b].astype(jnp.float32)
+    count, beams = q_ref.shape[0], cache_ref.shape[1]
+    for h in range(QUERY_HEADS):
+        q_rows[h * count:(h + 1) * count] = q_ref[
+            :, h * HEAD_SIZE:(h + 1) * HEAD_SIZE
+        ].astype(jnp.float32)
+    for h in range(2 * KEY_HEADS):
+        new_rows[h * count:(h + 1) * count] = new_ref[
+            :, h * HEAD_SIZE:(h + 1) * HEAD_SIZE
+        ].astype(jnp.float32)
+    for r in range(count):
+        request, parent = r // beams, parents[r]
+        q = q_rows[pl.ds(r, QUERY_HEADS, stride=count), :]
+        fresh = new_rows[pl.ds(r, 2 * KEY_HEADS, stride=count), :]
         scores, own = [], []
         for k in range(KEY_HEADS):
             qk = q[k * group:(k + 1) * group]
-            keys = cache_ref[0, 0, :, k * HEAD_SIZE:(k + 1) * HEAD_SIZE]
+            keys = cache_ref[request, parent, :, k * HEAD_SIZE:(k + 1) * HEAD_SIZE]
             scores.append(
                 lax.dot_general(
-                    qk, keys, (((1,), (1,)), ((), ())), preferred_element_type=jnp.float32
+                    qk.astype(jnp.bfloat16),
+                    keys,
+                    (((1,), (1,)), ((), ())),
+                    preferred_element_type=jnp.float32,
                 )
             )
-            own.append(
-                jnp.sum(qk.astype(jnp.float32) * fresh[k:k + 1], axis=-1, keepdims=True)
-            )
+            own.append(jnp.sum(qk * fresh[k:k + 1], axis=-1, keepdims=True))
         scores = jnp.concatenate(scores, axis=0) * scale
         own = jnp.concatenate(own, axis=0) * scale
         upper = jnp.maximum(jnp.max(scores, axis=-1, keepdims=True), own)
@@ -50,50 +64,46 @@
         probs = (expo / total).astype(jnp.bfloat16)
         own_prob = (own_expo / total).astype(jnp.bfloat16).astype(jnp.float32)
         for k in range(KEY_HEADS):
-            rows = slice(k * group, (k + 1) * group)
-            values = cache_ref[0, 0, :, width + k * HEAD_SIZE:width + (k + 1) * HEAD_SIZE]
-            result = jnp.dot(probs[rows], values, preferred_element_type=jnp.float32)
-            result = result + own_prob[rows] * fresh[KEY_HEADS + k:KEY_HEADS + k + 1]
-            out_ref[b, rows] = result.astype(out_ref.dtype)
+            heads = slice(k * group, (k + 1) * group)
+            columns = slice(width + k * HEAD_SIZE, width + (k + 1) * HEAD_SIZE)
+            result = jnp.dot(
+                probs[heads], cache_ref[request, parent, :, columns], preferred_element_type=jnp.float32
+            )
+            out_rows[pl.ds(k * group * count + r, group, stride=count), :] = (
+                result + own_prob[heads] * fresh[KEY_HEADS + k:KEY_HEADS + k + 1]
+            )
+    for h in range(QUERY_HEADS):
+        out_ref[:, h * HEAD_SIZE:(h + 1) * HEAD_SIZE] = out_rows[
+            h * count:(h + 1) * count
+        ].astype(out_ref.dtype)
 
 
 def attend(queries, new_key_value, cached_key_value, parents, after):
     rows = queries.shape[0]
-    _, beams, length, width = cached_key_value.shape
-    step = 4
-
-    def parent_of(b):
-        return lambda r, p: ((r * step + b) // beams, p[r * step + b], 0, 0)
-
-    out = pl.pallas_call(
-        functools.partial(attend_kernel, step),
-        grid_spec=pltpu.PrefetchScalarGridSpec(
-            num_scalar_prefetch=1,
-            grid=(rows // step,),
-            in_specs=[
-                pl.BlockSpec((step, QUERY_HEADS, HEAD_SIZE), lambda r, p: (r, 0, 0)),
-                pl.BlockSpec((step, 2 * KEY_HEADS, HEAD_SIZE), lambda r, p: (r, 0, 0)),
-            ]
-            + [pl.BlockSpec((1, 1, length, width), parent_of(b)) for b in range(step)]
-            + [pl.BlockSpec(memory_space=pl.ANY)],
-            out_specs=pl.BlockSpec((step, QUERY_HEADS, HEAD_SIZE), lambda r, p: (r, 0, 0)),
-        ),
-        out_shape=jax.ShapeDtypeStruct((rows, QUERY_HEADS, HEAD_SIZE), jnp.bfloat16),
-        compiler_params=params(40),
+    _, _, length, width = cached_key_value.shape
+    vmem = pl.BlockSpec(memory_space=pltpu.VMEM)
+    return pl.pallas_call(
+        attend_kernel,
+        in_specs=[pl.BlockSpec(memory_space=pltpu.SMEM), vmem, vmem, vmem]
+        + [pl.BlockSpec(memory_space=pl.ANY)],
+        out_specs=[vmem, vmem],
+        out_shape=[
+            jax.ShapeDtypeStruct(queries.shape, queries.dtype),
+            jax.ShapeDtypeStruct((8, LANES), jnp.float32),
+        ],
+        scratch_shapes=[
+            pltpu.VMEM((QUERY_HEADS * rows, HEAD_SIZE), jnp.float32),
+            pltpu.VMEM((2 * KEY_HEADS * rows, HEAD_SIZE), jnp.float32),
+            pltpu.VMEM((QUERY_HEADS * rows, HEAD_SIZE), jnp.float32),
+        ],
+        compiler_params=params(32),
         cost_estimate=pl.CostEstimate(
             flops=4 * rows * QUERY_HEADS * HEAD_SIZE * length,
             bytes_accessed=2 * rows * length * width,
             transcendentals=rows * QUERY_HEADS * length,
         ),
         name="attend",
-    )(
-        parents.reshape(-1),
-        queries.reshape(-1, QUERY_HEADS, HEAD_SIZE),
-        new_key_value.reshape(-1, 2 * KEY_HEADS, HEAD_SIZE),
-        *[cached_key_value] * step,
-        after,
-    )
-    return out
+    )(parents.reshape(rows), queries, new_key_value, cached_key_value, after)
 
 
 def spread(values, lanes, first):
@@ -385,14 +395,14 @@
         )
         others.append(traded(last[0], "inner", s))
     own, done = gate_up(level, inner, held, loaded, jnp.float32, True, last)
-    attended = attention(done)
+    attended, done = attention(done)
     active = call(
         activate_kernel,
         [],
         [own, *others],
         jax.ShapeDtypeStruct((experts, count, ff // inner), jnp.bfloat16),
         "activate",
-        after=[attended],
+        after=[done],
     )
     parts = trade([active] * inner, "inner")
     sums_shape = jax.ShapeDtypeStruct((experts, count, width), jnp.float32)
@@ -425,7 +435,7 @@
     outputs = jnp.einsum("sxf,xfd->xsd", active, down_weight, preferred_element_type=jnp.float32)
     outputs = outputs.astype(jnp.bfloat16).reshape(experts, owners, count // owners, -1)
     back = [outputs[:, t].reshape(experts * count // owners, -1) for t in range(owners)]
-    return back, attention(held)
+    return back, attention(held)[0]
 
 
 def body(
@@ -508,7 +518,7 @@
         jax.ShapeDtypeStruct((rows, model), jnp.bfloat16),
         "assemble",
     )
-    return attended.reshape(rows, QUERY_HEADS * HEAD_SIZE), expert_out
+    return attended, expert_out
 
 
 def solution(mesh):

time: 64.4 us -> 65.2 us (1.012)
  waiting for transfers between devices: 15.3 us -> 17.2 us
  starting transfers between devices: 22.8 us -> 21.9 us
  local copies, waits for them, and re-layouts: 8.38 us -> 7.63 us
    ppermute x18, waiting for transfers between devices: 15.3 us -> 17.2 us  [traded(): lax.ppermute(value, axis, [(i, i ^ index) for i in range(lax.axis_size(ax...]
    ppermute x18, starting transfers between devices: 22.8 us -> 21.9 us  [traded(): lax.ppermute(value, axis, [(i, i ^ index) for i in range(lax.axis_size(ax...]
    unnamed x25 -> x22, local copies, waits for them, and re-layouts: 8.38 us -> 7.63 us
  transfers between devices with their start and end apart: 18 -> 18, of which waited for: 9 -> 9; matrix products, arithmetic and copies ran while one was open for 1% -> 0% of each run, Pallas kernels for 21% -> 22%
where the time goes in v9:
time: 65.2 us; the launch traced here: 65 us
  starting transfers between devices  21.9 us (34%)
  Pallas kernels  17.3 us (27%)
  waiting for transfers between devices  17.2 us (26%)
  local copies, waits for them, and re-layouts  7.63 us (12%)
  between operations  0.92 us (1%)
    ppermute x18, starting transfers between devices, traded(): lax.ppermute(value, axis, [(i, i ^ index) for i in range(lax.axis_size(ax...  21.9 us
    ppermute x18, waiting for transfers between devices, traded(): lax.ppermute(value, axis, [(i, i ^ index) for i in range(lax.axis_size(ax...  17.2 us
    unnamed x22, local copies, waits for them, and re-layouts  7.63 us
    pallas_call x14, Pallas kernels, call(): pl.pallas_call(kernel, in_specs=[pl.BlockSpec(memory_space=pltpu.SMEM)] *...  5.98 us
    pallas_call x2, Pallas kernels, load(): pl.pallas_call(functools.partial(load_kernel, expert, pieces), in_specs=[...  5.8 us
    pallas_call x1, Pallas kernels, attend(): pl.pallas_call(attend_kernel, in_specs=[pl.BlockSpec(memory_space=pltpu.S...  5.53 us
  transfers between devices with their start and end apart: 18, of which 9 were waited for; matrix products, arithmetic and copies ran while one was open for 0% of the time, Pallas kernels for 22%

profile of v9, /device:TPU:0, one launch (start us, length us, event | category | flops | bytes accessed | tf_op | source)
XLA Modules:
  0.0 65.0 jit_solution(13472174567530683575)
XLA Ops:
  0.6 0.8 %copy-done.4 = bf16[8,4096]{1,0:T(8,128)(2,1)S(1)} copy-done((bf16[8,4096]{1,0:T(8,128)(2,1)S(1)}, bf16[8,4096]{1,0:T(8,128)(2,1)}, u32[]{:S(2)}) %copy-start.4) | copy-done | bytes 65560
  1.5 0.7 %copy-done.6 = s32[8,2]{0,1:T(2,128)S(1)} copy-done((s32[8,2]{0,1:T(2,128)S(1)}, s32[8,2]{0,1:T(2,128)}, u32[]{:S(2)}) %copy-start.6) | copy-done | bytes 88
  2.2 0.7 %copy-done.7 = bf16[8,2]{0,1:T(2,128)(2,1)S(1)} copy-done((bf16[8,2]{0,1:T(2,128)(2,1)S(1)}, bf16[8,2]{0,1:T(2,128)(2,1)}, u32[]{:S(2)}) %copy-start.7) | copy-done | bytes 56
  2.8 0.2 prepare.1
  3.0 3.0 %collective-permute-start = (bf16[8,1152]{1,0:T(8,128)(2,1)S(1)}, bf16[8,1152]{1,0:T(8,128)(2,1)S(1)}, u32[]{:S(2)}, u32[]{:S(2)}) collective-permute-start(bf16[8,1152]{1,0:T(8,128)(2,1)S(1)} %get-tuple-element.23), channel_id=1, source_target_pairs={{0,1},{1,0},{2,3},{3,2},{4,5},{5,4},{6,7},{7,6},{8,9},{9,8},{10,11... | collective-permute-start | bytes 55304 | tf_op jit(solution)/shard_map/ppermute | solution.py:356
  6.0 2.6 %collective-permute-start.1 = (bf16[8,1152]{1,0:T(8,128)(2,1)S(1)}, bf16[8,1152]{1,0:T(8,128)(2,1)S(1)}, u32[]{:S(2)}, u32[]{:S(2)}) collective-permute-start(bf16[8,1152]{1,0:T(8,128)(2,1)S(1)} %get-tuple-element.24), channel_id=1, source_target_pairs={{0,2},{1,3},{2,0},{3,1},{4,6},{5,7},{6,4},{7,5},{8,10},{9,11},{10,... | collective-permute-start | bytes 55304 | tf_op jit(solution)/shard_map/ppermute | solution.py:356
  8.6 2.9 %load.2.refs_4_.refs_1_.refs_0_ = bf16[2,1024,1536]{2,1,0:T(8,128)(2,1)S(1)} custom-call(bf16[2,2,1024,1536]{3,2,1,0:T(8,128)(2,1)} %weight_hbm.3, bf16[8,1152]{1,0:T(8,128)(2,1)S(1)} %get-tuple-element.22.refs_0_), custom_call_target="tpu_custom_call" | custom-call | flops 100000000 | tf_op jit(solution)/shard_map/load/pallas_call | solution.py:264
  11.5 2.6 %collective-permute-done.2.refs_3_ = bf16[8,1152]{1,0:T(8,128)(2,1)S(1)} collective-permute-done((bf16[8,1152]{1,0:T(8,128)(2,1)S(1)}, bf16[8,1152]{1,0:T(8,128)(2,1)S(1)}, u32[]{:S(2)}, u32[]{:S(2)}) %collective-permute-start.2) | collective-permute-done | bytes 18464 | tf_op jit(solution)/shard_map/ppermute | solution.py:356
  14.2 0.4 pack.1
  14.6 2.6 %copy-done = bf16[2,1024,1536]{2,1,0:T(8,128)(2,1)} copy-done((bf16[2,1024,1536]{2,1,0:T(8,128)(2,1)}, bf16[2,1024,1536]{2,1,0:T(8,128)(2,1)S(1)}, u32[]{:S(2)}) %copy-start) | copy-done | bytes 6291480
  17.2 1.5 %collective-permute-start.4 = (bf16[24,1024]{1,0:T(8,128)(2,1)S(1)}, bf16[24,1024]{1,0:T(8,128)(2,1)S(1)}, u32[]{:S(2)}, u32[]{:S(2)}) collective-permute-start(bf16[24,1024]{1,0:T(8,128)(2,1)S(1)} %get-tuple-element.28), channel_id=1, source_target_pairs={{0,8},{4,12},{8,0},{12,4},{1,9},{5,13},{9,1},{13,5},{2,10},{6,14},... | collective-permute-start | bytes 147464 | tf_op jit(solution)/shard_map/ppermute | solution.py:356
  18.7 0.4 collective-permute-start.5
  19.1 2.8 %copy-done.1 = bf16[2,1024,1536]{2,1,0:T(8,128)(2,1)S(1)} copy-done((bf16[2,1024,1536]{2,1,0:T(8,128)(2,1)S(1)}, bf16[2,1024,1536]{2,1,0:T(8,128)(2,1)}, u32[]{:S(2)}) %copy-start.1) | copy-done | bytes 6291480
  21.9 2.9 %load.3.refs_5_.refs_1_ = bf16[2,1024,1536]{2,1,0:T(8,128)(2,1)S(1)} custom-call(bf16[2,2,1024,1536]{3,2,1,0:T(8,128)(2,1)} %weight_hbm.3, bf16[24,1024]{1,0:T(8,128)(2,1)S(1)} %get-tuple-element.26.refs_0_, bf16[2,1024,1536]{2,1,0:T(8,128)(2,1)S(1)} %copy-done.1), custom_call_target="tpu_custom_call" | custom-call | flops 100000000 | tf_op jit(solution)/shard_map/load/pallas_call | solution.py:264
  24.8 0.2 select.1.rows_ref
  25.0 0.6 gate_up.4.refs_2_
  25.6 1.3 %collective-permute-start.6 = (bf16[2,48,768]{2,1,0:T(8,128)(2,1)S(1)}, bf16[2,48,768]{2,1,0:T(8,128)(2,1)S(1)}, u32[]{:S(2)}, u32[]{:S(2)}) collective-permute-start(bf16[2,48,768]{2,1,0:T(8,128)(2,1)S(1)} %gate_up.4.refs_2_), channel_id=1, source_target_pairs={{0,3},{1,2},{2,1},{3,0},{4,7},{5,6},{6,5},{7,4},{8,11},{9,10},{10,... | collective-permute-start | bytes 442376 | tf_op jit(solution)/shard_map/ppermute | solution.py:356
  26.9 0.6 gate_up.5.refs_2_
  27.5 0.1 collective-permute-start.7
  27.6 0.6 gate_up.6.refs_2_
  28.2 0.0 slice-start.1
  28.2 3.2 %collective-permute-start.8 = (bf16[2,48,768]{2,1,0:T(8,128)(2,1)S(1)}, bf16[2,48,768]{2,1,0:T(8,128)(2,1)S(1)}, u32[]{:S(2)}, u32[]{:S(2)}) collective-permute-start(bf16[2,48,768]{2,1,0:T(8,128)(2,1)S(1)} %gate_up.6.refs_2_), channel_id=1, source_target_pairs={{0,1},{1,0},{2,3},{3,2},{4,5},{5,4},{6,7},{7,6},{8,9},{9,8},{10,11... | collective-permute-start | bytes 442376 | tf_op jit(solution)/shard_map/ppermute | solution.py:356
  31.4 0.6 gate_up.7
  32.0 5.5 %attend.1 = (bf16[8,8192]{1,0:T(8,128)(2,1)}, f32[8,128]{1,0:T(8,128)S(1)}) custom-call(s32[8]{0:T(128)S(1)} %bitcast.12, bf16[8,8192]{1,0:T(8,128)(2,1)S(1)} %copy-done.3, bf16[8,1024]{1,0:T(8,128)(2,1)S(1)} %copy-done.5, bf16[1,8,192,1024]{3,2,1,0:T(8,128)(2,1)S(1)} %copy-done.2, f32[8,128]{1,0:T(8,128)S(1)} %get-tuple-element.30.after_ref), custom_call_target="tpu_custom_call" | custom-call | flops 50331648 | bytes 3145728 | tf_op jit(solution)/shard_map/attend/pallas_call | solution.py:85
  37.6 2.2 %collective-permute-done.7.refs_1_ = bf16[2,48,768]{2,1,0:T(8,128)(2,1)S(1)} collective-permute-done((bf16[2,48,768]{2,1,0:T(8,128)(2,1)S(1)}, bf16[2,48,768]{2,1,0:T(8,128)(2,1)S(1)}, u32[]{:S(2)}, u32[]{:S(2)}) %collective-permute-start.7) | collective-permute-done | bytes 147488 | tf_op jit(solution)/shard_map/ppermute | solution.py:356
  39.8 0.1 activate.1.part_ref
  39.9 0.1 collective-permute-start.9
  40.0 2.1 %collective-permute-start.11 = (bf16[2,48,384]{2,1,0:T(8,128)(2,1)S(1)}, bf16[2,48,384]{2,1,0:T(8,128)(2,1)S(1)}, u32[]{:S(2)}, u32[]{:S(2)}) collective-permute-start(bf16[2,48,384]{2,1,0:T(8,128)(2,1)S(1)} %activate.1.part_ref), channel_id=1, source_target_pairs={{0,3},{1,2},{2,1},{3,0},{4,7},{5,6},{6,5},{7,4},{8,11},{9,10},{10,... | collective-permute-start | bytes 221192 | tf_op jit(solution)/shard_map/ppermute | solution.py:356
  42.1 1.4 %collective-permute-start.10 = (bf16[2,48,384]{2,1,0:T(8,128)(2,1)S(1)}, bf16[2,48,384]{2,1,0:T(8,128)(2,1)S(1)}, u32[]{:S(2)}, u32[]{:S(2)}) collective-permute-start(bf16[2,48,384]{2,1,0:T(8,128)(2,1)S(1)} %activate.1.part_ref), channel_id=1, source_target_pairs={{0,2},{1,3},{2,0},{3,1},{4,6},{5,7},{6,4},{7,5},{8,10},{9,11},{10,... | collective-permute-start | bytes 221192 | tf_op jit(solution)/shard_map/ppermute | solution.py:356
  43.5 0.4 down_first.1.before_ref
  43.9 0.5 collective-permute-done.9.part_ref
  44.4 0.4 down_more.1.sum_ref
  44.8 2.2 %collective-permute-done.11.refs_1_ = bf16[2,48,384]{2,1,0:T(8,128)(2,1)S(1)} collective-permute-done((bf16[2,48,384]{2,1,0:T(8,128)(2,1)S(1)}, bf16[2,48,384]{2,1,0:T(8,128)(2,1)S(1)}, u32[]{:S(2)}, u32[]{:S(2)}) %collective-permute-start.11) | collective-permute-done | bytes 73760 | tf_op jit(solution)/shard_map/ppermute | solution.py:356
  47.0 3.2 %collective-permute-done.10.refs_0_ = bf16[2,48,384]{2,1,0:T(8,128)(2,1)S(1)} collective-permute-done((bf16[2,48,384]{2,1,0:T(8,128)(2,1)S(1)}, bf16[2,48,384]{2,1,0:T(8,128)(2,1)S(1)}, u32[]{:S(2)}, u32[]{:S(2)}) %collective-permute-start.10) | collective-permute-done | bytes 73760 | tf_op jit(solution)/shard_map/ppermute | solution.py:356
  50.1 0.8 %down_rest.1 = (bf16[24,1024]{1,0:T(8,128)(2,1)S(1)}, bf16[24,1024]{1,0:T(8,128)(2,1)S(1)}, bf16[24,1024]{1,0:T(8,128)(2,1)S(1)}, bf16[24,1024]{1,0:T(8,128)(2,1)S(1)}) custom-call(s32[1]{0:T(128)} %bitcast.1.me.level.chunk, f32[2,48,1024]{2,1,0:T(8,128)S(1)} %down_more.1.sum_ref, bf16[2,48,384]{2,1,0:T(8,128)(2,1)S(1)} %collective-permute-done.10.refs_0_, ...), custom_call_target="tpu_custom_call" | custom-call | tf_op jit(solution)/shard_map/down_rest/pallas_call | solution.py:368
  51.0 0.1 collective-permute-start.12
  51.0 1.6 %collective-permute-start.13 = (bf16[24,1024]{1,0:T(8,128)(2,1)S(1)}, bf16[24,1024]{1,0:T(8,128)(2,1)S(1)}, u32[]{:S(2)}, u32[]{:S(2)}) collective-permute-start(bf16[24,1024]{1,0:T(8,128)(2,1)S(1)} %get-tuple-element.36), channel_id=1, source_target_pairs={{0,8},{4,12},{8,0},{12,4},{1,9},{5,13},{9,1},{13,5},{2,10},{6,14},... | collective-permute-start | bytes 147464 | tf_op jit(solution)/shard_map/ppermute | solution.py:356
  52.6 0.3 collective-permute-start.14
  52.9 0.3 weigh.1.weight_ref
  53.2 2.0 %collective-permute-done.13.refs_2_ = bf16[24,1024]{1,0:T(8,128)(2,1)S(1)} collective-permute-done((bf16[24,1024]{1,0:T(8,128)(2,1)S(1)}, bf16[24,1024]{1,0:T(8,128)(2,1)S(1)}, u32[]{:S(2)}, u32[]{:S(2)}) %collective-permute-start.13) | collective-permute-done | bytes 49184 | tf_op jit(solution)/shard_map/ppermute | solution.py:356
  55.2 1.1 %collective-permute-done.14.refs_3_ = bf16[24,1024]{1,0:T(8,128)(2,1)S(1)} collective-permute-done((bf16[24,1024]{1,0:T(8,128)(2,1)S(1)}, bf16[24,1024]{1,0:T(8,128)(2,1)S(1)}, u32[]{:S(2)}, u32[]{:S(2)}) %collective-permute-start.14) | collective-permute-done | bytes 49184 | tf_op jit(solution)/shard_map/ppermute | solution.py:356
  56.3 0.2 combine.1
  56.5 0.1 collective-permute-start.15
  56.6 2.2 %collective-permute-start.16 = (bf16[8,1024]{1,0:T(8,128)(2,1)S(1)}, bf16[8,1024]{1,0:T(8,128)(2,1)S(1)}, u32[]{:S(2)}, u32[]{:S(2)}) collective-permute-start(bf16[8,1024]{1,0:T(8,128)(2,1)S(1)} %get-tuple-element.40), channel_id=1, source_target_pairs={{0,2},{1,3},{2,0},{3,1},{4,6},{5,7},{6,4},{7,5},{8,10},{9,11},{10,... | collective-permute-start | bytes 49160 | tf_op jit(solution)/shard_map/ppermute | solution.py:356
  58.8 2.1 %collective-permute-start.17 = (bf16[8,1024]{1,0:T(8,128)(2,1)S(1)}, bf16[8,1024]{1,0:T(8,128)(2,1)S(1)}, u32[]{:S(2)}, u32[]{:S(2)}) collective-permute-start(bf16[8,1024]{1,0:T(8,128)(2,1)S(1)} %get-tuple-element.41), channel_id=1, source_target_pairs={{0,3},{1,2},{2,1},{3,0},{4,7},{5,6},{6,5},{7,4},{8,11},{9,10},{10,... | collective-permute-start | bytes 49160 | tf_op jit(solution)/shard_map/ppermute | solution.py:356
  61.0 0.3 collective-permute-done.16.refs_2_
  61.3 3.1 %collective-permute-done.17.refs_3_ = bf16[8,1024]{1,0:T(8,128)(2,1)S(1)} collective-permute-done((bf16[8,1024]{1,0:T(8,128)(2,1)S(1)}, bf16[8,1024]{1,0:T(8,128)(2,1)S(1)}, u32[]{:S(2)}, u32[]{:S(2)}) %collective-permute-start.17) | collective-permute-done | bytes 16416 | tf_op jit(solution)/shard_map/ppermute | solution.py:356
  64.4 0.6 assemble.1
  (28 shorter events, 0.1 us)
Async XLA Ops:
  0.6 0.8 %copy-start.4 = (bf16[8,4096]{1,0:T(8,128)(2,1)S(1)}, bf16[8,4096]{1,0:T(8,128)(2,1)}, u32[]{:S(2)}) copy-start(bf16[8,4096]{1,0:T(8,128)(2,1)} %hidden_ref.1) | copy-start | bytes 196612
  1.5 0.7 %copy-start.6 = (s32[8,2]{0,1:T(2,128)S(1)}, s32[8,2]{0,1:T(2,128)}, u32[]{:S(2)}) copy-start(s32[8,2]{0,1:T(2,128)} %param.14) | copy-start | bytes 196
  2.2 0.7 %copy-start.7 = (bf16[8,2]{0,1:T(2,128)(2,1)S(1)}, bf16[8,2]{0,1:T(2,128)(2,1)}, u32[]{:S(2)}) copy-start(bf16[8,2]{0,1:T(2,128)(2,1)} %param.15) | copy-start | bytes 100
  3.0 8.5 %collective-permute-start = (bf16[8,1152]{1,0:T(8,128)(2,1)S(1)}, bf16[8,1152]{1,0:T(8,128)(2,1)S(1)}, u32[]{:S(2)}, u32[]{:S(2)}) collective-permute-start(bf16[8,1152]{1,0:T(8,128)(2,1)S(1)} %get-tuple-element.23), channel_id=1, source_target_pairs={{0,1},{1,0},{2,3},{3,2},{4,5},{5,4},{6,7},{7,6},{8,9},{9,8},{10,11... | collective-permute-start | bytes 55304 | tf_op jit(solution)/shard_map/ppermute | solution.py:356
  6.0 5.5 %collective-permute-start.1 = (bf16[8,1152]{1,0:T(8,128)(2,1)S(1)}, bf16[8,1152]{1,0:T(8,128)(2,1)S(1)}, u32[]{:S(2)}, u32[]{:S(2)}) collective-permute-start(bf16[8,1152]{1,0:T(8,128)(2,1)S(1)} %get-tuple-element.24), channel_id=1, source_target_pairs={{0,2},{1,3},{2,0},{3,1},{4,6},{5,7},{6,4},{7,5},{8,10},{9,11},{10,... | collective-permute-start | bytes 55304 | tf_op jit(solution)/shard_map/ppermute | solution.py:356
  8.6 5.6 %collective-permute-start.2 = (bf16[8,1152]{1,0:T(8,128)(2,1)S(1)}, bf16[8,1152]{1,0:T(8,128)(2,1)S(1)}, u32[]{:S(2)}, u32[]{:S(2)}) collective-permute-start(bf16[8,1152]{1,0:T(8,128)(2,1)S(1)} %get-tuple-element.25), channel_id=1, source_target_pairs={{0,3},{1,2},{2,1},{3,0},{4,7},{5,6},{6,5},{7,4},{8,11},{9,10},{10,... | collective-permute-start | bytes 55304 | tf_op jit(solution)/shard_map/ppermute | solution.py:356
  14.6 2.6 %copy-start = (bf16[2,1024,1536]{2,1,0:T(8,128)(2,1)}, bf16[2,1024,1536]{2,1,0:T(8,128)(2,1)S(1)}, u32[]{:S(2)}) copy-start(bf16[2,1024,1536]{2,1,0:T(8,128)(2,1)S(1)} %load.2.refs_4_.refs_1_.refs_0_) | copy-start | bytes 18874372
  17.2 7.6 %collective-permute-start.3 = (bf16[24,1024]{1,0:T(8,128)(2,1)S(1)}, bf16[24,1024]{1,0:T(8,128)(2,1)S(1)}, u32[]{:S(2)}, u32[]{:S(2)}) collective-permute-start(bf16[24,1024]{1,0:T(8,128)(2,1)S(1)} %get-tuple-element.27), channel_id=1, source_target_pairs={{0,4},{4,0},{8,12},{12,8},{1,5},{5,1},{9,13},{13,9},{2,6},{6,2},{1... | collective-permute-start | bytes 147464 | tf_op jit(solution)/shard_map/ppermute | solution.py:356
  17.2 7.6 %collective-permute-start.4 = (bf16[24,1024]{1,0:T(8,128)(2,1)S(1)}, bf16[24,1024]{1,0:T(8,128)(2,1)S(1)}, u32[]{:S(2)}, u32[]{:S(2)}) collective-permute-start(bf16[24,1024]{1,0:T(8,128)(2,1)S(1)} %get-tuple-element.28), channel_id=1, source_target_pairs={{0,8},{4,12},{8,0},{12,4},{1,9},{5,13},{9,1},{13,5},{2,10},{6,14},... | collective-permute-start | bytes 147464 | tf_op jit(solution)/shard_map/ppermute | solution.py:356
  18.7 6.1 %collective-permute-start.5 = (bf16[24,1024]{1,0:T(8,128)(2,1)S(1)}, bf16[24,1024]{1,0:T(8,128)(2,1)S(1)}, u32[]{:S(2)}, u32[]{:S(2)}) collective-permute-start(bf16[24,1024]{1,0:T(8,128)(2,1)S(1)} %get-tuple-element.29), channel_id=1, source_target_pairs={{0,12},{4,8},{8,4},{12,0},{1,13},{5,9},{9,5},{13,1},{2,14},{6,10},... | collective-permute-start | bytes 147464 | tf_op jit(solution)/shard_map/ppermute | solution.py:356
  19.1 2.8 %copy-start.1 = (bf16[2,1024,1536]{2,1,0:T(8,128)(2,1)S(1)}, bf16[2,1024,1536]{2,1,0:T(8,128)(2,1)}, u32[]{:S(2)}) copy-start(bf16[2,1024,1536]{2,1,0:T(8,128)(2,1)} %copy-done) | copy-start | bytes 18874372
  25.6 14.2 %collective-permute-start.6 = (bf16[2,48,768]{2,1,0:T(8,128)(2,1)S(1)}, bf16[2,48,768]{2,1,0:T(8,128)(2,1)S(1)}, u32[]{:S(2)}, u32[]{:S(2)}) collective-permute-start(bf16[2,48,768]{2,1,0:T(8,128)(2,1)S(1)} %gate_up.4.refs_2_), channel_id=1, source_target_pairs={{0,3},{1,2},{2,1},{3,0},{4,7},{5,6},{6,5},{7,4},{8,11},{9,10},{10,... | collective-permute-start | bytes 442376 | tf_op jit(solution)/shard_map/ppermute | solution.py:356
  27.5 12.3 %collective-permute-start.7 = (bf16[2,48,768]{2,1,0:T(8,128)(2,1)S(1)}, bf16[2,48,768]{2,1,0:T(8,128)(2,1)S(1)}, u32[]{:S(2)}, u32[]{:S(2)}) collective-permute-start(bf16[2,48,768]{2,1,0:T(8,128)(2,1)S(1)} %gate_up.5.refs_2_), channel_id=1, source_target_pairs={{0,2},{1,3},{2,0},{3,1},{4,6},{5,7},{6,4},{7,5},{8,10},{9,11},{10,... | collective-permute-start | bytes 442376 | tf_op jit(solution)/shard_map/ppermute | solution.py:356
  27.6 15.9 %slice-start = ((s8[6291456]{0:T(1024)(128)(4,1)}), s8[4194304]{0:T(1024)(128)(4,1)S(1)}, s32[]{:S(2)}) async-start(s8[6291456]{0:T(1024)(128)(4,1)} %bitcast.8), calls=%async_computation | async-start | bytes 8388608
  28.2 3.8 %copy-start.2 = (bf16[1,8,192,1024]{3,2,1,0:T(8,128)(2,1)S(1)}, bf16[1,8,192,1024]{3,2,1,0:T(8,128)(2,1)}, u32[]{:S(2)}) copy-start(bf16[1,8,192,1024]{3,2,1,0:T(8,128)(2,1)} %cache_ref.1) | copy-start | bytes 9437188
  28.2 3.8 %copy-start.3 = (bf16[8,8192]{1,0:T(8,128)(2,1)S(1)}, bf16[8,8192]{1,0:T(8,128)(2,1)}, u32[]{:S(2)}) copy-start(bf16[8,8192]{1,0:T(8,128)(2,1)} %q_ref.1) | copy-start | bytes 393220
  28.2 3.8 %copy-start.5 = (bf16[8,1024]{1,0:T(8,128)(2,1)S(1)}, bf16[8,1024]{1,0:T(8,128)(2,1)}, u32[]{:S(2)}) copy-start(bf16[8,1024]{1,0:T(8,128)(2,1)} %new_ref.1) | copy-start | bytes 49156
  28.2 3.8 %copy-start.8 = (s32[1,8]{1,0:T(1,128)S(1)}, s32[1,8]{1,0:T(1,128)}, u32[]{:S(2)}) copy-start(s32[1,8]{1,0:T(1,128)} %param.12) | copy-start | bytes 100
  28.2 15.3 %slice-start.1 = ((s8[6291456]{0:T(1024)(128)(4,1)}), s8[2097152]{0:T(1024)(128)(4,1)S(1)}, s32[]{:S(2)}) async-start(s8[6291456]{0:T(1024)(128)(4,1)} %bitcast.8), calls=%async_computation.1 | async-start | bytes 4194304
  28.2 9.3 %collective-permute-start.8 = (bf16[2,48,768]{2,1,0:T(8,128)(2,1)S(1)}, bf16[2,48,768]{2,1,0:T(8,128)(2,1)S(1)}, u32[]{:S(2)}, u32[]{:S(2)}) collective-permute-start(bf16[2,48,768]{2,1,0:T(8,128)(2,1)S(1)} %gate_up.6.refs_2_), channel_id=1, source_target_pairs={{0,1},{1,0},{2,3},{3,2},{4,5},{5,4},{6,7},{7,6},{8,9},{9,8},{10,11... | collective-permute-start | bytes 442376 | tf_op jit(solution)/shard_map/ppermute | solution.py:356
  39.9 4.4 %collective-permute-start.9 = (bf16[2,48,384]{2,1,0:T(8,128)(2,1)S(1)}, bf16[2,48,384]{2,1,0:T(8,128)(2,1)S(1)}, u32[]{:S(2)}, u32[]{:S(2)}) collective-permute-start(bf16[2,48,384]{2,1,0:T(8,128)(2,1)S(1)} %activate.1.part_ref), channel_id=1, source_target_pairs={{0,1},{1,0},{2,3},{3,2},{4,5},{5,4},{6,7},{7,6},{8,9},{9,8},{10,11... | collective-permute-start | bytes 221192 | tf_op jit(solution)/shard_map/ppermute | solution.py:356
  40.0 7.0 %collective-permute-start.11 = (bf16[2,48,384]{2,1,0:T(8,128)(2,1)S(1)}, bf16[2,48,384]{2,1,0:T(8,128)(2,1)S(1)}, u32[]{:S(2)}, u32[]{:S(2)}) collective-permute-start(bf16[2,48,384]{2,1,0:T(8,128)(2,1)S(1)} %activate.1.part_ref), channel_id=1, source_target_pairs={{0,3},{1,2},{2,1},{3,0},{4,7},{5,6},{6,5},{7,4},{8,11},{9,10},{10,... | collective-permute-start | bytes 221192 | tf_op jit(solution)/shard_map/ppermute | solution.py:356
  42.1 8.0 %collective-permute-start.10 = (bf16[2,48,384]{2,1,0:T(8,128)(2,1)S(1)}, bf16[2,48,384]{2,1,0:T(8,128)(2,1)S(1)}, u32[]{:S(2)}, u32[]{:S(2)}) collective-permute-start(bf16[2,48,384]{2,1,0:T(8,128)(2,1)S(1)} %activate.1.part_ref), channel_id=1, source_target_pairs={{0,2},{1,3},{2,0},{3,1},{4,6},{5,7},{6,4},{7,5},{8,10},{9,11},{10,... | collective-permute-start | bytes 221192 | tf_op jit(solution)/shard_map/ppermute | solution.py:356
  51.0 2.2 %collective-permute-start.12 = (bf16[24,1024]{1,0:T(8,128)(2,1)S(1)}, bf16[24,1024]{1,0:T(8,128)(2,1)S(1)}, u32[]{:S(2)}, u32[]{:S(2)}) collective-permute-start(bf16[24,1024]{1,0:T(8,128)(2,1)S(1)} %get-tuple-element.35), channel_id=1, source_target_pairs={{0,4},{4,0},{8,12},{12,8},{1,5},{5,1},{9,13},{13,9},{2,6},{6,2},{1... | collective-permute-start | bytes 147464 | tf_op jit(solution)/shard_map/ppermute | solution.py:356
  51.0 4.2 %collective-permute-start.13 = (bf16[24,1024]{1,0:T(8,128)(2,1)S(1)}, bf16[24,1024]{1,0:T(8,128)(2,1)S(1)}, u32[]{:S(2)}, u32[]{:S(2)}) collective-permute-start(bf16[24,1024]{1,0:T(8,128)(2,1)S(1)} %get-tuple-element.36), channel_id=1, source_target_pairs={{0,8},{4,12},{8,0},{12,4},{1,9},{5,13},{9,1},{13,5},{2,10},{6,14},... | collective-permute-start | bytes 147464 | tf_op jit(solution)/shard_map/ppermute | solution.py:356
  52.6 3.7 %collective-permute-start.14 = (bf16[24,1024]{1,0:T(8,128)(2,1)S(1)}, bf16[24,1024]{1,0:T(8,128)(2,1)S(1)}, u32[]{:S(2)}, u32[]{:S(2)}) collective-permute-start(bf16[24,1024]{1,0:T(8,128)(2,1)S(1)} %get-tuple-element.37), channel_id=1, source_target_pairs={{0,12},{4,8},{8,4},{12,0},{1,13},{5,9},{9,5},{13,1},{2,14},{6,10},... | collective-permute-start | bytes 147464 | tf_op jit(solution)/shard_map/ppermute | solution.py:356
  56.5 4.5 %collective-permute-start.15 = (bf16[8,1024]{1,0:T(8,128)(2,1)S(1)}, bf16[8,1024]{1,0:T(8,128)(2,1)S(1)}, u32[]{:S(2)}, u32[]{:S(2)}) collective-permute-start(bf16[8,1024]{1,0:T(8,128)(2,1)S(1)} %get-tuple-element.39), channel_id=1, source_target_pairs={{0,1},{1,0},{2,3},{3,2},{4,5},{5,4},{6,7},{7,6},{8,9},{9,8},{10,11... | collective-permute-start | bytes 49160 | tf_op jit(solution)/shard_map/ppermute | solution.py:356
  56.6 4.7 %collective-permute-start.16 = (bf16[8,1024]{1,0:T(8,128)(2,1)S(1)}, bf16[8,1024]{1,0:T(8,128)(2,1)S(1)}, u32[]{:S(2)}, u32[]{:S(2)}) collective-permute-start(bf16[8,1024]{1,0:T(8,128)(2,1)S(1)} %get-tuple-element.40), channel_id=1, source_target_pairs={{0,2},{1,3},{2,0},{3,1},{4,6},{5,7},{6,4},{7,5},{8,10},{9,11},{10,... | collective-permute-start | bytes 49160 | tf_op jit(solution)/shard_map/ppermute | solution.py:356
  58.8 5.5 %collective-permute-start.17 = (bf16[8,1024]{1,0:T(8,128)(2,1)S(1)}, bf16[8,1024]{1,0:T(8,128)(2,1)S(1)}, u32[]{:S(2)}, u32[]{:S(2)}) collective-permute-start(bf16[8,1024]{1,0:T(8,128)(2,1)S(1)} %get-tuple-element.41), channel_id=1, source_target_pairs={{0,3},{1,2},{2,1},{3,0},{4,7},{5,6},{6,5},{7,4},{8,11},{9,10},{10,... | collective-permute-start | bytes 49160 | tf_op jit(solution)/shard_map/ppermute | solution.py:356

commit v10 on v9

--- a/solution.py
+++ b/solution.py
@@ -165,8 +165,8 @@
     return jnp.where(ranks == rank.astype(jnp.float32), member, 0.0), expert
 
 
-def pack_kernel(top, experts, sources, afters, column, level, *refs):
-    held, out_refs = refs[:sources], refs[sources + afters:]
+def pack_kernel(top, experts, sources, column, level, *refs):
+    held, out_refs = refs[:sources], refs[sources:]
     slots, width = out_refs[0].shape
     rows = jnp.concatenate([ref[:, :width] for ref in held], axis=0)
     notes = jnp.concatenate([ref[:, width:] for ref in held], axis=0)
@@ -241,15 +241,18 @@
         out_ref[x] = moved[x * count:(x + 1) * count]
 
 
-def load_kernel(expert, pieces, weight_hbm, *refs):
-    out_ref, sems = refs[-2:]
-    step = out_ref.shape[1] // pieces
+def load_kernel(pieces, weight_hbm, after_ref, *refs):
+    del after_ref
+    out_refs, done_ref, sems = refs[:-2], refs[-2], refs[-1]
+    done_ref[...] = jnp.zeros_like(done_ref)
+    step = weight_hbm.shape[2] // pieces
     copies = [
         pltpu.make_async_copy(
-            weight_hbm.at[expert, k, pl.ds(n * step, step)],
+            weight_hbm.at[x, k, pl.ds(n * step, step)],
             out_ref.at[k, pl.ds(n * step, step)],
-            sems.at[k * pieces + n],
+            sems.at[(x * 2 + k) * pieces + n],
         )
+        for x, out_ref in enumerate(out_refs)
         for k in range(2)
         for n in range(pieces)
     ]
@@ -259,18 +262,19 @@
         copy.wait()
 
 
-def load(weight, expert, after, limit):
-    pieces = 8
+def load(weight, after):
+    experts, pieces = weight.shape[0], 4
     return pl.pallas_call(
-        functools.partial(load_kernel, expert, pieces),
-        in_specs=[pl.BlockSpec(memory_space=pl.ANY)] * (1 + len(after)),
-        out_specs=pl.BlockSpec(memory_space=pltpu.VMEM),
-        out_shape=jax.ShapeDtypeStruct(weight.shape[1:], weight.dtype),
-        scratch_shapes=[pltpu.SemaphoreType.DMA((2 * pieces,))],
-        compiler_params=params(limit),
+        functools.partial(load_kernel, pieces),
+        in_specs=[pl.BlockSpec(memory_space=pl.ANY)] * 2,
+        out_specs=[pl.BlockSpec(memory_space=pltpu.VMEM)] * (experts + 1),
+        out_shape=[jax.ShapeDtypeStruct(weight.shape[1:], weight.dtype)] * experts
+        + [jax.ShapeDtypeStruct((8, LANES), jnp.float32)],
+        scratch_shapes=[pltpu.SemaphoreType.DMA((experts * 2 * pieces,))],
+        compiler_params=params(40),
         cost_estimate=pl.CostEstimate(flops=10**8, bytes_accessed=0, transcendentals=0),
         name="load",
-    )(weight, *after)
+    )(weight, after)
 
 
 def gate_up_kernel(experts, afters, chunk, rows_ref, *refs):
@@ -408,17 +412,18 @@
     sums_shape = jax.ShapeDtypeStruct((experts, count, width), jnp.float32)
     sums = call(down_first_kernel, [level], [active, down_weight], sums_shape, "down_first", 24)
     sums = call(
-        functools.partial(down_more_kernel, 1),
+        functools.partial(down_more_kernel, inner - 1),
         [level],
-        [sums, parts[1], down_weight],
+        [sums, parts[-1], down_weight],
         sums_shape,
         "down_more",
         24,
     )
+    rest = list(range(1, inner - 1))
     back = call(
-        functools.partial(down_rest_kernel, list(range(2, inner))),
+        functools.partial(down_rest_kernel, rest),
         [level],
-        [sums, *parts[2:], down_weight],
+        [sums, *[parts[s] for s in rest], down_weight],
         [jax.ShapeDtypeStruct((experts * count // owners, width), jnp.bfloat16)] * owners,
         "down_rest",
         24,
@@ -468,19 +473,15 @@
         "prepare",
     )
     even = ff % (inner * LANES) == 0
-    loaded = [load(gate_up_weight, 0, slices[:1], 45)] if even else []
     slices = trade(slices, "inner")
     packs = call(
-        functools.partial(pack_kernel, top, experts, inner, len(loaded)),
+        functools.partial(pack_kernel, top, experts, inner),
         [column, level],
         slices,
         [jax.ShapeDtypeStruct((slots, depth), jnp.bfloat16)] * owners,
         "pack",
-        after=loaded,
-    )
-    if even:
-        for x in range(1, experts):
-            loaded = loaded + [load(gate_up_weight, x, [packs[0], *loaded], 40)]
+    )
+    *loaded, done = load(gate_up_weight, packs[0]) if even else [None]
     packs = trade(packs, "expert")
     held = call(
         functools.partial(select_kernel, owners),
@@ -489,7 +490,7 @@
         jax.ShapeDtypeStruct((experts, owners * CAP * inner, depth), jnp.bfloat16),
         "select",
         24,
-        after=loaded,
+        after=[done] if even else [],
     )
     back, attended = (experts_by_columns if even else experts_by_rows)(
         held, loaded or gate_up_weight, down_weight, owners, attention

time: 65.2 us -> 60.6 us (0.929)
  local copies, waits for them, and re-layouts: 7.63 us -> 2.21 us
  Pallas kernels: 17.3 us -> 16.2 us
  starting transfers between devices: 21.9 us -> 22.9 us
  waiting for transfers between devices: 17.2 us -> 18.1 us
    unnamed x22 -> x18, local copies, waits for them, and re-layouts: 7.63 us -> 2.21 us
    pallas_call x2 -> x1, Pallas kernels: 5.8 us -> 4.72 us  [load(): pl.pallas_call(functools.partial(load_kernel, pieces), in_specs=[pl.Block...]
    ppermute x18, starting transfers between devices: 21.9 us -> 22.9 us  [traded(): lax.ppermute(value, axis, [(i, i ^ index) for i in range(lax.axis_size(ax...]
    ppermute x18, waiting for transfers between devices: 17.2 us -> 18.1 us  [traded(): lax.ppermute(value, axis, [(i, i ^ index) for i in range(lax.axis_size(ax...]
where the time goes in v10:
time: 60.6 us; the launch traced here: 60.4 us
  starting transfers between devices  22.9 us (38%)
  waiting for transfers between devices  18.1 us (30%)
  Pallas kernels  16.2 us (27%)
  local copies, waits for them, and re-layouts  2.21 us (4%)
  between operations  0.88 us (1%)
    ppermute x18, starting transfers between devices, traded(): lax.ppermute(value, axis, [(i, i ^ index) for i in range(lax.axis_size(ax...  22.9 us
    ppermute x18, waiting for transfers between devices, traded(): lax.ppermute(value, axis, [(i, i ^ index) for i in range(lax.axis_size(ax...  18.1 us
    pallas_call x14, Pallas kernels, call(): pl.pallas_call(kernel, in_specs=[pl.BlockSpec(memory_space=pltpu.SMEM)] *...  5.99 us
    pallas_call x1, Pallas kernels, attend(): pl.pallas_call(attend_kernel, in_specs=[pl.BlockSpec(memory_space=pltpu.S...  5.53 us
    pallas_call x1, Pallas kernels, load(): pl.pallas_call(functools.partial(load_kernel, pieces), in_specs=[pl.Block...  4.72 us
    unnamed x18, local copies, waits for them, and re-layouts  2.21 us
  transfers between devices with their start and end apart: 18, of which 9 were waited for; matrix products, arithmetic and copies ran while one was open for 0% of the time, Pallas kernels for 22%

profile of v10, /device:TPU:0, one launch (start us, length us, event | category | flops | bytes accessed | tf_op | source)
XLA Modules:
  0.0 60.4 jit_solution(2999700633317119561)
XLA Ops:
  0.6 0.8 %copy-done.2 = bf16[8,4096]{1,0:T(8,128)(2,1)S(1)} copy-done((bf16[8,4096]{1,0:T(8,128)(2,1)S(1)}, bf16[8,4096]{1,0:T(8,128)(2,1)}, u32[]{:S(2)}) %copy-start.2) | copy-done | bytes 65560
  1.5 0.7 %copy-done.4 = s32[8,2]{0,1:T(2,128)S(1)} copy-done((s32[8,2]{0,1:T(2,128)S(1)}, s32[8,2]{0,1:T(2,128)}, u32[]{:S(2)}) %copy-start.4) | copy-done | bytes 88
  2.2 0.7 %copy-done.5 = bf16[8,2]{0,1:T(2,128)(2,1)S(1)} copy-done((bf16[8,2]{0,1:T(2,128)(2,1)S(1)}, bf16[8,2]{0,1:T(2,128)(2,1)}, u32[]{:S(2)}) %copy-start.5) | copy-done | bytes 56
  2.8 0.2 prepare.1
  3.0 3.0 %collective-permute-start = (bf16[8,1152]{1,0:T(8,128)(2,1)S(1)}, bf16[8,1152]{1,0:T(8,128)(2,1)S(1)}, u32[]{:S(2)}, u32[]{:S(2)}) collective-permute-start(bf16[8,1152]{1,0:T(8,128)(2,1)S(1)} %get-tuple-element.26), channel_id=1, source_target_pairs={{0,1},{1,0},{2,3},{3,2},{4,5},{5,4},{6,7},{7,6},{8,9},{9,8},{10,11... | collective-permute-start | bytes 55304 | tf_op jit(solution)/shard_map/ppermute | solution.py:360
  6.0 2.6 %collective-permute-start.1 = (bf16[8,1152]{1,0:T(8,128)(2,1)S(1)}, bf16[8,1152]{1,0:T(8,128)(2,1)S(1)}, u32[]{:S(2)}, u32[]{:S(2)}) collective-permute-start(bf16[8,1152]{1,0:T(8,128)(2,1)S(1)} %get-tuple-element.27), channel_id=1, source_target_pairs={{0,2},{1,3},{2,0},{3,1},{4,6},{5,7},{6,4},{7,5},{8,10},{9,11},{10,... | collective-permute-start | bytes 55304 | tf_op jit(solution)/shard_map/ppermute | solution.py:360
  8.6 2.2 %collective-permute-done.1.refs_2_ = bf16[8,1152]{1,0:T(8,128)(2,1)S(1)} collective-permute-done((bf16[8,1152]{1,0:T(8,128)(2,1)S(1)}, bf16[8,1152]{1,0:T(8,128)(2,1)S(1)}, u32[]{:S(2)}, u32[]{:S(2)}) %collective-permute-start.1) | collective-permute-done | bytes 18464 | tf_op jit(solution)/shard_map/ppermute | solution.py:360
  10.8 3.3 %collective-permute-done.2.refs_3_ = bf16[8,1152]{1,0:T(8,128)(2,1)S(1)} collective-permute-done((bf16[8,1152]{1,0:T(8,128)(2,1)S(1)}, bf16[8,1152]{1,0:T(8,128)(2,1)S(1)}, u32[]{:S(2)}, u32[]{:S(2)}) %collective-permute-start.2) | collective-permute-done | bytes 18464 | tf_op jit(solution)/shard_map/ppermute | solution.py:360
  14.2 0.4 pack.1
  14.6 0.1 collective-permute-start.3
  14.7 1.6 %collective-permute-start.4 = (bf16[24,1024]{1,0:T(8,128)(2,1)S(1)}, bf16[24,1024]{1,0:T(8,128)(2,1)S(1)}, u32[]{:S(2)}, u32[]{:S(2)}) collective-permute-start(bf16[24,1024]{1,0:T(8,128)(2,1)S(1)} %get-tuple-element.31), channel_id=1, source_target_pairs={{0,8},{4,12},{8,0},{12,4},{1,9},{5,13},{9,1},{13,5},{2,10},{6,14},... | collective-permute-start | bytes 147464 | tf_op jit(solution)/shard_map/ppermute | solution.py:360
  16.2 0.3 collective-permute-start.5
  16.5 4.7 %load.1 = (bf16[2,1024,1536]{2,1,0:T(8,128)(2,1)S(1)}, bf16[2,1024,1536]{2,1,0:T(8,128)(2,1)S(1)}, f32[8,128]{1,0:T(8,128)S(1)}) custom-call(bf16[2,2,1024,1536]{3,2,1,0:T(8,128)(2,1)} %weight_hbm.1, bf16[24,1024]{1,0:T(8,128)(2,1)S(1)} %get-tuple-element.29.after_ref.refs_0_), custom_call_target="tpu_custom_call" | custom-call | flops 100000000 | tf_op jit(solution)/shard_map/load/pallas_call | solution.py:267
  21.3 0.2 select.1.rows_ref
  21.5 0.6 gate_up.4.refs_2_
  22.1 0.3 collective-permute-start.6
  22.3 0.6 gate_up.5.refs_2_
  22.9 0.1 collective-permute-start.7
  23.0 0.0 slice-start
  23.0 0.6 gate_up.6.refs_2_
  23.7 0.0 copy-start.1
  23.7 0.0 copy-start.3
  23.7 0.0 slice-start.1
  23.7 4.2 %collective-permute-start.8 = (bf16[2,48,768]{2,1,0:T(8,128)(2,1)S(1)}, bf16[2,48,768]{2,1,0:T(8,128)(2,1)S(1)}, u32[]{:S(2)}, u32[]{:S(2)}) collective-permute-start(bf16[2,48,768]{2,1,0:T(8,128)(2,1)S(1)} %gate_up.6.refs_2_), channel_id=1, source_target_pairs={{0,1},{1,0},{2,3},{3,2},{4,5},{5,4},{6,7},{7,6},{8,9},{9,8},{10,11... | collective-permute-start | bytes 442376 | tf_op jit(solution)/shard_map/ppermute | solution.py:360
  27.9 0.6 gate_up.7
  28.5 5.5 %attend.1 = (bf16[8,8192]{1,0:T(8,128)(2,1)}, f32[8,128]{1,0:T(8,128)S(1)}) custom-call(s32[8]{0:T(128)S(1)} %bitcast.12, bf16[8,8192]{1,0:T(8,128)(2,1)S(1)} %copy-done.1, bf16[8,1024]{1,0:T(8,128)(2,1)S(1)} %copy-done.3, bf16[1,8,192,1024]{3,2,1,0:T(8,128)(2,1)S(1)} %copy-done, f32[8,128]{1,0:T(8,128)S(1)} %get-tuple-element.36.after_ref), custom_call_target="tpu_custom_call" | custom-call | flops 50331648 | bytes 3145728 | tf_op jit(solution)/shard_map/attend/pallas_call | solution.py:85
  34.1 2.1 %collective-permute-done.7.refs_1_ = bf16[2,48,768]{2,1,0:T(8,128)(2,1)S(1)} collective-permute-done((bf16[2,48,768]{2,1,0:T(8,128)(2,1)S(1)}, bf16[2,48,768]{2,1,0:T(8,128)(2,1)S(1)}, u32[]{:S(2)}, u32[]{:S(2)}) %collective-permute-start.7) | collective-permute-done | bytes 147488 | tf_op jit(solution)/shard_map/ppermute | solution.py:360
  36.2 0.1 activate.1.part_ref
  36.3 1.7 %collective-permute-start.9 = (bf16[2,48,384]{2,1,0:T(8,128)(2,1)S(1)}, bf16[2,48,384]{2,1,0:T(8,128)(2,1)S(1)}, u32[]{:S(2)}, u32[]{:S(2)}) collective-permute-start(bf16[2,48,384]{2,1,0:T(8,128)(2,1)S(1)} %activate.1.part_ref), channel_id=1, source_target_pairs={{0,3},{1,2},{2,1},{3,0},{4,7},{5,6},{6,5},{7,4},{8,11},{9,10},{10,... | collective-permute-start | bytes 221192 | tf_op jit(solution)/shard_map/ppermute | solution.py:360
  37.9 2.8 %collective-permute-start.10 = (bf16[2,48,384]{2,1,0:T(8,128)(2,1)S(1)}, bf16[2,48,384]{2,1,0:T(8,128)(2,1)S(1)}, u32[]{:S(2)}, u32[]{:S(2)}) collective-permute-start(bf16[2,48,384]{2,1,0:T(8,128)(2,1)S(1)} %activate.1.part_ref), channel_id=1, source_target_pairs={{0,1},{1,0},{2,3},{3,2},{4,5},{5,4},{6,7},{7,6},{8,9},{9,8},{10,11... | collective-permute-start | bytes 221192 | tf_op jit(solution)/shard_map/ppermute | solution.py:360
  40.7 0.4 down_first.1.before_ref
  41.1 2.3 %collective-permute-done.9.part_ref = bf16[2,48,384]{2,1,0:T(8,128)(2,1)S(1)} collective-permute-done((bf16[2,48,384]{2,1,0:T(8,128)(2,1)S(1)}, bf16[2,48,384]{2,1,0:T(8,128)(2,1)S(1)}, u32[]{:S(2)}, u32[]{:S(2)}) %collective-permute-start.9) | collective-permute-done | bytes 73760 | tf_op jit(solution)/shard_map/ppermute | solution.py:360
  43.4 0.4 down_more.1.sum_ref
  43.8 1.5 %collective-permute-done.11.refs_1_ = bf16[2,48,384]{2,1,0:T(8,128)(2,1)S(1)} collective-permute-done((bf16[2,48,384]{2,1,0:T(8,128)(2,1)S(1)}, bf16[2,48,384]{2,1,0:T(8,128)(2,1)S(1)}, u32[]{:S(2)}, u32[]{:S(2)}) %collective-permute-start.11) | collective-permute-done | bytes 73760 | tf_op jit(solution)/shard_map/ppermute | solution.py:360
  45.3 0.8 %down_rest.1 = (bf16[24,1024]{1,0:T(8,128)(2,1)S(1)}, bf16[24,1024]{1,0:T(8,128)(2,1)S(1)}, bf16[24,1024]{1,0:T(8,128)(2,1)S(1)}, bf16[24,1024]{1,0:T(8,128)(2,1)S(1)}) custom-call(s32[1]{0:T(128)} %bitcast.1.me.level.chunk, f32[2,48,1024]{2,1,0:T(8,128)S(1)} %down_more.1.sum_ref, bf16[2,48,384]{2,1,0:T(8,128)(2,1)S(1)} %collective-permute-done.10.refs_0_, ...), custom_call_target="tpu_custom_call" | custom-call | tf_op jit(solution)/shard_map/down_rest/pallas_call | solution.py:372
  46.1 0.1 collective-permute-start.12
  46.2 1.6 %collective-permute-start.13 = (bf16[24,1024]{1,0:T(8,128)(2,1)S(1)}, bf16[24,1024]{1,0:T(8,128)(2,1)S(1)}, u32[]{:S(2)}, u32[]{:S(2)}) collective-permute-start(bf16[24,1024]{1,0:T(8,128)(2,1)S(1)} %get-tuple-element.42), channel_id=1, source_target_pairs={{0,8},{4,12},{8,0},{12,4},{1,9},{5,13},{9,1},{13,5},{2,10},{6,14},... | collective-permute-start | bytes 147464 | tf_op jit(solution)/shard_map/ppermute | solution.py:360
  47.7 0.3 collective-permute-start.14
  48.1 0.3 weigh.1.weight_ref
  48.3 2.0 %collective-permute-done.13.refs_2_ = bf16[24,1024]{1,0:T(8,128)(2,1)S(1)} collective-permute-done((bf16[24,1024]{1,0:T(8,128)(2,1)S(1)}, bf16[24,1024]{1,0:T(8,128)(2,1)S(1)}, u32[]{:S(2)}, u32[]{:S(2)}) %collective-permute-start.13) | collective-permute-done | bytes 49184 | tf_op jit(solution)/shard_map/ppermute | solution.py:360
  50.4 1.1 %collective-permute-done.14.refs_3_ = bf16[24,1024]{1,0:T(8,128)(2,1)S(1)} collective-permute-done((bf16[24,1024]{1,0:T(8,128)(2,1)S(1)}, bf16[24,1024]{1,0:T(8,128)(2,1)S(1)}, u32[]{:S(2)}, u32[]{:S(2)}) %collective-permute-start.14) | collective-permute-done | bytes 49184 | tf_op jit(solution)/shard_map/ppermute | solution.py:360
  51.4 0.2 combine.1
  51.7 0.1 collective-permute-start.15
  51.8 2.4 %collective-permute-start.16 = (bf16[8,1024]{1,0:T(8,128)(2,1)S(1)}, bf16[8,1024]{1,0:T(8,128)(2,1)S(1)}, u32[]{:S(2)}, u32[]{:S(2)}) collective-permute-start(bf16[8,1024]{1,0:T(8,128)(2,1)S(1)} %get-tuple-element.46), channel_id=1, source_target_pairs={{0,2},{1,3},{2,0},{3,1},{4,6},{5,7},{6,4},{7,5},{8,10},{9,11},{10,... | collective-permute-start | bytes 49160 | tf_op jit(solution)/shard_map/ppermute | solution.py:360
  54.2 2.0 %collective-permute-start.17 = (bf16[8,1024]{1,0:T(8,128)(2,1)S(1)}, bf16[8,1024]{1,0:T(8,128)(2,1)S(1)}, u32[]{:S(2)}, u32[]{:S(2)}) collective-permute-start(bf16[8,1024]{1,0:T(8,128)(2,1)S(1)} %get-tuple-element.47), channel_id=1, source_target_pairs={{0,3},{1,2},{2,1},{3,0},{4,7},{5,6},{6,5},{7,4},{8,11},{9,10},{10,... | collective-permute-start | bytes 49160 | tf_op jit(solution)/shard_map/ppermute | solution.py:360
  56.2 0.4 collective-permute-done.16.refs_2_
  56.5 3.2 %collective-permute-done.17.refs_3_ = bf16[8,1024]{1,0:T(8,128)(2,1)S(1)} collective-permute-done((bf16[8,1024]{1,0:T(8,128)(2,1)S(1)}, bf16[8,1024]{1,0:T(8,128)(2,1)S(1)}, u32[]{:S(2)}, u32[]{:S(2)}) %collective-permute-start.17) | collective-permute-done | bytes 16416 | tf_op jit(solution)/shard_map/ppermute | solution.py:360
  59.7 0.6 %assemble.1 = bf16[8,4096]{1,0:T(8,128)(2,1)} custom-call(s32[1]{0:T(128)} %bitcast.1.me.level.chunk, bf16[8,1024]{1,0:T(8,128)(2,1)S(1)} %get-tuple-element.44.refs_0_, bf16[8,1024]{1,0:T(8,128)(2,1)S(1)} %collective-permute-done.15.refs_1_, bf16[8,1024]{1,0:T(8,128)(2,1)S(1)} %collective-permute-done.16.refs_2_, ...), custom_call_target="tpu_custom_call" | custom-call | tf_op jit(solution)/shard_map/assemble/pallas_call | solution.py:372
  (23 shorter events, 0.1 us)
Async XLA Ops:
  0.6 0.8 %copy-start.2 = (bf16[8,4096]{1,0:T(8,128)(2,1)S(1)}, bf16[8,4096]{1,0:T(8,128)(2,1)}, u32[]{:S(2)}) copy-start(bf16[8,4096]{1,0:T(8,128)(2,1)} %hidden_ref.1) | copy-start | bytes 196612
  1.5 0.7 %copy-start.4 = (s32[8,2]{0,1:T(2,128)S(1)}, s32[8,2]{0,1:T(2,128)}, u32[]{:S(2)}) copy-start(s32[8,2]{0,1:T(2,128)} %param.14) | copy-start | bytes 196
  2.2 0.7 %copy-start.5 = (bf16[8,2]{0,1:T(2,128)(2,1)S(1)}, bf16[8,2]{0,1:T(2,128)(2,1)}, u32[]{:S(2)}) copy-start(bf16[8,2]{0,1:T(2,128)(2,1)} %param.15) | copy-start | bytes 100
  3.0 5.6 %collective-permute-start = (bf16[8,1152]{1,0:T(8,128)(2,1)S(1)}, bf16[8,1152]{1,0:T(8,128)(2,1)S(1)}, u32[]{:S(2)}, u32[]{:S(2)}) collective-permute-start(bf16[8,1152]{1,0:T(8,128)(2,1)S(1)} %get-tuple-element.26), channel_id=1, source_target_pairs={{0,1},{1,0},{2,3},{3,2},{4,5},{5,4},{6,7},{7,6},{8,9},{9,8},{10,11... | collective-permute-start | bytes 55304 | tf_op jit(solution)/shard_map/ppermute | solution.py:360
  6.0 4.8 %collective-permute-start.1 = (bf16[8,1152]{1,0:T(8,128)(2,1)S(1)}, bf16[8,1152]{1,0:T(8,128)(2,1)S(1)}, u32[]{:S(2)}, u32[]{:S(2)}) collective-permute-start(bf16[8,1152]{1,0:T(8,128)(2,1)S(1)} %get-tuple-element.27), channel_id=1, source_target_pairs={{0,2},{1,3},{2,0},{3,1},{4,6},{5,7},{6,4},{7,5},{8,10},{9,11},{10,... | collective-permute-start | bytes 55304 | tf_op jit(solution)/shard_map/ppermute | solution.py:360
  8.6 5.6 %collective-permute-start.2 = (bf16[8,1152]{1,0:T(8,128)(2,1)S(1)}, bf16[8,1152]{1,0:T(8,128)(2,1)S(1)}, u32[]{:S(2)}, u32[]{:S(2)}) collective-permute-start(bf16[8,1152]{1,0:T(8,128)(2,1)S(1)} %get-tuple-element.28), channel_id=1, source_target_pairs={{0,3},{1,2},{2,1},{3,0},{4,7},{5,6},{6,5},{7,4},{8,11},{9,10},{10,... | collective-permute-start | bytes 55304 | tf_op jit(solution)/shard_map/ppermute | solution.py:360
  14.6 6.7 %collective-permute-start.3 = (bf16[24,1024]{1,0:T(8,128)(2,1)S(1)}, bf16[24,1024]{1,0:T(8,128)(2,1)S(1)}, u32[]{:S(2)}, u32[]{:S(2)}) collective-permute-start(bf16[24,1024]{1,0:T(8,128)(2,1)S(1)} %get-tuple-element.30), channel_id=1, source_target_pairs={{0,4},{4,0},{8,12},{12,8},{1,5},{5,1},{9,13},{13,9},{2,6},{6,2},{1... | collective-permute-start | bytes 147464 | tf_op jit(solution)/shard_map/ppermute | solution.py:360
  14.7 6.6 %collective-permute-start.4 = (bf16[24,1024]{1,0:T(8,128)(2,1)S(1)}, bf16[24,1024]{1,0:T(8,128)(2,1)S(1)}, u32[]{:S(2)}, u32[]{:S(2)}) collective-permute-start(bf16[24,1024]{1,0:T(8,128)(2,1)S(1)} %get-tuple-element.31), channel_id=1, source_target_pairs={{0,8},{4,12},{8,0},{12,4},{1,9},{5,13},{9,1},{13,5},{2,10},{6,14},... | collective-permute-start | bytes 147464 | tf_op jit(solution)/shard_map/ppermute | solution.py:360
  16.2 5.1 %collective-permute-start.5 = (bf16[24,1024]{1,0:T(8,128)(2,1)S(1)}, bf16[24,1024]{1,0:T(8,128)(2,1)S(1)}, u32[]{:S(2)}, u32[]{:S(2)}) collective-permute-start(bf16[24,1024]{1,0:T(8,128)(2,1)S(1)} %get-tuple-element.32), channel_id=1, source_target_pairs={{0,12},{4,8},{8,4},{12,0},{1,13},{5,9},{9,5},{13,1},{2,14},{6,10},... | collective-permute-start | bytes 147464 | tf_op jit(solution)/shard_map/ppermute | solution.py:360
  22.1 14.1 %collective-permute-start.6 = (bf16[2,48,768]{2,1,0:T(8,128)(2,1)S(1)}, bf16[2,48,768]{2,1,0:T(8,128)(2,1)S(1)}, u32[]{:S(2)}, u32[]{:S(2)}) collective-permute-start(bf16[2,48,768]{2,1,0:T(8,128)(2,1)S(1)} %gate_up.4.refs_2_), channel_id=1, source_target_pairs={{0,3},{1,2},{2,1},{3,0},{4,7},{5,6},{6,5},{7,4},{8,11},{9,10},{10,... | collective-permute-start | bytes 442376 | tf_op jit(solution)/shard_map/ppermute | solution.py:360
  22.9 13.2 %collective-permute-start.7 = (bf16[2,48,768]{2,1,0:T(8,128)(2,1)S(1)}, bf16[2,48,768]{2,1,0:T(8,128)(2,1)S(1)}, u32[]{:S(2)}, u32[]{:S(2)}) collective-permute-start(bf16[2,48,768]{2,1,0:T(8,128)(2,1)S(1)} %gate_up.5.refs_2_), channel_id=1, source_target_pairs={{0,2},{1,3},{2,0},{3,1},{4,6},{5,7},{6,4},{7,5},{8,10},{9,11},{10,... | collective-permute-start | bytes 442376 | tf_op jit(solution)/shard_map/ppermute | solution.py:360
  23.0 17.7 %slice-start = ((s8[6291456]{0:T(1024)(128)(4,1)}), s8[4194304]{0:T(1024)(128)(4,1)S(1)}, s32[]{:S(2)}) async-start(s8[6291456]{0:T(1024)(128)(4,1)} %bitcast.8), calls=%async_computation | async-start | bytes 8388608
  23.6 4.8 %copy-start = (bf16[1,8,192,1024]{3,2,1,0:T(8,128)(2,1)S(1)}, bf16[1,8,192,1024]{3,2,1,0:T(8,128)(2,1)}, u32[]{:S(2)}) copy-start(bf16[1,8,192,1024]{3,2,1,0:T(8,128)(2,1)} %cache_ref.1) | copy-start | bytes 9437188
  23.7 4.8 %copy-start.1 = (bf16[8,8192]{1,0:T(8,128)(2,1)S(1)}, bf16[8,8192]{1,0:T(8,128)(2,1)}, u32[]{:S(2)}) copy-start(bf16[8,8192]{1,0:T(8,128)(2,1)} %q_ref.1) | copy-start | bytes 393220
  23.7 4.8 %copy-start.3 = (bf16[8,1024]{1,0:T(8,128)(2,1)S(1)}, bf16[8,1024]{1,0:T(8,128)(2,1)}, u32[]{:S(2)}) copy-start(bf16[8,1024]{1,0:T(8,128)(2,1)} %new_ref.1) | copy-start | bytes 49156
  23.7 4.8 %copy-start.6 = (s32[1,8]{1,0:T(1,128)S(1)}, s32[1,8]{1,0:T(1,128)}, u32[]{:S(2)}) copy-start(s32[1,8]{1,0:T(1,128)} %param.12) | copy-start | bytes 100
  23.7 17.0 %slice-start.1 = ((s8[6291456]{0:T(1024)(128)(4,1)}), s8[2097152]{0:T(1024)(128)(4,1)S(1)}, s32[]{:S(2)}) async-start(s8[6291456]{0:T(1024)(128)(4,1)} %bitcast.8), calls=%async_computation.1 | async-start | bytes 4194304
  23.7 10.4 %collective-permute-start.8 = (bf16[2,48,768]{2,1,0:T(8,128)(2,1)S(1)}, bf16[2,48,768]{2,1,0:T(8,128)(2,1)S(1)}, u32[]{:S(2)}, u32[]{:S(2)}) collective-permute-start(bf16[2,48,768]{2,1,0:T(8,128)(2,1)S(1)} %gate_up.6.refs_2_), channel_id=1, source_target_pairs={{0,1},{1,0},{2,3},{3,2},{4,5},{5,4},{6,7},{7,6},{8,9},{9,8},{10,11... | collective-permute-start | bytes 442376 | tf_op jit(solution)/shard_map/ppermute | solution.py:360
  36.3 7.1 %collective-permute-start.9 = (bf16[2,48,384]{2,1,0:T(8,128)(2,1)S(1)}, bf16[2,48,384]{2,1,0:T(8,128)(2,1)S(1)}, u32[]{:S(2)}, u32[]{:S(2)}) collective-permute-start(bf16[2,48,384]{2,1,0:T(8,128)(2,1)S(1)} %activate.1.part_ref), channel_id=1, source_target_pairs={{0,3},{1,2},{2,1},{3,0},{4,7},{5,6},{6,5},{7,4},{8,11},{9,10},{10,... | collective-permute-start | bytes 221192 | tf_op jit(solution)/shard_map/ppermute | solution.py:360
  37.9 7.4 %collective-permute-start.11 = (bf16[2,48,384]{2,1,0:T(8,128)(2,1)S(1)}, bf16[2,48,384]{2,1,0:T(8,128)(2,1)S(1)}, u32[]{:S(2)}, u32[]{:S(2)}) collective-permute-start(bf16[2,48,384]{2,1,0:T(8,128)(2,1)S(1)} %activate.1.part_ref), channel_id=1, source_target_pairs={{0,2},{1,3},{2,0},{3,1},{4,6},{5,7},{6,4},{7,5},{8,10},{9,11},{10,... | collective-permute-start | bytes 221192 | tf_op jit(solution)/shard_map/ppermute | solution.py:360
  37.9 7.4 %collective-permute-start.10 = (bf16[2,48,384]{2,1,0:T(8,128)(2,1)S(1)}, bf16[2,48,384]{2,1,0:T(8,128)(2,1)S(1)}, u32[]{:S(2)}, u32[]{:S(2)}) collective-permute-start(bf16[2,48,384]{2,1,0:T(8,128)(2,1)S(1)} %activate.1.part_ref), channel_id=1, source_target_pairs={{0,1},{1,0},{2,3},{3,2},{4,5},{5,4},{6,7},{7,6},{8,9},{9,8},{10,11... | collective-permute-start | bytes 221192 | tf_op jit(solution)/shard_map/ppermute | solution.py:360
  46.1 2.2 %collective-permute-start.12 = (bf16[24,1024]{1,0:T(8,128)(2,1)S(1)}, bf16[24,1024]{1,0:T(8,128)(2,1)S(1)}, u32[]{:S(2)}, u32[]{:S(2)}) collective-permute-start(bf16[24,1024]{1,0:T(8,128)(2,1)S(1)} %get-tuple-element.41), channel_id=1, source_target_pairs={{0,4},{4,0},{8,12},{12,8},{1,5},{5,1},{9,13},{13,9},{2,6},{6,2},{1... | collective-permute-start | bytes 147464 | tf_op jit(solution)/shard_map/ppermute | solution.py:360
  46.2 4.2 %collective-permute-start.13 = (bf16[24,1024]{1,0:T(8,128)(2,1)S(1)}, bf16[24,1024]{1,0:T(8,128)(2,1)S(1)}, u32[]{:S(2)}, u32[]{:S(2)}) collective-permute-start(bf16[24,1024]{1,0:T(8,128)(2,1)S(1)} %get-tuple-element.42), channel_id=1, source_target_pairs={{0,8},{4,12},{8,0},{12,4},{1,9},{5,13},{9,1},{13,5},{2,10},{6,14},... | collective-permute-start | bytes 147464 | tf_op jit(solution)/shard_map/ppermute | solution.py:360
  47.7 3.7 %collective-permute-start.14 = (bf16[24,1024]{1,0:T(8,128)(2,1)S(1)}, bf16[24,1024]{1,0:T(8,128)(2,1)S(1)}, u32[]{:S(2)}, u32[]{:S(2)}) collective-permute-start(bf16[24,1024]{1,0:T(8,128)(2,1)S(1)} %get-tuple-element.43), channel_id=1, source_target_pairs={{0,12},{4,8},{8,4},{12,0},{1,13},{5,9},{9,5},{13,1},{2,14},{6,10},... | collective-permute-start | bytes 147464 | tf_op jit(solution)/shard_map/ppermute | solution.py:360
  51.7 4.5 %collective-permute-start.15 = (bf16[8,1024]{1,0:T(8,128)(2,1)S(1)}, bf16[8,1024]{1,0:T(8,128)(2,1)S(1)}, u32[]{:S(2)}, u32[]{:S(2)}) collective-permute-start(bf16[8,1024]{1,0:T(8,128)(2,1)S(1)} %get-tuple-element.45), channel_id=1, source_target_pairs={{0,1},{1,0},{2,3},{3,2},{4,5},{5,4},{6,7},{7,6},{8,9},{9,8},{10,11... | collective-permute-start | bytes 49160 | tf_op jit(solution)/shard_map/ppermute | solution.py:360
  51.8 4.8 %collective-permute-start.16 = (bf16[8,1024]{1,0:T(8,128)(2,1)S(1)}, bf16[8,1024]{1,0:T(8,128)(2,1)S(1)}, u32[]{:S(2)}, u32[]{:S(2)}) collective-permute-start(bf16[8,1024]{1,0:T(8,128)(2,1)S(1)} %get-tuple-element.46), channel_id=1, source_target_pairs={{0,2},{1,3},{2,0},{3,1},{4,6},{5,7},{6,4},{7,5},{8,10},{9,11},{10,... | collective-permute-start | bytes 49160 | tf_op jit(solution)/shard_map/ppermute | solution.py:360
  54.2 5.5 %collective-permute-start.17 = (bf16[8,1024]{1,0:T(8,128)(2,1)S(1)}, bf16[8,1024]{1,0:T(8,128)(2,1)S(1)}, u32[]{:S(2)}, u32[]{:S(2)}) collective-permute-start(bf16[8,1024]{1,0:T(8,128)(2,1)S(1)} %get-tuple-element.47), channel_id=1, source_target_pairs={{0,3},{1,2},{2,1},{3,0},{4,7},{5,6},{6,5},{7,4},{8,11},{9,10},{10,... | collective-permute-start | bytes 49160 | tf_op jit(solution)/shard_map/ppermute | solution.py:360

commit v11 on v10

--- a/solution.py
+++ b/solution.py
@@ -17,7 +17,7 @@
 
 def params(limit, *semantics):
     return pltpu.CompilerParams(
-        dimension_semantics=semantics or None, vmem_limit_bytes=limit * 1024 * 1024
+        dimension_semantics=semantics or None, vmem_limit_bytes=int(limit * 1024 * 1024)
     )
 
 
@@ -118,12 +118,12 @@
     )
 
 
-def prepare_kernel(me, routes_ref, gates_ref, hidden_ref, *out_refs):
-    width = hidden_ref.shape[1] // len(out_refs)
+def prepare_kernel(indices, me, routes_ref, gates_ref, hidden_ref, *out_refs):
+    width = out_refs[0].shape[1] - LANES
     top = routes_ref.shape[0]
     notes = spread(routes_ref[...], LANES, 0) + spread(gates_ref[...], LANES, top)
     notes = notes.astype(jnp.bfloat16)
-    for s, out_ref in enumerate(out_refs):
+    for s, out_ref in zip(indices, out_refs):
         start = pl.multiple_of((me[0] ^ s) * width, width)
         out_ref[:, :width] = hidden_ref[:, pl.ds(start, width)]
         out_ref[:, width:] = notes
@@ -465,14 +465,21 @@
 
     attention = functools.partial(attend, queries, new_key_value, cached_key_value, parents)
 
-    slices = call(
-        prepare_kernel,
+    even = ff % (inner * LANES) == 0
+    shape = jax.ShapeDtypeStruct((rows, depth + LANES), jnp.bfloat16)
+    arrays = [routes.T, gate_values.T, hidden]
+    sent = call(
+        functools.partial(prepare_kernel, range(1, inner)),
         [level],
-        [routes.T, gate_values.T, hidden],
-        [jax.ShapeDtypeStruct((rows, depth + LANES), jnp.bfloat16)] * inner,
+        arrays,
+        [shape] * (inner - 1),
         "prepare",
-    )
-    even = ff % (inner * LANES) == 0
+        66633728 / 1024 / 1024,
+    )
+    (kept,) = call(
+        functools.partial(prepare_kernel, [0]), [level], arrays, [shape], "keep", cost=1
+    )
+    slices = [kept, *sent]
     slices = trade(slices, "inner")
     packs = call(
         functools.partial(pack_kernel, top, experts, inner),

time: 60.6 us -> 60.1 us (level)
  waiting for transfers between devices: 18.1 us -> 16 us
  Pallas kernels: 16.2 us -> 17.9 us
    ppermute x18, waiting for transfers between devices: 18.1 us -> 16 us  [traded(): lax.ppermute(value, axis, [(i, i ^ index) for i in range(lax.axis_size(ax...]
    pallas_call x14 -> x15, Pallas kernels: 5.99 us -> 7.66 us  [call(): pl.pallas_call(kernel, in_specs=[pl.BlockSpec(memory_space=pltpu.SMEM)] *...]
where the time goes in v11:
time: 60.1 us; the launch traced here: 59.9 us
  starting transfers between devices  22.9 us (38%)
  Pallas kernels  17.9 us (30%)
  waiting for transfers between devices  16 us (27%)
  local copies, waits for them, and re-layouts  2.21 us (4%)
  between operations  0.88 us (1%)
    ppermute x18, starting transfers between devices, traded(): lax.ppermute(value, axis, [(i, i ^ index) for i in range(lax.axis_size(ax...  22.9 us
    ppermute x18, waiting for transfers between devices, traded(): lax.ppermute(value, axis, [(i, i ^ index) for i in range(lax.axis_size(ax...  16 us
    pallas_call x15, Pallas kernels, call(): pl.pallas_call(kernel, in_specs=[pl.BlockSpec(memory_space=pltpu.SMEM)] *...  7.66 us
    pallas_call x1, Pallas kernels, attend(): pl.pallas_call(attend_kernel, in_specs=[pl.BlockSpec(memory_space=pltpu.S...  5.53 us
    pallas_call x1, Pallas kernels, load(): pl.pallas_call(functools.partial(load_kernel, pieces), in_specs=[pl.Block...  4.72 us
    unnamed x18, local copies, waits for them, and re-layouts  2.21 us
  transfers between devices with their start and end apart: 18, of which 9 were waited for; matrix products, arithmetic and copies ran while one was open for 0% of the time, Pallas kernels for 22%

profile of v11, /device:TPU:0, one launch (start us, length us, event | category | flops | bytes accessed | tf_op | source)
XLA Modules:
  0.0 59.9 jit_solution(2328644332495934842)
XLA Ops:
  0.6 1.7 %prepare.1 = (bf16[8,1152]{1,0:T(8,128)(2,1)}, bf16[8,1152]{1,0:T(8,128)(2,1)}, bf16[8,1152]{1,0:T(8,128)(2,1)}) custom-call(s32[1]{0:T(128)} %bitcast.1.me.level.chunk, s32[2,8]{1,0:T(2,128)} %bitcast.10, bf16[2,8]{1,0:T(2,128)(2,1)} %bitcast.12, bf16[8,4096]{1,0:T(8,128)(2,1)} %hidden_ref.3), custom_call_target="tpu_custom_call" | custom-call | tf_op jit(solution)/shard_map/prepare/pallas_call | solution.py:372
  2.3 3.0 %collective-permute-start = (bf16[8,1152]{1,0:T(8,128)(2,1)}, bf16[8,1152]{1,0:T(8,128)(2,1)S(1)}, u32[]{:S(2)}, u32[]{:S(2)}) collective-permute-start(bf16[8,1152]{1,0:T(8,128)(2,1)} %get-tuple-element.24), channel_id=1, source_target_pairs={{0,1},{1,0},{2,3},{3,2},{4,5},{5,4},{6,7},{7,6},{8,9},{9,8},{10,11... | collective-permute-start | bytes 55304 | tf_op jit(solution)/shard_map/ppermute | solution.py:360
  5.3 2.6 %collective-permute-start.1 = (bf16[8,1152]{1,0:T(8,128)(2,1)}, bf16[8,1152]{1,0:T(8,128)(2,1)S(1)}, u32[]{:S(2)}, u32[]{:S(2)}) collective-permute-start(bf16[8,1152]{1,0:T(8,128)(2,1)} %get-tuple-element.25), channel_id=1, source_target_pairs={{0,2},{1,3},{2,0},{3,1},{4,6},{5,7},{6,4},{7,5},{8,10},{9,11},{10,... | collective-permute-start | bytes 55304 | tf_op jit(solution)/shard_map/ppermute | solution.py:360
  7.9 0.8 %copy-done.2 = bf16[8,4096]{1,0:T(8,128)(2,1)S(1)} copy-done((bf16[8,4096]{1,0:T(8,128)(2,1)S(1)}, bf16[8,4096]{1,0:T(8,128)(2,1)}, u32[]{:S(2)}) %copy-start.2) | copy-done | bytes 65560
  8.8 0.7 %copy-done.4 = s32[8,2]{0,1:T(2,128)S(1)} copy-done((s32[8,2]{0,1:T(2,128)S(1)}, s32[8,2]{0,1:T(2,128)}, u32[]{:S(2)}) %copy-start.4) | copy-done | bytes 88
  9.4 0.7 %copy-done.5 = bf16[8,2]{0,1:T(2,128)(2,1)S(1)} copy-done((bf16[8,2]{0,1:T(2,128)(2,1)S(1)}, bf16[8,2]{0,1:T(2,128)(2,1)}, u32[]{:S(2)}) %copy-start.5) | copy-done | bytes 56
  10.1 0.2 keep.1.refs_0_
  10.3 0.1 collective-permute-done.1.refs_2_
  10.3 3.3 %collective-permute-done.2.refs_3_ = bf16[8,1152]{1,0:T(8,128)(2,1)S(1)} collective-permute-done((bf16[8,1152]{1,0:T(8,128)(2,1)}, bf16[8,1152]{1,0:T(8,128)(2,1)S(1)}, u32[]{:S(2)}, u32[]{:S(2)}) %collective-permute-start.2) | collective-permute-done | bytes 18464 | tf_op jit(solution)/shard_map/ppermute | solution.py:360
  13.7 0.4 pack.1
  14.1 0.1 collective-permute-start.3
  14.2 1.6 %collective-permute-start.4 = (bf16[24,1024]{1,0:T(8,128)(2,1)S(1)}, bf16[24,1024]{1,0:T(8,128)(2,1)S(1)}, u32[]{:S(2)}, u32[]{:S(2)}) collective-permute-start(bf16[24,1024]{1,0:T(8,128)(2,1)S(1)} %get-tuple-element.29), channel_id=1, source_target_pairs={{0,8},{4,12},{8,0},{12,4},{1,9},{5,13},{9,1},{13,5},{2,10},{6,14},... | collective-permute-start | bytes 147464 | tf_op jit(solution)/shard_map/ppermute | solution.py:360
  15.7 0.3 collective-permute-start.5
  16.0 4.7 %load.1 = (bf16[2,1024,1536]{2,1,0:T(8,128)(2,1)S(1)}, bf16[2,1024,1536]{2,1,0:T(8,128)(2,1)S(1)}, f32[8,128]{1,0:T(8,128)S(1)}) custom-call(bf16[2,2,1024,1536]{3,2,1,0:T(8,128)(2,1)} %weight_hbm.1, bf16[24,1024]{1,0:T(8,128)(2,1)S(1)} %get-tuple-element.27.after_ref.refs_0_), custom_call_target="tpu_custom_call" | custom-call | flops 100000000 | tf_op jit(solution)/shard_map/load/pallas_call | solution.py:267
  20.8 0.2 select.1.rows_ref
  21.0 0.6 gate_up.4.refs_2_
  21.6 0.5 collective-permute-start.6
  22.1 0.6 %gate_up.5.refs_2_ = bf16[2,48,768]{2,1,0:T(8,128)(2,1)S(1)} custom-call(s32[1]{0:T(128)} %bitcast.6.chunk, bf16[2,48,1024]{2,1,0:T(8,128)(2,1)S(1)} %select.1.rows_ref, bf16[2,1024,1536]{2,1,0:T(8,128)(2,1)S(1)} %get-tuple-element.32.refs_0_, bf16[2,1024,1536]{2,1,0:T(8,128)(2,1)S(1)} %get-tuple-element.33.refs_1_, bf16[2,48,768]{2,1,0:T(8,128)(2,1)S(1)} %gate_up.4.refs_2_), custom_call_target="tpu_custom_call" | custom-call | flops 2000000000 | tf_op jit(solution)/shard_map/gate_up/pallas_call | solution.py:372
  22.7 0.1 collective-permute-start.7
  22.8 0.0 slice-start
  22.8 0.6 %gate_up.6.refs_2_ = bf16[2,48,768]{2,1,0:T(8,128)(2,1)S(1)} custom-call(s32[1]{0:T(128)} %bitcast.5.chunk, bf16[2,48,1024]{2,1,0:T(8,128)(2,1)S(1)} %select.1.rows_ref, bf16[2,1024,1536]{2,1,0:T(8,128)(2,1)S(1)} %get-tuple-element.32.refs_0_, bf16[2,1024,1536]{2,1,0:T(8,128)(2,1)S(1)} %get-tuple-element.33.refs_1_, bf16[2,48,768]{2,1,0:T(8,128)(2,1)S(1)} %gate_up.5.refs_2_), custom_call_target="tpu_custom_call" | custom-call | flops 2000000000 | tf_op jit(solution)/shard_map/gate_up/pallas_call | solution.py:372
  23.4 0.0 copy-start
  23.4 0.0 slice-start.1
  23.5 4.0 %collective-permute-start.8 = (bf16[2,48,768]{2,1,0:T(8,128)(2,1)S(1)}, bf16[2,48,768]{2,1,0:T(8,128)(2,1)S(1)}, u32[]{:S(2)}, u32[]{:S(2)}) collective-permute-start(bf16[2,48,768]{2,1,0:T(8,128)(2,1)S(1)} %gate_up.6.refs_2_), channel_id=1, source_target_pairs={{0,1},{1,0},{2,3},{3,2},{4,5},{5,4},{6,7},{7,6},{8,9},{9,8},{10,11... | collective-permute-start | bytes 442376 | tf_op jit(solution)/shard_map/ppermute | solution.py:360
  27.4 0.6 gate_up.7
  28.0 5.5 %attend.1 = (bf16[8,8192]{1,0:T(8,128)(2,1)}, f32[8,128]{1,0:T(8,128)S(1)}) custom-call(s32[8]{0:T(128)S(1)} %bitcast.14, bf16[8,8192]{1,0:T(8,128)(2,1)S(1)} %copy-done.1, bf16[8,1024]{1,0:T(8,128)(2,1)S(1)} %copy-done.3, bf16[1,8,192,1024]{3,2,1,0:T(8,128)(2,1)S(1)} %copy-done, f32[8,128]{1,0:T(8,128)S(1)} %get-tuple-element.34.after_ref), custom_call_target="tpu_custom_call" | custom-call | flops 50331648 | bytes 3145728 | tf_op jit(solution)/shard_map/attend/pallas_call | solution.py:85
  33.6 2.2 %collective-permute-done.7.refs_1_ = bf16[2,48,768]{2,1,0:T(8,128)(2,1)S(1)} collective-permute-done((bf16[2,48,768]{2,1,0:T(8,128)(2,1)S(1)}, bf16[2,48,768]{2,1,0:T(8,128)(2,1)S(1)}, u32[]{:S(2)}, u32[]{:S(2)}) %collective-permute-start.7) | collective-permute-done | bytes 147488 | tf_op jit(solution)/shard_map/ppermute | solution.py:360
  35.8 0.1 activate.1.part_ref
  35.9 1.5 %collective-permute-start.9 = (bf16[2,48,384]{2,1,0:T(8,128)(2,1)S(1)}, bf16[2,48,384]{2,1,0:T(8,128)(2,1)S(1)}, u32[]{:S(2)}, u32[]{:S(2)}) collective-permute-start(bf16[2,48,384]{2,1,0:T(8,128)(2,1)S(1)} %activate.1.part_ref), channel_id=1, source_target_pairs={{0,3},{1,2},{2,1},{3,0},{4,7},{5,6},{6,5},{7,4},{8,11},{9,10},{10,... | collective-permute-start | bytes 221192 | tf_op jit(solution)/shard_map/ppermute | solution.py:360
  37.5 2.9 %collective-permute-start.10 = (bf16[2,48,384]{2,1,0:T(8,128)(2,1)S(1)}, bf16[2,48,384]{2,1,0:T(8,128)(2,1)S(1)}, u32[]{:S(2)}, u32[]{:S(2)}) collective-permute-start(bf16[2,48,384]{2,1,0:T(8,128)(2,1)S(1)} %activate.1.part_ref), channel_id=1, source_target_pairs={{0,1},{1,0},{2,3},{3,2},{4,5},{5,4},{6,7},{7,6},{8,9},{9,8},{10,11... | collective-permute-start | bytes 221192 | tf_op jit(solution)/shard_map/ppermute | solution.py:360
  40.4 0.4 down_first.1.before_ref
  40.8 2.2 %collective-permute-done.9.part_ref = bf16[2,48,384]{2,1,0:T(8,128)(2,1)S(1)} collective-permute-done((bf16[2,48,384]{2,1,0:T(8,128)(2,1)S(1)}, bf16[2,48,384]{2,1,0:T(8,128)(2,1)S(1)}, u32[]{:S(2)}, u32[]{:S(2)}) %collective-permute-start.9) | collective-permute-done | bytes 73760 | tf_op jit(solution)/shard_map/ppermute | solution.py:360
  43.0 0.4 down_more.1.sum_ref
  43.4 1.6 %collective-permute-done.11.refs_1_ = bf16[2,48,384]{2,1,0:T(8,128)(2,1)S(1)} collective-permute-done((bf16[2,48,384]{2,1,0:T(8,128)(2,1)S(1)}, bf16[2,48,384]{2,1,0:T(8,128)(2,1)S(1)}, u32[]{:S(2)}, u32[]{:S(2)}) %collective-permute-start.11) | collective-permute-done | bytes 73760 | tf_op jit(solution)/shard_map/ppermute | solution.py:360
  44.9 0.8 %down_rest.1 = (bf16[24,1024]{1,0:T(8,128)(2,1)S(1)}, bf16[24,1024]{1,0:T(8,128)(2,1)S(1)}, bf16[24,1024]{1,0:T(8,128)(2,1)S(1)}, bf16[24,1024]{1,0:T(8,128)(2,1)S(1)}) custom-call(s32[1]{0:T(128)} %bitcast.1.me.level.chunk, f32[2,48,1024]{2,1,0:T(8,128)S(1)} %down_more.1.sum_ref, bf16[2,48,384]{2,1,0:T(8,128)(2,1)S(1)} %collective-permute-done.10.refs_0_, ...), custom_call_target="tpu_custom_call" | custom-call | tf_op jit(solution)/shard_map/down_rest/pallas_call | solution.py:372
  45.8 0.1 collective-permute-start.12
  45.8 1.6 %collective-permute-start.13 = (bf16[24,1024]{1,0:T(8,128)(2,1)S(1)}, bf16[24,1024]{1,0:T(8,128)(2,1)S(1)}, u32[]{:S(2)}, u32[]{:S(2)}) collective-permute-start(bf16[24,1024]{1,0:T(8,128)(2,1)S(1)} %get-tuple-element.40), channel_id=1, source_target_pairs={{0,8},{4,12},{8,0},{12,4},{1,9},{5,13},{9,1},{13,5},{2,10},{6,14},... | collective-permute-start | bytes 147464 | tf_op jit(solution)/shard_map/ppermute | solution.py:360
  47.4 0.3 collective-permute-start.14
  47.7 0.3 weigh.1.weight_ref
  48.0 2.0 %collective-permute-done.13.refs_2_ = bf16[24,1024]{1,0:T(8,128)(2,1)S(1)} collective-permute-done((bf16[24,1024]{1,0:T(8,128)(2,1)S(1)}, bf16[24,1024]{1,0:T(8,128)(2,1)S(1)}, u32[]{:S(2)}, u32[]{:S(2)}) %collective-permute-start.13) | collective-permute-done | bytes 49184 | tf_op jit(solution)/shard_map/ppermute | solution.py:360
  50.0 1.1 %collective-permute-done.14.refs_3_ = bf16[24,1024]{1,0:T(8,128)(2,1)S(1)} collective-permute-done((bf16[24,1024]{1,0:T(8,128)(2,1)S(1)}, bf16[24,1024]{1,0:T(8,128)(2,1)S(1)}, u32[]{:S(2)}, u32[]{:S(2)}) %collective-permute-start.14) | collective-permute-done | bytes 49184 | tf_op jit(solution)/shard_map/ppermute | solution.py:360
  51.1 0.2 combine.1
  51.4 0.1 collective-permute-start.15
  51.4 2.3 %collective-permute-start.16 = (bf16[8,1024]{1,0:T(8,128)(2,1)S(1)}, bf16[8,1024]{1,0:T(8,128)(2,1)S(1)}, u32[]{:S(2)}, u32[]{:S(2)}) collective-permute-start(bf16[8,1024]{1,0:T(8,128)(2,1)S(1)} %get-tuple-element.44), channel_id=1, source_target_pairs={{0,2},{1,3},{2,0},{3,1},{4,6},{5,7},{6,4},{7,5},{8,10},{9,11},{10,... | collective-permute-start | bytes 49160 | tf_op jit(solution)/shard_map/ppermute | solution.py:360
  53.7 2.1 %collective-permute-start.17 = (bf16[8,1024]{1,0:T(8,128)(2,1)S(1)}, bf16[8,1024]{1,0:T(8,128)(2,1)S(1)}, u32[]{:S(2)}, u32[]{:S(2)}) collective-permute-start(bf16[8,1024]{1,0:T(8,128)(2,1)S(1)} %get-tuple-element.45), channel_id=1, source_target_pairs={{0,3},{1,2},{2,1},{3,0},{4,7},{5,6},{6,5},{7,4},{8,11},{9,10},{10,... | collective-permute-start | bytes 49160 | tf_op jit(solution)/shard_map/ppermute | solution.py:360
  55.8 0.3 collective-permute-done.16.refs_2_
  56.2 3.1 %collective-permute-done.17.refs_3_ = bf16[8,1024]{1,0:T(8,128)(2,1)S(1)} collective-permute-done((bf16[8,1024]{1,0:T(8,128)(2,1)S(1)}, bf16[8,1024]{1,0:T(8,128)(2,1)S(1)}, u32[]{:S(2)}, u32[]{:S(2)}) %collective-permute-start.17) | collective-permute-done | bytes 16416 | tf_op jit(solution)/shard_map/ppermute | solution.py:360
  59.2 0.6 %assemble.1 = bf16[8,4096]{1,0:T(8,128)(2,1)} custom-call(s32[1]{0:T(128)} %bitcast.1.me.level.chunk, bf16[8,1024]{1,0:T(8,128)(2,1)S(1)} %get-tuple-element.42.refs_0_, bf16[8,1024]{1,0:T(8,128)(2,1)S(1)} %collective-permute-done.15.refs_1_, bf16[8,1024]{1,0:T(8,128)(2,1)S(1)} %collective-permute-done.16.refs_2_, ...), custom_call_target="tpu_custom_call" | custom-call | tf_op jit(solution)/shard_map/assemble/pallas_call | solution.py:372
  (24 shorter events, 0.1 us)
Async XLA Ops:
  2.3 8.0 %collective-permute-start = (bf16[8,1152]{1,0:T(8,128)(2,1)}, bf16[8,1152]{1,0:T(8,128)(2,1)S(1)}, u32[]{:S(2)}, u32[]{:S(2)}) collective-permute-start(bf16[8,1152]{1,0:T(8,128)(2,1)} %get-tuple-element.24), channel_id=1, source_target_pairs={{0,1},{1,0},{2,3},{3,2},{4,5},{5,4},{6,7},{7,6},{8,9},{9,8},{10,11... | collective-permute-start | bytes 55304 | tf_op jit(solution)/shard_map/ppermute | solution.py:360
  5.3 5.0 %collective-permute-start.1 = (bf16[8,1152]{1,0:T(8,128)(2,1)}, bf16[8,1152]{1,0:T(8,128)(2,1)S(1)}, u32[]{:S(2)}, u32[]{:S(2)}) collective-permute-start(bf16[8,1152]{1,0:T(8,128)(2,1)} %get-tuple-element.25), channel_id=1, source_target_pairs={{0,2},{1,3},{2,0},{3,1},{4,6},{5,7},{6,4},{7,5},{8,10},{9,11},{10,... | collective-permute-start | bytes 55304 | tf_op jit(solution)/shard_map/ppermute | solution.py:360
  7.9 5.8 %collective-permute-start.2 = (bf16[8,1152]{1,0:T(8,128)(2,1)}, bf16[8,1152]{1,0:T(8,128)(2,1)S(1)}, u32[]{:S(2)}, u32[]{:S(2)}) collective-permute-start(bf16[8,1152]{1,0:T(8,128)(2,1)} %get-tuple-element.26), channel_id=1, source_target_pairs={{0,3},{1,2},{2,1},{3,0},{4,7},{5,6},{6,5},{7,4},{8,11},{9,10},{10,... | collective-permute-start | bytes 55304 | tf_op jit(solution)/shard_map/ppermute | solution.py:360
  7.9 0.8 %copy-start.2 = (bf16[8,4096]{1,0:T(8,128)(2,1)S(1)}, bf16[8,4096]{1,0:T(8,128)(2,1)}, u32[]{:S(2)}) copy-start(bf16[8,4096]{1,0:T(8,128)(2,1)} %hidden_ref.3) | copy-start | bytes 196612
  8.8 0.7 %copy-start.4 = (s32[8,2]{0,1:T(2,128)S(1)}, s32[8,2]{0,1:T(2,128)}, u32[]{:S(2)}) copy-start(s32[8,2]{0,1:T(2,128)} %param.14) | copy-start | bytes 196
  9.4 0.7 %copy-start.5 = (bf16[8,2]{0,1:T(2,128)(2,1)S(1)}, bf16[8,2]{0,1:T(2,128)(2,1)}, u32[]{:S(2)}) copy-start(bf16[8,2]{0,1:T(2,128)(2,1)} %param.15) | copy-start | bytes 100
  14.1 6.7 %collective-permute-start.3 = (bf16[24,1024]{1,0:T(8,128)(2,1)S(1)}, bf16[24,1024]{1,0:T(8,128)(2,1)S(1)}, u32[]{:S(2)}, u32[]{:S(2)}) collective-permute-start(bf16[24,1024]{1,0:T(8,128)(2,1)S(1)} %get-tuple-element.28), channel_id=1, source_target_pairs={{0,4},{4,0},{8,12},{12,8},{1,5},{5,1},{9,13},{13,9},{2,6},{6,2},{1... | collective-permute-start | bytes 147464 | tf_op jit(solution)/shard_map/ppermute | solution.py:360
  14.2 6.6 %collective-permute-start.4 = (bf16[24,1024]{1,0:T(8,128)(2,1)S(1)}, bf16[24,1024]{1,0:T(8,128)(2,1)S(1)}, u32[]{:S(2)}, u32[]{:S(2)}) collective-permute-start(bf16[24,1024]{1,0:T(8,128)(2,1)S(1)} %get-tuple-element.29), channel_id=1, source_target_pairs={{0,8},{4,12},{8,0},{12,4},{1,9},{5,13},{9,1},{13,5},{2,10},{6,14},... | collective-permute-start | bytes 147464 | tf_op jit(solution)/shard_map/ppermute | solution.py:360
  15.7 5.1 %collective-permute-start.5 = (bf16[24,1024]{1,0:T(8,128)(2,1)S(1)}, bf16[24,1024]{1,0:T(8,128)(2,1)S(1)}, u32[]{:S(2)}, u32[]{:S(2)}) collective-permute-start(bf16[24,1024]{1,0:T(8,128)(2,1)S(1)} %get-tuple-element.30), channel_id=1, source_target_pairs={{0,12},{4,8},{8,4},{12,0},{1,13},{5,9},{9,5},{13,1},{2,14},{6,10},... | collective-permute-start | bytes 147464 | tf_op jit(solution)/shard_map/ppermute | solution.py:360
  21.6 14.2 %collective-permute-start.6 = (bf16[2,48,768]{2,1,0:T(8,128)(2,1)S(1)}, bf16[2,48,768]{2,1,0:T(8,128)(2,1)S(1)}, u32[]{:S(2)}, u32[]{:S(2)}) collective-permute-start(bf16[2,48,768]{2,1,0:T(8,128)(2,1)S(1)} %gate_up.4.refs_2_), channel_id=1, source_target_pairs={{0,3},{1,2},{2,1},{3,0},{4,7},{5,6},{6,5},{7,4},{8,11},{9,10},{10,... | collective-permute-start | bytes 442376 | tf_op jit(solution)/shard_map/ppermute | solution.py:360
  22.7 13.1 %collective-permute-start.7 = (bf16[2,48,768]{2,1,0:T(8,128)(2,1)S(1)}, bf16[2,48,768]{2,1,0:T(8,128)(2,1)S(1)}, u32[]{:S(2)}, u32[]{:S(2)}) collective-permute-start(bf16[2,48,768]{2,1,0:T(8,128)(2,1)S(1)} %gate_up.5.refs_2_), channel_id=1, source_target_pairs={{0,2},{1,3},{2,0},{3,1},{4,6},{5,7},{6,4},{7,5},{8,10},{9,11},{10,... | collective-permute-start | bytes 442376 | tf_op jit(solution)/shard_map/ppermute | solution.py:360
  22.8 17.6 %slice-start = ((s8[6291456]{0:T(1024)(128)(4,1)}), s8[4194304]{0:T(1024)(128)(4,1)S(1)}, s32[]{:S(2)}) async-start(s8[6291456]{0:T(1024)(128)(4,1)} %bitcast.8), calls=%async_computation | async-start | bytes 8388608
  23.4 4.6 %copy-start = (bf16[1,8,192,1024]{3,2,1,0:T(8,128)(2,1)S(1)}, bf16[1,8,192,1024]{3,2,1,0:T(8,128)(2,1)}, u32[]{:S(2)}) copy-start(bf16[1,8,192,1024]{3,2,1,0:T(8,128)(2,1)} %cache_ref.1) | copy-start | bytes 9437188
  23.4 4.6 %copy-start.1 = (bf16[8,8192]{1,0:T(8,128)(2,1)S(1)}, bf16[8,8192]{1,0:T(8,128)(2,1)}, u32[]{:S(2)}) copy-start(bf16[8,8192]{1,0:T(8,128)(2,1)} %q_ref.1) | copy-start | bytes 393220
  23.4 4.6 %copy-start.3 = (bf16[8,1024]{1,0:T(8,128)(2,1)S(1)}, bf16[8,1024]{1,0:T(8,128)(2,1)}, u32[]{:S(2)}) copy-start(bf16[8,1024]{1,0:T(8,128)(2,1)} %new_ref.1) | copy-start | bytes 49156
  23.4 4.6 %copy-start.6 = (s32[1,8]{1,0:T(1,128)S(1)}, s32[1,8]{1,0:T(1,128)}, u32[]{:S(2)}) copy-start(s32[1,8]{1,0:T(1,128)} %param.12) | copy-start | bytes 100
  23.4 16.9 %slice-start.1 = ((s8[6291456]{0:T(1024)(128)(4,1)}), s8[2097152]{0:T(1024)(128)(4,1)S(1)}, s32[]{:S(2)}) async-start(s8[6291456]{0:T(1024)(128)(4,1)} %bitcast.8), calls=%async_computation.1 | async-start | bytes 4194304
  23.5 10.1 %collective-permute-start.8 = (bf16[2,48,768]{2,1,0:T(8,128)(2,1)S(1)}, bf16[2,48,768]{2,1,0:T(8,128)(2,1)S(1)}, u32[]{:S(2)}, u32[]{:S(2)}) collective-permute-start(bf16[2,48,768]{2,1,0:T(8,128)(2,1)S(1)} %gate_up.6.refs_2_), channel_id=1, source_target_pairs={{0,1},{1,0},{2,3},{3,2},{4,5},{5,4},{6,7},{7,6},{8,9},{9,8},{10,11... | collective-permute-start | bytes 442376 | tf_op jit(solution)/shard_map/ppermute | solution.py:360
  35.9 7.0 %collective-permute-start.9 = (bf16[2,48,384]{2,1,0:T(8,128)(2,1)S(1)}, bf16[2,48,384]{2,1,0:T(8,128)(2,1)S(1)}, u32[]{:S(2)}, u32[]{:S(2)}) collective-permute-start(bf16[2,48,384]{2,1,0:T(8,128)(2,1)S(1)} %activate.1.part_ref), channel_id=1, source_target_pairs={{0,3},{1,2},{2,1},{3,0},{4,7},{5,6},{6,5},{7,4},{8,11},{9,10},{10,... | collective-permute-start | bytes 221192 | tf_op jit(solution)/shard_map/ppermute | solution.py:360
  37.4 7.5 %collective-permute-start.11 = (bf16[2,48,384]{2,1,0:T(8,128)(2,1)S(1)}, bf16[2,48,384]{2,1,0:T(8,128)(2,1)S(1)}, u32[]{:S(2)}, u32[]{:S(2)}) collective-permute-start(bf16[2,48,384]{2,1,0:T(8,128)(2,1)S(1)} %activate.1.part_ref), channel_id=1, source_target_pairs={{0,2},{1,3},{2,0},{3,1},{4,6},{5,7},{6,4},{7,5},{8,10},{9,11},{10,... | collective-permute-start | bytes 221192 | tf_op jit(solution)/shard_map/ppermute | solution.py:360
  37.5 7.5 %collective-permute-start.10 = (bf16[2,48,384]{2,1,0:T(8,128)(2,1)S(1)}, bf16[2,48,384]{2,1,0:T(8,128)(2,1)S(1)}, u32[]{:S(2)}, u32[]{:S(2)}) collective-permute-start(bf16[2,48,384]{2,1,0:T(8,128)(2,1)S(1)} %activate.1.part_ref), channel_id=1, source_target_pairs={{0,1},{1,0},{2,3},{3,2},{4,5},{5,4},{6,7},{7,6},{8,9},{9,8},{10,11... | collective-permute-start | bytes 221192 | tf_op jit(solution)/shard_map/ppermute | solution.py:360
  45.8 2.2 %collective-permute-start.12 = (bf16[24,1024]{1,0:T(8,128)(2,1)S(1)}, bf16[24,1024]{1,0:T(8,128)(2,1)S(1)}, u32[]{:S(2)}, u32[]{:S(2)}) collective-permute-start(bf16[24,1024]{1,0:T(8,128)(2,1)S(1)} %get-tuple-element.39), channel_id=1, source_target_pairs={{0,4},{4,0},{8,12},{12,8},{1,5},{5,1},{9,13},{13,9},{2,6},{6,2},{1... | collective-permute-start | bytes 147464 | tf_op jit(solution)/shard_map/ppermute | solution.py:360
  45.8 4.2 %collective-permute-start.13 = (bf16[24,1024]{1,0:T(8,128)(2,1)S(1)}, bf16[24,1024]{1,0:T(8,128)(2,1)S(1)}, u32[]{:S(2)}, u32[]{:S(2)}) collective-permute-start(bf16[24,1024]{1,0:T(8,128)(2,1)S(1)} %get-tuple-element.40), channel_id=1, source_target_pairs={{0,8},{4,12},{8,0},{12,4},{1,9},{5,13},{9,1},{13,5},{2,10},{6,14},... | collective-permute-start | bytes 147464 | tf_op jit(solution)/shard_map/ppermute | solution.py:360
  47.4 3.7 %collective-permute-start.14 = (bf16[24,1024]{1,0:T(8,128)(2,1)S(1)}, bf16[24,1024]{1,0:T(8,128)(2,1)S(1)}, u32[]{:S(2)}, u32[]{:S(2)}) collective-permute-start(bf16[24,1024]{1,0:T(8,128)(2,1)S(1)} %get-tuple-element.41), channel_id=1, source_target_pairs={{0,12},{4,8},{8,4},{12,0},{1,13},{5,9},{9,5},{13,1},{2,14},{6,10},... | collective-permute-start | bytes 147464 | tf_op jit(solution)/shard_map/ppermute | solution.py:360
  51.4 4.5 %collective-permute-start.15 = (bf16[8,1024]{1,0:T(8,128)(2,1)S(1)}, bf16[8,1024]{1,0:T(8,128)(2,1)S(1)}, u32[]{:S(2)}, u32[]{:S(2)}) collective-permute-start(bf16[8,1024]{1,0:T(8,128)(2,1)S(1)} %get-tuple-element.43), channel_id=1, source_target_pairs={{0,1},{1,0},{2,3},{3,2},{4,5},{5,4},{6,7},{7,6},{8,9},{9,8},{10,11... | collective-permute-start | bytes 49160 | tf_op jit(solution)/shard_map/ppermute | solution.py:360
  51.4 4.7 %collective-permute-start.16 = (bf16[8,1024]{1,0:T(8,128)(2,1)S(1)}, bf16[8,1024]{1,0:T(8,128)(2,1)S(1)}, u32[]{:S(2)}, u32[]{:S(2)}) collective-permute-start(bf16[8,1024]{1,0:T(8,128)(2,1)S(1)} %get-tuple-element.44), channel_id=1, source_target_pairs={{0,2},{1,3},{2,0},{3,1},{4,6},{5,7},{6,4},{7,5},{8,10},{9,11},{10,... | collective-permute-start | bytes 49160 | tf_op jit(solution)/shard_map/ppermute | solution.py:360
  53.7 5.5 %collective-permute-start.17 = (bf16[8,1024]{1,0:T(8,128)(2,1)S(1)}, bf16[8,1024]{1,0:T(8,128)(2,1)S(1)}, u32[]{:S(2)}, u32[]{:S(2)}) collective-permute-start(bf16[8,1024]{1,0:T(8,128)(2,1)S(1)} %get-tuple-element.45), channel_id=1, source_target_pairs={{0,3},{1,2},{2,1},{3,0},{4,7},{5,6},{6,5},{7,4},{8,11},{9,10},{10,... | collective-permute-start | bytes 49160 | tf_op jit(solution)/shard_map/ppermute | solution.py:360

commit v12 on v11

--- a/solution.py
+++ b/solution.py
@@ -92,9 +92,9 @@
             jax.ShapeDtypeStruct((8, LANES), jnp.float32),
         ],
         scratch_shapes=[
-            pltpu.VMEM((QUERY_HEADS * rows, HEAD_SIZE), jnp.float32),
-            pltpu.VMEM((2 * KEY_HEADS * rows, HEAD_SIZE), jnp.float32),
-            pltpu.VMEM((QUERY_HEADS * rows, HEAD_SIZE), jnp.float32),
+            pltpu.VMEM(((QUERY_HEADS + 1) * rows, HEAD_SIZE), jnp.float32),
+            pltpu.VMEM(((2 * KEY_HEADS + 1) * rows, HEAD_SIZE), jnp.float32),
+            pltpu.VMEM(((QUERY_HEADS + 1) * rows, HEAD_SIZE), jnp.float32),
         ],
         compiler_params=params(32),
         cost_estimate=pl.CostEstimate(

time: 60.1 us -> 60.1 us (level)
  no operation moved by 1% of the time
where the time goes in v12:
time: 60.1 us; the launch traced here: 59.9 us
  starting transfers between devices  22.9 us (38%)
  Pallas kernels  17.9 us (30%)
  waiting for transfers between devices  16 us (27%)
  local copies, waits for them, and re-layouts  2.21 us (4%)
  between operations  0.88 us (1%)
    ppermute x18, starting transfers between devices, traded(): lax.ppermute(value, axis, [(i, i ^ index) for i in range(lax.axis_size(ax...  22.9 us
    ppermute x18, waiting for transfers between devices, traded(): lax.ppermute(value, axis, [(i, i ^ index) for i in range(lax.axis_size(ax...  16 us
    pallas_call x15, Pallas kernels, call(): pl.pallas_call(kernel, in_specs=[pl.BlockSpec(memory_space=pltpu.SMEM)] *...  7.66 us
    pallas_call x1, Pallas kernels, attend(): pl.pallas_call(attend_kernel, in_specs=[pl.BlockSpec(memory_space=pltpu.S...  5.53 us
    pallas_call x1, Pallas kernels, load(): pl.pallas_call(functools.partial(load_kernel, pieces), in_specs=[pl.Block...  4.72 us
    unnamed x18, local copies, waits for them, and re-layouts  2.21 us
  transfers between devices with their start and end apart: 18, of which 9 were waited for; matrix products, arithmetic and copies ran while one was open for 0% of the time, Pallas kernels for 22%

profile of v12, /device:TPU:0, one launch (start us, length us, event | category | flops | bytes accessed | tf_op | source)
XLA Modules:
  0.0 59.9 jit_solution(12005953784825107843)
XLA Ops:
  0.6 1.7 %prepare.1 = (bf16[8,1152]{1,0:T(8,128)(2,1)}, bf16[8,1152]{1,0:T(8,128)(2,1)}, bf16[8,1152]{1,0:T(8,128)(2,1)}) custom-call(s32[1]{0:T(128)} %bitcast.1.me.level.chunk, s32[2,8]{1,0:T(2,128)} %bitcast.10, bf16[2,8]{1,0:T(2,128)(2,1)} %bitcast.12, bf16[8,4096]{1,0:T(8,128)(2,1)} %hidden_ref.3), custom_call_target="tpu_custom_call" | custom-call | tf_op jit(solution)/shard_map/prepare/pallas_call | solution.py:372
  2.3 3.0 %collective-permute-start = (bf16[8,1152]{1,0:T(8,128)(2,1)}, bf16[8,1152]{1,0:T(8,128)(2,1)S(1)}, u32[]{:S(2)}, u32[]{:S(2)}) collective-permute-start(bf16[8,1152]{1,0:T(8,128)(2,1)} %get-tuple-element.24), channel_id=1, source_target_pairs={{0,1},{1,0},{2,3},{3,2},{4,5},{5,4},{6,7},{7,6},{8,9},{9,8},{10,11... | collective-permute-start | bytes 55304 | tf_op jit(solution)/shard_map/ppermute | solution.py:360
  5.3 2.6 %collective-permute-start.1 = (bf16[8,1152]{1,0:T(8,128)(2,1)}, bf16[8,1152]{1,0:T(8,128)(2,1)S(1)}, u32[]{:S(2)}, u32[]{:S(2)}) collective-permute-start(bf16[8,1152]{1,0:T(8,128)(2,1)} %get-tuple-element.25), channel_id=1, source_target_pairs={{0,2},{1,3},{2,0},{3,1},{4,6},{5,7},{6,4},{7,5},{8,10},{9,11},{10,... | collective-permute-start | bytes 55304 | tf_op jit(solution)/shard_map/ppermute | solution.py:360
  7.9 0.8 %copy-done.2 = bf16[8,4096]{1,0:T(8,128)(2,1)S(1)} copy-done((bf16[8,4096]{1,0:T(8,128)(2,1)S(1)}, bf16[8,4096]{1,0:T(8,128)(2,1)}, u32[]{:S(2)}) %copy-start.2) | copy-done | bytes 65560
  8.8 0.7 %copy-done.4 = s32[8,2]{0,1:T(2,128)S(1)} copy-done((s32[8,2]{0,1:T(2,128)S(1)}, s32[8,2]{0,1:T(2,128)}, u32[]{:S(2)}) %copy-start.4) | copy-done | bytes 88
  9.4 0.7 %copy-done.5 = bf16[8,2]{0,1:T(2,128)(2,1)S(1)} copy-done((bf16[8,2]{0,1:T(2,128)(2,1)S(1)}, bf16[8,2]{0,1:T(2,128)(2,1)}, u32[]{:S(2)}) %copy-start.5) | copy-done | bytes 56
  10.1 0.2 keep.1.refs_0_
  10.3 0.1 collective-permute-done.1.refs_2_
  10.3 3.3 %collective-permute-done.2.refs_3_ = bf16[8,1152]{1,0:T(8,128)(2,1)S(1)} collective-permute-done((bf16[8,1152]{1,0:T(8,128)(2,1)}, bf16[8,1152]{1,0:T(8,128)(2,1)S(1)}, u32[]{:S(2)}, u32[]{:S(2)}) %collective-permute-start.2) | collective-permute-done | bytes 18464 | tf_op jit(solution)/shard_map/ppermute | solution.py:360
  13.7 0.4 pack.1
  14.1 0.1 collective-permute-start.3
  14.2 1.6 %collective-permute-start.4 = (bf16[24,1024]{1,0:T(8,128)(2,1)S(1)}, bf16[24,1024]{1,0:T(8,128)(2,1)S(1)}, u32[]{:S(2)}, u32[]{:S(2)}) collective-permute-start(bf16[24,1024]{1,0:T(8,128)(2,1)S(1)} %get-tuple-element.29), channel_id=1, source_target_pairs={{0,8},{4,12},{8,0},{12,4},{1,9},{5,13},{9,1},{13,5},{2,10},{6,14},... | collective-permute-start | bytes 147464 | tf_op jit(solution)/shard_map/ppermute | solution.py:360
  15.7 0.3 collective-permute-start.5
  16.0 4.7 %load.1 = (bf16[2,1024,1536]{2,1,0:T(8,128)(2,1)S(1)}, bf16[2,1024,1536]{2,1,0:T(8,128)(2,1)S(1)}, f32[8,128]{1,0:T(8,128)S(1)}) custom-call(bf16[2,2,1024,1536]{3,2,1,0:T(8,128)(2,1)} %weight_hbm.1, bf16[24,1024]{1,0:T(8,128)(2,1)S(1)} %get-tuple-element.27.after_ref.refs_0_), custom_call_target="tpu_custom_call" | custom-call | flops 100000000 | tf_op jit(solution)/shard_map/load/pallas_call | solution.py:267
  20.8 0.2 select.1.rows_ref
  21.0 0.6 gate_up.4.refs_2_
  21.6 0.5 collective-permute-start.6
  22.1 0.6 %gate_up.5.refs_2_ = bf16[2,48,768]{2,1,0:T(8,128)(2,1)S(1)} custom-call(s32[1]{0:T(128)} %bitcast.6.chunk, bf16[2,48,1024]{2,1,0:T(8,128)(2,1)S(1)} %select.1.rows_ref, bf16[2,1024,1536]{2,1,0:T(8,128)(2,1)S(1)} %get-tuple-element.32.refs_0_, bf16[2,1024,1536]{2,1,0:T(8,128)(2,1)S(1)} %get-tuple-element.33.refs_1_, bf16[2,48,768]{2,1,0:T(8,128)(2,1)S(1)} %gate_up.4.refs_2_), custom_call_target="tpu_custom_call" | custom-call | flops 2000000000 | tf_op jit(solution)/shard_map/gate_up/pallas_call | solution.py:372
  22.7 0.1 collective-permute-start.7
  22.8 0.0 slice-start
  22.8 0.6 %gate_up.6.refs_2_ = bf16[2,48,768]{2,1,0:T(8,128)(2,1)S(1)} custom-call(s32[1]{0:T(128)} %bitcast.5.chunk, bf16[2,48,1024]{2,1,0:T(8,128)(2,1)S(1)} %select.1.rows_ref, bf16[2,1024,1536]{2,1,0:T(8,128)(2,1)S(1)} %get-tuple-element.32.refs_0_, bf16[2,1024,1536]{2,1,0:T(8,128)(2,1)S(1)} %get-tuple-element.33.refs_1_, bf16[2,48,768]{2,1,0:T(8,128)(2,1)S(1)} %gate_up.5.refs_2_), custom_call_target="tpu_custom_call" | custom-call | flops 2000000000 | tf_op jit(solution)/shard_map/gate_up/pallas_call | solution.py:372
  23.4 0.0 copy-start
  23.4 0.0 slice-start.1
  23.5 4.0 %collective-permute-start.8 = (bf16[2,48,768]{2,1,0:T(8,128)(2,1)S(1)}, bf16[2,48,768]{2,1,0:T(8,128)(2,1)S(1)}, u32[]{:S(2)}, u32[]{:S(2)}) collective-permute-start(bf16[2,48,768]{2,1,0:T(8,128)(2,1)S(1)} %gate_up.6.refs_2_), channel_id=1, source_target_pairs={{0,1},{1,0},{2,3},{3,2},{4,5},{5,4},{6,7},{7,6},{8,9},{9,8},{10,11... | collective-permute-start | bytes 442376 | tf_op jit(solution)/shard_map/ppermute | solution.py:360
  27.4 0.6 gate_up.7
  28.0 5.5 %attend.1 = (bf16[8,8192]{1,0:T(8,128)(2,1)}, f32[8,128]{1,0:T(8,128)S(1)}) custom-call(s32[8]{0:T(128)S(1)} %bitcast.14, bf16[8,8192]{1,0:T(8,128)(2,1)S(1)} %copy-done.1, bf16[8,1024]{1,0:T(8,128)(2,1)S(1)} %copy-done.3, bf16[1,8,192,1024]{3,2,1,0:T(8,128)(2,1)S(1)} %copy-done, f32[8,128]{1,0:T(8,128)S(1)} %get-tuple-element.34.after_ref), custom_call_target="tpu_custom_call" | custom-call | flops 50331648 | bytes 3145728 | tf_op jit(solution)/shard_map/attend/pallas_call | solution.py:85
  33.6 2.2 %collective-permute-done.7.refs_1_ = bf16[2,48,768]{2,1,0:T(8,128)(2,1)S(1)} collective-permute-done((bf16[2,48,768]{2,1,0:T(8,128)(2,1)S(1)}, bf16[2,48,768]{2,1,0:T(8,128)(2,1)S(1)}, u32[]{:S(2)}, u32[]{:S(2)}) %collective-permute-start.7) | collective-permute-done | bytes 147488 | tf_op jit(solution)/shard_map/ppermute | solution.py:360
  35.8 0.1 activate.1.part_ref
  35.9 1.5 %collective-permute-start.9 = (bf16[2,48,384]{2,1,0:T(8,128)(2,1)S(1)}, bf16[2,48,384]{2,1,0:T(8,128)(2,1)S(1)}, u32[]{:S(2)}, u32[]{:S(2)}) collective-permute-start(bf16[2,48,384]{2,1,0:T(8,128)(2,1)S(1)} %activate.1.part_ref), channel_id=1, source_target_pairs={{0,3},{1,2},{2,1},{3,0},{4,7},{5,6},{6,5},{7,4},{8,11},{9,10},{10,... | collective-permute-start | bytes 221192 | tf_op jit(solution)/shard_map/ppermute | solution.py:360
  37.5 2.9 %collective-permute-start.10 = (bf16[2,48,384]{2,1,0:T(8,128)(2,1)S(1)}, bf16[2,48,384]{2,1,0:T(8,128)(2,1)S(1)}, u32[]{:S(2)}, u32[]{:S(2)}) collective-permute-start(bf16[2,48,384]{2,1,0:T(8,128)(2,1)S(1)} %activate.1.part_ref), channel_id=1, source_target_pairs={{0,1},{1,0},{2,3},{3,2},{4,5},{5,4},{6,7},{7,6},{8,9},{9,8},{10,11... | collective-permute-start | bytes 221192 | tf_op jit(solution)/shard_map/ppermute | solution.py:360
  40.4 0.4 down_first.1.before_ref
  40.8 2.2 %collective-permute-done.9.part_ref = bf16[2,48,384]{2,1,0:T(8,128)(2,1)S(1)} collective-permute-done((bf16[2,48,384]{2,1,0:T(8,128)(2,1)S(1)}, bf16[2,48,384]{2,1,0:T(8,128)(2,1)S(1)}, u32[]{:S(2)}, u32[]{:S(2)}) %collective-permute-start.9) | collective-permute-done | bytes 73760 | tf_op jit(solution)/shard_map/ppermute | solution.py:360
  43.0 0.4 down_more.1.sum_ref
  43.4 1.6 %collective-permute-done.11.refs_1_ = bf16[2,48,384]{2,1,0:T(8,128)(2,1)S(1)} collective-permute-done((bf16[2,48,384]{2,1,0:T(8,128)(2,1)S(1)}, bf16[2,48,384]{2,1,0:T(8,128)(2,1)S(1)}, u32[]{:S(2)}, u32[]{:S(2)}) %collective-permute-start.11) | collective-permute-done | bytes 73760 | tf_op jit(solution)/shard_map/ppermute | solution.py:360
  44.9 0.8 %down_rest.1 = (bf16[24,1024]{1,0:T(8,128)(2,1)S(1)}, bf16[24,1024]{1,0:T(8,128)(2,1)S(1)}, bf16[24,1024]{1,0:T(8,128)(2,1)S(1)}, bf16[24,1024]{1,0:T(8,128)(2,1)S(1)}) custom-call(s32[1]{0:T(128)} %bitcast.1.me.level.chunk, f32[2,48,1024]{2,1,0:T(8,128)S(1)} %down_more.1.sum_ref, bf16[2,48,384]{2,1,0:T(8,128)(2,1)S(1)} %collective-permute-done.10.refs_0_, ...), custom_call_target="tpu_custom_call" | custom-call | tf_op jit(solution)/shard_map/down_rest/pallas_call | solution.py:372
  45.8 0.1 collective-permute-start.12
  45.8 1.6 %collective-permute-start.13 = (bf16[24,1024]{1,0:T(8,128)(2,1)S(1)}, bf16[24,1024]{1,0:T(8,128)(2,1)S(1)}, u32[]{:S(2)}, u32[]{:S(2)}) collective-permute-start(bf16[24,1024]{1,0:T(8,128)(2,1)S(1)} %get-tuple-element.40), channel_id=1, source_target_pairs={{0,8},{4,12},{8,0},{12,4},{1,9},{5,13},{9,1},{13,5},{2,10},{6,14},... | collective-permute-start | bytes 147464 | tf_op jit(solution)/shard_map/ppermute | solution.py:360
  47.4 0.3 collective-permute-start.14
  47.7 0.3 weigh.1.weight_ref
  48.0 2.0 %collective-permute-done.13.refs_2_ = bf16[24,1024]{1,0:T(8,128)(2,1)S(1)} collective-permute-done((bf16[24,1024]{1,0:T(8,128)(2,1)S(1)}, bf16[24,1024]{1,0:T(8,128)(2,1)S(1)}, u32[]{:S(2)}, u32[]{:S(2)}) %collective-permute-start.13) | collective-permute-done | bytes 49184 | tf_op jit(solution)/shard_map/ppermute | solution.py:360
  50.0 1.1 %collective-permute-done.14.refs_3_ = bf16[24,1024]{1,0:T(8,128)(2,1)S(1)} collective-permute-done((bf16[24,1024]{1,0:T(8,128)(2,1)S(1)}, bf16[24,1024]{1,0:T(8,128)(2,1)S(1)}, u32[]{:S(2)}, u32[]{:S(2)}) %collective-permute-start.14) | collective-permute-done | bytes 49184 | tf_op jit(solution)/shard_map/ppermute | solution.py:360
  51.1 0.2 combine.1
  51.4 0.1 collective-permute-start.15
  51.4 2.3 %collective-permute-start.16 = (bf16[8,1024]{1,0:T(8,128)(2,1)S(1)}, bf16[8,1024]{1,0:T(8,128)(2,1)S(1)}, u32[]{:S(2)}, u32[]{:S(2)}) collective-permute-start(bf16[8,1024]{1,0:T(8,128)(2,1)S(1)} %get-tuple-element.44), channel_id=1, source_target_pairs={{0,2},{1,3},{2,0},{3,1},{4,6},{5,7},{6,4},{7,5},{8,10},{9,11},{10,... | collective-permute-start | bytes 49160 | tf_op jit(solution)/shard_map/ppermute | solution.py:360
  53.7 2.1 %collective-permute-start.17 = (bf16[8,1024]{1,0:T(8,128)(2,1)S(1)}, bf16[8,1024]{1,0:T(8,128)(2,1)S(1)}, u32[]{:S(2)}, u32[]{:S(2)}) collective-permute-start(bf16[8,1024]{1,0:T(8,128)(2,1)S(1)} %get-tuple-element.45), channel_id=1, source_target_pairs={{0,3},{1,2},{2,1},{3,0},{4,7},{5,6},{6,5},{7,4},{8,11},{9,10},{10,... | collective-permute-start | bytes 49160 | tf_op jit(solution)/shard_map/ppermute | solution.py:360
  55.8 0.3 collective-permute-done.16.refs_2_
  56.2 3.1 %collective-permute-done.17.refs_3_ = bf16[8,1024]{1,0:T(8,128)(2,1)S(1)} collective-permute-done((bf16[8,1024]{1,0:T(8,128)(2,1)S(1)}, bf16[8,1024]{1,0:T(8,128)(2,1)S(1)}, u32[]{:S(2)}, u32[]{:S(2)}) %collective-permute-start.17) | collective-permute-done | bytes 16416 | tf_op jit(solution)/shard_map/ppermute | solution.py:360
  59.2 0.6 %assemble.1 = bf16[8,4096]{1,0:T(8,128)(2,1)} custom-call(s32[1]{0:T(128)} %bitcast.1.me.level.chunk, bf16[8,1024]{1,0:T(8,128)(2,1)S(1)} %get-tuple-element.42.refs_0_, bf16[8,1024]{1,0:T(8,128)(2,1)S(1)} %collective-permute-done.15.refs_1_, bf16[8,1024]{1,0:T(8,128)(2,1)S(1)} %collective-permute-done.16.refs_2_, ...), custom_call_target="tpu_custom_call" | custom-call | tf_op jit(solution)/shard_map/assemble/pallas_call | solution.py:372
  (24 shorter events, 0.1 us)
Async XLA Ops:
  2.3 8.0 %collective-permute-start = (bf16[8,1152]{1,0:T(8,128)(2,1)}, bf16[8,1152]{1,0:T(8,128)(2,1)S(1)}, u32[]{:S(2)}, u32[]{:S(2)}) collective-permute-start(bf16[8,1152]{1,0:T(8,128)(2,1)} %get-tuple-element.24), channel_id=1, source_target_pairs={{0,1},{1,0},{2,3},{3,2},{4,5},{5,4},{6,7},{7,6},{8,9},{9,8},{10,11... | collective-permute-start | bytes 55304 | tf_op jit(solution)/shard_map/ppermute | solution.py:360
  5.3 5.0 %collective-permute-start.1 = (bf16[8,1152]{1,0:T(8,128)(2,1)}, bf16[8,1152]{1,0:T(8,128)(2,1)S(1)}, u32[]{:S(2)}, u32[]{:S(2)}) collective-permute-start(bf16[8,1152]{1,0:T(8,128)(2,1)} %get-tuple-element.25), channel_id=1, source_target_pairs={{0,2},{1,3},{2,0},{3,1},{4,6},{5,7},{6,4},{7,5},{8,10},{9,11},{10,... | collective-permute-start | bytes 55304 | tf_op jit(solution)/shard_map/ppermute | solution.py:360
  7.9 5.8 %collective-permute-start.2 = (bf16[8,1152]{1,0:T(8,128)(2,1)}, bf16[8,1152]{1,0:T(8,128)(2,1)S(1)}, u32[]{:S(2)}, u32[]{:S(2)}) collective-permute-start(bf16[8,1152]{1,0:T(8,128)(2,1)} %get-tuple-element.26), channel_id=1, source_target_pairs={{0,3},{1,2},{2,1},{3,0},{4,7},{5,6},{6,5},{7,4},{8,11},{9,10},{10,... | collective-permute-start | bytes 55304 | tf_op jit(solution)/shard_map/ppermute | solution.py:360
  7.9 0.8 %copy-start.2 = (bf16[8,4096]{1,0:T(8,128)(2,1)S(1)}, bf16[8,4096]{1,0:T(8,128)(2,1)}, u32[]{:S(2)}) copy-start(bf16[8,4096]{1,0:T(8,128)(2,1)} %hidden_ref.3) | copy-start | bytes 196612
  8.8 0.7 %copy-start.4 = (s32[8,2]{0,1:T(2,128)S(1)}, s32[8,2]{0,1:T(2,128)}, u32[]{:S(2)}) copy-start(s32[8,2]{0,1:T(2,128)} %param.14) | copy-start | bytes 196
  9.4 0.7 %copy-start.5 = (bf16[8,2]{0,1:T(2,128)(2,1)S(1)}, bf16[8,2]{0,1:T(2,128)(2,1)}, u32[]{:S(2)}) copy-start(bf16[8,2]{0,1:T(2,128)(2,1)} %param.15) | copy-start | bytes 100
  14.1 6.7 %collective-permute-start.3 = (bf16[24,1024]{1,0:T(8,128)(2,1)S(1)}, bf16[24,1024]{1,0:T(8,128)(2,1)S(1)}, u32[]{:S(2)}, u32[]{:S(2)}) collective-permute-start(bf16[24,1024]{1,0:T(8,128)(2,1)S(1)} %get-tuple-element.28), channel_id=1, source_target_pairs={{0,4},{4,0},{8,12},{12,8},{1,5},{5,1},{9,13},{13,9},{2,6},{6,2},{1... | collective-permute-start | bytes 147464 | tf_op jit(solution)/shard_map/ppermute | solution.py:360
  14.2 6.6 %collective-permute-start.4 = (bf16[24,1024]{1,0:T(8,128)(2,1)S(1)}, bf16[24,1024]{1,0:T(8,128)(2,1)S(1)}, u32[]{:S(2)}, u32[]{:S(2)}) collective-permute-start(bf16[24,1024]{1,0:T(8,128)(2,1)S(1)} %get-tuple-element.29), channel_id=1, source_target_pairs={{0,8},{4,12},{8,0},{12,4},{1,9},{5,13},{9,1},{13,5},{2,10},{6,14},... | collective-permute-start | bytes 147464 | tf_op jit(solution)/shard_map/ppermute | solution.py:360
  15.7 5.1 %collective-permute-start.5 = (bf16[24,1024]{1,0:T(8,128)(2,1)S(1)}, bf16[24,1024]{1,0:T(8,128)(2,1)S(1)}, u32[]{:S(2)}, u32[]{:S(2)}) collective-permute-start(bf16[24,1024]{1,0:T(8,128)(2,1)S(1)} %get-tuple-element.30), channel_id=1, source_target_pairs={{0,12},{4,8},{8,4},{12,0},{1,13},{5,9},{9,5},{13,1},{2,14},{6,10},... | collective-permute-start | bytes 147464 | tf_op jit(solution)/shard_map/ppermute | solution.py:360
  21.6 14.2 %collective-permute-start.6 = (bf16[2,48,768]{2,1,0:T(8,128)(2,1)S(1)}, bf16[2,48,768]{2,1,0:T(8,128)(2,1)S(1)}, u32[]{:S(2)}, u32[]{:S(2)}) collective-permute-start(bf16[2,48,768]{2,1,0:T(8,128)(2,1)S(1)} %gate_up.4.refs_2_), channel_id=1, source_target_pairs={{0,3},{1,2},{2,1},{3,0},{4,7},{5,6},{6,5},{7,4},{8,11},{9,10},{10,... | collective-permute-start | bytes 442376 | tf_op jit(solution)/shard_map/ppermute | solution.py:360
  22.7 13.1 %collective-permute-start.7 = (bf16[2,48,768]{2,1,0:T(8,128)(2,1)S(1)}, bf16[2,48,768]{2,1,0:T(8,128)(2,1)S(1)}, u32[]{:S(2)}, u32[]{:S(2)}) collective-permute-start(bf16[2,48,768]{2,1,0:T(8,128)(2,1)S(1)} %gate_up.5.refs_2_), channel_id=1, source_target_pairs={{0,2},{1,3},{2,0},{3,1},{4,6},{5,7},{6,4},{7,5},{8,10},{9,11},{10,... | collective-permute-start | bytes 442376 | tf_op jit(solution)/shard_map/ppermute | solution.py:360
  22.8 17.6 %slice-start = ((s8[6291456]{0:T(1024)(128)(4,1)}), s8[4194304]{0:T(1024)(128)(4,1)S(1)}, s32[]{:S(2)}) async-start(s8[6291456]{0:T(1024)(128)(4,1)} %bitcast.8), calls=%async_computation | async-start | bytes 8388608
  23.4 4.6 %copy-start = (bf16[1,8,192,1024]{3,2,1,0:T(8,128)(2,1)S(1)}, bf16[1,8,192,1024]{3,2,1,0:T(8,128)(2,1)}, u32[]{:S(2)}) copy-start(bf16[1,8,192,1024]{3,2,1,0:T(8,128)(2,1)} %cache_ref.1) | copy-start | bytes 9437188
  23.4 4.6 %copy-start.1 = (bf16[8,8192]{1,0:T(8,128)(2,1)S(1)}, bf16[8,8192]{1,0:T(8,128)(2,1)}, u32[]{:S(2)}) copy-start(bf16[8,8192]{1,0:T(8,128)(2,1)} %q_ref.1) | copy-start | bytes 393220
  23.4 4.6 %copy-start.3 = (bf16[8,1024]{1,0:T(8,128)(2,1)S(1)}, bf16[8,1024]{1,0:T(8,128)(2,1)}, u32[]{:S(2)}) copy-start(bf16[8,1024]{1,0:T(8,128)(2,1)} %new_ref.1) | copy-start | bytes 49156
  23.4 4.6 %copy-start.6 = (s32[1,8]{1,0:T(1,128)S(1)}, s32[1,8]{1,0:T(1,128)}, u32[]{:S(2)}) copy-start(s32[1,8]{1,0:T(1,128)} %param.12) | copy-start | bytes 100
  23.4 16.9 %slice-start.1 = ((s8[6291456]{0:T(1024)(128)(4,1)}), s8[2097152]{0:T(1024)(128)(4,1)S(1)}, s32[]{:S(2)}) async-start(s8[6291456]{0:T(1024)(128)(4,1)} %bitcast.8), calls=%async_computation.1 | async-start | bytes 4194304
  23.5 10.1 %collective-permute-start.8 = (bf16[2,48,768]{2,1,0:T(8,128)(2,1)S(1)}, bf16[2,48,768]{2,1,0:T(8,128)(2,1)S(1)}, u32[]{:S(2)}, u32[]{:S(2)}) collective-permute-start(bf16[2,48,768]{2,1,0:T(8,128)(2,1)S(1)} %gate_up.6.refs_2_), channel_id=1, source_target_pairs={{0,1},{1,0},{2,3},{3,2},{4,5},{5,4},{6,7},{7,6},{8,9},{9,8},{10,11... | collective-permute-start | bytes 442376 | tf_op jit(solution)/shard_map/ppermute | solution.py:360
  35.9 7.0 %collective-permute-start.9 = (bf16[2,48,384]{2,1,0:T(8,128)(2,1)S(1)}, bf16[2,48,384]{2,1,0:T(8,128)(2,1)S(1)}, u32[]{:S(2)}, u32[]{:S(2)}) collective-permute-start(bf16[2,48,384]{2,1,0:T(8,128)(2,1)S(1)} %activate.1.part_ref), channel_id=1, source_target_pairs={{0,3},{1,2},{2,1},{3,0},{4,7},{5,6},{6,5},{7,4},{8,11},{9,10},{10,... | collective-permute-start | bytes 221192 | tf_op jit(solution)/shard_map/ppermute | solution.py:360
  37.4 7.5 %collective-permute-start.11 = (bf16[2,48,384]{2,1,0:T(8,128)(2,1)S(1)}, bf16[2,48,384]{2,1,0:T(8,128)(2,1)S(1)}, u32[]{:S(2)}, u32[]{:S(2)}) collective-permute-start(bf16[2,48,384]{2,1,0:T(8,128)(2,1)S(1)} %activate.1.part_ref), channel_id=1, source_target_pairs={{0,2},{1,3},{2,0},{3,1},{4,6},{5,7},{6,4},{7,5},{8,10},{9,11},{10,... | collective-permute-start | bytes 221192 | tf_op jit(solution)/shard_map/ppermute | solution.py:360
  37.5 7.5 %collective-permute-start.10 = (bf16[2,48,384]{2,1,0:T(8,128)(2,1)S(1)}, bf16[2,48,384]{2,1,0:T(8,128)(2,1)S(1)}, u32[]{:S(2)}, u32[]{:S(2)}) collective-permute-start(bf16[2,48,384]{2,1,0:T(8,128)(2,1)S(1)} %activate.1.part_ref), channel_id=1, source_target_pairs={{0,1},{1,0},{2,3},{3,2},{4,5},{5,4},{6,7},{7,6},{8,9},{9,8},{10,11... | collective-permute-start | bytes 221192 | tf_op jit(solution)/shard_map/ppermute | solution.py:360
  45.8 2.2 %collective-permute-start.12 = (bf16[24,1024]{1,0:T(8,128)(2,1)S(1)}, bf16[24,1024]{1,0:T(8,128)(2,1)S(1)}, u32[]{:S(2)}, u32[]{:S(2)}) collective-permute-start(bf16[24,1024]{1,0:T(8,128)(2,1)S(1)} %get-tuple-element.39), channel_id=1, source_target_pairs={{0,4},{4,0},{8,12},{12,8},{1,5},{5,1},{9,13},{13,9},{2,6},{6,2},{1... | collective-permute-start | bytes 147464 | tf_op jit(solution)/shard_map/ppermute | solution.py:360
  45.8 4.2 %collective-permute-start.13 = (bf16[24,1024]{1,0:T(8,128)(2,1)S(1)}, bf16[24,1024]{1,0:T(8,128)(2,1)S(1)}, u32[]{:S(2)}, u32[]{:S(2)}) collective-permute-start(bf16[24,1024]{1,0:T(8,128)(2,1)S(1)} %get-tuple-element.40), channel_id=1, source_target_pairs={{0,8},{4,12},{8,0},{12,4},{1,9},{5,13},{9,1},{13,5},{2,10},{6,14},... | collective-permute-start | bytes 147464 | tf_op jit(solution)/shard_map/ppermute | solution.py:360
  47.4 3.7 %collective-permute-start.14 = (bf16[24,1024]{1,0:T(8,128)(2,1)S(1)}, bf16[24,1024]{1,0:T(8,128)(2,1)S(1)}, u32[]{:S(2)}, u32[]{:S(2)}) collective-permute-start(bf16[24,1024]{1,0:T(8,128)(2,1)S(1)} %get-tuple-element.41), channel_id=1, source_target_pairs={{0,12},{4,8},{8,4},{12,0},{1,13},{5,9},{9,5},{13,1},{2,14},{6,10},... | collective-permute-start | bytes 147464 | tf_op jit(solution)/shard_map/ppermute | solution.py:360
  51.4 4.5 %collective-permute-start.15 = (bf16[8,1024]{1,0:T(8,128)(2,1)S(1)}, bf16[8,1024]{1,0:T(8,128)(2,1)S(1)}, u32[]{:S(2)}, u32[]{:S(2)}) collective-permute-start(bf16[8,1024]{1,0:T(8,128)(2,1)S(1)} %get-tuple-element.43), channel_id=1, source_target_pairs={{0,1},{1,0},{2,3},{3,2},{4,5},{5,4},{6,7},{7,6},{8,9},{9,8},{10,11... | collective-permute-start | bytes 49160 | tf_op jit(solution)/shard_map/ppermute | solution.py:360
  51.4 4.7 %collective-permute-start.16 = (bf16[8,1024]{1,0:T(8,128)(2,1)S(1)}, bf16[8,1024]{1,0:T(8,128)(2,1)S(1)}, u32[]{:S(2)}, u32[]{:S(2)}) collective-permute-start(bf16[8,1024]{1,0:T(8,128)(2,1)S(1)} %get-tuple-element.44), channel_id=1, source_target_pairs={{0,2},{1,3},{2,0},{3,1},{4,6},{5,7},{6,4},{7,5},{8,10},{9,11},{10,... | collective-permute-start | bytes 49160 | tf_op jit(solution)/shard_map/ppermute | solution.py:360
  53.7 5.5 %collective-permute-start.17 = (bf16[8,1024]{1,0:T(8,128)(2,1)S(1)}, bf16[8,1024]{1,0:T(8,128)(2,1)S(1)}, u32[]{:S(2)}, u32[]{:S(2)}) collective-permute-start(bf16[8,1024]{1,0:T(8,128)(2,1)S(1)} %get-tuple-element.45), channel_id=1, source_target_pairs={{0,3},{1,2},{2,1},{3,0},{4,7},{5,6},{6,5},{7,4},{8,11},{9,10},{10,... | collective-permute-start | bytes 49160 | tf_op jit(solution)/shard_map/ppermute | solution.py:360

commit v13 on v12

--- a/solution.py
+++ b/solution.py
@@ -411,15 +411,16 @@
     parts = trade([active] * inner, "inner")
     sums_shape = jax.ShapeDtypeStruct((experts, count, width), jnp.float32)
     sums = call(down_first_kernel, [level], [active, down_weight], sums_shape, "down_first", 24)
-    sums = call(
-        functools.partial(down_more_kernel, inner - 1),
-        [level],
-        [sums, parts[-1], down_weight],
-        sums_shape,
-        "down_more",
-        24,
-    )
-    rest = list(range(1, inner - 1))
+    for index in [inner - 1, *range(1, inner - 2)]:
+        sums = call(
+            functools.partial(down_more_kernel, index),
+            [level],
+            [sums, parts[index], down_weight],
+            sums_shape,
+            "down_more",
+            24,
+        )
+    rest = [inner - 2]
     back = call(
         functools.partial(down_rest_kernel, rest),
         [level],

time: 60.1 us -> 60.1 us (level)
    pallas_call x15 -> x16, Pallas kernels: 7.66 us -> 7.77 us  [call(): pl.pallas_call(kernel, in_specs=[pl.BlockSpec(memory_space=pltpu.SMEM)] *...]
  transfers between devices with their start and end apart: 18 -> 18, of which waited for: 9 -> 9; matrix products, arithmetic and copies ran while one was open for 0% -> 0% of each run, Pallas kernels for 22% -> 23%
where the time goes in v13:
time: 60.1 us; the launch traced here: 59.8 us
  starting transfers between devices  22.9 us (38%)
  Pallas kernels  18 us (30%)
  waiting for transfers between devices  15.8 us (26%)
  local copies, waits for them, and re-layouts  2.21 us (4%)
  between operations  0.89 us (1%)
    ppermute x18, starting transfers between devices, traded(): lax.ppermute(value, axis, [(i, i ^ index) for i in range(lax.axis_size(ax...  22.9 us
    ppermute x18, waiting for transfers between devices, traded(): lax.ppermute(value, axis, [(i, i ^ index) for i in range(lax.axis_size(ax...  15.8 us
    pallas_call x16, Pallas kernels, call(): pl.pallas_call(kernel, in_specs=[pl.BlockSpec(memory_space=pltpu.SMEM)] *...  7.77 us
    pallas_call x1, Pallas kernels, attend(): pl.pallas_call(attend_kernel, in_specs=[pl.BlockSpec(memory_space=pltpu.S...  5.53 us
    pallas_call x1, Pallas kernels, load(): pl.pallas_call(functools.partial(load_kernel, pieces), in_specs=[pl.Block...  4.72 us
    unnamed x18, local copies, waits for them, and re-layouts  2.21 us
  transfers between devices with their start and end apart: 18, of which 9 were waited for; matrix products, arithmetic and copies ran while one was open for 0% of the time, Pallas kernels for 23%

profile of v13, /device:TPU:0, one launch (start us, length us, event | category | flops | bytes accessed | tf_op | source)
XLA Modules:
  0.0 59.8 jit_solution(3481091091774226534)
XLA Ops:
  0.6 1.7 %prepare.1 = (bf16[8,1152]{1,0:T(8,128)(2,1)}, bf16[8,1152]{1,0:T(8,128)(2,1)}, bf16[8,1152]{1,0:T(8,128)(2,1)}) custom-call(s32[1]{0:T(128)} %bitcast.1.me.level.chunk, s32[2,8]{1,0:T(2,128)} %bitcast.10, bf16[2,8]{1,0:T(2,128)(2,1)} %bitcast.12, bf16[8,4096]{1,0:T(8,128)(2,1)} %hidden_ref.3), custom_call_target="tpu_custom_call" | custom-call | tf_op jit(solution)/shard_map/prepare/pallas_call | solution.py:372
  2.3 3.0 %collective-permute-start = (bf16[8,1152]{1,0:T(8,128)(2,1)}, bf16[8,1152]{1,0:T(8,128)(2,1)S(1)}, u32[]{:S(2)}, u32[]{:S(2)}) collective-permute-start(bf16[8,1152]{1,0:T(8,128)(2,1)} %get-tuple-element.24), channel_id=1, source_target_pairs={{0,1},{1,0},{2,3},{3,2},{4,5},{5,4},{6,7},{7,6},{8,9},{9,8},{10,11... | collective-permute-start | bytes 55304 | tf_op jit(solution)/shard_map/ppermute | solution.py:360
  5.3 2.6 %collective-permute-start.1 = (bf16[8,1152]{1,0:T(8,128)(2,1)}, bf16[8,1152]{1,0:T(8,128)(2,1)S(1)}, u32[]{:S(2)}, u32[]{:S(2)}) collective-permute-start(bf16[8,1152]{1,0:T(8,128)(2,1)} %get-tuple-element.25), channel_id=1, source_target_pairs={{0,2},{1,3},{2,0},{3,1},{4,6},{5,7},{6,4},{7,5},{8,10},{9,11},{10,... | collective-permute-start | bytes 55304 | tf_op jit(solution)/shard_map/ppermute | solution.py:360
  7.9 0.8 %copy-done.2 = bf16[8,4096]{1,0:T(8,128)(2,1)S(1)} copy-done((bf16[8,4096]{1,0:T(8,128)(2,1)S(1)}, bf16[8,4096]{1,0:T(8,128)(2,1)}, u32[]{:S(2)}) %copy-start.2) | copy-done | bytes 65560
  8.8 0.7 %copy-done.4 = s32[8,2]{0,1:T(2,128)S(1)} copy-done((s32[8,2]{0,1:T(2,128)S(1)}, s32[8,2]{0,1:T(2,128)}, u32[]{:S(2)}) %copy-start.4) | copy-done | bytes 88
  9.4 0.7 %copy-done.5 = bf16[8,2]{0,1:T(2,128)(2,1)S(1)} copy-done((bf16[8,2]{0,1:T(2,128)(2,1)S(1)}, bf16[8,2]{0,1:T(2,128)(2,1)}, u32[]{:S(2)}) %copy-start.5) | copy-done | bytes 56
  10.1 0.2 keep.1.refs_0_
  10.3 0.1 collective-permute-done.1.refs_2_
  10.3 3.3 %collective-permute-done.2.refs_3_ = bf16[8,1152]{1,0:T(8,128)(2,1)S(1)} collective-permute-done((bf16[8,1152]{1,0:T(8,128)(2,1)}, bf16[8,1152]{1,0:T(8,128)(2,1)S(1)}, u32[]{:S(2)}, u32[]{:S(2)}) %collective-permute-start.2) | collective-permute-done | bytes 18464 | tf_op jit(solution)/shard_map/ppermute | solution.py:360
  13.7 0.4 pack.1
  14.1 0.1 collective-permute-start.3
  14.2 1.6 %collective-permute-start.4 = (bf16[24,1024]{1,0:T(8,128)(2,1)S(1)}, bf16[24,1024]{1,0:T(8,128)(2,1)S(1)}, u32[]{:S(2)}, u32[]{:S(2)}) collective-permute-start(bf16[24,1024]{1,0:T(8,128)(2,1)S(1)} %get-tuple-element.29), channel_id=1, source_target_pairs={{0,8},{4,12},{8,0},{12,4},{1,9},{5,13},{9,1},{13,5},{2,10},{6,14},... | collective-permute-start | bytes 147464 | tf_op jit(solution)/shard_map/ppermute | solution.py:360
  15.7 0.3 collective-permute-start.5
  16.0 4.7 %load.1 = (bf16[2,1024,1536]{2,1,0:T(8,128)(2,1)S(1)}, bf16[2,1024,1536]{2,1,0:T(8,128)(2,1)S(1)}, f32[8,128]{1,0:T(8,128)S(1)}) custom-call(bf16[2,2,1024,1536]{3,2,1,0:T(8,128)(2,1)} %weight_hbm.1, bf16[24,1024]{1,0:T(8,128)(2,1)S(1)} %get-tuple-element.27.after_ref.refs_0_), custom_call_target="tpu_custom_call" | custom-call | flops 100000000 | tf_op jit(solution)/shard_map/load/pallas_call | solution.py:267
  20.8 0.2 select.1.rows_ref
  21.0 0.6 gate_up.4.refs_2_
  21.6 0.5 collective-permute-start.6
  22.1 0.6 %gate_up.5.refs_2_ = bf16[2,48,768]{2,1,0:T(8,128)(2,1)S(1)} custom-call(s32[1]{0:T(128)} %bitcast.6.chunk, bf16[2,48,1024]{2,1,0:T(8,128)(2,1)S(1)} %select.1.rows_ref, bf16[2,1024,1536]{2,1,0:T(8,128)(2,1)S(1)} %get-tuple-element.32.refs_0_, bf16[2,1024,1536]{2,1,0:T(8,128)(2,1)S(1)} %get-tuple-element.33.refs_1_, bf16[2,48,768]{2,1,0:T(8,128)(2,1)S(1)} %gate_up.4.refs_2_), custom_call_target="tpu_custom_call" | custom-call | flops 2000000000 | tf_op jit(solution)/shard_map/gate_up/pallas_call | solution.py:372
  22.7 0.1 collective-permute-start.7
  22.8 0.0 slice-start
  22.8 0.6 %gate_up.6.refs_2_ = bf16[2,48,768]{2,1,0:T(8,128)(2,1)S(1)} custom-call(s32[1]{0:T(128)} %bitcast.5.chunk, bf16[2,48,1024]{2,1,0:T(8,128)(2,1)S(1)} %select.1.rows_ref, bf16[2,1024,1536]{2,1,0:T(8,128)(2,1)S(1)} %get-tuple-element.32.refs_0_, bf16[2,1024,1536]{2,1,0:T(8,128)(2,1)S(1)} %get-tuple-element.33.refs_1_, bf16[2,48,768]{2,1,0:T(8,128)(2,1)S(1)} %gate_up.5.refs_2_), custom_call_target="tpu_custom_call" | custom-call | flops 2000000000 | tf_op jit(solution)/shard_map/gate_up/pallas_call | solution.py:372
  23.4 0.0 slice-start.1
  23.5 4.0 %collective-permute-start.8 = (bf16[2,48,768]{2,1,0:T(8,128)(2,1)S(1)}, bf16[2,48,768]{2,1,0:T(8,128)(2,1)S(1)}, u32[]{:S(2)}, u32[]{:S(2)}) collective-permute-start(bf16[2,48,768]{2,1,0:T(8,128)(2,1)S(1)} %gate_up.6.refs_2_), channel_id=1, source_target_pairs={{0,1},{1,0},{2,3},{3,2},{4,5},{5,4},{6,7},{7,6},{8,9},{9,8},{10,11... | collective-permute-start | bytes 442376 | tf_op jit(solution)/shard_map/ppermute | solution.py:360
  27.4 0.6 gate_up.7
  28.0 5.5 %attend.1 = (bf16[8,8192]{1,0:T(8,128)(2,1)}, f32[8,128]{1,0:T(8,128)S(1)}) custom-call(s32[8]{0:T(128)S(1)} %bitcast.14, bf16[8,8192]{1,0:T(8,128)(2,1)S(1)} %copy-done.1, bf16[8,1024]{1,0:T(8,128)(2,1)S(1)} %copy-done.3, bf16[1,8,192,1024]{3,2,1,0:T(8,128)(2,1)S(1)} %copy-done, f32[8,128]{1,0:T(8,128)S(1)} %get-tuple-element.34.after_ref), custom_call_target="tpu_custom_call" | custom-call | flops 50331648 | bytes 3145728 | tf_op jit(solution)/shard_map/attend/pallas_call | solution.py:85
  33.6 2.2 %collective-permute-done.7.refs_1_ = bf16[2,48,768]{2,1,0:T(8,128)(2,1)S(1)} collective-permute-done((bf16[2,48,768]{2,1,0:T(8,128)(2,1)S(1)}, bf16[2,48,768]{2,1,0:T(8,128)(2,1)S(1)}, u32[]{:S(2)}, u32[]{:S(2)}) %collective-permute-start.7) | collective-permute-done | bytes 147488 | tf_op jit(solution)/shard_map/ppermute | solution.py:360
  35.8 0.1 activate.1.part_ref
  35.9 1.5 %collective-permute-start.9 = (bf16[2,48,384]{2,1,0:T(8,128)(2,1)S(1)}, bf16[2,48,384]{2,1,0:T(8,128)(2,1)S(1)}, u32[]{:S(2)}, u32[]{:S(2)}) collective-permute-start(bf16[2,48,384]{2,1,0:T(8,128)(2,1)S(1)} %activate.1.part_ref), channel_id=1, source_target_pairs={{0,3},{1,2},{2,1},{3,0},{4,7},{5,6},{6,5},{7,4},{8,11},{9,10},{10,... | collective-permute-start | bytes 221192 | tf_op jit(solution)/shard_map/ppermute | solution.py:360
  37.5 2.9 %collective-permute-start.11 = (bf16[2,48,384]{2,1,0:T(8,128)(2,1)S(1)}, bf16[2,48,384]{2,1,0:T(8,128)(2,1)S(1)}, u32[]{:S(2)}, u32[]{:S(2)}) collective-permute-start(bf16[2,48,384]{2,1,0:T(8,128)(2,1)S(1)} %activate.1.part_ref), channel_id=1, source_target_pairs={{0,2},{1,3},{2,0},{3,1},{4,6},{5,7},{6,4},{7,5},{8,10},{9,11},{10,... | collective-permute-start | bytes 221192 | tf_op jit(solution)/shard_map/ppermute | solution.py:360
  40.4 0.4 down_first.1.before_ref
  40.8 2.2 %collective-permute-done.9.part_ref = bf16[2,48,384]{2,1,0:T(8,128)(2,1)S(1)} collective-permute-done((bf16[2,48,384]{2,1,0:T(8,128)(2,1)S(1)}, bf16[2,48,384]{2,1,0:T(8,128)(2,1)S(1)}, u32[]{:S(2)}, u32[]{:S(2)}) %collective-permute-start.9) | collective-permute-done | bytes 73760 | tf_op jit(solution)/shard_map/ppermute | solution.py:360
  42.9 0.4 down_more.2.before_ref
  43.3 0.7 %collective-permute-done.10.part_ref = bf16[2,48,384]{2,1,0:T(8,128)(2,1)S(1)} collective-permute-done((bf16[2,48,384]{2,1,0:T(8,128)(2,1)S(1)}, bf16[2,48,384]{2,1,0:T(8,128)(2,1)S(1)}, u32[]{:S(2)}, u32[]{:S(2)}) %collective-permute-start.10) | collective-permute-done | bytes 73760 | tf_op jit(solution)/shard_map/ppermute | solution.py:360
  44.0 0.4 down_more.3.sum_ref
  44.4 0.5 down_rest.1
  45.0 0.1 collective-permute-start.12
  45.1 1.6 %collective-permute-start.13 = (bf16[24,1024]{1,0:T(8,128)(2,1)S(1)}, bf16[24,1024]{1,0:T(8,128)(2,1)S(1)}, u32[]{:S(2)}, u32[]{:S(2)}) collective-permute-start(bf16[24,1024]{1,0:T(8,128)(2,1)S(1)} %get-tuple-element.40), channel_id=1, source_target_pairs={{0,8},{4,12},{8,0},{12,4},{1,9},{5,13},{9,1},{13,5},{2,10},{6,14},... | collective-permute-start | bytes 147464 | tf_op jit(solution)/shard_map/ppermute | solution.py:360
  46.6 0.3 collective-permute-start.14
  46.9 0.3 weigh.1.weight_ref
  47.2 2.0 %collective-permute-done.13.refs_2_ = bf16[24,1024]{1,0:T(8,128)(2,1)S(1)} collective-permute-done((bf16[24,1024]{1,0:T(8,128)(2,1)S(1)}, bf16[24,1024]{1,0:T(8,128)(2,1)S(1)}, u32[]{:S(2)}, u32[]{:S(2)}) %collective-permute-start.13) | collective-permute-done | bytes 49184 | tf_op jit(solution)/shard_map/ppermute | solution.py:360
  49.2 1.1 %collective-permute-done.14.refs_3_ = bf16[24,1024]{1,0:T(8,128)(2,1)S(1)} collective-permute-done((bf16[24,1024]{1,0:T(8,128)(2,1)S(1)}, bf16[24,1024]{1,0:T(8,128)(2,1)S(1)}, u32[]{:S(2)}, u32[]{:S(2)}) %collective-permute-start.14) | collective-permute-done | bytes 49184 | tf_op jit(solution)/shard_map/ppermute | solution.py:360
  50.3 0.2 combine.1
  50.6 1.2 %collective-permute-start.15 = (bf16[8,1024]{1,0:T(8,128)(2,1)S(1)}, bf16[8,1024]{1,0:T(8,128)(2,1)S(1)}, u32[]{:S(2)}, u32[]{:S(2)}) collective-permute-start(bf16[8,1024]{1,0:T(8,128)(2,1)S(1)} %get-tuple-element.43), channel_id=1, source_target_pairs={{0,1},{1,0},{2,3},{3,2},{4,5},{5,4},{6,7},{7,6},{8,9},{9,8},{10,11... | collective-permute-start | bytes 49160 | tf_op jit(solution)/shard_map/ppermute | solution.py:360
  51.8 1.9 %collective-permute-start.16 = (bf16[8,1024]{1,0:T(8,128)(2,1)S(1)}, bf16[8,1024]{1,0:T(8,128)(2,1)S(1)}, u32[]{:S(2)}, u32[]{:S(2)}) collective-permute-start(bf16[8,1024]{1,0:T(8,128)(2,1)S(1)} %get-tuple-element.44), channel_id=1, source_target_pairs={{0,2},{1,3},{2,0},{3,1},{4,6},{5,7},{6,4},{7,5},{8,10},{9,11},{10,... | collective-permute-start | bytes 49160 | tf_op jit(solution)/shard_map/ppermute | solution.py:360
  53.7 1.4 %collective-permute-start.17 = (bf16[8,1024]{1,0:T(8,128)(2,1)S(1)}, bf16[8,1024]{1,0:T(8,128)(2,1)S(1)}, u32[]{:S(2)}, u32[]{:S(2)}) collective-permute-start(bf16[8,1024]{1,0:T(8,128)(2,1)S(1)} %get-tuple-element.45), channel_id=1, source_target_pairs={{0,3},{1,2},{2,1},{3,0},{4,7},{5,6},{6,5},{7,4},{8,11},{9,10},{10,... | collective-permute-start | bytes 49160 | tf_op jit(solution)/shard_map/ppermute | solution.py:360
  55.0 1.4 %collective-permute-done.16.refs_2_ = bf16[8,1024]{1,0:T(8,128)(2,1)S(1)} collective-permute-done((bf16[8,1024]{1,0:T(8,128)(2,1)S(1)}, bf16[8,1024]{1,0:T(8,128)(2,1)S(1)}, u32[]{:S(2)}, u32[]{:S(2)}) %collective-permute-start.16) | collective-permute-done | bytes 16416 | tf_op jit(solution)/shard_map/ppermute | solution.py:360
  56.4 2.8 %collective-permute-done.17.refs_3_ = bf16[8,1024]{1,0:T(8,128)(2,1)S(1)} collective-permute-done((bf16[8,1024]{1,0:T(8,128)(2,1)S(1)}, bf16[8,1024]{1,0:T(8,128)(2,1)S(1)}, u32[]{:S(2)}, u32[]{:S(2)}) %collective-permute-start.17) | collective-permute-done | bytes 16416 | tf_op jit(solution)/shard_map/ppermute | solution.py:360
  59.2 0.6 %assemble.1 = bf16[8,4096]{1,0:T(8,128)(2,1)} custom-call(s32[1]{0:T(128)} %bitcast.1.me.level.chunk, bf16[8,1024]{1,0:T(8,128)(2,1)S(1)} %get-tuple-element.42.refs_0_, bf16[8,1024]{1,0:T(8,128)(2,1)S(1)} %collective-permute-done.15.refs_1_, bf16[8,1024]{1,0:T(8,128)(2,1)S(1)} %collective-permute-done.16.refs_2_, ...), custom_call_target="tpu_custom_call" | custom-call | tf_op jit(solution)/shard_map/assemble/pallas_call | solution.py:372
  (25 shorter events, 0.1 us)
Async XLA Ops:
  2.3 8.0 %collective-permute-start = (bf16[8,1152]{1,0:T(8,128)(2,1)}, bf16[8,1152]{1,0:T(8,128)(2,1)S(1)}, u32[]{:S(2)}, u32[]{:S(2)}) collective-permute-start(bf16[8,1152]{1,0:T(8,128)(2,1)} %get-tuple-element.24), channel_id=1, source_target_pairs={{0,1},{1,0},{2,3},{3,2},{4,5},{5,4},{6,7},{7,6},{8,9},{9,8},{10,11... | collective-permute-start | bytes 55304 | tf_op jit(solution)/shard_map/ppermute | solution.py:360
  5.3 5.0 %collective-permute-start.1 = (bf16[8,1152]{1,0:T(8,128)(2,1)}, bf16[8,1152]{1,0:T(8,128)(2,1)S(1)}, u32[]{:S(2)}, u32[]{:S(2)}) collective-permute-start(bf16[8,1152]{1,0:T(8,128)(2,1)} %get-tuple-element.25), channel_id=1, source_target_pairs={{0,2},{1,3},{2,0},{3,1},{4,6},{5,7},{6,4},{7,5},{8,10},{9,11},{10,... | collective-permute-start | bytes 55304 | tf_op jit(solution)/shard_map/ppermute | solution.py:360
  7.9 5.8 %collective-permute-start.2 = (bf16[8,1152]{1,0:T(8,128)(2,1)}, bf16[8,1152]{1,0:T(8,128)(2,1)S(1)}, u32[]{:S(2)}, u32[]{:S(2)}) collective-permute-start(bf16[8,1152]{1,0:T(8,128)(2,1)} %get-tuple-element.26), channel_id=1, source_target_pairs={{0,3},{1,2},{2,1},{3,0},{4,7},{5,6},{6,5},{7,4},{8,11},{9,10},{10,... | collective-permute-start | bytes 55304 | tf_op jit(solution)/shard_map/ppermute | solution.py:360
  7.9 0.8 %copy-start.2 = (bf16[8,4096]{1,0:T(8,128)(2,1)S(1)}, bf16[8,4096]{1,0:T(8,128)(2,1)}, u32[]{:S(2)}) copy-start(bf16[8,4096]{1,0:T(8,128)(2,1)} %hidden_ref.3) | copy-start | bytes 196612
  8.8 0.7 %copy-start.4 = (s32[8,2]{0,1:T(2,128)S(1)}, s32[8,2]{0,1:T(2,128)}, u32[]{:S(2)}) copy-start(s32[8,2]{0,1:T(2,128)} %param.14) | copy-start | bytes 196
  9.4 0.7 %copy-start.5 = (bf16[8,2]{0,1:T(2,128)(2,1)S(1)}, bf16[8,2]{0,1:T(2,128)(2,1)}, u32[]{:S(2)}) copy-start(bf16[8,2]{0,1:T(2,128)(2,1)} %param.15) | copy-start | bytes 100
  14.1 6.7 %collective-permute-start.3 = (bf16[24,1024]{1,0:T(8,128)(2,1)S(1)}, bf16[24,1024]{1,0:T(8,128)(2,1)S(1)}, u32[]{:S(2)}, u32[]{:S(2)}) collective-permute-start(bf16[24,1024]{1,0:T(8,128)(2,1)S(1)} %get-tuple-element.28), channel_id=1, source_target_pairs={{0,4},{4,0},{8,12},{12,8},{1,5},{5,1},{9,13},{13,9},{2,6},{6,2},{1... | collective-permute-start | bytes 147464 | tf_op jit(solution)/shard_map/ppermute | solution.py:360
  14.2 6.6 %collective-permute-start.4 = (bf16[24,1024]{1,0:T(8,128)(2,1)S(1)}, bf16[24,1024]{1,0:T(8,128)(2,1)S(1)}, u32[]{:S(2)}, u32[]{:S(2)}) collective-permute-start(bf16[24,1024]{1,0:T(8,128)(2,1)S(1)} %get-tuple-element.29), channel_id=1, source_target_pairs={{0,8},{4,12},{8,0},{12,4},{1,9},{5,13},{9,1},{13,5},{2,10},{6,14},... | collective-permute-start | bytes 147464 | tf_op jit(solution)/shard_map/ppermute | solution.py:360
  15.7 5.1 %collective-permute-start.5 = (bf16[24,1024]{1,0:T(8,128)(2,1)S(1)}, bf16[24,1024]{1,0:T(8,128)(2,1)S(1)}, u32[]{:S(2)}, u32[]{:S(2)}) collective-permute-start(bf16[24,1024]{1,0:T(8,128)(2,1)S(1)} %get-tuple-element.30), channel_id=1, source_target_pairs={{0,12},{4,8},{8,4},{12,0},{1,13},{5,9},{9,5},{13,1},{2,14},{6,10},... | collective-permute-start | bytes 147464 | tf_op jit(solution)/shard_map/ppermute | solution.py:360
  21.6 14.2 %collective-permute-start.6 = (bf16[2,48,768]{2,1,0:T(8,128)(2,1)S(1)}, bf16[2,48,768]{2,1,0:T(8,128)(2,1)S(1)}, u32[]{:S(2)}, u32[]{:S(2)}) collective-permute-start(bf16[2,48,768]{2,1,0:T(8,128)(2,1)S(1)} %gate_up.4.refs_2_), channel_id=1, source_target_pairs={{0,3},{1,2},{2,1},{3,0},{4,7},{5,6},{6,5},{7,4},{8,11},{9,10},{10,... | collective-permute-start | bytes 442376 | tf_op jit(solution)/shard_map/ppermute | solution.py:360
  22.7 13.1 %collective-permute-start.7 = (bf16[2,48,768]{2,1,0:T(8,128)(2,1)S(1)}, bf16[2,48,768]{2,1,0:T(8,128)(2,1)S(1)}, u32[]{:S(2)}, u32[]{:S(2)}) collective-permute-start(bf16[2,48,768]{2,1,0:T(8,128)(2,1)S(1)} %gate_up.5.refs_2_), channel_id=1, source_target_pairs={{0,2},{1,3},{2,0},{3,1},{4,6},{5,7},{6,4},{7,5},{8,10},{9,11},{10,... | collective-permute-start | bytes 442376 | tf_op jit(solution)/shard_map/ppermute | solution.py:360
  22.8 17.6 %slice-start = ((s8[6291456]{0:T(1024)(128)(4,1)}), s8[4194304]{0:T(1024)(128)(4,1)S(1)}, s32[]{:S(2)}) async-start(s8[6291456]{0:T(1024)(128)(4,1)} %bitcast.8), calls=%async_computation | async-start | bytes 8388608
  23.4 4.6 %copy-start = (bf16[1,8,192,1024]{3,2,1,0:T(8,128)(2,1)S(1)}, bf16[1,8,192,1024]{3,2,1,0:T(8,128)(2,1)}, u32[]{:S(2)}) copy-start(bf16[1,8,192,1024]{3,2,1,0:T(8,128)(2,1)} %cache_ref.1) | copy-start | bytes 9437188
  23.4 4.6 %copy-start.1 = (bf16[8,8192]{1,0:T(8,128)(2,1)S(1)}, bf16[8,8192]{1,0:T(8,128)(2,1)}, u32[]{:S(2)}) copy-start(bf16[8,8192]{1,0:T(8,128)(2,1)} %q_ref.1) | copy-start | bytes 393220
  23.4 4.6 %copy-start.3 = (bf16[8,1024]{1,0:T(8,128)(2,1)S(1)}, bf16[8,1024]{1,0:T(8,128)(2,1)}, u32[]{:S(2)}) copy-start(bf16[8,1024]{1,0:T(8,128)(2,1)} %new_ref.1) | copy-start | bytes 49156
  23.4 4.6 %copy-start.6 = (s32[1,8]{1,0:T(1,128)S(1)}, s32[1,8]{1,0:T(1,128)}, u32[]{:S(2)}) copy-start(s32[1,8]{1,0:T(1,128)} %param.12) | copy-start | bytes 100
  23.4 16.9 %slice-start.1 = ((s8[6291456]{0:T(1024)(128)(4,1)}), s8[2097152]{0:T(1024)(128)(4,1)S(1)}, s32[]{:S(2)}) async-start(s8[6291456]{0:T(1024)(128)(4,1)} %bitcast.8), calls=%async_computation.1 | async-start | bytes 4194304
  23.5 10.1 %collective-permute-start.8 = (bf16[2,48,768]{2,1,0:T(8,128)(2,1)S(1)}, bf16[2,48,768]{2,1,0:T(8,128)(2,1)S(1)}, u32[]{:S(2)}, u32[]{:S(2)}) collective-permute-start(bf16[2,48,768]{2,1,0:T(8,128)(2,1)S(1)} %gate_up.6.refs_2_), channel_id=1, source_target_pairs={{0,1},{1,0},{2,3},{3,2},{4,5},{5,4},{6,7},{7,6},{8,9},{9,8},{10,11... | collective-permute-start | bytes 442376 | tf_op jit(solution)/shard_map/ppermute | solution.py:360
  35.9 7.0 %collective-permute-start.9 = (bf16[2,48,384]{2,1,0:T(8,128)(2,1)S(1)}, bf16[2,48,384]{2,1,0:T(8,128)(2,1)S(1)}, u32[]{:S(2)}, u32[]{:S(2)}) collective-permute-start(bf16[2,48,384]{2,1,0:T(8,128)(2,1)S(1)} %activate.1.part_ref), channel_id=1, source_target_pairs={{0,3},{1,2},{2,1},{3,0},{4,7},{5,6},{6,5},{7,4},{8,11},{9,10},{10,... | collective-permute-start | bytes 221192 | tf_op jit(solution)/shard_map/ppermute | solution.py:360
  37.4 6.6 %collective-permute-start.10 = (bf16[2,48,384]{2,1,0:T(8,128)(2,1)S(1)}, bf16[2,48,384]{2,1,0:T(8,128)(2,1)S(1)}, u32[]{:S(2)}, u32[]{:S(2)}) collective-permute-start(bf16[2,48,384]{2,1,0:T(8,128)(2,1)S(1)} %activate.1.part_ref), channel_id=1, source_target_pairs={{0,1},{1,0},{2,3},{3,2},{4,5},{5,4},{6,7},{7,6},{8,9},{9,8},{10,11... | collective-permute-start | bytes 221192 | tf_op jit(solution)/shard_map/ppermute | solution.py:360
  37.5 7.0 %collective-permute-start.11 = (bf16[2,48,384]{2,1,0:T(8,128)(2,1)S(1)}, bf16[2,48,384]{2,1,0:T(8,128)(2,1)S(1)}, u32[]{:S(2)}, u32[]{:S(2)}) collective-permute-start(bf16[2,48,384]{2,1,0:T(8,128)(2,1)S(1)} %activate.1.part_ref), channel_id=1, source_target_pairs={{0,2},{1,3},{2,0},{3,1},{4,6},{5,7},{6,4},{7,5},{8,10},{9,11},{10,... | collective-permute-start | bytes 221192 | tf_op jit(solution)/shard_map/ppermute | solution.py:360
  45.0 2.2 %collective-permute-start.12 = (bf16[24,1024]{1,0:T(8,128)(2,1)S(1)}, bf16[24,1024]{1,0:T(8,128)(2,1)S(1)}, u32[]{:S(2)}, u32[]{:S(2)}) collective-permute-start(bf16[24,1024]{1,0:T(8,128)(2,1)S(1)} %get-tuple-element.39), channel_id=1, source_target_pairs={{0,4},{4,0},{8,12},{12,8},{1,5},{5,1},{9,13},{13,9},{2,6},{6,2},{1... | collective-permute-start | bytes 147464 | tf_op jit(solution)/shard_map/ppermute | solution.py:360
  45.1 4.2 %collective-permute-start.13 = (bf16[24,1024]{1,0:T(8,128)(2,1)S(1)}, bf16[24,1024]{1,0:T(8,128)(2,1)S(1)}, u32[]{:S(2)}, u32[]{:S(2)}) collective-permute-start(bf16[24,1024]{1,0:T(8,128)(2,1)S(1)} %get-tuple-element.40), channel_id=1, source_target_pairs={{0,8},{4,12},{8,0},{12,4},{1,9},{5,13},{9,1},{13,5},{2,10},{6,14},... | collective-permute-start | bytes 147464 | tf_op jit(solution)/shard_map/ppermute | solution.py:360
  46.6 3.7 %collective-permute-start.14 = (bf16[24,1024]{1,0:T(8,128)(2,1)S(1)}, bf16[24,1024]{1,0:T(8,128)(2,1)S(1)}, u32[]{:S(2)}, u32[]{:S(2)}) collective-permute-start(bf16[24,1024]{1,0:T(8,128)(2,1)S(1)} %get-tuple-element.41), channel_id=1, source_target_pairs={{0,12},{4,8},{8,4},{12,0},{1,13},{5,9},{9,5},{13,1},{2,14},{6,10},... | collective-permute-start | bytes 147464 | tf_op jit(solution)/shard_map/ppermute | solution.py:360
  50.6 4.5 %collective-permute-start.15 = (bf16[8,1024]{1,0:T(8,128)(2,1)S(1)}, bf16[8,1024]{1,0:T(8,128)(2,1)S(1)}, u32[]{:S(2)}, u32[]{:S(2)}) collective-permute-start(bf16[8,1024]{1,0:T(8,128)(2,1)S(1)} %get-tuple-element.43), channel_id=1, source_target_pairs={{0,1},{1,0},{2,3},{3,2},{4,5},{5,4},{6,7},{7,6},{8,9},{9,8},{10,11... | collective-permute-start | bytes 49160 | tf_op jit(solution)/shard_map/ppermute | solution.py:360
  51.8 4.6 %collective-permute-start.16 = (bf16[8,1024]{1,0:T(8,128)(2,1)S(1)}, bf16[8,1024]{1,0:T(8,128)(2,1)S(1)}, u32[]{:S(2)}, u32[]{:S(2)}) collective-permute-start(bf16[8,1024]{1,0:T(8,128)(2,1)S(1)} %get-tuple-element.44), channel_id=1, source_target_pairs={{0,2},{1,3},{2,0},{3,1},{4,6},{5,7},{6,4},{7,5},{8,10},{9,11},{10,... | collective-permute-start | bytes 49160 | tf_op jit(solution)/shard_map/ppermute | solution.py:360
  53.7 5.5 %collective-permute-start.17 = (bf16[8,1024]{1,0:T(8,128)(2,1)S(1)}, bf16[8,1024]{1,0:T(8,128)(2,1)S(1)}, u32[]{:S(2)}, u32[]{:S(2)}) collective-permute-start(bf16[8,1024]{1,0:T(8,128)(2,1)S(1)} %get-tuple-element.45), channel_id=1, source_target_pairs={{0,3},{1,2},{2,1},{3,0},{4,7},{5,6},{6,5},{7,4},{8,11},{9,10},{10,... | collective-permute-start | bytes 49160 | tf_op jit(solution)/shard_map/ppermute | solution.py:360
